TPU v7x, 32 devices: a whole 2x2x4 slice. The times are simulated.
32 devices in a mesh: dp: 2 (over x), wide: 4 (over y, core), narrow: 4 (over z).
Axes of the slice: x: 2, y: 2, z: 4, core: 2. Of those that a mesh axis runs over, the one named last changes fastest.
Arguments:
- out_grad: bfloat16 [512, 2048], P(('dp', 'wide', 'narrow')), may hold values from -6 to 6
- routes: int32 [512, 8], P(('dp', 'wide', 'narrow')), may hold values from 0 to 15, as said below
- gates: bfloat16 [512, 8], P(('dp', 'wide', 'narrow')), may hold values from 0.029907227 to 0.59765625
- pre_gate: bfloat16 [2, 16, 256, 768], P('dp', ('wide', 'narrow')), may hold values from -5 to 5
- pre_up: bfloat16 [2, 16, 256, 768], P('dp', ('wide', 'narrow')), may hold values from -5 to 5
- down_weight: bfloat16 [16, 768, 2048], P(('wide', 'narrow')), may hold values from -0.125 to 0.125
Outputs:
- grad_down: bfloat16 [16, 768, 2048], P(('wide', 'narrow'), None, 'dp')
- grad_pre_gate: bfloat16 [2, 16, 256, 768], P('dp', ('wide', 'narrow'))
- grad_pre_up: bfloat16 [2, 16, 256, 768], P('dp', ('wide', 'narrow'))
- grad_gates: float32 [512, 8], P(('dp', 'wide', 'narrow'))
Inputs may be any that keep to these rules, and one draw needn't show every extreme that they name: `routes`: each token names 8 different experts. The tokens of one device name each expert either 0 or 16 times. In every group some expert is named 16 times by every device of the group.
All inputs are finite; a program needn't handle non-finite values.
Results may differ from a plain program's by a relative error of at most 0.012.
Values may be sent and summed in bfloat16 or wider, within the bound.
No kernel may reach another device: no remote copies, remote signals or barrier semaphores. Data moves between devices by JAX's collectives and lax.ppermute only.
A program may use at most 64 MiB of HBM per device.

v0:
```python
import jax
import jax.numpy as jnp
from jax import lax
from jax.sharding import PartitionSpec as P


def shards(out_grad, routes, gates, pre_gate, pre_up, down_weight):
    wide_count = lax.axis_size("wide")
    narrow_count = lax.axis_size("narrow")
    experts = wide_count * narrow_count
    token_count, top_count = routes.shape
    slot_count = pre_gate.shape[2]
    capacity = slot_count // experts
    expert_ids = jnp.arange(experts, dtype=jnp.int32)
    named_hits = (routes[:, :, None] == expert_ids[None, None, :]).astype(jnp.int32)
    hit_counts = jnp.sum(named_hits, axis=1)
    before = jnp.cumsum(hit_counts, axis=0) - hit_counts
    position = jnp.sum(named_hits * before[:, None, :], axis=2)
    target = routes * capacity + position
    slot_ids = jnp.arange(slot_count, dtype=jnp.int32)
    placed = target[:, :, None] == slot_ids[None, None, :]
    choose = jnp.sum(placed.astype(jnp.bfloat16), axis=1)
    outgoing = lax.dot_general(
        choose, out_grad, (((0,), (0,)), ((), ())), preferred_element_type=jnp.float32
    ).astype(jnp.bfloat16)
    gate_out = jnp.sum(
        jnp.where(placed, gates[:, :, None].astype(jnp.float32), 0.0), axis=(0, 1)
    ).astype(jnp.bfloat16)
    outgoing = outgoing.reshape(wide_count, narrow_count, capacity, outgoing.shape[1])
    gate_out = gate_out.reshape(wide_count, narrow_count, capacity)
    incoming, gate_in = (
        lax.all_to_all(
            lax.all_to_all(outgoing, "wide", split_axis=0, concat_axis=0, tiled=True),
            "narrow",
            split_axis=1,
            concat_axis=1,
            tiled=True,
        ),
        lax.all_to_all(
            lax.all_to_all(gate_out, "wide", split_axis=0, concat_axis=0, tiled=True),
            "narrow",
            split_axis=1,
            concat_axis=1,
            tiled=True,
        ),
    )
    routed_rows = incoming.reshape(slot_count, incoming.shape[3])
    gate_col = gate_in.reshape(slot_count).astype(jnp.float32)
    gate_pre = pre_gate[0, 0].astype(jnp.float32)
    up_pre = pre_up[0, 0].astype(jnp.float32)
    weight = down_weight[0]
    sigmoid_a = jax.nn.sigmoid(gate_pre)
    hidden = (gate_pre * sigmoid_a * up_pre).astype(jnp.bfloat16)
    back_prop = lax.dot_general(
        routed_rows, weight, (((1,), (1,)), ((), ())), preferred_element_type=jnp.float32
    )
    slot_grad = jnp.sum(hidden.astype(jnp.float32) * back_prop, axis=1)
    carried = gate_col[:, None] * back_prop
    grad_a = (carried * up_pre * sigmoid_a * (1.0 + gate_pre * (1.0 - sigmoid_a))).astype(
        jnp.bfloat16
    )
    grad_b = (carried * gate_pre * sigmoid_a).astype(jnp.bfloat16)
    scaled = (gate_col[:, None] * hidden.astype(jnp.float32)).astype(jnp.bfloat16)
    all_scaled = lax.all_gather(scaled, "dp", axis=0, tiled=True)
    columns = lax.all_to_all(routed_rows, "dp", split_axis=1, concat_axis=0, tiled=True)
    grad_down = lax.dot_general(
        all_scaled, columns, (((0,), (0,)), ((), ())), preferred_element_type=jnp.float32
    ).astype(jnp.bfloat16)
    slot_back = slot_grad.reshape(wide_count, narrow_count, capacity)
    returned = lax.all_to_all(
        lax.all_to_all(slot_back, "wide", split_axis=0, concat_axis=0, tiled=True),
        "narrow",
        split_axis=1,
        concat_axis=1,
        tiled=True,
    )
    grad_gates = jnp.take(returned.reshape(slot_count), target.reshape(-1)).reshape(
        token_count, top_count
    )
    return (grad_down[None], grad_a[None, None], grad_b[None, None], grad_gates)


def solution(mesh):
    placed = (
        P(("dp", "wide", "narrow"), None),
        P(("dp", "wide", "narrow"), None),
        P(("dp", "wide", "narrow"), None),
        P("dp", ("wide", "narrow"), None, None),
        P("dp", ("wide", "narrow"), None, None),
        P(("wide", "narrow"), None, None),
    )
    return jax.shard_map(
        shards,
        mesh=mesh,
        in_specs=placed,
        out_specs=(
            P(("wide", "narrow"), None, "dp"),
            P("dp", ("wide", "narrow"), None, None),
            P("dp", ("wide", "narrow"), None, None),
            P(("dp", "wide", "narrow"), None),
        ),
        check_vma=False,
    )
```

profile of v0, /device:TPU:0, one launch (start us, length us, event | category | flops | bytes accessed | tf_op | source)
XLA Modules:
  0.0 125.8 jit_solution(14458384854052510292)
XLA Ops:
  0.6 0.0 copy-start
  0.6 0.9 copy.54
  1.6 0.1 convert_reduce_fusion
  1.7 0.4 select_reduce_fusion.1
  2.1 0.8 copy.56
  2.9 0.1 select_reduce_fusion
  3.0 0.7 convert_element_type.66
  3.7 4.2 %all-to-all-start = ((bf16[4,4,16]{2,1,0:T(4,128)(2,1)}), bf16[4,4,16]{2,1,0:T(4,128)(2,1)S(1)}, u32[]{:S(2)}, u32[]{:S(2)}) async-start(bf16[4,4,16]{2,1,0:T(4,128)(2,1)} %convert_element_type.66), calls=%async_computation | async-start | bytes 8192 | tf_op jit(solution)/shard_map/all_to_all | solution.py:40
  7.9 0.1 fusion.18
  8.0 2.3 %convolution_convert_fusion = bf16[256,2048]{1,0:T(8,128)(2,1)} fusion(bf16[16,256]{1,0:T(8,128)(2,1)S(1)} %fusion.18, bf16[16,2048]{1,0:T(8,128)(2,1)} %param.6), kind=kOutput, calls=%fused_computation.3 | convolution fusion | flops 17301504 | bytes 1122304 | tf_op jit(solution)/shard_map/dot_general | solution.py:23
  10.3 1.4 %all-to-all-done = bf16[4,4,16]{2,1,0:T(4,128)(2,1)S(1)} async-done(((bf16[4,4,16]{2,1,0:T(4,128)(2,1)}), bf16[4,4,16]{2,1,0:T(4,128)(2,1)S(1)}, u32[]{:S(2)}, u32[]{:S(2)}) %all-to-all-start) | async-done | bytes 544 | tf_op jit(solution)/shard_map/all_to_all | solution.py:40
  11.7 4.2 %all-to-all-start.2 = ((bf16[4,4,16,2048]{3,2,1,0:T(8,128)(2,1)}), bf16[4,4,16,2048]{3,2,1,0:T(8,128)(2,1)}, u32[]{:S(2)}, u32[]{:S(2)}) async-start(bf16[4,4,16,2048]{3,2,1,0:T(8,128)(2,1)} %bitcast.43), calls=%async_computation.2 | async-start | bytes 2097152 | tf_op jit(solution)/shard_map/all_to_all | solution.py:33
  16.0 0.6 copy.57
  16.6 13.9 %all-to-all-done.2 = bf16[4,4,16,2048]{3,2,1,0:T(8,128)(2,1)} async-done(((bf16[4,4,16,2048]{3,2,1,0:T(8,128)(2,1)}), bf16[4,4,16,2048]{3,2,1,0:T(8,128)(2,1)}, u32[]{:S(2)}, u32[]{:S(2)}) %all-to-all-start.2) | async-done | bytes 1048608 | tf_op jit(solution)/shard_map/all_to_all | solution.py:33
  30.5 5.3 %all-to-all-start.1 = ((bf16[4,4,16]{2,0,1:T(4,128)(2,1)}), bf16[4,4,16]{2,0,1:T(4,128)(2,1)S(1)}, u32[]{:S(2)}, u32[]{:S(2)}) async-start(bf16[4,4,16]{2,0,1:T(4,128)(2,1)} %copy.57), calls=%async_computation.1 | async-start | bytes 8192 | tf_op jit(solution)/shard_map/all_to_all | solution.py:39
  35.8 2.3 %copy.59 = bf16[4,4,16,2048]{3,2,0,1:T(8,128)(2,1)} copy(bf16[4,4,16,2048]{3,2,1,0:T(8,128)(2,1)} %all-to-all-done.2) | data formatting | bytes 2097152 | tf_op jit(solution)/shard_map/all_to_all | solution.py:33
  38.1 3.3 %all-to-all-done.1 = bf16[4,4,16]{2,0,1:T(4,128)(2,1)S(1)} async-done(((bf16[4,4,16]{2,0,1:T(4,128)(2,1)}), bf16[4,4,16]{2,0,1:T(4,128)(2,1)S(1)}, u32[]{:S(2)}, u32[]{:S(2)}) %all-to-all-start.1) | async-done | bytes 544 | tf_op jit(solution)/shard_map/all_to_all | solution.py:39
  41.4 4.2 %all-to-all-start.3 = ((bf16[4,4,16,2048]{3,2,0,1:T(8,128)(2,1)}), bf16[4,4,16,2048]{3,2,0,1:T(8,128)(2,1)}, u32[]{:S(2)}, u32[]{:S(2)}) async-start(bf16[4,4,16,2048]{3,2,0,1:T(8,128)(2,1)} %copy.59), calls=%async_computation.3 | async-start | bytes 2097152 | tf_op jit(solution)/shard_map/all_to_all | solution.py:32
  45.6 0.6 reshape.95
  46.2 0.1 reshape.96
  46.3 0.0 copy-start.2
  46.3 23.7 %all-to-all-done.3 = bf16[4,4,16,2048]{3,2,0,1:T(8,128)(2,1)} async-done(((bf16[4,4,16,2048]{3,2,0,1:T(8,128)(2,1)}), bf16[4,4,16,2048]{3,2,0,1:T(8,128)(2,1)}, u32[]{:S(2)}, u32[]{:S(2)}) %all-to-all-start.3) | async-done | bytes 1048608 | tf_op jit(solution)/shard_map/all_to_all | solution.py:32
  70.0 1.3 %copy.60 = bf16[4,4,16,2048]{3,2,1,0:T(8,128)(2,1)S(1)} copy(bf16[4,4,16,2048]{3,2,0,1:T(8,128)(2,1)} %all-to-all-done.3) | data formatting | bytes 2097152 | tf_op jit(solution)/shard_map/all_to_all | solution.py:32
  71.3 0.0 copy-start.1
  71.3 0.0 copy-done
  71.4 4.0 %fusion.4 = (f32[256]{0:T(256)S(1)}, bf16[256,768]{1,0:T(8,128)(2,1)S(1)}, bf16[1,1,256,768]{3,2,1,0:T(8,128)(2,1)}, bf16[1,1,256,768]{3,2,1,0:T(8,128)(2,1)}) fusion(bf16[1,1,256,768]{3,2,1,0:T(8,128)(2,1)} %param.10, bf16[1,1,256,768]{3,2,1,0:T(8,128)(2,1)} %param.9, f32[256]{0:T(256)S(1)} %reshape.96, bf16[256,2048]{1,0:T(8,128)(2,1)S(1)} %bitcast.42, ...), kind=kOutput, calls=%fused_computation.15 | convolution fusion | flops 809631488 | bytes 6162432 | tf_op jit(solution)/shard_map/dot_general | solution.py:54
  75.3 0.0 copy-done.2
  75.3 0.0 copy-done.1
  75.3 0.7 reshape.93
  76.0 3.2 %all-to-all-start.5 = ((f32[4,4,16]{2,1,0:T(4,128)}), f32[4,4,16]{2,1,0:T(4,128)S(1)}, u32[]{:S(2)}, u32[]{:S(2)}) async-start(f32[4,4,16]{2,1,0:T(4,128)} %reshape.93), calls=%async_computation.5 | async-start | bytes 16384 | tf_op jit(solution)/shard_map/all_to_all | solution.py:71
  79.3 1.2 fusion.19
  80.5 2.6 %all-to-all-done.5 = f32[4,4,16]{2,1,0:T(4,128)S(1)} async-done(((f32[4,4,16]{2,1,0:T(4,128)}), f32[4,4,16]{2,1,0:T(4,128)S(1)}, u32[]{:S(2)}, u32[]{:S(2)}) %all-to-all-start.5) | async-done | bytes 1056 | tf_op jit(solution)/shard_map/all_to_all | solution.py:71
  83.0 0.6 copy.63
  83.6 3.2 %all-to-all-start.6 = ((f32[4,4,16]{2,0,1:T(4,128)}), f32[4,4,16]{2,0,1:T(4,128)S(1)}, u32[]{:S(2)}, u32[]{:S(2)}) async-start(f32[4,4,16]{2,0,1:T(4,128)} %copy.63), calls=%async_computation.6 | async-start | bytes 16384 | tf_op jit(solution)/shard_map/all_to_all | solution.py:70
  86.9 1.2 pad_clamp_fusion
  88.1 2.6 %all_to_all.36 = bf16[256,2,1024]{2,1,0:T(2,128)(2,1)} reshape(bf16[4,4,16,2048]{3,2,1,0:T(8,128)(2,1)} %copy-done.1) | data formatting | bytes 2097152 | tf_op jit(solution)/shard_map/all_to_all | solution.py:65
  90.7 2.5 %copy.61 = bf16[256,2,1024]{2,0,1:T(8,128)(2,1)} copy(bf16[256,2,1024]{2,1,0:T(2,128)(2,1)} %all_to_all.36) | data formatting | bytes 2097152 | tf_op jit(solution)/shard_map/all_to_all | solution.py:65
  93.2 0.0 all-to-all-done.6
  93.2 4.4 %all-to-all-start.4 = ((bf16[256,2,1024]{2,0,1:T(8,128)(2,1)}), bf16[256,2,1024]{2,0,1:T(8,128)(2,1)}, u32[]{:S(2)}, u32[]{:S(2)}) async-start(bf16[256,2,1024]{2,0,1:T(8,128)(2,1)} %copy.61), calls=%async_computation.4 | async-start | bytes 2097152 | tf_op jit(solution)/shard_map/all_to_all | solution.py:65
  97.6 0.8 fusion.3
  98.4 21.6 %all_gather.3 = bf16[512,768]{1,0:T(8,128)(2,1)} all-gather(bf16[256,768]{1,0:T(8,128)(2,1)S(1)} %fusion.3), channel_id=1, replica_groups=mesh['dp'=2,'wide'=4,'narrow'=4] {'dp'}, dimensions={0}, use_global_device_ids=true | all-gather | bytes 1179648 | tf_op jit(solution)/shard_map/all_gather | solution.py:64
  120.0 0.1 reshape.94
  120.1 1.4 %gather_fusion = f32[128]{0:T(128)S(1)} fusion(f32[256]{0:T(256)S(1)} %reshape.94, s32[1024]{0:T(1024)} %pad_clamp_fusion), kind=kCustom, calls=%fused_computation | custom fusion | bytes 1536 | tf_op jit(solution)/shard_map/jit(_take)/gather | solution.py:77
  121.5 0.1 gather.7
  121.6 0.7 copy.65
  122.2 0.0 all-to-all-done.4
  122.2 3.6 %fusion.2 = bf16[1,768,1024]{2,1,0:T(8,128)(2,1)} fusion(bf16[512,768]{1,0:T(8,128)(2,1)} %all_gather.3, bf16[512,1024]{1,0:T(8,128)(2,1)} %bitcast.5), kind=kOutput, calls=%fused_computation.5 | convolution fusion | flops 806092800 | bytes 3407872 | tf_op jit(solution)/shard_map/dot_general | solution.py:66
  (6 shorter events, 0.1 us)
Async XLA Ops:
  0.6 70.7 %copy-start = (bf16[1,768,2048]{2,1,0:T(8,128)(2,1)S(1)}, bf16[1,768,2048]{2,1,0:T(8,128)(2,1)}, u32[]{:S(2)}) copy-start(bf16[1,768,2048]{2,1,0:T(8,128)(2,1)} %param.11) | copy-start | bytes 9437188
  3.7 8.0 %all-to-all-start = ((bf16[4,4,16]{2,1,0:T(4,128)(2,1)}), bf16[4,4,16]{2,1,0:T(4,128)(2,1)S(1)}, u32[]{:S(2)}, u32[]{:S(2)}) async-start(bf16[4,4,16]{2,1,0:T(4,128)(2,1)} %convert_element_type.66), calls=%async_computation | async-start | bytes 8192 | tf_op jit(solution)/shard_map/all_to_all | solution.py:40
  11.7 18.8 %all-to-all-start.2 = ((bf16[4,4,16,2048]{3,2,1,0:T(8,128)(2,1)}), bf16[4,4,16,2048]{3,2,1,0:T(8,128)(2,1)}, u32[]{:S(2)}, u32[]{:S(2)}) async-start(bf16[4,4,16,2048]{3,2,1,0:T(8,128)(2,1)} %bitcast.43), calls=%async_computation.2 | async-start | bytes 2097152 | tf_op jit(solution)/shard_map/all_to_all | solution.py:33
  30.5 10.9 %all-to-all-start.1 = ((bf16[4,4,16]{2,0,1:T(4,128)(2,1)}), bf16[4,4,16]{2,0,1:T(4,128)(2,1)S(1)}, u32[]{:S(2)}, u32[]{:S(2)}) async-start(bf16[4,4,16]{2,0,1:T(4,128)(2,1)} %copy.57), calls=%async_computation.1 | async-start | bytes 8192 | tf_op jit(solution)/shard_map/all_to_all | solution.py:39
  41.4 28.7 %all-to-all-start.3 = ((bf16[4,4,16,2048]{3,2,0,1:T(8,128)(2,1)}), bf16[4,4,16,2048]{3,2,0,1:T(8,128)(2,1)}, u32[]{:S(2)}, u32[]{:S(2)}) async-start(bf16[4,4,16,2048]{3,2,0,1:T(8,128)(2,1)} %copy.59), calls=%async_computation.3 | async-start | bytes 2097152 | tf_op jit(solution)/shard_map/all_to_all | solution.py:32
  46.3 29.0 %copy-start.2 = (f32[256]{0:T(256)}, f32[256]{0:T(256)S(1)}, u32[]{:S(2)}) copy-start(f32[256]{0:T(256)S(1)} %reshape.96) | copy-start | bytes 3076
  71.3 4.0 %copy-start.1 = (bf16[4,4,16,2048]{3,2,1,0:T(8,128)(2,1)}, bf16[4,4,16,2048]{3,2,1,0:T(8,128)(2,1)S(1)}, u32[]{:S(2)}) copy-start(bf16[4,4,16,2048]{3,2,1,0:T(8,128)(2,1)S(1)} %copy.60) | copy-start | bytes 3145732
  76.0 7.0 %all-to-all-start.5 = ((f32[4,4,16]{2,1,0:T(4,128)}), f32[4,4,16]{2,1,0:T(4,128)S(1)}, u32[]{:S(2)}, u32[]{:S(2)}) async-start(f32[4,4,16]{2,1,0:T(4,128)} %reshape.93), calls=%async_computation.5 | async-start | bytes 16384 | tf_op jit(solution)/shard_map/all_to_all | solution.py:71
  83.6 9.6 %all-to-all-start.6 = ((f32[4,4,16]{2,0,1:T(4,128)}), f32[4,4,16]{2,0,1:T(4,128)S(1)}, u32[]{:S(2)}, u32[]{:S(2)}) async-start(f32[4,4,16]{2,0,1:T(4,128)} %copy.63), calls=%async_computation.6 | async-start | bytes 16384 | tf_op jit(solution)/shard_map/all_to_all | solution.py:70
  93.2 29.0 %all-to-all-start.4 = ((bf16[256,2,1024]{2,0,1:T(8,128)(2,1)}), bf16[256,2,1024]{2,0,1:T(8,128)(2,1)}, u32[]{:S(2)}, u32[]{:S(2)}) async-start(bf16[256,2,1024]{2,0,1:T(8,128)(2,1)} %copy.61), calls=%async_computation.4 | async-start | bytes 2097152 | tf_op jit(solution)/shard_map/all_to_all | solution.py:65
where the time goes:
time: 127 us; the launch traced here: 126 us
  waiting for transfers between devices  44.9 us (35%)
  starting transfers between devices  28.9 us (23%)
  blocking collectives  21.6 us (17%)
  local copies, waits for them, and re-layouts  15.8 us (12%)
  matrix products  9.86 us (8%)
  other arithmetic  3.99 us (3%)
    all_to_all x1, waiting for transfers between devices, shards(): lax.all_to_all(lax.all_to_all(outgoing, 'wide', split_axis=0, concat_axis...  23.7 us
    all_gather x1, blocking collectives, shards(): all_scaled = lax.all_gather(scaled, 'dp', axis=0, tiled=True)  21.6 us
    all_to_all x1, waiting for transfers between devices, shards(): lax.all_to_all(outgoing, 'wide', split_axis=0, concat_axis=0, tiled=True)  13.9 us
    all_to_all x1, starting transfers between devices, shards(): lax.all_to_all(lax.all_to_all(gate_out, 'wide', split_axis=0, concat_axis...  5.3 us
    all_to_all x2, local copies, waits for them, and re-layouts, shards(): lax.all_to_all(routed_rows, 'dp', split_axis=1, concat_axis=0, tiled=True)  5.09 us
    all_to_all x1, starting transfers between devices, shards(): lax.all_to_all(routed_rows, 'dp', split_axis=1, concat_axis=0, tiled=True)  4.4 us
    all_to_all x1, starting transfers between devices, shards(): lax.all_to_all(outgoing, 'wide', split_axis=0, concat_axis=0, tiled=True)  4.24 us
    all_to_all x1, starting transfers between devices, shards(): lax.all_to_all(lax.all_to_all(outgoing, 'wide', split_axis=0, concat_axis...  4.24 us
  transfers between devices with their start and end apart: 7, of which 5 were waited for; matrix products, arithmetic and copies ran while one was open for 11% of the time, Pallas kernels for 0%

commit v1 on v0

--- a/solution.py
+++ b/solution.py
@@ -1,10 +1,17 @@
+import functools
+
 import jax
 import jax.numpy as jnp
 from jax import lax
+from jax.experimental import pallas as pl
+from jax.experimental.pallas import tpu as pltpu
 from jax.sharding import PartitionSpec as P
 
-
-def shards(out_grad, routes, gates, pre_gate, pre_up, down_weight):
+LANES = 128
+VMEM_LIMIT = 48 * 1024 * 1024
+
+
+def shards_exchange(out_grad, routes, gates, pre_gate, pre_up, down_weight):
     wide_count = lax.axis_size("wide")
     narrow_count = lax.axis_size("narrow")
     experts = wide_count * narrow_count
@@ -80,6 +87,267 @@
     return (grad_down[None], grad_a[None, None], grad_b[None, None], grad_gates)
 
 
+def swap(x, axis, bits):
+    count = lax.axis_size(axis)
+    return lax.ppermute(x, axis, [(i, i ^ bits) for i in range(count)])
+
+
+def call(kernel, outs, cost, *args):
+    flops, moved = cost
+    return pl.pallas_call(
+        kernel,
+        out_shape=outs,
+        in_specs=[pl.BlockSpec(memory_space=pltpu.VMEM)] * len(args),
+        out_specs=jax.tree.map(lambda _: pl.BlockSpec(memory_space=pltpu.VMEM), outs),
+        compiler_params=pltpu.CompilerParams(vmem_limit_bytes=VMEM_LIMIT),
+        cost_estimate=pl.CostEstimate(flops=flops, bytes_accessed=moved, transcendentals=0),
+    )(*args)
+
+
+def peer(xors):
+    wide_bits, narrow_bits = xors
+    return (lax.axis_index("wide") ^ wide_bits) * lax.axis_size("narrow") + (
+        lax.axis_index("narrow") ^ narrow_bits
+    )
+
+
+def payload_kernel(grad_ref, routes_ref, gates_ref, out_ref):
+    features = grad_ref.shape[1]
+    rows = grad_ref.shape[0]
+    out_ref[:, :features] = grad_ref[...]
+    routes = routes_ref[...]
+    gates = gates_ref[...].astype(jnp.float32)
+    ids = lax.broadcasted_iota(jnp.int32, (LANES, rows), 0)
+    table = jnp.zeros((LANES, rows), jnp.float32)
+    for k in range(routes.shape[0]):
+        table = table + jnp.where(ids == routes[k : k + 1, :], gates[k : k + 1, :], 0.0)
+    table = jnp.concatenate([table, jnp.zeros((LANES, LANES - rows), jnp.float32)], axis=1)
+    out_ref[:, features:] = table.T[:rows, :].astype(out_ref.dtype)
+
+
+def hidden_kernel(order, rows, pre_gate_ref, pre_up_ref, out_ref):
+    for place, xors in enumerate(order):
+        source = pl.ds(pl.multiple_of(peer(xors) * rows, rows), rows)
+        value = pre_gate_ref[source, :].astype(jnp.float32)
+        up = pre_up_ref[source, :].astype(jnp.float32)
+        out_ref[place * rows : (place + 1) * rows, :] = (
+            value * jax.nn.sigmoid(value) * up
+        ).astype(out_ref.dtype)
+
+
+def back_kernel(features, half_ref, rest_ref, weight_ref, hidden_ref, back_ref, sums_ref):
+    rows = half_ref.shape[0]
+    for part, ref in enumerate((half_ref, rest_ref)):
+        here = slice(part * rows, (part + 1) * rows)
+        back = lax.dot_general(
+            ref[:, :features],
+            weight_ref[...],
+            (((1,), (1,)), ((), ())),
+            preferred_element_type=jnp.float32,
+        )
+        back_ref[here, :] = back
+        product = hidden_ref[here, :].astype(jnp.float32) * back
+        folded = product[:, :LANES]
+        for at in range(LANES, product.shape[1], LANES):
+            folded = folded + product[:, at : at + LANES]
+        for at in range(0, rows, LANES):
+            row = (part * rows + at) // LANES
+            sums_ref[row : row + 1, :] = jnp.sum(
+                folded[at : at + LANES, :].T, axis=0, keepdims=True
+            )
+
+
+def own_gates(table):
+    lane = lax.broadcasted_iota(jnp.int32, table.shape, 1)
+    return jnp.sum(
+        jnp.where(lane == peer((0, 0)), table.astype(jnp.float32), 0.0), axis=1, keepdims=True
+    )
+
+
+def grads_kernel(
+    order,
+    rows,
+    features,
+    half_ref,
+    rest_ref,
+    back_ref,
+    hidden_ref,
+    pre_gate_ref,
+    pre_up_ref,
+    grad_gate_ref,
+    grad_up_ref,
+    scaled_ref,
+):
+    per = half_ref.shape[0] // rows
+    for place, xors in enumerate(order):
+        ref = (half_ref, rest_ref)[place // per]
+        start = (place % per) * rows
+        gate = own_gates(ref[start : start + rows, features:])
+        here = slice(place * rows, (place + 1) * rows)
+        source = pl.ds(pl.multiple_of(peer(xors) * rows, rows), rows)
+        value = pre_gate_ref[source, :].astype(jnp.float32)
+        up = pre_up_ref[source, :].astype(jnp.float32)
+        sig = jax.nn.sigmoid(value)
+        carried = gate * back_ref[here, :]
+        grad_gate_ref[source, :] = (carried * up * sig * (1.0 + value * (1.0 - sig))).astype(
+            grad_gate_ref.dtype
+        )
+        grad_up_ref[source, :] = (carried * value * sig).astype(grad_up_ref.dtype)
+        scaled_ref[here, :] = (gate * hidden_ref[here, :].astype(jnp.float32)).astype(
+            scaled_ref.dtype
+        )
+
+
+def down_kernel(pairs, scaled_ref, half_ref, rest_ref, *refs):
+    out_ref = refs[-1]
+    columns = out_ref.shape[1]
+    rows = half_ref.shape[0]
+    contract = (((0,), (0,)), ((), ()))
+    mine = pl.ds(pl.multiple_of(lax.axis_index("dp") * columns, columns), columns)
+    scaled = [scaled_ref[...]]
+    tokens = [half_ref[:, mine], rest_ref[:, mine]]
+    for pair in range(pairs):
+        hidden_ref, one_ref, two_ref = refs[3 * pair : 3 * pair + 3]
+        gate = jnp.concatenate(
+            [own_gates(one_ref[:, columns:]), own_gates(two_ref[:, columns:])], axis=0
+        )
+        scaled.append((gate * hidden_ref[...].astype(jnp.float32)).astype(scaled_ref.dtype))
+        tokens += [one_ref[:, :columns], two_ref[:, :columns]]
+    out_ref[...] = lax.dot_general(
+        jnp.concatenate(scaled, axis=0),
+        jnp.concatenate(tokens, axis=0),
+        contract,
+        preferred_element_type=jnp.float32,
+    ).astype(out_ref.dtype)
+
+
+def pick_kernel(order, back_order, rows, routes_ref, sums_ref, out_ref):
+    routes = routes_ref[...]
+    total = jnp.zeros(out_ref.shape, jnp.float32)
+    for line, xors in enumerate(back_order):
+        start = order.index(xors) * rows
+        at = start % LANES
+        found = sums_ref[line, start // LANES : start // LANES + 1, :][:, at : at + rows]
+        total = total + jnp.where(routes == peer(xors), found, 0.0)
+    out_ref[...] = total
+
+
+def shards_gather(out_grad, routes, gates, pre_gate, pre_up, down_weight):
+    dp_count = lax.axis_size("dp")
+    wide_count = lax.axis_size("wide")
+    narrow_count = lax.axis_size("narrow")
+    rows, features = out_grad.shape
+    slot_count, units = pre_gate.shape[2:]
+    columns = features // dp_count
+    routes_t = routes.T
+    gates_t = gates.T
+    pre_gate = pre_gate[0, 0]
+    pre_up = pre_up[0, 0]
+    weight = down_weight[0]
+    bf16, f32 = jnp.bfloat16, jnp.float32
+    shape = jax.ShapeDtypeStruct
+
+    payload = call(
+        payload_kernel,
+        shape((rows, features + LANES), bf16),
+        (rows * features, 4 * rows * features),
+        out_grad,
+        routes_t,
+        gates_t,
+    )
+    held = jnp.concatenate(
+        [payload] + [swap(payload, "narrow", bits) for bits in range(1, narrow_count)], axis=0
+    )
+    order = [(0, bits) for bits in range(narrow_count)]
+    wide_bits = [1 << b for b in range(1, wide_count.bit_length() - 1)]
+    for bits in wide_bits:
+        held = jnp.concatenate([held, swap(held, "wide", bits)], axis=0)
+        order += [(w ^ bits, n) for w, n in order]
+    rest = swap(held, "wide", 1)
+    order += [(w ^ 1, n) for w, n in order]
+    order = tuple(order)
+
+    hidden = call(
+        functools.partial(hidden_kernel, order, rows),
+        shape((slot_count, units), bf16),
+        (20 * slot_count * units, 6 * slot_count * units),
+        pre_gate,
+        pre_up,
+    )
+    others = []
+    for bits in range(1, dp_count):
+        partner = lax.axis_index("dp") ^ bits
+        cut = lax.dynamic_slice_in_dim(held[:, :features], partner * columns, columns, axis=1)
+        one = swap(jnp.concatenate([cut, held[:, features:]], axis=1), "dp", bits)
+        others += [swap(hidden, "dp", bits), one, swap(one, "wide", 1)]
+
+    back, sums = call(
+        functools.partial(back_kernel, features),
+        (shape((slot_count, units), f32), shape((slot_count // LANES, LANES), f32)),
+        (2 * slot_count * units * features, 2 * units * features),
+        held,
+        rest,
+        weight,
+        hidden,
+    )
+    grad_a, grad_b, scaled = call(
+        functools.partial(grads_kernel, order, rows, features),
+        (shape((slot_count, units), bf16),) * 3,
+        (30 * slot_count * units, 12 * slot_count * units),
+        held,
+        rest,
+        back,
+        hidden,
+        pre_gate,
+        pre_up,
+    )
+    grad_down = call(
+        functools.partial(down_kernel, dp_count - 1),
+        shape((units, columns), bf16),
+        (2 * dp_count * slot_count * units * columns, 4 * units * columns),
+        scaled,
+        held,
+        rest,
+        *others,
+    )
+    found = sums[None]
+    back_order = [(0, 0)]
+    for axis, bits in (
+        [("wide", 1)]
+        + [("wide", b) for b in wide_bits]
+        + [("narrow", 1 << b) for b in range(narrow_count.bit_length() - 1)]
+    ):
+        found = jnp.concatenate([found, swap(found, axis, bits)], axis=0)
+        step = (bits, 0) if axis == "wide" else (0, bits)
+        back_order += [(w ^ step[0], n ^ step[1]) for w, n in back_order]
+    picked = call(
+        functools.partial(pick_kernel, order, tuple(back_order), rows),
+        shape(routes_t.shape, f32),
+        (slot_count, slot_count),
+        routes_t,
+        found,
+    )
+    return (grad_down[None], grad_a[None, None], grad_b[None, None], picked.T)
+
+
+def shards(out_grad, routes, gates, pre_gate, pre_up, down_weight):
+    wide_count = lax.axis_size("wide")
+    narrow_count = lax.axis_size("narrow")
+    experts = wide_count * narrow_count
+    rows = out_grad.shape[0]
+    slot_count = pre_gate.shape[2]
+    whole_blocks = (
+        slot_count == experts * rows
+        and wide_count > 1
+        and all(n & (n - 1) == 0 for n in (lax.axis_size("dp"), wide_count, narrow_count))
+        and experts <= LANES
+        and LANES % rows == 0
+        and (slot_count // 2) % LANES == 0
+    )
+    plan = shards_gather if whole_blocks else shards_exchange
+    return plan(out_grad, routes, gates, pre_gate, pre_up, down_weight)
+
+
 def solution(mesh):
     placed = (
         P(("dp", "wide", "narrow"), None),

time: 127 us -> 52.3 us (0.41)
  blocking collectives: 21.6 us -> 0 us
  starting transfers between devices: 28.9 us -> 12.2 us
  waiting for transfers between devices: 44.9 us -> 29.8 us
  local copies, waits for them, and re-layouts: 15.8 us -> 2.46 us
  matrix products: 9.86 us -> 0 us
  Pallas kernels: 0 us -> 6.85 us
  other arithmetic: 3.99 us -> 0.06 us
    all_to_all x7 -> x0, waiting for transfers between devices: 44.9 us -> none  [the longest x1 23.7 us: shards(): lax.all_to_all(lax.all_to_all(outgoing, 'wide', split_axis=0, concat_axis...]
    ppermute x0 -> x12, waiting for transfers between devices: none -> 29.8 us  [swap(): return lax.ppermute(x, axis, [(i, i ^ bits) for i in range(count)])]
    all_to_all x7 -> x0, starting transfers between devices: 28.9 us -> none  [the longest x1 5.3 us: shards(): lax.all_to_all(lax.all_to_all(gate_out, 'wide', split_axis=0, concat_axis...]
    all_gather x1 -> x0, blocking collectives: 21.6 us -> none  [shards(): all_scaled = lax.all_gather(scaled, 'dp', axis=0, tiled=True)]
    ppermute x0 -> x12, starting transfers between devices: none -> 12.2 us  [swap(): return lax.ppermute(x, axis, [(i, i ^ bits) for i in range(count)])]
    all_to_all x7 -> x0, local copies, waits for them, and re-layouts: 9.89 us -> none  [the longest x2 5.09 us: shards(): lax.all_to_all(routed_rows, 'dp', split_axis=1, concat_axis=0, tiled=True)]
    dot_general x3 -> x0, matrix products: 9.86 us -> none  [the longest x1 3.98 us: shards(): lax.dot_general(routed_rows, weight, (((1,), (1,)), ((), ())), preferred_...]
    pallas_call x0 -> x6, Pallas kernels: none -> 6.85 us  [call(): pl.pallas_call(kernel, out_shape=outs, in_specs=[pl.BlockSpec(memory_spac...]
  transfers between devices with their start and end apart: 7 -> 12, of which waited for: 5 -> 8; matrix products, arithmetic and copies ran while one was open for 11% -> 0% of each run, Pallas kernels for 0% -> 9%
where the time goes in v1:
time: 52.3 us; the launch traced here: 52.1 us
  waiting for transfers between devices  29.8 us (57%)
  starting transfers between devices  12.2 us (23%)
  Pallas kernels  6.85 us (13%)
  local copies, waits for them, and re-layouts  2.46 us (5%)
  between operations  0.74 us (1%)
    ppermute x12, waiting for transfers between devices, swap(): return lax.ppermute(x, axis, [(i, i ^ bits) for i in range(count)])  29.8 us
    ppermute x12, starting transfers between devices, swap(): return lax.ppermute(x, axis, [(i, i ^ bits) for i in range(count)])  12.2 us
    pallas_call x6, Pallas kernels, call(): pl.pallas_call(kernel, out_shape=outs, in_specs=[pl.BlockSpec(memory_spac...  6.85 us
    unnamed x22, local copies, waits for them, and re-layouts  2.35 us
  transfers between devices with their start and end apart: 12, of which 8 were waited for; matrix products, arithmetic and copies ran while one was open for 0% of the time, Pallas kernels for 9%

profile of v1, /device:TPU:0, one launch (start us, length us, event | category | flops | bytes accessed | tf_op | source)
XLA Modules:
  0.0 52.1 jit_solution(16461118995010103030)
XLA Ops:
  0.6 0.0 copy-start.2
  0.6 0.0 copy-start.1
  0.7 0.0 copy-start.3
  0.7 0.9 %copy-done.3 = bf16[16,2048]{1,0:T(8,128)(2,1)S(1)} copy-done((bf16[16,2048]{1,0:T(8,128)(2,1)S(1)}, bf16[16,2048]{1,0:T(8,128)(2,1)}, u32[]{:S(2)}) %copy-start.3) | copy-done | bytes 65560
  1.6 0.0 copy-start.4
  1.6 0.7 %copy-done.4 = s32[16,8]{0,1:T(8,128)S(1)} copy-done((s32[16,8]{0,1:T(8,128)S(1)}, s32[16,8]{0,1:T(8,128)}, u32[]{:S(2)}) %copy-start.4) | copy-done | bytes 536
  2.2 0.0 copy-start.6
  2.3 0.7 %copy-done.6 = bf16[16,8]{0,1:T(8,128)(2,1)S(1)} copy-done((bf16[16,8]{0,1:T(8,128)(2,1)S(1)}, bf16[16,8]{0,1:T(8,128)(2,1)}, u32[]{:S(2)}) %copy-start.6) | copy-done | bytes 280
  2.9 0.1 shard_map.93
  3.0 5.1 %collective-permute-start.2 = (bf16[16,2176]{1,0:T(8,128)(2,1)S(1)}, bf16[16,2176]{1,0:T(8,128)(2,1)S(1)}, u32[]{:S(2)}, u32[]{:S(2)}) collective-permute-start(bf16[16,2176]{1,0:T(8,128)(2,1)S(1)} %shard_map.93), channel_id=1, source_target_pairs={{0,3},{1,2},{2,1},{3,0},{4,7},{5,6},{6,5},{7,4},{8,11},{9,10},{10,... | collective-permute-start | bytes 208904 | tf_op jit(solution)/shard_map/ppermute | solution.py:92
  8.1 0.0 collective-permute-start.1
  8.1 0.6 %collective-permute-start = (bf16[16,2176]{1,0:T(8,128)(2,1)S(1)}, bf16[16,2176]{1,0:T(8,128)(2,1)S(1)}, u32[]{:S(2)}, u32[]{:S(2)}) collective-permute-start(bf16[16,2176]{1,0:T(8,128)(2,1)S(1)} %shard_map.93), channel_id=1, source_target_pairs={{0,1},{1,0},{2,3},{3,2},{4,5},{5,4},{6,7},{7,6},{8,9},{9,8},{10,11... | collective-permute-start | bytes 208904 | tf_op jit(solution)/shard_map/ppermute | solution.py:92
  8.8 0.0 copy-start
  8.8 2.0 %collective-permute-done.2 = bf16[16,2176]{1,0:T(8,128)(2,1)S(1)} collective-permute-done((bf16[16,2176]{1,0:T(8,128)(2,1)S(1)}, bf16[16,2176]{1,0:T(8,128)(2,1)S(1)}, u32[]{:S(2)}, u32[]{:S(2)}) %collective-permute-start.2) | collective-permute-done | bytes 69664 | tf_op jit(solution)/shard_map/ppermute | solution.py:92
  10.8 3.2 %collective-permute-done.1 = bf16[16,2176]{1,0:T(8,128)(2,1)S(1)} collective-permute-done((bf16[16,2176]{1,0:T(8,128)(2,1)S(1)}, bf16[16,2176]{1,0:T(8,128)(2,1)S(1)}, u32[]{:S(2)}, u32[]{:S(2)}) %collective-permute-start.1) | collective-permute-done | bytes 69664 | tf_op jit(solution)/shard_map/ppermute | solution.py:92
  14.0 0.0 collective-permute-done
  14.1 1.6 %collective-permute-start.3 = (bf16[64,2176]{1,0:T(8,128)(2,1)S(1)}, bf16[64,2176]{1,0:T(8,128)(2,1)S(1)}, u32[]{:S(2)}, u32[]{:S(2)}) collective-permute-start(bf16[64,2176]{1,0:T(8,128)(2,1)S(1)} %pad_maximum_fusion.1), channel_id=1, source_target_pairs={{0,8},{4,12},{8,0},{12,4},{1,9},{5,13},{9,1},{13,5},{2,10},{6,14},... | collective-permute-start | bytes 835592 | tf_op jit(solution)/shard_map/ppermute | solution.py:92
  15.7 6.6 %collective-permute-done.3 = bf16[64,2176]{1,0:T(8,128)(2,1)S(1)} collective-permute-done((bf16[64,2176]{1,0:T(8,128)(2,1)S(1)}, bf16[64,2176]{1,0:T(8,128)(2,1)S(1)}, u32[]{:S(2)}, u32[]{:S(2)}) %collective-permute-start.3) | collective-permute-done | bytes 278560 | tf_op jit(solution)/shard_map/ppermute | solution.py:92
  22.3 0.1 collective-permute-start.4
  22.5 1.8 %collective-permute-start.6 = (bf16[128,1152]{1,0:T(8,128)(2,1)S(1)}, bf16[128,1152]{1,0:T(8,128)(2,1)S(1)}, u32[]{:S(2)}, u32[]{:S(2)}) collective-permute-start(bf16[128,1152]{1,0:T(8,128)(2,1)S(1)} %pad_maximum_fusion), channel_id=1, source_target_pairs={{0,16},{16,0},{1,17},{17,1},{2,18},{18,2},{3,19},{19,3},{4,20},{20... | collective-permute-start | bytes 884744 | tf_op jit(solution)/shard_map/ppermute | solution.py:92
  24.3 0.0 copy-done.2
  24.3 0.0 copy-done.1
  24.3 0.2 shard_map.94.hidden_ref
  24.5 0.4 collective-permute-start.5
  24.8 7.5 %collective-permute-done.6.refs_1_ = bf16[128,1152]{1,0:T(8,128)(2,1)S(1)} collective-permute-done((bf16[128,1152]{1,0:T(8,128)(2,1)S(1)}, bf16[128,1152]{1,0:T(8,128)(2,1)S(1)}, u32[]{:S(2)}, u32[]{:S(2)}) %collective-permute-start.6) | collective-permute-done | bytes 294944 | tf_op jit(solution)/shard_map/ppermute | solution.py:92
  32.4 0.0 collective-permute-start.7
  32.4 0.0 collective-permute-done.4.rest_ref
  32.4 0.0 copy-done
  32.4 0.0 copy-start.5
  32.4 2.3 %shard_map.95 = (f32[256,768]{1,0:T(8,128)S(1)}, f32[2,128]{1,0:T(2,128)S(1)}) custom-call(bf16[128,2176]{1,0:T(8,128)(2,1)S(1)} %constant_dynamic-update-slice_fusion.half_ref, bf16[128,2176]{1,0:T(8,128)(2,1)S(1)} %collective-permute-done.4.rest_ref, bf16[768,2048]{1,0:T(8,128)(2,1)S(1)} %bitcast.11, bf16[256,768]{1,0:T(8,128)(2,1)S(1)} %shard_map.94.hidden_ref), custom_call_target="tpu_custom_call" | custom-call | flops 805306368 | bytes 3145728 | tf_op jit(solution)/shard_map/pallas_call | solution.py:97
  34.7 0.6 %collective-permute-start.8 = (f32[1,2,128]{2,1,0:T(2,128)S(1)}, f32[1,2,128]{2,1,0:T(2,128)S(1)}, u32[]{:S(2)}, u32[]{:S(2)}) collective-permute-start(f32[1,2,128]{2,1,0:T(2,128)S(1)} %bitcast.18), channel_id=1, source_target_pairs={{0,4},{4,0},{8,12},{12,8},{1,5},{5,1},{9,13},{13,9},{2,6},{6,2},{1... | collective-permute-start | bytes 3080 | tf_op jit(solution)/shard_map/ppermute | solution.py:92
  35.2 0.8 %collective-permute-done.8 = f32[1,2,128]{2,1,0:T(2,128)S(1)} collective-permute-done((f32[1,2,128]{2,1,0:T(2,128)S(1)}, f32[1,2,128]{2,1,0:T(2,128)S(1)}, u32[]{:S(2)}, u32[]{:S(2)}) %collective-permute-start.8) | collective-permute-done | bytes 1056 | tf_op jit(solution)/shard_map/ppermute | solution.py:92
  36.0 1.7 %collective-permute-start.9 = (f32[2,2,128]{2,1,0:T(2,128)S(1)}, f32[2,2,128]{2,1,0:T(2,128)S(1)}, u32[]{:S(2)}, u32[]{:S(2)}) collective-permute-start(f32[2,2,128]{2,1,0:T(2,128)S(1)} %pad_maximum_fusion.4), channel_id=1, source_target_pairs={{0,8},{4,12},{8,0},{12,4},{1,9},{5,13},{9,1},{13,5},{2,10},{6,14},... | collective-permute-start | bytes 6152 | tf_op jit(solution)/shard_map/ppermute | solution.py:92
  37.8 1.8 %collective-permute-done.9 = f32[2,2,128]{2,1,0:T(2,128)S(1)} collective-permute-done((f32[2,2,128]{2,1,0:T(2,128)S(1)}, f32[2,2,128]{2,1,0:T(2,128)S(1)}, u32[]{:S(2)}, u32[]{:S(2)}) %collective-permute-start.9) | collective-permute-done | bytes 2080 | tf_op jit(solution)/shard_map/ppermute | solution.py:92
  39.6 0.2 collective-permute-start.10
  39.8 3.4 %collective-permute-done.10 = f32[4,2,128]{2,1,0:T(2,128)S(1)} collective-permute-done((f32[4,2,128]{2,1,0:T(2,128)S(1)}, f32[4,2,128]{2,1,0:T(2,128)S(1)}, u32[]{:S(2)}, u32[]{:S(2)}) %collective-permute-start.10) | collective-permute-done | bytes 4128 | tf_op jit(solution)/shard_map/ppermute | solution.py:92
  43.2 0.2 collective-permute-start.11
  43.4 4.4 %collective-permute-done.11 = f32[8,2,128]{2,1,0:T(2,128)S(1)} collective-permute-done((f32[8,2,128]{2,1,0:T(2,128)S(1)}, f32[8,2,128]{2,1,0:T(2,128)S(1)}, u32[]{:S(2)}, u32[]{:S(2)}) %collective-permute-start.11) | collective-permute-done | bytes 8224 | tf_op jit(solution)/shard_map/ppermute | solution.py:92
  47.8 1.4 %shard_map.96 = (bf16[256,768]{1,0:T(8,128)(2,1)}, bf16[256,768]{1,0:T(8,128)(2,1)}, bf16[256,768]{1,0:T(8,128)(2,1)S(1)}) custom-call(bf16[128,2176]{1,0:T(8,128)(2,1)S(1)} %constant_dynamic-update-slice_fusion.half_ref, bf16[128,2176]{1,0:T(8,128)(2,1)S(1)} %collective-permute-done.4.rest_ref, f32[256,768]{1,0:T(8,128)S(1)} %get-tuple-element.9.back_ref, ...), custom_call_target="tpu_custom_call" | custom-call | flops 5898240 | bytes 2359296 | tf_op jit(solution)/shard_map/pallas_call | solution.py:97
  49.2 0.0 copy-done.5
  49.2 0.7 %shard_map.98 = f32[8,16]{1,0:T(8,128)} custom-call(s32[8,16]{1,0:T(8,128)S(1)} %bitcast.17, f32[16,2,128]{2,1,0:T(2,128)S(1)} %constant_dynamic-update-slice_fusion.5.sums_ref), custom_call_target="tpu_custom_call" | custom-call | flops 256 | bytes 256 | tf_op jit(solution)/shard_map/pallas_call | solution.py:97
  49.9 0.0 collective-permute-done.5.refs_0_
  49.9 0.0 collective-permute-done.7.refs_2_
  49.9 2.3 %shard_map.97 = bf16[768,1024]{1,0:T(8,128)(2,1)} custom-call(bf16[256,768]{1,0:T(8,128)(2,1)S(1)} %get-tuple-element.10.scaled_ref, bf16[128,2176]{1,0:T(8,128)(2,1)S(1)} %constant_dynamic-update-slice_fusion.half_ref, bf16[128,2176]{1,0:T(8,128)(2,1)S(1)} %collective-permute-done.4.rest_ref, bf16[256,768]{1,0:T(8,128)(2,1)S(1)} %collective-permute-done.5.refs_0_, ...), custom_call_target="tpu_custom_call" | custom-call | flops 805306368 | bytes 3145728 | tf_op jit(solution)/shard_map/pallas_call | solution.py:97
  (18 shorter events, 0.2 us)
Async XLA Ops:
  0.6 23.7 %copy-start.2 = (bf16[1,1,256,768]{3,2,1,0:T(8,128)(2,1)S(1)}, bf16[1,1,256,768]{3,2,1,0:T(8,128)(2,1)}, u32[]{:S(2)}) copy-start(bf16[1,1,256,768]{3,2,1,0:T(8,128)(2,1)} %param.10) | copy-start | bytes 1179652
  0.6 23.6 %copy-start.1 = (bf16[1,1,256,768]{3,2,1,0:T(8,128)(2,1)S(1)}, bf16[1,1,256,768]{3,2,1,0:T(8,128)(2,1)}, u32[]{:S(2)}) copy-start(bf16[1,1,256,768]{3,2,1,0:T(8,128)(2,1)} %param.9) | copy-start | bytes 1179652
  0.7 0.9 %copy-start.3 = (bf16[16,2048]{1,0:T(8,128)(2,1)S(1)}, bf16[16,2048]{1,0:T(8,128)(2,1)}, u32[]{:S(2)}) copy-start(bf16[16,2048]{1,0:T(8,128)(2,1)} %grad_ref.1) | copy-start | bytes 196612
  1.6 0.7 %copy-start.4 = (s32[16,8]{0,1:T(8,128)S(1)}, s32[16,8]{0,1:T(8,128)}, u32[]{:S(2)}) copy-start(s32[16,8]{0,1:T(8,128)} %param.7) | copy-start | bytes 1540
  2.2 0.7 %copy-start.6 = (bf16[16,8]{0,1:T(8,128)(2,1)S(1)}, bf16[16,8]{0,1:T(8,128)(2,1)}, u32[]{:S(2)}) copy-start(bf16[16,8]{0,1:T(8,128)(2,1)} %param.8) | copy-start | bytes 772
  3.0 7.7 %collective-permute-start.2 = (bf16[16,2176]{1,0:T(8,128)(2,1)S(1)}, bf16[16,2176]{1,0:T(8,128)(2,1)S(1)}, u32[]{:S(2)}, u32[]{:S(2)}) collective-permute-start(bf16[16,2176]{1,0:T(8,128)(2,1)S(1)} %shard_map.93), channel_id=1, source_target_pairs={{0,3},{1,2},{2,1},{3,0},{4,7},{5,6},{6,5},{7,4},{8,11},{9,10},{10,... | collective-permute-start | bytes 208904 | tf_op jit(solution)/shard_map/ppermute | solution.py:92
  8.1 5.9 %collective-permute-start.1 = (bf16[16,2176]{1,0:T(8,128)(2,1)S(1)}, bf16[16,2176]{1,0:T(8,128)(2,1)S(1)}, u32[]{:S(2)}, u32[]{:S(2)}) collective-permute-start(bf16[16,2176]{1,0:T(8,128)(2,1)S(1)} %shard_map.93), channel_id=1, source_target_pairs={{0,2},{1,3},{2,0},{3,1},{4,6},{5,7},{6,4},{7,5},{8,10},{9,11},{10,... | collective-permute-start | bytes 208904 | tf_op jit(solution)/shard_map/ppermute | solution.py:92
  8.1 5.9 %collective-permute-start = (bf16[16,2176]{1,0:T(8,128)(2,1)S(1)}, bf16[16,2176]{1,0:T(8,128)(2,1)S(1)}, u32[]{:S(2)}, u32[]{:S(2)}) collective-permute-start(bf16[16,2176]{1,0:T(8,128)(2,1)S(1)} %shard_map.93), channel_id=1, source_target_pairs={{0,1},{1,0},{2,3},{3,2},{4,5},{5,4},{6,7},{7,6},{8,9},{9,8},{10,11... | collective-permute-start | bytes 208904 | tf_op jit(solution)/shard_map/ppermute | solution.py:92
  8.8 23.6 %copy-start = (bf16[1,768,2048]{2,1,0:T(8,128)(2,1)S(1)}, bf16[1,768,2048]{2,1,0:T(8,128)(2,1)}, u32[]{:S(2)}) copy-start(bf16[1,768,2048]{2,1,0:T(8,128)(2,1)} %param.11) | copy-start | bytes 9437188
  14.1 8.2 %collective-permute-start.3 = (bf16[64,2176]{1,0:T(8,128)(2,1)S(1)}, bf16[64,2176]{1,0:T(8,128)(2,1)S(1)}, u32[]{:S(2)}, u32[]{:S(2)}) collective-permute-start(bf16[64,2176]{1,0:T(8,128)(2,1)S(1)} %pad_maximum_fusion.1), channel_id=1, source_target_pairs={{0,8},{4,12},{8,0},{12,4},{1,9},{5,13},{9,1},{13,5},{2,10},{6,14},... | collective-permute-start | bytes 835592 | tf_op jit(solution)/shard_map/ppermute | solution.py:92
  22.3 10.0 %collective-permute-start.4 = (bf16[128,2176]{1,0:T(8,128)(2,1)S(1)}, bf16[128,2176]{1,0:T(8,128)(2,1)S(1)}, u32[]{:S(2)}, u32[]{:S(2)}) collective-permute-start(bf16[128,2176]{1,0:T(8,128)(2,1)S(1)} %constant_dynamic-update-slice_fusion.half_ref), channel_id=1, source_target_pairs={{0,4},{4,0},{8,12},{12,8},{1,5},{5,1},{9,13},{13,9},{2,6},{6,2},{1... | collective-permute-start | bytes 1671176 | tf_op jit(solution)/shard_map/ppermute | solution.py:92
  22.5 9.9 %collective-permute-start.6 = (bf16[128,1152]{1,0:T(8,128)(2,1)S(1)}, bf16[128,1152]{1,0:T(8,128)(2,1)S(1)}, u32[]{:S(2)}, u32[]{:S(2)}) collective-permute-start(bf16[128,1152]{1,0:T(8,128)(2,1)S(1)} %pad_maximum_fusion), channel_id=1, source_target_pairs={{0,16},{16,0},{1,17},{17,1},{2,18},{18,2},{3,19},{19,3},{4,20},{20... | collective-permute-start | bytes 884744 | tf_op jit(solution)/shard_map/ppermute | solution.py:92
  24.5 25.4 %collective-permute-start.5 = (bf16[256,768]{1,0:T(8,128)(2,1)S(1)}, bf16[256,768]{1,0:T(8,128)(2,1)S(1)}, u32[]{:S(2)}, u32[]{:S(2)}) collective-permute-start(bf16[256,768]{1,0:T(8,128)(2,1)S(1)} %shard_map.94.hidden_ref), channel_id=1, source_target_pairs={{0,16},{16,0},{1,17},{17,1},{2,18},{18,2},{3,19},{19,3},{4,20},{20... | collective-permute-start | bytes 1179656 | tf_op jit(solution)/shard_map/ppermute | solution.py:92
  32.4 17.5 %collective-permute-start.7 = (bf16[128,1152]{1,0:T(8,128)(2,1)S(1)}, bf16[128,1152]{1,0:T(8,128)(2,1)S(1)}, u32[]{:S(2)}, u32[]{:S(2)}) collective-permute-start(bf16[128,1152]{1,0:T(8,128)(2,1)S(1)} %collective-permute-done.6.refs_1_), channel_id=1, source_target_pairs={{0,4},{4,0},{8,12},{12,8},{1,5},{5,1},{9,13},{13,9},{2,6},{6,2},{1... | collective-permute-start | bytes 884744 | tf_op jit(solution)/shard_map/ppermute | solution.py:92
  32.4 16.8 %copy-start.5 = (s32[16,8]{0,1:T(8,128)S(1)}, s32[16,8]{0,1:T(8,128)}, u32[]{:S(2)}) copy-start(s32[16,8]{0,1:T(8,128)} %param.7) | copy-start | bytes 1540
  34.7 1.4 %collective-permute-start.8 = (f32[1,2,128]{2,1,0:T(2,128)S(1)}, f32[1,2,128]{2,1,0:T(2,128)S(1)}, u32[]{:S(2)}, u32[]{:S(2)}) collective-permute-start(f32[1,2,128]{2,1,0:T(2,128)S(1)} %bitcast.18), channel_id=1, source_target_pairs={{0,4},{4,0},{8,12},{12,8},{1,5},{5,1},{9,13},{13,9},{2,6},{6,2},{1... | collective-permute-start | bytes 3080 | tf_op jit(solution)/shard_map/ppermute | solution.py:92
  36.0 3.6 %collective-permute-start.9 = (f32[2,2,128]{2,1,0:T(2,128)S(1)}, f32[2,2,128]{2,1,0:T(2,128)S(1)}, u32[]{:S(2)}, u32[]{:S(2)}) collective-permute-start(f32[2,2,128]{2,1,0:T(2,128)S(1)} %pad_maximum_fusion.4), channel_id=1, source_target_pairs={{0,8},{4,12},{8,0},{12,4},{1,9},{5,13},{9,1},{13,5},{2,10},{6,14},... | collective-permute-start | bytes 6152 | tf_op jit(solution)/shard_map/ppermute | solution.py:92
  39.6 3.6 %collective-permute-start.10 = (f32[4,2,128]{2,1,0:T(2,128)S(1)}, f32[4,2,128]{2,1,0:T(2,128)S(1)}, u32[]{:S(2)}, u32[]{:S(2)}) collective-permute-start(f32[4,2,128]{2,1,0:T(2,128)S(1)} %pad_maximum_fusion.3), channel_id=1, source_target_pairs={{0,1},{1,0},{2,3},{3,2},{4,5},{5,4},{6,7},{7,6},{8,9},{9,8},{10,11... | collective-permute-start | bytes 12296 | tf_op jit(solution)/shard_map/ppermute | solution.py:92
  43.2 4.5 %collective-permute-start.11 = (f32[8,2,128]{2,1,0:T(2,128)S(1)}, f32[8,2,128]{2,1,0:T(2,128)S(1)}, u32[]{:S(2)}, u32[]{:S(2)}) collective-permute-start(f32[8,2,128]{2,1,0:T(2,128)S(1)} %pad_maximum_fusion.2), channel_id=1, source_target_pairs={{0,2},{1,3},{2,0},{3,1},{4,6},{5,7},{6,4},{7,5},{8,10},{9,11},{10,... | collective-permute-start | bytes 24584 | tf_op jit(solution)/shard_map/ppermute | solution.py:92

commit v2 on v1

--- a/solution.py
+++ b/solution.py
@@ -8,7 +8,8 @@
 from jax.sharding import PartitionSpec as P
 
 LANES = 128
-VMEM_LIMIT = 48 * 1024 * 1024
+FIRST_LIMIT = 16 * 1024 * 1024
+VMEM_LIMIT = 24 * 1024 * 1024
 
 
 def shards_exchange(out_grad, routes, gates, pre_gate, pre_up, down_weight):
@@ -92,16 +93,29 @@
     return lax.ppermute(x, axis, [(i, i ^ bits) for i in range(count)])
 
 
-def call(kernel, outs, cost, *args):
+def after(x, *done):
+    return lax.optimization_barrier((x,) + done)[0]
+
+
+def call(kernel, outs, cost, *args, hbm=0, scratch=(), deps=(), limit=VMEM_LIMIT):
     flops, moved = cost
+    body = kernel
+    if deps:
+
+        def body(*refs):
+            return kernel(*refs[: len(args)], *refs[len(args) + len(deps) :])
+
     return pl.pallas_call(
-        kernel,
+        body,
         out_shape=outs,
-        in_specs=[pl.BlockSpec(memory_space=pltpu.VMEM)] * len(args),
+        in_specs=[pl.BlockSpec(memory_space=pltpu.HBM)] * hbm
+        + [pl.BlockSpec(memory_space=pltpu.VMEM)] * (len(args) - hbm)
+        + [pl.BlockSpec(memory_space=pl.ANY)] * len(deps),
         out_specs=jax.tree.map(lambda _: pl.BlockSpec(memory_space=pltpu.VMEM), outs),
-        compiler_params=pltpu.CompilerParams(vmem_limit_bytes=VMEM_LIMIT),
+        scratch_shapes=scratch,
+        compiler_params=pltpu.CompilerParams(vmem_limit_bytes=limit),
         cost_estimate=pl.CostEstimate(flops=flops, bytes_accessed=moved, transcendentals=0),
-    )(*args)
+    )(*args, *deps)
 
 
 def peer(xors):
@@ -111,10 +125,39 @@
     )
 
 
-def payload_kernel(grad_ref, routes_ref, gates_ref, out_ref):
-    features = grad_ref.shape[1]
-    rows = grad_ref.shape[0]
-    out_ref[:, :features] = grad_ref[...]
+def first_kernel(
+    order,
+    grad_hbm,
+    routes_hbm,
+    gates_hbm,
+    pre_gate_hbm,
+    pre_up_hbm,
+    out_ref,
+    hidden_ref,
+    rest_ref,
+    routes_ref,
+    gates_ref,
+    pre_gate_ref,
+    pre_up_ref,
+    sems,
+):
+    rows, features = grad_hbm.shape
+    copies = [
+        pltpu.make_async_copy(source, target, sems.at[at])
+        for at, (source, target) in enumerate(
+            (
+                (routes_hbm, routes_ref),
+                (gates_hbm, gates_ref),
+                (grad_hbm, out_ref.at[:, pl.ds(0, features)]),
+                (pre_gate_hbm, pre_gate_ref),
+                (pre_up_hbm, pre_up_ref),
+            )
+        )
+    ]
+    for copy in copies:
+        copy.start()
+    copies[0].wait()
+    copies[1].wait()
     routes = routes_ref[...]
     gates = gates_ref[...].astype(jnp.float32)
     ids = lax.broadcasted_iota(jnp.int32, (LANES, rows), 0)
@@ -123,35 +166,50 @@
         table = table + jnp.where(ids == routes[k : k + 1, :], gates[k : k + 1, :], 0.0)
     table = jnp.concatenate([table, jnp.zeros((LANES, LANES - rows), jnp.float32)], axis=1)
     out_ref[:, features:] = table.T[:rows, :].astype(out_ref.dtype)
-
-
-def hidden_kernel(order, rows, pre_gate_ref, pre_up_ref, out_ref):
+    for copy in copies[2:]:
+        copy.wait()
+    half = len(order) // 2
     for place, xors in enumerate(order):
         source = pl.ds(pl.multiple_of(peer(xors) * rows, rows), rows)
         value = pre_gate_ref[source, :].astype(jnp.float32)
         up = pre_up_ref[source, :].astype(jnp.float32)
-        out_ref[place * rows : (place + 1) * rows, :] = (
-            value * jax.nn.sigmoid(value) * up
-        ).astype(out_ref.dtype)
-
-
-def back_kernel(features, half_ref, rest_ref, weight_ref, hidden_ref, back_ref, sums_ref):
-    rows = half_ref.shape[0]
-    for part, ref in enumerate((half_ref, rest_ref)):
-        here = slice(part * rows, (part + 1) * rows)
+        result = (value * jax.nn.sigmoid(value) * up).astype(hidden_ref.dtype)
+        hidden_ref[place * rows : (place + 1) * rows, :] = result
+        if place >= half:
+            rest_ref[(place - half) * rows : (place - half + 1) * rows, :] = result
+
+
+def back_kernel(
+    features,
+    held_ref,
+    weight_ref,
+    other_weight_ref,
+    hidden_ref,
+    other_hidden_ref,
+    back_ref,
+    other_back_ref,
+    sums_ref,
+):
+    rows = held_ref.shape[0]
+    for expert, (matrix_ref, act_ref, result_ref) in enumerate(
+        (
+            (weight_ref, hidden_ref, back_ref),
+            (other_weight_ref, other_hidden_ref, other_back_ref),
+        )
+    ):
         back = lax.dot_general(
-            ref[:, :features],
-            weight_ref[...],
+            held_ref[:, :features],
+            matrix_ref[...],
             (((1,), (1,)), ((), ())),
             preferred_element_type=jnp.float32,
         )
-        back_ref[here, :] = back
-        product = hidden_ref[here, :].astype(jnp.float32) * back
+        result_ref[...] = back
+        product = act_ref[:rows, :].astype(jnp.float32) * back
         folded = product[:, :LANES]
         for at in range(LANES, product.shape[1], LANES):
             folded = folded + product[:, at : at + LANES]
         for at in range(0, rows, LANES):
-            row = (part * rows + at) // LANES
+            row = (expert * rows + at) // LANES
             sums_ref[row : row + 1, :] = jnp.sum(
                 folded[at : at + LANES, :].T, axis=0, keepdims=True
             )
@@ -168,9 +226,10 @@
     order,
     rows,
     features,
-    half_ref,
+    held_ref,
     rest_ref,
     back_ref,
+    rest_back_ref,
     hidden_ref,
     pre_gate_ref,
     pre_up_ref,
@@ -178,17 +237,17 @@
     grad_up_ref,
     scaled_ref,
 ):
-    per = half_ref.shape[0] // rows
+    half = len(order) // 2
     for place, xors in enumerate(order):
-        ref = (half_ref, rest_ref)[place // per]
-        start = (place % per) * rows
-        gate = own_gates(ref[start : start + rows, features:])
+        tokens_ref, products_ref = ((held_ref, back_ref), (rest_ref, rest_back_ref))[place // half]
+        there = slice((place % half) * rows, (place % half + 1) * rows)
+        gate = own_gates(tokens_ref[there, features:])
         here = slice(place * rows, (place + 1) * rows)
         source = pl.ds(pl.multiple_of(peer(xors) * rows, rows), rows)
         value = pre_gate_ref[source, :].astype(jnp.float32)
         up = pre_up_ref[source, :].astype(jnp.float32)
         sig = jax.nn.sigmoid(value)
-        carried = gate * back_ref[here, :]
+        carried = gate * products_ref[there, :]
         grad_gate_ref[source, :] = (carried * up * sig * (1.0 + value * (1.0 - sig))).astype(
             grad_gate_ref.dtype
         )
@@ -198,14 +257,13 @@
         )
 
 
-def down_kernel(pairs, scaled_ref, half_ref, rest_ref, *refs):
-    out_ref = refs[-1]
+def down_kernel(pairs, scaled_ref, held_ref, rest_ref, *refs):
+    out_ref, token_ref = refs[-2:]
+    token_ref[...] = jnp.zeros(token_ref.shape, token_ref.dtype)
     columns = out_ref.shape[1]
-    rows = half_ref.shape[0]
-    contract = (((0,), (0,)), ((), ()))
     mine = pl.ds(pl.multiple_of(lax.axis_index("dp") * columns, columns), columns)
     scaled = [scaled_ref[...]]
-    tokens = [half_ref[:, mine], rest_ref[:, mine]]
+    tokens = [held_ref[:, mine], rest_ref[:, mine]]
     for pair in range(pairs):
         hidden_ref, one_ref, two_ref = refs[3 * pair : 3 * pair + 3]
         gate = jnp.concatenate(
@@ -216,7 +274,7 @@
     out_ref[...] = lax.dot_general(
         jnp.concatenate(scaled, axis=0),
         jnp.concatenate(tokens, axis=0),
-        contract,
+        (((0,), (0,)), ((), ())),
         preferred_element_type=jnp.float32,
     ).astype(out_ref.dtype)
 
@@ -224,11 +282,15 @@
 def pick_kernel(order, back_order, rows, routes_ref, sums_ref, out_ref):
     routes = routes_ref[...]
     total = jnp.zeros(out_ref.shape, jnp.float32)
-    for line, xors in enumerate(back_order):
-        start = order.index(xors) * rows
+    per = sums_ref.shape[1] // 2
+    for line, (wide_bits, narrow_bits) in enumerate(back_order):
+        start = order.index((wide_bits, narrow_bits)) * rows
         at = start % LANES
-        found = sums_ref[line, start // LANES : start // LANES + 1, :][:, at : at + rows]
-        total = total + jnp.where(routes == peer(xors), found, 0.0)
+        for expert in range(2):
+            row = expert * per + start // LANES
+            found = sums_ref[line, row : row + 1, :][:, at : at + rows]
+            chosen = routes == peer((wide_bits ^ expert, narrow_bits))
+            total = total + jnp.where(chosen, found, 0.0)
     out_ref[...] = total
 
 
@@ -238,6 +300,7 @@
     narrow_count = lax.axis_size("narrow")
     rows, features = out_grad.shape
     slot_count, units = pre_gate.shape[2:]
+    half_count = slot_count // 2
     columns = features // dp_count
     routes_t = routes.T
     gates_t = gates.T
@@ -247,85 +310,116 @@
     bf16, f32 = jnp.bfloat16, jnp.float32
     shape = jax.ShapeDtypeStruct
 
-    payload = call(
-        payload_kernel,
-        shape((rows, features + LANES), bf16),
-        (rows * features, 4 * rows * features),
-        out_grad,
-        routes_t,
-        gates_t,
-    )
-    held = jnp.concatenate(
-        [payload] + [swap(payload, "narrow", bits) for bits in range(1, narrow_count)], axis=0
-    )
+    near = max(narrow_count // 2, 1)
+    wide_bits = [1 << b for b in range(1, wide_count.bit_length() - 1)]
     order = [(0, bits) for bits in range(narrow_count)]
-    wide_bits = [1 << b for b in range(1, wide_count.bit_length() - 1)]
+    for bits in wide_bits + [1]:
+        order += [(w ^ bits, n) for w, n in order]
+    order = tuple(order)
+
+    payload, hidden, rest_hidden = call(
+        functools.partial(first_kernel, order),
+        (
+            shape((rows, features + LANES), bf16),
+            shape((slot_count, units), bf16),
+            shape((half_count, units), bf16),
+        ),
+        (20 * slot_count * units, 6 * slot_count * units),
+        *(
+            pltpu.with_memory_space_constraint(x, pltpu.HBM)
+            for x in (out_grad, routes_t, gates_t, pre_gate, pre_up)
+        ),
+        hbm=5,
+        limit=FIRST_LIMIT,
+        scratch=[
+            pltpu.VMEM(routes_t.shape, routes_t.dtype),
+            pltpu.VMEM(gates_t.shape, gates_t.dtype),
+            pltpu.VMEM(pre_gate.shape, pre_gate.dtype),
+            pltpu.VMEM(pre_up.shape, pre_up.dtype),
+            pltpu.SemaphoreType.DMA((5,)),
+        ],
+    )
+    along = [payload] + [swap(payload, "narrow", bits) for bits in range(1, narrow_count)]
+    groups = [jnp.concatenate(along[:near], axis=0)]
+    if along[near:]:
+        groups.append(jnp.concatenate(along[near:], axis=0))
     for bits in wide_bits:
-        held = jnp.concatenate([held, swap(held, "wide", bits)], axis=0)
-        order += [(w ^ bits, n) for w, n in order]
-    rest = swap(held, "wide", 1)
-    order += [(w ^ 1, n) for w, n in order]
-    order = tuple(order)
-
-    hidden = call(
-        functools.partial(hidden_kernel, order, rows),
-        shape((slot_count, units), bf16),
-        (20 * slot_count * units, 6 * slot_count * units),
-        pre_gate,
-        pre_up,
-    )
+        groups += [swap(group, "wide", bits) for group in groups]
+    held = jnp.concatenate(groups, axis=0)
+    late = along[near % len(along)]
+    other_weight = swap(weight, "wide", 1)
+    other_hidden = swap(after(rest_hidden, late), "wide", 1)
+    over = [swap(after(hidden, late), "dp", bits) for bits in range(1, dp_count)]
+    back, other_back, sums = call(
+        functools.partial(back_kernel, features),
+        (
+            shape((half_count, units), f32),
+            shape((half_count, units), f32),
+            shape((slot_count // LANES, LANES), f32),
+        ),
+        (2 * slot_count * units * features, 4 * units * features),
+        held,
+        weight,
+        other_weight,
+        hidden,
+        other_hidden,
+    )
+    steps = [("wide", b) for b in wide_bits] + [
+        ("narrow", 1 << b) for b in range(narrow_count.bit_length() - 1)
+    ]
+    found = sums[None]
+    back_order = [(0, 0)]
+    waits = []
+    for axis, bits in steps:
+        found = jnp.concatenate([after(found, *waits), swap(found, axis, bits)], axis=0)
+        step = (bits, 0) if axis == "wide" else (0, bits)
+        back_order += [(w ^ step[0], n ^ step[1]) for w, n in back_order]
+        if len(back_order) == 2:
+            rest = swap(after(held, sums), "wide", 1)
+            rest_back = swap(other_back, "wide", 1)
+            crossed = []
+            for bits in range(1, dp_count):
+                partner = lax.axis_index("dp") ^ bits
+                cut = lax.dynamic_slice_in_dim(
+                    held[:, :features], partner * columns, columns, axis=1
+                )
+                cut = jnp.concatenate([cut, held[:, features:]], axis=1)
+                crossed.append(swap(after(cut, found, *over), "dp", bits))
+        if len(back_order) == 4:
+            grad_a, grad_b, scaled = call(
+                functools.partial(grads_kernel, order, rows, features),
+                (shape((slot_count, units), bf16),) * 3,
+                (30 * slot_count * units, 12 * slot_count * units),
+                held,
+                rest,
+                back,
+                rest_back,
+                hidden,
+                pre_gate,
+                pre_up,
+            )
+            waits = [scaled]
+            half_found = found
     others = []
     for bits in range(1, dp_count):
-        partner = lax.axis_index("dp") ^ bits
-        cut = lax.dynamic_slice_in_dim(held[:, :features], partner * columns, columns, axis=1)
-        one = swap(jnp.concatenate([cut, held[:, features:]], axis=1), "dp", bits)
-        others += [swap(hidden, "dp", bits), one, swap(one, "wide", 1)]
-
-    back, sums = call(
-        functools.partial(back_kernel, features),
-        (shape((slot_count, units), f32), shape((slot_count // LANES, LANES), f32)),
-        (2 * slot_count * units * features, 2 * units * features),
-        held,
-        rest,
-        weight,
-        hidden,
-    )
-    grad_a, grad_b, scaled = call(
-        functools.partial(grads_kernel, order, rows, features),
-        (shape((slot_count, units), bf16),) * 3,
-        (30 * slot_count * units, 12 * slot_count * units),
-        held,
-        rest,
-        back,
-        hidden,
-        pre_gate,
-        pre_up,
-    )
-    grad_down = call(
+        one = after(crossed[bits - 1], half_found)
+        others += [over[bits - 1], one, swap(one, "wide", 1)]
+    grad_down, token = call(
         functools.partial(down_kernel, dp_count - 1),
-        shape((units, columns), bf16),
+        (shape((units, columns), bf16), shape((8, LANES), f32)),
         (2 * dp_count * slot_count * units * columns, 4 * units * columns),
         scaled,
         held,
         rest,
         *others,
     )
-    found = sums[None]
-    back_order = [(0, 0)]
-    for axis, bits in (
-        [("wide", 1)]
-        + [("wide", b) for b in wide_bits]
-        + [("narrow", 1 << b) for b in range(narrow_count.bit_length() - 1)]
-    ):
-        found = jnp.concatenate([found, swap(found, axis, bits)], axis=0)
-        step = (bits, 0) if axis == "wide" else (0, bits)
-        back_order += [(w ^ step[0], n ^ step[1]) for w, n in back_order]
     picked = call(
         functools.partial(pick_kernel, order, tuple(back_order), rows),
         shape(routes_t.shape, f32),
         (slot_count, slot_count),
         routes_t,
         found,
+        deps=(token,),
     )
     return (grad_down[None], grad_a[None, None], grad_b[None, None], picked.T)
 

time: 52.3 us -> 43.4 us (0.83)
  waiting for transfers between devices: 29.8 us -> 14.3 us
  starting transfers between devices: 12.2 us -> 18 us
  Pallas kernels: 6.85 us -> 9.91 us
  local copies, waits for them, and re-layouts: 2.46 us -> 0.18 us
    ppermute x12 -> x15, waiting for transfers between devices: 29.8 us -> 14.3 us  [swap(): return lax.ppermute(x, axis, [(i, i ^ bits) for i in range(count)])]
    ppermute x12 -> x15, starting transfers between devices: 12.2 us -> 18 us  [swap(): return lax.ppermute(x, axis, [(i, i ^ bits) for i in range(count)])]
    pallas_call x6 -> x5, Pallas kernels: 6.85 us -> 9.91 us  [call(): pl.pallas_call(body, out_shape=outs, in_specs=[pl.BlockSpec(memory_space=...]
    unnamed x22 -> x13, local copies, waits for them, and re-layouts: 2.35 us -> 0.08 us
  transfers between devices with their start and end apart: 12 -> 15, of which waited for: 8 -> 8; matrix products, arithmetic and copies ran while one was open for 0% -> 0% of each run, Pallas kernels for 9% -> 16%
where the time goes in v2:
time: 43.4 us; the launch traced here: 43.2 us
  starting transfers between devices  18 us (41%)
  waiting for transfers between devices  14.3 us (33%)
  Pallas kernels  9.91 us (23%)
  between operations  0.79 us (2%)
    ppermute x15, starting transfers between devices, swap(): return lax.ppermute(x, axis, [(i, i ^ bits) for i in range(count)])  18 us
    ppermute x15, waiting for transfers between devices, swap(): return lax.ppermute(x, axis, [(i, i ^ bits) for i in range(count)])  14.3 us
    pallas_call x5, Pallas kernels, call(): pl.pallas_call(body, out_shape=outs, in_specs=[pl.BlockSpec(memory_space=...  9.91 us
  transfers between devices with their start and end apart: 15, of which 8 were waited for; matrix products, arithmetic and copies ran while one was open for 0% of the time, Pallas kernels for 16%

profile of v2, /device:TPU:0, one launch (start us, length us, event | category | flops | bytes accessed | tf_op | source)
XLA Modules:
  0.0 43.2 jit_solution(12896463274558918415)
XLA Ops:
  0.6 0.5 %collective-permute-start.5 = (bf16[768,2048]{1,0:T(8,128)(2,1)}, bf16[768,2048]{1,0:T(8,128)(2,1)}, u32[]{:S(2)}, u32[]{:S(2)}) collective-permute-start(bf16[768,2048]{1,0:T(8,128)(2,1)} %bitcast.10), channel_id=1, source_target_pairs={{0,4},{4,0},{8,12},{12,8},{1,5},{5,1},{9,13},{13,9},{2,6},{6,2},{1... | collective-permute-start | bytes 9437192 | tf_op jit(solution)/shard_map/ppermute | solution.py:93
  1.1 1.4 %shard_map.93 = (bf16[16,2176]{1,0:T(8,128)(2,1)S(1)}, bf16[256,768]{1,0:T(8,128)(2,1)S(1)}, bf16[128,768]{1,0:T(8,128)(2,1)S(1)}) custom-call(bf16[16,2048]{1,0:T(8,128)(2,1)} %grad_hbm.1, s32[8,16]{1,0:T(8,128)} %bitcast.16, bf16[8,16]{1,0:T(8,128)(2,1)} %bitcast.21, bf16[256,768]{1,0:T(8,128)(2,1)} %bitcast.12, bf16[256,768]{1,0:T(8,128)(2,1)} %bitcast.14), custom_call_target="tpu_custom_call" | custom-call | flops 3932160 | bytes 1179648 | tf_op jit(solution)/shard_map/pallas_call | solution.py:108
  2.6 2.7 %collective-permute-start = (bf16[16,2176]{1,0:T(8,128)(2,1)S(1)}, bf16[16,2176]{1,0:T(8,128)(2,1)S(1)}, u32[]{:S(2)}, u32[]{:S(2)}) collective-permute-start(bf16[16,2176]{1,0:T(8,128)(2,1)S(1)} %get-tuple-element.21), channel_id=1, source_target_pairs={{0,1},{1,0},{2,3},{3,2},{4,5},{5,4},{6,7},{7,6},{8,9},{9,8},{10,11... | collective-permute-start | bytes 208904 | tf_op jit(solution)/shard_map/ppermute | solution.py:93
  5.2 2.6 %collective-permute-start.1 = (bf16[16,2176]{1,0:T(8,128)(2,1)S(1)}, bf16[16,2176]{1,0:T(8,128)(2,1)S(1)}, u32[]{:S(2)}, u32[]{:S(2)}) collective-permute-start(bf16[16,2176]{1,0:T(8,128)(2,1)S(1)} %get-tuple-element.21), channel_id=1, source_target_pairs={{0,2},{1,3},{2,0},{3,1},{4,6},{5,7},{6,4},{7,5},{8,10},{9,11},{10,... | collective-permute-start | bytes 208904 | tf_op jit(solution)/shard_map/ppermute | solution.py:93
  7.8 0.0 collective-permute-start.2
  7.8 0.0 copy-start
  7.8 0.2 collective-permute-done
  8.1 1.7 %collective-permute-start.3 = (bf16[32,2176]{1,0:T(8,128)(2,1)S(1)}, bf16[32,2176]{1,0:T(8,128)(2,1)S(1)}, u32[]{:S(2)}, u32[]{:S(2)}) collective-permute-start(bf16[32,2176]{1,0:T(8,128)(2,1)S(1)} %pad_maximum_fusion.1), channel_id=1, source_target_pairs={{0,8},{4,12},{8,0},{12,4},{1,9},{5,13},{9,1},{13,5},{2,10},{6,14},... | collective-permute-start | bytes 417800 | tf_op jit(solution)/shard_map/ppermute | solution.py:93
  9.8 3.3 %collective-permute-done.1 = bf16[16,2176]{1,0:T(8,128)(2,1)S(1)} collective-permute-done((bf16[16,2176]{1,0:T(8,128)(2,1)S(1)}, bf16[16,2176]{1,0:T(8,128)(2,1)S(1)}, u32[]{:S(2)}, u32[]{:S(2)}) %collective-permute-start.1) | collective-permute-done | bytes 69664 | tf_op jit(solution)/shard_map/ppermute | solution.py:93
  13.1 0.8 %collective-permute-done.2 = bf16[16,2176]{1,0:T(8,128)(2,1)S(1)} collective-permute-done((bf16[16,2176]{1,0:T(8,128)(2,1)S(1)}, bf16[16,2176]{1,0:T(8,128)(2,1)S(1)}, u32[]{:S(2)}, u32[]{:S(2)}) %collective-permute-start.2) | collective-permute-done | bytes 69664 | tf_op jit(solution)/shard_map/ppermute | solution.py:93
  14.0 1.6 %collective-permute-start.4 = (bf16[32,2176]{1,0:T(8,128)(2,1)S(1)}, bf16[32,2176]{1,0:T(8,128)(2,1)S(1)}, u32[]{:S(2)}, u32[]{:S(2)}) collective-permute-start(bf16[32,2176]{1,0:T(8,128)(2,1)S(1)} %pad_maximum_fusion.2), channel_id=1, source_target_pairs={{0,8},{4,12},{8,0},{12,4},{1,9},{5,13},{9,1},{13,5},{2,10},{6,14},... | collective-permute-start | bytes 417800 | tf_op jit(solution)/shard_map/ppermute | solution.py:93
  15.6 0.0 collective-permute-start.6
  15.6 1.5 %collective-permute-start.9 = (bf16[256,768]{1,0:T(8,128)(2,1)S(1)}, bf16[256,768]{1,0:T(8,128)(2,1)S(1)}, u32[]{:S(2)}, u32[]{:S(2)}) collective-permute-start(bf16[256,768]{1,0:T(8,128)(2,1)S(1)} %get-tuple-element.30.hidden_ref), channel_id=1, source_target_pairs={{0,16},{16,0},{1,17},{17,1},{2,18},{18,2},{3,19},{19,3},{4,20},{20... | collective-permute-start | bytes 1179656 | tf_op jit(solution)/shard_map/ppermute | solution.py:93
  17.1 0.0 collective-permute-done.3
  17.1 2.0 %collective-permute-done.4 = bf16[32,2176]{1,0:T(8,128)(2,1)S(1)} collective-permute-done((bf16[32,2176]{1,0:T(8,128)(2,1)S(1)}, bf16[32,2176]{1,0:T(8,128)(2,1)S(1)}, u32[]{:S(2)}, u32[]{:S(2)}) %collective-permute-start.4) | collective-permute-done | bytes 139296 | tf_op jit(solution)/shard_map/ppermute | solution.py:93
  19.2 0.0 copy-start.1
  19.2 0.0 copy-start.2
  19.2 0.0 collective-permute-done.6.other_hidden_ref
  19.3 0.0 collective-permute-done.5.other_weight_ref
  19.3 0.0 copy-done
  19.3 4.2 %shard_map.94 = (f32[128,768]{1,0:T(8,128)S(1)}, f32[128,768]{1,0:T(8,128)S(1)}, f32[2,128]{1,0:T(2,128)S(1)}) custom-call(bf16[128,2176]{1,0:T(8,128)(2,1)S(1)} %constant_dynamic-update-slice_fusion.held_ref, bf16[768,2048]{1,0:T(8,128)(2,1)S(1)} %bitcast.11, bf16[768,2048]{1,0:T(8,128)(2,1)} %collective-permute-done.5.other_weight_ref, ...), custom_call_target="tpu_custom_call" | custom-call | flops 805306368 | bytes 6291456 | tf_op jit(solution)/shard_map/pallas_call | solution.py:108
  23.5 1.6 %collective-permute-start.10 = (f32[1,2,128]{2,1,0:T(2,128)S(1)}, f32[1,2,128]{2,1,0:T(2,128)S(1)}, u32[]{:S(2)}, u32[]{:S(2)}) collective-permute-start(f32[1,2,128]{2,1,0:T(2,128)S(1)} %bitcast.18), channel_id=1, source_target_pairs={{0,8},{4,12},{8,0},{12,4},{1,9},{5,13},{9,1},{13,5},{2,10},{6,14},... | collective-permute-start | bytes 3080 | tf_op jit(solution)/shard_map/ppermute | solution.py:93
  25.1 0.0 copy-start.3
  25.1 0.1 collective-permute-start.7
  25.2 1.9 %collective-permute-done.10 = f32[1,2,128]{2,1,0:T(2,128)S(1)} collective-permute-done((f32[1,2,128]{2,1,0:T(2,128)S(1)}, f32[1,2,128]{2,1,0:T(2,128)S(1)}, u32[]{:S(2)}, u32[]{:S(2)}) %collective-permute-start.10) | collective-permute-done | bytes 1056 | tf_op jit(solution)/shard_map/ppermute | solution.py:93
  27.1 0.0 collective-permute-done.9.refs_0_
  27.1 1.5 %collective-permute-start.11 = (bf16[128,1152]{1,0:T(8,128)(2,1)S(1)}, bf16[128,1152]{1,0:T(8,128)(2,1)S(1)}, u32[]{:S(2)}, u32[]{:S(2)}) collective-permute-start(bf16[128,1152]{1,0:T(8,128)(2,1)S(1)} %pad_maximum_fusion), channel_id=1, source_target_pairs={{0,16},{16,0},{1,17},{17,1},{2,18},{18,2},{3,19},{19,3},{4,20},{20... | collective-permute-start | bytes 884744 | tf_op jit(solution)/shard_map/ppermute | solution.py:93
  28.7 0.0 collective-permute-start.8
  28.7 1.7 %collective-permute-start.12 = (f32[2,2,128]{2,1,0:T(2,128)S(1)}, f32[2,2,128]{2,1,0:T(2,128)S(1)}, u32[]{:S(2)}, u32[]{:S(2)}) collective-permute-start(f32[2,2,128]{2,1,0:T(2,128)S(1)} %pad_maximum_fusion.5), channel_id=1, source_target_pairs={{0,1},{1,0},{2,3},{3,2},{4,5},{5,4},{6,7},{7,6},{8,9},{9,8},{10,11... | collective-permute-start | bytes 6152 | tf_op jit(solution)/shard_map/ppermute | solution.py:93
  30.3 1.9 %collective-permute-done.12 = f32[2,2,128]{2,1,0:T(2,128)S(1)} collective-permute-done((f32[2,2,128]{2,1,0:T(2,128)S(1)}, f32[2,2,128]{2,1,0:T(2,128)S(1)}, u32[]{:S(2)}, u32[]{:S(2)}) %collective-permute-start.12) | collective-permute-done | bytes 2080 | tf_op jit(solution)/shard_map/ppermute | solution.py:93
  32.3 3.5 %collective-permute-done.11.refs_1_ = bf16[128,1152]{1,0:T(8,128)(2,1)S(1)} collective-permute-done((bf16[128,1152]{1,0:T(8,128)(2,1)S(1)}, bf16[128,1152]{1,0:T(8,128)(2,1)S(1)}, u32[]{:S(2)}, u32[]{:S(2)}) %collective-permute-start.11) | collective-permute-done | bytes 294944 | tf_op jit(solution)/shard_map/ppermute | solution.py:93
  35.7 0.0 collective-permute-start.13
  35.7 2.5 %collective-permute-start.14 = (f32[4,2,128]{2,1,0:T(2,128)S(1)}, f32[4,2,128]{2,1,0:T(2,128)S(1)}, u32[]{:S(2)}, u32[]{:S(2)}) collective-permute-start(f32[4,2,128]{2,1,0:T(2,128)S(1)} %pad_maximum_fusion.4), channel_id=1, source_target_pairs={{0,2},{1,3},{2,0},{3,1},{4,6},{5,7},{6,4},{7,5},{8,10},{9,11},{10,... | collective-permute-start | bytes 12296 | tf_op jit(solution)/shard_map/ppermute | solution.py:93
  38.2 0.0 collective-permute-done.8.rest_back_ref
  38.2 0.0 collective-permute-done.7.rest_ref
  38.2 0.0 copy-done.1
  38.2 0.0 copy-done.2
  38.3 1.4 %shard_map.95 = (bf16[256,768]{1,0:T(8,128)(2,1)}, bf16[256,768]{1,0:T(8,128)(2,1)}, bf16[256,768]{1,0:T(8,128)(2,1)S(1)}) custom-call(bf16[128,2176]{1,0:T(8,128)(2,1)S(1)} %constant_dynamic-update-slice_fusion.held_ref, bf16[128,2176]{1,0:T(8,128)(2,1)S(1)} %collective-permute-done.7.rest_ref, f32[128,768]{1,0:T(8,128)S(1)} %get-tuple-element.27.back_ref, ...), custom_call_target="tpu_custom_call" | custom-call | flops 5898240 | bytes 2359296 | tf_op jit(solution)/shard_map/pallas_call | solution.py:108
  39.6 0.6 %collective-permute-done.14 = f32[4,2,128]{2,1,0:T(2,128)S(1)} collective-permute-done((f32[4,2,128]{2,1,0:T(2,128)S(1)}, f32[4,2,128]{2,1,0:T(2,128)S(1)}, u32[]{:S(2)}, u32[]{:S(2)}) %collective-permute-start.14) | collective-permute-done | bytes 4128 | tf_op jit(solution)/shard_map/ppermute | solution.py:93
  40.3 0.0 collective-permute-done.13.refs_2_
  40.3 2.3 %shard_map.96 = (bf16[768,1024]{1,0:T(8,128)(2,1)}, f32[8,128]{1,0:T(8,128)S(1)}) custom-call(bf16[256,768]{1,0:T(8,128)(2,1)S(1)} %get-tuple-element.29.scaled_ref, bf16[128,2176]{1,0:T(8,128)(2,1)S(1)} %constant_dynamic-update-slice_fusion.held_ref, bf16[128,2176]{1,0:T(8,128)(2,1)S(1)} %collective-permute-done.7.rest_ref, ...), custom_call_target="tpu_custom_call" | custom-call | flops 805306368 | bytes 3145728 | tf_op jit(solution)/shard_map/pallas_call | solution.py:108
  42.5 0.0 copy-done.3
  42.5 0.7 %shard_map.97 = f32[8,16]{1,0:T(8,128)} custom-call(s32[8,16]{1,0:T(8,128)S(1)} %bitcast.17, f32[8,2,128]{2,1,0:T(2,128)S(1)} %pad_maximum_fusion.3.refs_1_, f32[8,128]{1,0:T(8,128)S(1)} %get-tuple-element.37.refs_2_), custom_call_target="tpu_custom_call" | custom-call | flops 256 | bytes 256 | tf_op jit(solution)/shard_map/pallas_call | solution.py:108
  (15 shorter events, 0.2 us)
Async XLA Ops:
  0.6 18.6 %collective-permute-start.5 = (bf16[768,2048]{1,0:T(8,128)(2,1)}, bf16[768,2048]{1,0:T(8,128)(2,1)}, u32[]{:S(2)}, u32[]{:S(2)}) collective-permute-start(bf16[768,2048]{1,0:T(8,128)(2,1)} %bitcast.10), channel_id=1, source_target_pairs={{0,4},{4,0},{8,12},{12,8},{1,5},{5,1},{9,13},{13,9},{2,6},{6,2},{1... | collective-permute-start | bytes 9437192 | tf_op jit(solution)/shard_map/ppermute | solution.py:93
  2.6 5.5 %collective-permute-start = (bf16[16,2176]{1,0:T(8,128)(2,1)S(1)}, bf16[16,2176]{1,0:T(8,128)(2,1)S(1)}, u32[]{:S(2)}, u32[]{:S(2)}) collective-permute-start(bf16[16,2176]{1,0:T(8,128)(2,1)S(1)} %get-tuple-element.21), channel_id=1, source_target_pairs={{0,1},{1,0},{2,3},{3,2},{4,5},{5,4},{6,7},{7,6},{8,9},{9,8},{10,11... | collective-permute-start | bytes 208904 | tf_op jit(solution)/shard_map/ppermute | solution.py:93
  5.2 7.9 %collective-permute-start.1 = (bf16[16,2176]{1,0:T(8,128)(2,1)S(1)}, bf16[16,2176]{1,0:T(8,128)(2,1)S(1)}, u32[]{:S(2)}, u32[]{:S(2)}) collective-permute-start(bf16[16,2176]{1,0:T(8,128)(2,1)S(1)} %get-tuple-element.21), channel_id=1, source_target_pairs={{0,2},{1,3},{2,0},{3,1},{4,6},{5,7},{6,4},{7,5},{8,10},{9,11},{10,... | collective-permute-start | bytes 208904 | tf_op jit(solution)/shard_map/ppermute | solution.py:93
  7.8 6.2 %collective-permute-start.2 = (bf16[16,2176]{1,0:T(8,128)(2,1)S(1)}, bf16[16,2176]{1,0:T(8,128)(2,1)S(1)}, u32[]{:S(2)}, u32[]{:S(2)}) collective-permute-start(bf16[16,2176]{1,0:T(8,128)(2,1)S(1)} %get-tuple-element.21), channel_id=1, source_target_pairs={{0,3},{1,2},{2,1},{3,0},{4,7},{5,6},{6,5},{7,4},{8,11},{9,10},{10,... | collective-permute-start | bytes 208904 | tf_op jit(solution)/shard_map/ppermute | solution.py:93
  7.8 11.4 %copy-start = (bf16[1,768,2048]{2,1,0:T(8,128)(2,1)S(1)}, bf16[1,768,2048]{2,1,0:T(8,128)(2,1)}, u32[]{:S(2)}) copy-start(bf16[1,768,2048]{2,1,0:T(8,128)(2,1)} %param.11) | copy-start | bytes 9437188
  8.1 9.0 %collective-permute-start.3 = (bf16[32,2176]{1,0:T(8,128)(2,1)S(1)}, bf16[32,2176]{1,0:T(8,128)(2,1)S(1)}, u32[]{:S(2)}, u32[]{:S(2)}) collective-permute-start(bf16[32,2176]{1,0:T(8,128)(2,1)S(1)} %pad_maximum_fusion.1), channel_id=1, source_target_pairs={{0,8},{4,12},{8,0},{12,4},{1,9},{5,13},{9,1},{13,5},{2,10},{6,14},... | collective-permute-start | bytes 417800 | tf_op jit(solution)/shard_map/ppermute | solution.py:93
  14.0 5.1 %collective-permute-start.4 = (bf16[32,2176]{1,0:T(8,128)(2,1)S(1)}, bf16[32,2176]{1,0:T(8,128)(2,1)S(1)}, u32[]{:S(2)}, u32[]{:S(2)}) collective-permute-start(bf16[32,2176]{1,0:T(8,128)(2,1)S(1)} %pad_maximum_fusion.2), channel_id=1, source_target_pairs={{0,8},{4,12},{8,0},{12,4},{1,9},{5,13},{9,1},{13,5},{2,10},{6,14},... | collective-permute-start | bytes 417800 | tf_op jit(solution)/shard_map/ppermute | solution.py:93
  15.6 3.7 %collective-permute-start.6 = (bf16[128,768]{1,0:T(8,128)(2,1)S(1)}, bf16[128,768]{1,0:T(8,128)(2,1)S(1)}, u32[]{:S(2)}, u32[]{:S(2)}) collective-permute-start(bf16[128,768]{1,0:T(8,128)(2,1)S(1)} %get-tuple-element.24), channel_id=1, source_target_pairs={{0,4},{4,0},{8,12},{12,8},{1,5},{5,1},{9,13},{13,9},{2,6},{6,2},{1... | collective-permute-start | bytes 589832 | tf_op jit(solution)/shard_map/ppermute | solution.py:93
  15.6 11.5 %collective-permute-start.9 = (bf16[256,768]{1,0:T(8,128)(2,1)S(1)}, bf16[256,768]{1,0:T(8,128)(2,1)S(1)}, u32[]{:S(2)}, u32[]{:S(2)}) collective-permute-start(bf16[256,768]{1,0:T(8,128)(2,1)S(1)} %get-tuple-element.30.hidden_ref), channel_id=1, source_target_pairs={{0,16},{16,0},{1,17},{17,1},{2,18},{18,2},{3,19},{19,3},{4,20},{20... | collective-permute-start | bytes 1179656 | tf_op jit(solution)/shard_map/ppermute | solution.py:93
  19.2 19.0 %copy-start.1 = (bf16[1,1,256,768]{3,2,1,0:T(8,128)(2,1)S(1)}, bf16[1,1,256,768]{3,2,1,0:T(8,128)(2,1)}, u32[]{:S(2)}) copy-start(bf16[1,1,256,768]{3,2,1,0:T(8,128)(2,1)} %param.9) | copy-start | bytes 1179652
  19.2 19.0 %copy-start.2 = (bf16[1,1,256,768]{3,2,1,0:T(8,128)(2,1)S(1)}, bf16[1,1,256,768]{3,2,1,0:T(8,128)(2,1)}, u32[]{:S(2)}) copy-start(bf16[1,1,256,768]{3,2,1,0:T(8,128)(2,1)} %param.10) | copy-start | bytes 1179652
  23.5 3.6 %collective-permute-start.10 = (f32[1,2,128]{2,1,0:T(2,128)S(1)}, f32[1,2,128]{2,1,0:T(2,128)S(1)}, u32[]{:S(2)}, u32[]{:S(2)}) collective-permute-start(f32[1,2,128]{2,1,0:T(2,128)S(1)} %bitcast.18), channel_id=1, source_target_pairs={{0,8},{4,12},{8,0},{12,4},{1,9},{5,13},{9,1},{13,5},{2,10},{6,14},... | collective-permute-start | bytes 3080 | tf_op jit(solution)/shard_map/ppermute | solution.py:93
  25.1 17.5 %copy-start.3 = (s32[16,8]{0,1:T(8,128)S(1)}, s32[16,8]{0,1:T(8,128)}, u32[]{:S(2)}) copy-start(s32[16,8]{0,1:T(8,128)} %param.7) | copy-start | bytes 1540
  25.1 13.2 %collective-permute-start.7 = (bf16[128,2176]{1,0:T(8,128)(2,1)S(1)}, bf16[128,2176]{1,0:T(8,128)(2,1)S(1)}, u32[]{:S(2)}, u32[]{:S(2)}) collective-permute-start(bf16[128,2176]{1,0:T(8,128)(2,1)S(1)} %constant_dynamic-update-slice_fusion.held_ref), channel_id=1, source_target_pairs={{0,4},{4,0},{8,12},{12,8},{1,5},{5,1},{9,13},{13,9},{2,6},{6,2},{1... | collective-permute-start | bytes 1671176 | tf_op jit(solution)/shard_map/ppermute | solution.py:93
  27.1 8.6 %collective-permute-start.11 = (bf16[128,1152]{1,0:T(8,128)(2,1)S(1)}, bf16[128,1152]{1,0:T(8,128)(2,1)S(1)}, u32[]{:S(2)}, u32[]{:S(2)}) collective-permute-start(bf16[128,1152]{1,0:T(8,128)(2,1)S(1)} %pad_maximum_fusion), channel_id=1, source_target_pairs={{0,16},{16,0},{1,17},{17,1},{2,18},{18,2},{3,19},{19,3},{4,20},{20... | collective-permute-start | bytes 884744 | tf_op jit(solution)/shard_map/ppermute | solution.py:93
  28.7 9.6 %collective-permute-start.8 = (f32[128,768]{1,0:T(8,128)S(1)}, f32[128,768]{1,0:T(8,128)S(1)}, u32[]{:S(2)}, u32[]{:S(2)}) collective-permute-start(f32[128,768]{1,0:T(8,128)S(1)} %get-tuple-element.28), channel_id=1, source_target_pairs={{0,4},{4,0},{8,12},{12,8},{1,5},{5,1},{9,13},{13,9},{2,6},{6,2},{1... | collective-permute-start | bytes 1179656 | tf_op jit(solution)/shard_map/ppermute | solution.py:93
  28.7 3.6 %collective-permute-start.12 = (f32[2,2,128]{2,1,0:T(2,128)S(1)}, f32[2,2,128]{2,1,0:T(2,128)S(1)}, u32[]{:S(2)}, u32[]{:S(2)}) collective-permute-start(f32[2,2,128]{2,1,0:T(2,128)S(1)} %pad_maximum_fusion.5), channel_id=1, source_target_pairs={{0,1},{1,0},{2,3},{3,2},{4,5},{5,4},{6,7},{7,6},{8,9},{9,8},{10,11... | collective-permute-start | bytes 6152 | tf_op jit(solution)/shard_map/ppermute | solution.py:93
  35.7 4.5 %collective-permute-start.13 = (bf16[128,1152]{1,0:T(8,128)(2,1)S(1)}, bf16[128,1152]{1,0:T(8,128)(2,1)S(1)}, u32[]{:S(2)}, u32[]{:S(2)}) collective-permute-start(bf16[128,1152]{1,0:T(8,128)(2,1)S(1)} %collective-permute-done.11.refs_1_), channel_id=1, source_target_pairs={{0,4},{4,0},{8,12},{12,8},{1,5},{5,1},{9,13},{13,9},{2,6},{6,2},{1... | collective-permute-start | bytes 884744 | tf_op jit(solution)/shard_map/ppermute | solution.py:93
  35.7 4.5 %collective-permute-start.14 = (f32[4,2,128]{2,1,0:T(2,128)S(1)}, f32[4,2,128]{2,1,0:T(2,128)S(1)}, u32[]{:S(2)}, u32[]{:S(2)}) collective-permute-start(f32[4,2,128]{2,1,0:T(2,128)S(1)} %pad_maximum_fusion.4), channel_id=1, source_target_pairs={{0,2},{1,3},{2,0},{3,1},{4,6},{5,7},{6,4},{7,5},{8,10},{9,11},{10,... | collective-permute-start | bytes 12296 | tf_op jit(solution)/shard_map/ppermute | solution.py:93

commit v3 on v2

--- a/solution.py
+++ b/solution.py
@@ -8,8 +8,7 @@
 from jax.sharding import PartitionSpec as P
 
 LANES = 128
-FIRST_LIMIT = 16 * 1024 * 1024
-VMEM_LIMIT = 24 * 1024 * 1024
+VMEM_LIMIT = 14 * 1024 * 1024
 
 
 def shards_exchange(out_grad, routes, gates, pre_gate, pre_up, down_weight):
@@ -118,6 +117,10 @@
     )(*args, *deps)
 
 
+def in_hbm(*arrays):
+    return [pltpu.with_memory_space_constraint(x, pltpu.HBM) for x in arrays]
+
+
 def peer(xors):
     wide_bits, narrow_bits = xors
     return (lax.axis_index("wide") ^ wide_bits) * lax.axis_size("narrow") + (
@@ -126,33 +129,14 @@
 
 
 def first_kernel(
-    order,
-    grad_hbm,
-    routes_hbm,
-    gates_hbm,
-    pre_gate_hbm,
-    pre_up_hbm,
-    out_ref,
-    hidden_ref,
-    rest_ref,
-    routes_ref,
-    gates_ref,
-    pre_gate_ref,
-    pre_up_ref,
-    sems,
+    grad_hbm, routes_hbm, gates_hbm, out_ref, token_ref, routes_ref, gates_ref, sems
 ):
     rows, features = grad_hbm.shape
+    token_ref[...] = jnp.zeros(token_ref.shape, token_ref.dtype)
     copies = [
-        pltpu.make_async_copy(source, target, sems.at[at])
-        for at, (source, target) in enumerate(
-            (
-                (routes_hbm, routes_ref),
-                (gates_hbm, gates_ref),
-                (grad_hbm, out_ref.at[:, pl.ds(0, features)]),
-                (pre_gate_hbm, pre_gate_ref),
-                (pre_up_hbm, pre_up_ref),
-            )
-        )
+        pltpu.make_async_copy(routes_hbm, routes_ref, sems.at[0]),
+        pltpu.make_async_copy(gates_hbm, gates_ref, sems.at[1]),
+        pltpu.make_async_copy(grad_hbm, out_ref.at[:, pl.ds(0, features)], sems.at[2]),
     ]
     for copy in copies:
         copy.start()
@@ -166,7 +150,19 @@
         table = table + jnp.where(ids == routes[k : k + 1, :], gates[k : k + 1, :], 0.0)
     table = jnp.concatenate([table, jnp.zeros((LANES, LANES - rows), jnp.float32)], axis=1)
     out_ref[:, features:] = table.T[:rows, :].astype(out_ref.dtype)
-    for copy in copies[2:]:
+    copies[2].wait()
+
+
+def hidden_kernel(
+    order, rows, pre_gate_hbm, pre_up_hbm, hidden_ref, rest_ref, pre_gate_ref, pre_up_ref, sems
+):
+    copies = [
+        pltpu.make_async_copy(pre_gate_hbm, pre_gate_ref, sems.at[0]),
+        pltpu.make_async_copy(pre_up_hbm, pre_up_ref, sems.at[1]),
+    ]
+    for copy in copies:
+        copy.start()
+    for copy in copies:
         copy.wait()
     half = len(order) // 2
     for place, xors in enumerate(order):
@@ -179,11 +175,32 @@
             rest_ref[(place - half) * rows : (place - half + 1) * rows, :] = result
 
 
+def turn_kernel(one_hbm, two_hbm, one_out, two_out, one_ref, two_ref, sems):
+    units, features = one_ref.shape
+    moves = [
+        (at, source, held, out)
+        for source, held, out in ((one_hbm, one_ref, one_out), (two_hbm, two_ref, two_out))
+        for at in range(0, units, LANES)
+    ]
+    copies = [
+        pltpu.make_async_copy(
+            source.at[pl.ds(at, LANES)], held.at[pl.ds(at, LANES)], sems.at[step]
+        )
+        for step, (at, source, held, _) in enumerate(moves)
+    ]
+    for copy in copies:
+        copy.start()
+    for copy, (at, _, held, out) in zip(copies, moves):
+        copy.wait()
+        for to in range(0, features, LANES):
+            out[to : to + LANES, at : at + LANES] = held[at : at + LANES, to : to + LANES].T
+
+
 def back_kernel(
     features,
     held_ref,
-    weight_ref,
-    other_weight_ref,
+    turned_ref,
+    other_turned_ref,
     hidden_ref,
     other_hidden_ref,
     back_ref,
@@ -192,16 +209,10 @@
 ):
     rows = held_ref.shape[0]
     for expert, (matrix_ref, act_ref, result_ref) in enumerate(
-        (
-            (weight_ref, hidden_ref, back_ref),
-            (other_weight_ref, other_hidden_ref, other_back_ref),
-        )
+        ((turned_ref, hidden_ref, back_ref), (other_turned_ref, other_hidden_ref, other_back_ref))
     ):
-        back = lax.dot_general(
-            held_ref[:, :features],
-            matrix_ref[...],
-            (((1,), (1,)), ((), ())),
-            preferred_element_type=jnp.float32,
+        back = jnp.dot(
+            held_ref[:, :features], matrix_ref[...], preferred_element_type=jnp.float32
         )
         result_ref[...] = back
         product = act_ref[:rows, :].astype(jnp.float32) * back
@@ -258,8 +269,7 @@
 
 
 def down_kernel(pairs, scaled_ref, held_ref, rest_ref, *refs):
-    out_ref, token_ref = refs[-2:]
-    token_ref[...] = jnp.zeros(token_ref.shape, token_ref.dtype)
+    out_ref = refs[-1]
     columns = out_ref.shape[1]
     mine = pl.ds(pl.multiple_of(lax.axis_index("dp") * columns, columns), columns)
     scaled = [scaled_ref[...]]
@@ -312,44 +322,60 @@
 
     near = max(narrow_count // 2, 1)
     wide_bits = [1 << b for b in range(1, wide_count.bit_length() - 1)]
-    order = [(0, bits) for bits in range(narrow_count)]
+    reach = [0] + list(range(near, narrow_count)) + list(range(1, near))
+    order = [(0, bits) for bits in reach]
     for bits in wide_bits + [1]:
         order += [(w ^ bits, n) for w, n in order]
     order = tuple(order)
 
-    payload, hidden, rest_hidden = call(
-        functools.partial(first_kernel, order),
-        (
-            shape((rows, features + LANES), bf16),
-            shape((slot_count, units), bf16),
-            shape((half_count, units), bf16),
-        ),
-        (20 * slot_count * units, 6 * slot_count * units),
-        *(
-            pltpu.with_memory_space_constraint(x, pltpu.HBM)
-            for x in (out_grad, routes_t, gates_t, pre_gate, pre_up)
-        ),
-        hbm=5,
-        limit=FIRST_LIMIT,
+    other_weight = swap(weight, "wide", 1)
+    payload, token = call(
+        first_kernel,
+        (shape((rows, features + LANES), bf16), shape((8, LANES), f32)),
+        (rows * features, 4 * rows * features),
+        *in_hbm(out_grad, routes_t, gates_t),
+        hbm=3,
         scratch=[
             pltpu.VMEM(routes_t.shape, routes_t.dtype),
             pltpu.VMEM(gates_t.shape, gates_t.dtype),
+            pltpu.SemaphoreType.DMA((3,)),
+        ],
+    )
+    along = [swap(payload, "narrow", bits) if bits else payload for bits in reach]
+    hidden, rest_hidden = call(
+        functools.partial(hidden_kernel, order, rows),
+        (shape((slot_count, units), bf16), shape((half_count, units), bf16)),
+        (20 * slot_count * units, 6 * slot_count * units),
+        *in_hbm(pre_gate, pre_up),
+        hbm=2,
+        deps=(token,),
+        scratch=[
             pltpu.VMEM(pre_gate.shape, pre_gate.dtype),
             pltpu.VMEM(pre_up.shape, pre_up.dtype),
-            pltpu.SemaphoreType.DMA((5,)),
+            pltpu.SemaphoreType.DMA((2,)),
         ],
     )
-    along = [payload] + [swap(payload, "narrow", bits) for bits in range(1, narrow_count)]
-    groups = [jnp.concatenate(along[:near], axis=0)]
+    turned = call(
+        turn_kernel,
+        (shape((features, units), bf16),) * 2,
+        (0, 8 * features * units),
+        *in_hbm(weight, other_weight),
+        hbm=2,
+        deps=(token,),
+        scratch=[
+            pltpu.VMEM(weight.shape, weight.dtype),
+            pltpu.VMEM(weight.shape, weight.dtype),
+            pltpu.SemaphoreType.DMA((2 * units // LANES,)),
+        ],
+    )
+    over = [swap(after(hidden, *along[near:]), "dp", bits) for bits in range(1, dp_count)]
+    other_hidden = swap(rest_hidden, "wide", 1)
+    groups = [after(jnp.concatenate(along[:near], axis=0), hidden)]
     if along[near:]:
         groups.append(jnp.concatenate(along[near:], axis=0))
     for bits in wide_bits:
         groups += [swap(group, "wide", bits) for group in groups]
-    held = jnp.concatenate(groups, axis=0)
-    late = along[near % len(along)]
-    other_weight = swap(weight, "wide", 1)
-    other_hidden = swap(after(rest_hidden, late), "wide", 1)
-    over = [swap(after(hidden, late), "dp", bits) for bits in range(1, dp_count)]
+    held = jnp.concatenate([after(groups[0], *turned)] + groups[1:], axis=0)
     back, other_back, sums = call(
         functools.partial(back_kernel, features),
         (
@@ -359,8 +385,7 @@
         ),
         (2 * slot_count * units * features, 4 * units * features),
         held,
-        weight,
-        other_weight,
+        *turned,
         hidden,
         other_hidden,
     )
@@ -371,7 +396,9 @@
     back_order = [(0, 0)]
     waits = []
     for axis, bits in steps:
-        found = jnp.concatenate([after(found, *waits), swap(found, axis, bits)], axis=0)
+        found = after(found, *waits)
+        kept = after(found, scaled) if len(back_order) >= 4 else found
+        found = jnp.concatenate([kept, swap(found, axis, bits)], axis=0)
         step = (bits, 0) if axis == "wide" else (0, bits)
         back_order += [(w ^ step[0], n ^ step[1]) for w, n in back_order]
         if len(back_order) == 2:
@@ -384,7 +411,7 @@
                     held[:, :features], partner * columns, columns, axis=1
                 )
                 cut = jnp.concatenate([cut, held[:, features:]], axis=1)
-                crossed.append(swap(after(cut, found, *over), "dp", bits))
+                crossed.append(swap(after(cut, sums), "dp", bits))
         if len(back_order) == 4:
             grad_a, grad_b, scaled = call(
                 functools.partial(grads_kernel, order, rows, features),
@@ -398,15 +425,14 @@
                 pre_gate,
                 pre_up,
             )
-            waits = [scaled]
-            half_found = found
+            waits = [*over]
     others = []
     for bits in range(1, dp_count):
-        one = after(crossed[bits - 1], half_found)
+        one = after(crossed[bits - 1], found)
         others += [over[bits - 1], one, swap(one, "wide", 1)]
-    grad_down, token = call(
+    grad_down = call(
         functools.partial(down_kernel, dp_count - 1),
-        (shape((units, columns), bf16), shape((8, LANES), f32)),
+        shape((units, columns), bf16),
         (2 * dp_count * slot_count * units * columns, 4 * units * columns),
         scaled,
         held,
@@ -419,7 +445,6 @@
         (slot_count, slot_count),
         routes_t,
         found,
-        deps=(token,),
     )
     return (grad_down[None], grad_a[None, None], grad_b[None, None], picked.T)
 

time: 43.4 us -> 37.2 us (0.86)
  waiting for transfers between devices: 14.3 us -> 7.37 us
  Pallas kernels: 9.91 us -> 11 us
    ppermute x15, waiting for transfers between devices: 14.3 us -> 7.37 us  [swap(): return lax.ppermute(x, axis, [(i, i ^ bits) for i in range(count)])]
    pallas_call x5 -> x7, Pallas kernels: 9.91 us -> 11 us  [call(): pl.pallas_call(body, out_shape=outs, in_specs=[pl.BlockSpec(memory_space=...]
  transfers between devices with their start and end apart: 15 -> 15, of which waited for: 8 -> 8; matrix products, arithmetic and copies ran while one was open for 0% -> 1% of each run, Pallas kernels for 16% -> 24%
where the time goes in v3:
time: 37.2 us; the launch traced here: 37 us
  starting transfers between devices  17.6 us (47%)
  Pallas kernels  11 us (30%)
  waiting for transfers between devices  7.37 us (20%)
  between operations  0.8 us (2%)
    ppermute x15, starting transfers between devices, swap(): return lax.ppermute(x, axis, [(i, i ^ bits) for i in range(count)])  17.6 us
    pallas_call x7, Pallas kernels, call(): pl.pallas_call(body, out_shape=outs, in_specs=[pl.BlockSpec(memory_space=...  11 us
    ppermute x15, waiting for transfers between devices, swap(): return lax.ppermute(x, axis, [(i, i ^ bits) for i in range(count)])  7.37 us
  transfers between devices with their start and end apart: 15, of which 8 were waited for; matrix products, arithmetic and copies ran while one was open for 1% of the time, Pallas kernels for 24%

profile of v3, /device:TPU:0, one launch (start us, length us, event | category | flops | bytes accessed | tf_op | source)
XLA Modules:
  0.0 37.0 jit_solution(4093944679003897067)
XLA Ops:
  0.6 0.5 %collective-permute-start.1 = (bf16[768,2048]{1,0:T(8,128)(2,1)}, bf16[768,2048]{1,0:T(8,128)(2,1)}, u32[]{:S(2)}, u32[]{:S(2)}) collective-permute-start(bf16[768,2048]{1,0:T(8,128)(2,1)} %bitcast.18), channel_id=1, source_target_pairs={{0,4},{4,0},{8,12},{12,8},{1,5},{5,1},{9,13},{13,9},{2,6},{6,2},{1... | collective-permute-start | bytes 9437192 | tf_op jit(solution)/shard_map/ppermute | solution.py:92
  1.1 0.9 %shard_map.93 = (bf16[16,2176]{1,0:T(8,128)(2,1)S(1)}, f32[8,128]{1,0:T(8,128)S(1)}) custom-call(bf16[16,2048]{1,0:T(8,128)(2,1)} %grad_hbm.1, s32[8,16]{1,0:T(8,128)} %bitcast.14, bf16[8,16]{1,0:T(8,128)(2,1)} %bitcast.22), custom_call_target="tpu_custom_call" | custom-call | flops 32768 | bytes 131072 | tf_op jit(solution)/shard_map/pallas_call | solution.py:107
  2.1 3.7 %collective-permute-start = (bf16[16,2176]{1,0:T(8,128)(2,1)S(1)}, bf16[16,2176]{1,0:T(8,128)(2,1)S(1)}, u32[]{:S(2)}, u32[]{:S(2)}) collective-permute-start(bf16[16,2176]{1,0:T(8,128)(2,1)S(1)} %get-tuple-element.24), channel_id=1, source_target_pairs={{0,2},{1,3},{2,0},{3,1},{4,6},{5,7},{6,4},{7,5},{8,10},{9,11},{10,... | collective-permute-start | bytes 208904 | tf_op jit(solution)/shard_map/ppermute | solution.py:92
  5.7 1.3 %collective-permute-start.2 = (bf16[16,2176]{1,0:T(8,128)(2,1)S(1)}, bf16[16,2176]{1,0:T(8,128)(2,1)S(1)}, u32[]{:S(2)}, u32[]{:S(2)}) collective-permute-start(bf16[16,2176]{1,0:T(8,128)(2,1)S(1)} %get-tuple-element.24), channel_id=1, source_target_pairs={{0,3},{1,2},{2,1},{3,0},{4,7},{5,6},{6,5},{7,4},{8,11},{9,10},{10,... | collective-permute-start | bytes 208904 | tf_op jit(solution)/shard_map/ppermute | solution.py:92
  7.1 0.2 collective-permute-start.3
  7.3 1.3 %shard_map.94 = (bf16[256,768]{1,0:T(8,128)(2,1)S(1)}, bf16[128,768]{1,0:T(8,128)(2,1)S(1)}) custom-call(bf16[256,768]{1,0:T(8,128)(2,1)} %bitcast.10, bf16[256,768]{1,0:T(8,128)(2,1)} %bitcast.12, f32[8,128]{1,0:T(8,128)S(1)} %get-tuple-element.25.refs_2_), custom_call_target="tpu_custom_call" | custom-call | flops 3932160 | bytes 1179648 | tf_op jit(solution)/shard_map/pallas_call | solution.py:107
  8.6 0.1 collective-permute-start.6
  8.7 1.5 %collective-permute-done = bf16[16,2176]{1,0:T(8,128)(2,1)S(1)} collective-permute-done((bf16[16,2176]{1,0:T(8,128)(2,1)S(1)}, bf16[16,2176]{1,0:T(8,128)(2,1)S(1)}, u32[]{:S(2)}, u32[]{:S(2)}) %collective-permute-start) | collective-permute-done | bytes 69664 | tf_op jit(solution)/shard_map/ppermute | solution.py:92
  10.3 1.8 %collective-permute-start.4 = (bf16[32,2176]{1,0:T(8,128)(2,1)S(1)}, bf16[32,2176]{1,0:T(8,128)(2,1)S(1)}, u32[]{:S(2)}, u32[]{:S(2)}) collective-permute-start(bf16[32,2176]{1,0:T(8,128)(2,1)S(1)} %pad_maximum_fusion.1), channel_id=1, source_target_pairs={{0,8},{4,12},{8,0},{12,4},{1,9},{5,13},{9,1},{13,5},{2,10},{6,14},... | collective-permute-start | bytes 417800 | tf_op jit(solution)/shard_map/ppermute | solution.py:92
  12.0 0.5 %collective-permute-done.2 = bf16[16,2176]{1,0:T(8,128)(2,1)S(1)} collective-permute-done((bf16[16,2176]{1,0:T(8,128)(2,1)S(1)}, bf16[16,2176]{1,0:T(8,128)(2,1)S(1)}, u32[]{:S(2)}, u32[]{:S(2)}) %collective-permute-start.2) | collective-permute-done | bytes 69664 | tf_op jit(solution)/shard_map/ppermute | solution.py:92
  12.5 0.4 %collective-permute-done.3 = bf16[16,2176]{1,0:T(8,128)(2,1)S(1)} collective-permute-done((bf16[16,2176]{1,0:T(8,128)(2,1)S(1)}, bf16[16,2176]{1,0:T(8,128)(2,1)S(1)}, u32[]{:S(2)}, u32[]{:S(2)}) %collective-permute-start.3) | collective-permute-done | bytes 69664 | tf_op jit(solution)/shard_map/ppermute | solution.py:92
  12.9 1.6 %collective-permute-start.5 = (bf16[32,2176]{1,0:T(8,128)(2,1)S(1)}, bf16[32,2176]{1,0:T(8,128)(2,1)S(1)}, u32[]{:S(2)}, u32[]{:S(2)}) collective-permute-start(bf16[32,2176]{1,0:T(8,128)(2,1)S(1)} %pad_maximum_fusion.2), channel_id=1, source_target_pairs={{0,8},{4,12},{8,0},{12,4},{1,9},{5,13},{9,1},{13,5},{2,10},{6,14},... | collective-permute-start | bytes 417800 | tf_op jit(solution)/shard_map/ppermute | solution.py:92
  14.6 1.5 %collective-permute-start.9 = (bf16[256,768]{1,0:T(8,128)(2,1)S(1)}, bf16[256,768]{1,0:T(8,128)(2,1)S(1)}, u32[]{:S(2)}, u32[]{:S(2)}) collective-permute-start(bf16[256,768]{1,0:T(8,128)(2,1)S(1)} %get-tuple-element.37.hidden_ref), channel_id=1, source_target_pairs={{0,16},{16,0},{1,17},{17,1},{2,18},{18,2},{3,19},{19,3},{4,20},{20... | collective-permute-start | bytes 1179656 | tf_op jit(solution)/shard_map/ppermute | solution.py:92
  16.1 0.0 collective-permute-done.1.refs_1_
  16.1 3.5 %shard_map.95 = (bf16[2048,768]{1,0:T(8,128)(2,1)S(1)}, bf16[2048,768]{1,0:T(8,128)(2,1)S(1)}) custom-call(bf16[768,2048]{1,0:T(8,128)(2,1)} %bitcast.19, bf16[768,2048]{1,0:T(8,128)(2,1)} %collective-permute-done.1.refs_1_, f32[8,128]{1,0:T(8,128)S(1)} %get-tuple-element.25.refs_2_), custom_call_target="tpu_custom_call" | custom-call | bytes 12582912 | tf_op jit(solution)/shard_map/pallas_call | solution.py:107
  19.6 0.0 collective-permute-done.4
  19.6 0.0 collective-permute-done.5
  19.7 0.0 copy-start
  19.7 0.0 copy-start.1
  19.7 0.0 collective-permute-done.6.other_hidden_ref
  19.8 1.1 %shard_map.96 = (f32[128,768]{1,0:T(8,128)S(1)}, f32[128,768]{1,0:T(8,128)S(1)}, f32[2,128]{1,0:T(2,128)S(1)}) custom-call(bf16[128,2176]{1,0:T(8,128)(2,1)S(1)} %constant_dynamic-update-slice_fusion.held_ref, bf16[2048,768]{1,0:T(8,128)(2,1)S(1)} %get-tuple-element.28.turned_ref, bf16[2048,768]{1,0:T(8,128)(2,1)S(1)} %get-tuple-element.29.other_turned_ref, ...), custom_call_target="tpu_custom_call" | custom-call | flops 805306368 | bytes 6291456 | tf_op jit(solution)/shard_map/pallas_call | solution.py:107
  20.8 0.0 copy-start.2
  20.8 0.6 %collective-permute-start.11 = (f32[1,2,128]{2,1,0:T(2,128)S(1)}, f32[1,2,128]{2,1,0:T(2,128)S(1)}, u32[]{:S(2)}, u32[]{:S(2)}) collective-permute-start(f32[1,2,128]{2,1,0:T(2,128)S(1)} %bitcast.16), channel_id=1, source_target_pairs={{0,8},{4,12},{8,0},{12,4},{1,9},{5,13},{9,1},{13,5},{2,10},{6,14},... | collective-permute-start | bytes 3080 | tf_op jit(solution)/shard_map/ppermute | solution.py:92
  21.4 0.0 collective-permute-start.7
  21.4 0.5 %collective-permute-start.8 = (f32[128,768]{1,0:T(8,128)S(1)}, f32[128,768]{1,0:T(8,128)S(1)}, u32[]{:S(2)}, u32[]{:S(2)}) collective-permute-start(f32[128,768]{1,0:T(8,128)S(1)} %get-tuple-element.35), channel_id=1, source_target_pairs={{0,4},{4,0},{8,12},{12,8},{1,5},{5,1},{9,13},{13,9},{2,6},{6,2},{1... | collective-permute-start | bytes 1179656 | tf_op jit(solution)/shard_map/ppermute | solution.py:92
  21.9 2.5 %collective-permute-done.11 = f32[1,2,128]{2,1,0:T(2,128)S(1)} collective-permute-done((f32[1,2,128]{2,1,0:T(2,128)S(1)}, f32[1,2,128]{2,1,0:T(2,128)S(1)}, u32[]{:S(2)}, u32[]{:S(2)}) %collective-permute-start.11) | collective-permute-done | bytes 1056 | tf_op jit(solution)/shard_map/ppermute | solution.py:92
  24.5 1.4 %collective-permute-start.12 = (f32[2,2,128]{2,1,0:T(2,128)S(1)}, f32[2,2,128]{2,1,0:T(2,128)S(1)}, u32[]{:S(2)}, u32[]{:S(2)}) collective-permute-start(f32[2,2,128]{2,1,0:T(2,128)S(1)} %pad_maximum_fusion.4), channel_id=1, source_target_pairs={{0,1},{1,0},{2,3},{3,2},{4,5},{5,4},{6,7},{7,6},{8,9},{9,8},{10,11... | collective-permute-start | bytes 6152 | tf_op jit(solution)/shard_map/ppermute | solution.py:92
  25.9 1.6 %collective-permute-start.10 = (bf16[128,1152]{1,0:T(8,128)(2,1)S(1)}, bf16[128,1152]{1,0:T(8,128)(2,1)S(1)}, u32[]{:S(2)}, u32[]{:S(2)}) collective-permute-start(bf16[128,1152]{1,0:T(8,128)(2,1)S(1)} %pad_maximum_fusion), channel_id=1, source_target_pairs={{0,16},{16,0},{1,17},{17,1},{2,18},{18,2},{3,19},{19,3},{4,20},{20... | collective-permute-start | bytes 884744 | tf_op jit(solution)/shard_map/ppermute | solution.py:92
  27.5 0.6 %collective-permute-done.12 = f32[2,2,128]{2,1,0:T(2,128)S(1)} collective-permute-done((f32[2,2,128]{2,1,0:T(2,128)S(1)}, f32[2,2,128]{2,1,0:T(2,128)S(1)}, u32[]{:S(2)}, u32[]{:S(2)}) %collective-permute-start.12) | collective-permute-done | bytes 2080 | tf_op jit(solution)/shard_map/ppermute | solution.py:92
  28.1 0.0 collective-permute-done.9.refs_0_
  28.1 2.8 %collective-permute-start.13 = (f32[4,2,128]{2,1,0:T(2,128)S(1)}, f32[4,2,128]{2,1,0:T(2,128)S(1)}, u32[]{:S(2)}, u32[]{:S(2)}) collective-permute-start(f32[4,2,128]{2,1,0:T(2,128)S(1)} %pad_maximum_fusion.3), channel_id=1, source_target_pairs={{0,2},{1,3},{2,0},{3,1},{4,6},{5,7},{6,4},{7,5},{8,10},{9,11},{10,... | collective-permute-start | bytes 12296 | tf_op jit(solution)/shard_map/ppermute | solution.py:92
  30.9 0.0 collective-permute-done.8.rest_back_ref
  30.9 0.0 collective-permute-done.7.rest_ref
  30.9 0.0 copy-done
  30.9 0.0 copy-done.1
  30.9 1.4 %shard_map.97 = (bf16[256,768]{1,0:T(8,128)(2,1)}, bf16[256,768]{1,0:T(8,128)(2,1)}, bf16[256,768]{1,0:T(8,128)(2,1)S(1)}) custom-call(bf16[128,2176]{1,0:T(8,128)(2,1)S(1)} %constant_dynamic-update-slice_fusion.held_ref, bf16[128,2176]{1,0:T(8,128)(2,1)S(1)} %collective-permute-done.7.rest_ref, f32[128,768]{1,0:T(8,128)S(1)} %get-tuple-element.34.back_ref, ...), custom_call_target="tpu_custom_call" | custom-call | flops 5898240 | bytes 2359296 | tf_op jit(solution)/shard_map/pallas_call | solution.py:107
  32.3 0.3 collective-permute-done.13
  32.7 0.5 %collective-permute-done.10.refs_1_ = bf16[128,1152]{1,0:T(8,128)(2,1)S(1)} collective-permute-done((bf16[128,1152]{1,0:T(8,128)(2,1)S(1)}, bf16[128,1152]{1,0:T(8,128)(2,1)S(1)}, u32[]{:S(2)}, u32[]{:S(2)}) %collective-permute-start.10) | collective-permute-done | bytes 294944 | tf_op jit(solution)/shard_map/ppermute | solution.py:92
  33.2 0.0 collective-permute-start.14
  33.2 0.0 copy-done.2
  33.2 0.7 %shard_map.99 = f32[8,16]{1,0:T(8,128)} custom-call(s32[8,16]{1,0:T(8,128)S(1)} %bitcast.15, f32[8,2,128]{2,1,0:T(2,128)S(1)} %constant_dynamic-update-slice_fusion.5.sums_ref), custom_call_target="tpu_custom_call" | custom-call | flops 256 | bytes 256 | tf_op jit(solution)/shard_map/pallas_call | solution.py:107
  33.8 0.9 %collective-permute-done.14.refs_2_ = bf16[128,1152]{1,0:T(8,128)(2,1)S(1)} collective-permute-done((bf16[128,1152]{1,0:T(8,128)(2,1)S(1)}, bf16[128,1152]{1,0:T(8,128)(2,1)S(1)}, u32[]{:S(2)}, u32[]{:S(2)}) %collective-permute-start.14) | collective-permute-done | bytes 294944 | tf_op jit(solution)/shard_map/ppermute | solution.py:92
  34.7 2.3 %shard_map.98 = bf16[768,1024]{1,0:T(8,128)(2,1)} custom-call(bf16[256,768]{1,0:T(8,128)(2,1)S(1)} %get-tuple-element.36.scaled_ref, bf16[128,2176]{1,0:T(8,128)(2,1)S(1)} %constant_dynamic-update-slice_fusion.held_ref, bf16[128,2176]{1,0:T(8,128)(2,1)S(1)} %collective-permute-done.7.rest_ref, bf16[256,768]{1,0:T(8,128)(2,1)S(1)} %collective-permute-done.9.refs_0_, ...), custom_call_target="tpu_custom_call" | custom-call | flops 805306368 | bytes 3145728 | tf_op jit(solution)/shard_map/pallas_call | solution.py:107
  (15 shorter events, 0.2 us)
Async XLA Ops:
  0.6 15.4 %collective-permute-start.1 = (bf16[768,2048]{1,0:T(8,128)(2,1)}, bf16[768,2048]{1,0:T(8,128)(2,1)}, u32[]{:S(2)}, u32[]{:S(2)}) collective-permute-start(bf16[768,2048]{1,0:T(8,128)(2,1)} %bitcast.18), channel_id=1, source_target_pairs={{0,4},{4,0},{8,12},{12,8},{1,5},{5,1},{9,13},{13,9},{2,6},{6,2},{1... | collective-permute-start | bytes 9437192 | tf_op jit(solution)/shard_map/ppermute | solution.py:92
  2.1 8.2 %collective-permute-start = (bf16[16,2176]{1,0:T(8,128)(2,1)S(1)}, bf16[16,2176]{1,0:T(8,128)(2,1)S(1)}, u32[]{:S(2)}, u32[]{:S(2)}) collective-permute-start(bf16[16,2176]{1,0:T(8,128)(2,1)S(1)} %get-tuple-element.24), channel_id=1, source_target_pairs={{0,2},{1,3},{2,0},{3,1},{4,6},{5,7},{6,4},{7,5},{8,10},{9,11},{10,... | collective-permute-start | bytes 208904 | tf_op jit(solution)/shard_map/ppermute | solution.py:92
  5.7 6.8 %collective-permute-start.2 = (bf16[16,2176]{1,0:T(8,128)(2,1)S(1)}, bf16[16,2176]{1,0:T(8,128)(2,1)S(1)}, u32[]{:S(2)}, u32[]{:S(2)}) collective-permute-start(bf16[16,2176]{1,0:T(8,128)(2,1)S(1)} %get-tuple-element.24), channel_id=1, source_target_pairs={{0,3},{1,2},{2,1},{3,0},{4,7},{5,6},{6,5},{7,4},{8,11},{9,10},{10,... | collective-permute-start | bytes 208904 | tf_op jit(solution)/shard_map/ppermute | solution.py:92
  7.1 5.9 %collective-permute-start.3 = (bf16[16,2176]{1,0:T(8,128)(2,1)S(1)}, bf16[16,2176]{1,0:T(8,128)(2,1)S(1)}, u32[]{:S(2)}, u32[]{:S(2)}) collective-permute-start(bf16[16,2176]{1,0:T(8,128)(2,1)S(1)} %get-tuple-element.24), channel_id=1, source_target_pairs={{0,1},{1,0},{2,3},{3,2},{4,5},{5,4},{6,7},{7,6},{8,9},{9,8},{10,11... | collective-permute-start | bytes 208904 | tf_op jit(solution)/shard_map/ppermute | solution.py:92
  8.6 11.1 %collective-permute-start.6 = (bf16[128,768]{1,0:T(8,128)(2,1)S(1)}, bf16[128,768]{1,0:T(8,128)(2,1)S(1)}, u32[]{:S(2)}, u32[]{:S(2)}) collective-permute-start(bf16[128,768]{1,0:T(8,128)(2,1)S(1)} %get-tuple-element.31), channel_id=1, source_target_pairs={{0,4},{4,0},{8,12},{12,8},{1,5},{5,1},{9,13},{13,9},{2,6},{6,2},{1... | collective-permute-start | bytes 589832 | tf_op jit(solution)/shard_map/ppermute | solution.py:92
  10.3 9.3 %collective-permute-start.4 = (bf16[32,2176]{1,0:T(8,128)(2,1)S(1)}, bf16[32,2176]{1,0:T(8,128)(2,1)S(1)}, u32[]{:S(2)}, u32[]{:S(2)}) collective-permute-start(bf16[32,2176]{1,0:T(8,128)(2,1)S(1)} %pad_maximum_fusion.1), channel_id=1, source_target_pairs={{0,8},{4,12},{8,0},{12,4},{1,9},{5,13},{9,1},{13,5},{2,10},{6,14},... | collective-permute-start | bytes 417800 | tf_op jit(solution)/shard_map/ppermute | solution.py:92
  12.9 6.7 %collective-permute-start.5 = (bf16[32,2176]{1,0:T(8,128)(2,1)S(1)}, bf16[32,2176]{1,0:T(8,128)(2,1)S(1)}, u32[]{:S(2)}, u32[]{:S(2)}) collective-permute-start(bf16[32,2176]{1,0:T(8,128)(2,1)S(1)} %pad_maximum_fusion.2), channel_id=1, source_target_pairs={{0,8},{4,12},{8,0},{12,4},{1,9},{5,13},{9,1},{13,5},{2,10},{6,14},... | collective-permute-start | bytes 417800 | tf_op jit(solution)/shard_map/ppermute | solution.py:92
  14.6 13.5 %collective-permute-start.9 = (bf16[256,768]{1,0:T(8,128)(2,1)S(1)}, bf16[256,768]{1,0:T(8,128)(2,1)S(1)}, u32[]{:S(2)}, u32[]{:S(2)}) collective-permute-start(bf16[256,768]{1,0:T(8,128)(2,1)S(1)} %get-tuple-element.37.hidden_ref), channel_id=1, source_target_pairs={{0,16},{16,0},{1,17},{17,1},{2,18},{18,2},{3,19},{19,3},{4,20},{20... | collective-permute-start | bytes 1179656 | tf_op jit(solution)/shard_map/ppermute | solution.py:92
  19.7 11.2 %copy-start = (bf16[1,1,256,768]{3,2,1,0:T(8,128)(2,1)S(1)}, bf16[1,1,256,768]{3,2,1,0:T(8,128)(2,1)}, u32[]{:S(2)}) copy-start(bf16[1,1,256,768]{3,2,1,0:T(8,128)(2,1)} %param.9) | copy-start | bytes 1179652
  19.7 11.2 %copy-start.1 = (bf16[1,1,256,768]{3,2,1,0:T(8,128)(2,1)S(1)}, bf16[1,1,256,768]{3,2,1,0:T(8,128)(2,1)}, u32[]{:S(2)}) copy-start(bf16[1,1,256,768]{3,2,1,0:T(8,128)(2,1)} %param.10) | copy-start | bytes 1179652
  20.8 12.3 %copy-start.2 = (s32[16,8]{0,1:T(8,128)S(1)}, s32[16,8]{0,1:T(8,128)}, u32[]{:S(2)}) copy-start(s32[16,8]{0,1:T(8,128)} %param.7) | copy-start | bytes 1540
  20.8 3.6 %collective-permute-start.11 = (f32[1,2,128]{2,1,0:T(2,128)S(1)}, f32[1,2,128]{2,1,0:T(2,128)S(1)}, u32[]{:S(2)}, u32[]{:S(2)}) collective-permute-start(f32[1,2,128]{2,1,0:T(2,128)S(1)} %bitcast.16), channel_id=1, source_target_pairs={{0,8},{4,12},{8,0},{12,4},{1,9},{5,13},{9,1},{13,5},{2,10},{6,14},... | collective-permute-start | bytes 3080 | tf_op jit(solution)/shard_map/ppermute | solution.py:92
  21.4 9.5 %collective-permute-start.7 = (bf16[128,2176]{1,0:T(8,128)(2,1)S(1)}, bf16[128,2176]{1,0:T(8,128)(2,1)S(1)}, u32[]{:S(2)}, u32[]{:S(2)}) collective-permute-start(bf16[128,2176]{1,0:T(8,128)(2,1)S(1)} %constant_dynamic-update-slice_fusion.held_ref), channel_id=1, source_target_pairs={{0,4},{4,0},{8,12},{12,8},{1,5},{5,1},{9,13},{13,9},{2,6},{6,2},{1... | collective-permute-start | bytes 1671176 | tf_op jit(solution)/shard_map/ppermute | solution.py:92
  21.4 9.5 %collective-permute-start.8 = (f32[128,768]{1,0:T(8,128)S(1)}, f32[128,768]{1,0:T(8,128)S(1)}, u32[]{:S(2)}, u32[]{:S(2)}) collective-permute-start(f32[128,768]{1,0:T(8,128)S(1)} %get-tuple-element.35), channel_id=1, source_target_pairs={{0,4},{4,0},{8,12},{12,8},{1,5},{5,1},{9,13},{13,9},{2,6},{6,2},{1... | collective-permute-start | bytes 1179656 | tf_op jit(solution)/shard_map/ppermute | solution.py:92
  24.5 3.6 %collective-permute-start.12 = (f32[2,2,128]{2,1,0:T(2,128)S(1)}, f32[2,2,128]{2,1,0:T(2,128)S(1)}, u32[]{:S(2)}, u32[]{:S(2)}) collective-permute-start(f32[2,2,128]{2,1,0:T(2,128)S(1)} %pad_maximum_fusion.4), channel_id=1, source_target_pairs={{0,1},{1,0},{2,3},{3,2},{4,5},{5,4},{6,7},{7,6},{8,9},{9,8},{10,11... | collective-permute-start | bytes 6152 | tf_op jit(solution)/shard_map/ppermute | solution.py:92
  25.9 7.3 %collective-permute-start.10 = (bf16[128,1152]{1,0:T(8,128)(2,1)S(1)}, bf16[128,1152]{1,0:T(8,128)(2,1)S(1)}, u32[]{:S(2)}, u32[]{:S(2)}) collective-permute-start(bf16[128,1152]{1,0:T(8,128)(2,1)S(1)} %pad_maximum_fusion), channel_id=1, source_target_pairs={{0,16},{16,0},{1,17},{17,1},{2,18},{18,2},{3,19},{19,3},{4,20},{20... | collective-permute-start | bytes 884744 | tf_op jit(solution)/shard_map/ppermute | solution.py:92
  28.1 4.6 %collective-permute-start.13 = (f32[4,2,128]{2,1,0:T(2,128)S(1)}, f32[4,2,128]{2,1,0:T(2,128)S(1)}, u32[]{:S(2)}, u32[]{:S(2)}) collective-permute-start(f32[4,2,128]{2,1,0:T(2,128)S(1)} %pad_maximum_fusion.3), channel_id=1, source_target_pairs={{0,2},{1,3},{2,0},{3,1},{4,6},{5,7},{6,4},{7,5},{8,10},{9,11},{10,... | collective-permute-start | bytes 12296 | tf_op jit(solution)/shard_map/ppermute | solution.py:92
  33.2 1.6 %collective-permute-start.14 = (bf16[128,1152]{1,0:T(8,128)(2,1)S(1)}, bf16[128,1152]{1,0:T(8,128)(2,1)S(1)}, u32[]{:S(2)}, u32[]{:S(2)}) collective-permute-start(bf16[128,1152]{1,0:T(8,128)(2,1)S(1)} %collective-permute-done.10.refs_1_), channel_id=1, source_target_pairs={{0,4},{4,0},{8,12},{12,8},{1,5},{5,1},{9,13},{13,9},{2,6},{6,2},{1... | collective-permute-start | bytes 884744 | tf_op jit(solution)/shard_map/ppermute | solution.py:92

commit v4 on v2

--- a/solution.py
+++ b/solution.py
@@ -8,8 +8,8 @@
 from jax.sharding import PartitionSpec as P
 
 LANES = 128
-FIRST_LIMIT = 16 * 1024 * 1024
-VMEM_LIMIT = 24 * 1024 * 1024
+PARTS = 4
+VMEM_LIMIT = 14 * 1024 * 1024
 
 
 def shards_exchange(out_grad, routes, gates, pre_gate, pre_up, down_weight):
@@ -97,7 +97,7 @@
     return lax.optimization_barrier((x,) + done)[0]
 
 
-def call(kernel, outs, cost, *args, hbm=0, scratch=(), deps=(), limit=VMEM_LIMIT):
+def call(kernel, outs, cost, *args, hbm=0, scratch=(), deps=(), out_space=pltpu.VMEM):
     flops, moved = cost
     body = kernel
     if deps:
@@ -111,11 +111,15 @@
         in_specs=[pl.BlockSpec(memory_space=pltpu.HBM)] * hbm
         + [pl.BlockSpec(memory_space=pltpu.VMEM)] * (len(args) - hbm)
         + [pl.BlockSpec(memory_space=pl.ANY)] * len(deps),
-        out_specs=jax.tree.map(lambda _: pl.BlockSpec(memory_space=pltpu.VMEM), outs),
+        out_specs=jax.tree.map(lambda _: pl.BlockSpec(memory_space=out_space), outs),
         scratch_shapes=scratch,
-        compiler_params=pltpu.CompilerParams(vmem_limit_bytes=limit),
+        compiler_params=pltpu.CompilerParams(vmem_limit_bytes=VMEM_LIMIT),
         cost_estimate=pl.CostEstimate(flops=flops, bytes_accessed=moved, transcendentals=0),
     )(*args, *deps)
+
+
+def in_hbm(*arrays):
+    return [pltpu.with_memory_space_constraint(x, pltpu.HBM) for x in arrays]
 
 
 def peer(xors):
@@ -135,6 +139,7 @@
     out_ref,
     hidden_ref,
     rest_ref,
+    token_ref,
     routes_ref,
     gates_ref,
     pre_gate_ref,
@@ -156,6 +161,7 @@
     ]
     for copy in copies:
         copy.start()
+    token_ref[...] = jnp.zeros(token_ref.shape, token_ref.dtype)
     copies[0].wait()
     copies[1].wait()
     routes = routes_ref[...]
@@ -179,30 +185,45 @@
             rest_ref[(place - half) * rows : (place - half + 1) * rows, :] = result
 
 
-def back_kernel(
-    features,
-    held_ref,
-    weight_ref,
-    other_weight_ref,
-    hidden_ref,
-    other_hidden_ref,
-    back_ref,
-    other_back_ref,
-    sums_ref,
-):
+def turn_kernel(one_hbm, two_ref, *refs):
+    one_ref, sems = refs[-2:]
+    outs = refs[:-2]
+    units, features = one_ref.shape
+    cut = outs[0].shape[0]
+    copies = [
+        pltpu.make_async_copy(
+            one_hbm.at[pl.ds(at, LANES)], one_ref.at[pl.ds(at, LANES)], sems.at[step]
+        )
+        for step, at in enumerate(range(0, units, LANES))
+    ]
+    for copy in copies:
+        copy.start()
+    for held, parts, waits in ((two_ref, outs[PARTS:], ()), (one_ref, outs[:PARTS], copies)):
+        for step, at in enumerate(range(0, units, LANES)):
+            if waits:
+                waits[step].wait()
+            for to in range(0, features, LANES):
+                line = to % cut
+                parts[to // cut][line : line + LANES, at : at + LANES] = held[
+                    at : at + LANES, to : to + LANES
+                ].T
+
+
+def back_kernel(features, held_ref, hidden_ref, other_hidden_ref, *refs):
+    back_ref, other_back_ref, sums_ref = refs[-3:]
     rows = held_ref.shape[0]
-    for expert, (matrix_ref, act_ref, result_ref) in enumerate(
-        (
-            (weight_ref, hidden_ref, back_ref),
-            (other_weight_ref, other_hidden_ref, other_back_ref),
-        )
+    for expert, (act_ref, result_ref) in enumerate(
+        ((hidden_ref, back_ref), (other_hidden_ref, other_back_ref))
     ):
-        back = lax.dot_general(
-            held_ref[:, :features],
-            matrix_ref[...],
-            (((1,), (1,)), ((), ())),
-            preferred_element_type=jnp.float32,
-        )
+        back = jnp.zeros(result_ref.shape, jnp.float32)
+        for part in range(PARTS):
+            part_ref = refs[expert * PARTS + part]
+            depth = part_ref.shape[0]
+            back = back + jnp.dot(
+                held_ref[:, part * depth : (part + 1) * depth],
+                part_ref[...],
+                preferred_element_type=jnp.float32,
+            )
         result_ref[...] = back
         product = act_ref[:rows, :].astype(jnp.float32) * back
         folded = product[:, :LANES]
@@ -258,8 +279,7 @@
 
 
 def down_kernel(pairs, scaled_ref, held_ref, rest_ref, *refs):
-    out_ref, token_ref = refs[-2:]
-    token_ref[...] = jnp.zeros(token_ref.shape, token_ref.dtype)
+    out_ref, held_out_ref, sems = refs[-3:]
     columns = out_ref.shape[1]
     mine = pl.ds(pl.multiple_of(lax.axis_index("dp") * columns, columns), columns)
     scaled = [scaled_ref[...]]
@@ -271,12 +291,23 @@
         )
         scaled.append((gate * hidden_ref[...].astype(jnp.float32)).astype(scaled_ref.dtype))
         tokens += [one_ref[:, :columns], two_ref[:, :columns]]
-    out_ref[...] = lax.dot_general(
-        jnp.concatenate(scaled, axis=0),
-        jnp.concatenate(tokens, axis=0),
-        (((0,), (0,)), ((), ())),
-        preferred_element_type=jnp.float32,
-    ).astype(out_ref.dtype)
+    scaled = jnp.concatenate(scaled, axis=0)
+    tokens = jnp.concatenate(tokens, axis=0)
+    copies = []
+    for at in range(0, out_ref.shape[0], 2 * LANES):
+        here = pl.ds(at, 2 * LANES)
+        held_out_ref[here, :] = lax.dot_general(
+            scaled[:, at : at + 2 * LANES],
+            tokens,
+            (((0,), (0,)), ((), ())),
+            preferred_element_type=jnp.float32,
+        ).astype(out_ref.dtype)
+        copies.append(
+            pltpu.make_async_copy(held_out_ref.at[here], out_ref.at[here], sems.at[len(copies)])
+        )
+        copies[-1].start()
+    for copy in copies:
+        copy.wait()
 
 
 def pick_kernel(order, back_order, rows, routes_ref, sums_ref, out_ref):
@@ -312,25 +343,24 @@
 
     near = max(narrow_count // 2, 1)
     wide_bits = [1 << b for b in range(1, wide_count.bit_length() - 1)]
-    order = [(0, bits) for bits in range(narrow_count)]
+    reach = [0] + list(range(near, narrow_count)) + list(range(1, near))
+    order = [(0, bits) for bits in reach]
     for bits in wide_bits + [1]:
         order += [(w ^ bits, n) for w, n in order]
     order = tuple(order)
 
-    payload, hidden, rest_hidden = call(
+    other_weight = swap(weight, "wide", 1)
+    payload, hidden, rest_hidden, token = call(
         functools.partial(first_kernel, order),
         (
             shape((rows, features + LANES), bf16),
             shape((slot_count, units), bf16),
             shape((half_count, units), bf16),
+            shape((8, LANES), f32),
         ),
         (20 * slot_count * units, 6 * slot_count * units),
-        *(
-            pltpu.with_memory_space_constraint(x, pltpu.HBM)
-            for x in (out_grad, routes_t, gates_t, pre_gate, pre_up)
-        ),
+        *in_hbm(out_grad, routes_t, gates_t, pre_gate, pre_up),
         hbm=5,
-        limit=FIRST_LIMIT,
         scratch=[
             pltpu.VMEM(routes_t.shape, routes_t.dtype),
             pltpu.VMEM(gates_t.shape, gates_t.dtype),
@@ -339,17 +369,28 @@
             pltpu.SemaphoreType.DMA((5,)),
         ],
     )
-    along = [payload] + [swap(payload, "narrow", bits) for bits in range(1, narrow_count)]
+    along = [swap(payload, "narrow", bits) if bits else payload for bits in reach]
+    turned = call(
+        turn_kernel,
+        (shape((features // PARTS, units), bf16),) * (2 * PARTS),
+        (0, 8 * features * units),
+        *in_hbm(weight),
+        other_weight,
+        hbm=1,
+        deps=(token,),
+        scratch=[
+            pltpu.VMEM(weight.shape, weight.dtype),
+            pltpu.SemaphoreType.DMA((units // LANES,)),
+        ],
+    )
+    over = [swap(hidden, "dp", bits) for bits in range(1, dp_count)]
+    other_hidden = swap(after(rest_hidden, *along[near:]), "wide", 1)
     groups = [jnp.concatenate(along[:near], axis=0)]
     if along[near:]:
         groups.append(jnp.concatenate(along[near:], axis=0))
     for bits in wide_bits:
         groups += [swap(group, "wide", bits) for group in groups]
-    held = jnp.concatenate(groups, axis=0)
-    late = along[near % len(along)]
-    other_weight = swap(weight, "wide", 1)
-    other_hidden = swap(after(rest_hidden, late), "wide", 1)
-    over = [swap(after(hidden, late), "dp", bits) for bits in range(1, dp_count)]
+    held = jnp.concatenate([after(groups[0], *turned, *over)] + groups[1:], axis=0)
     back, other_back, sums = call(
         functools.partial(back_kernel, features),
         (
@@ -359,59 +400,56 @@
         ),
         (2 * slot_count * units * features, 4 * units * features),
         held,
-        weight,
-        other_weight,
         hidden,
         other_hidden,
-    )
-    steps = [("wide", b) for b in wide_bits] + [
-        ("narrow", 1 << b) for b in range(narrow_count.bit_length() - 1)
-    ]
+        *turned,
+    )
     found = sums[None]
     back_order = [(0, 0)]
-    waits = []
-    for axis, bits in steps:
-        found = jnp.concatenate([after(found, *waits), swap(found, axis, bits)], axis=0)
-        step = (bits, 0) if axis == "wide" else (0, bits)
-        back_order += [(w ^ step[0], n ^ step[1]) for w, n in back_order]
-        if len(back_order) == 2:
-            rest = swap(after(held, sums), "wide", 1)
-            rest_back = swap(other_back, "wide", 1)
-            crossed = []
-            for bits in range(1, dp_count):
-                partner = lax.axis_index("dp") ^ bits
-                cut = lax.dynamic_slice_in_dim(
-                    held[:, :features], partner * columns, columns, axis=1
-                )
-                cut = jnp.concatenate([cut, held[:, features:]], axis=1)
-                crossed.append(swap(after(cut, found, *over), "dp", bits))
-        if len(back_order) == 4:
-            grad_a, grad_b, scaled = call(
-                functools.partial(grads_kernel, order, rows, features),
-                (shape((slot_count, units), bf16),) * 3,
-                (30 * slot_count * units, 12 * slot_count * units),
-                held,
-                rest,
-                back,
-                rest_back,
-                hidden,
-                pre_gate,
-                pre_up,
-            )
-            waits = [scaled]
-            half_found = found
+    for bits in wide_bits:
+        found = jnp.concatenate([found, swap(found, "wide", bits)], axis=0)
+        back_order += [(w ^ bits, n) for w, n in back_order]
+    rest = swap(after(held, sums), "wide", 1)
+    rest_back = swap(other_back, "wide", 1)
+    crossed = []
+    for bits in range(1, dp_count):
+        partner = lax.axis_index("dp") ^ bits
+        cut = lax.dynamic_slice_in_dim(held[:, :features], partner * columns, columns, axis=1)
+        cut = jnp.concatenate([cut, held[:, features:]], axis=1)
+        crossed.append(swap(after(cut, sums), "dp", bits))
+    grad_a, grad_b, scaled = call(
+        functools.partial(grads_kernel, order, rows, features),
+        (shape((slot_count, units), bf16),) * 3,
+        (30 * slot_count * units, 12 * slot_count * units),
+        held,
+        rest,
+        back,
+        rest_back,
+        hidden,
+        pre_gate,
+        pre_up,
+    )
+    mine = found
+    parts = [swap(mine, "narrow", bits) for bits in reach[1:]]
+    found = jnp.concatenate([after(mine, scaled)] + parts, axis=0)
+    back_order = [(w, n ^ bits) for bits in reach for w, n in back_order]
     others = []
     for bits in range(1, dp_count):
-        one = after(crossed[bits - 1], half_found)
+        one = after(crossed[bits - 1], found)
         others += [over[bits - 1], one, swap(one, "wide", 1)]
-    grad_down, token = call(
+    grad_down = call(
         functools.partial(down_kernel, dp_count - 1),
-        (shape((units, columns), bf16), shape((8, LANES), f32)),
+        shape((units, columns), bf16),
         (2 * dp_count * slot_count * units * columns, 4 * units * columns),
         scaled,
         held,
         rest,
         *others,
+        out_space=pltpu.HBM,
+        scratch=[
+            pltpu.VMEM((units, columns), bf16),
+            pltpu.SemaphoreType.DMA((units // (2 * LANES),)),
+        ],
     )
     picked = call(
         functools.partial(pick_kernel, order, tuple(back_order), rows),
@@ -419,7 +457,6 @@
         (slot_count, slot_count),
         routes_t,
         found,
-        deps=(token,),
     )
     return (grad_down[None], grad_a[None, None], grad_b[None, None], picked.T)
 

time: 43.4 us -> 36.7 us (0.85)
  waiting for transfers between devices: 14.3 us -> 6.56 us
  starting transfers between devices: 18 us -> 19.8 us
  Pallas kernels: 9.91 us -> 9.14 us
    ppermute x15 -> x16, waiting for transfers between devices: 14.3 us -> 6.56 us  [swap(): return lax.ppermute(x, axis, [(i, i ^ bits) for i in range(count)])]
    ppermute x15 -> x16, starting transfers between devices: 18 us -> 19.8 us  [swap(): return lax.ppermute(x, axis, [(i, i ^ bits) for i in range(count)])]
    pallas_call x5 -> x6, Pallas kernels: 9.91 us -> 9.14 us  [call(): pl.pallas_call(body, out_shape=outs, in_specs=[pl.BlockSpec(memory_space=...]
  transfers between devices with their start and end apart: 15 -> 16, of which waited for: 8 -> 9; matrix products, arithmetic and copies ran while one was open for 0% -> 1% of each run, Pallas kernels for 16% -> 17%
where the time goes in v4:
time: 36.7 us; the launch traced here: 36.5 us
  starting transfers between devices  19.8 us (54%)
  Pallas kernels  9.14 us (25%)
  waiting for transfers between devices  6.56 us (18%)
  between operations  0.79 us (2%)
    ppermute x16, starting transfers between devices, swap(): return lax.ppermute(x, axis, [(i, i ^ bits) for i in range(count)])  19.8 us
    pallas_call x6, Pallas kernels, call(): pl.pallas_call(body, out_shape=outs, in_specs=[pl.BlockSpec(memory_space=...  9.14 us
    ppermute x16, waiting for transfers between devices, swap(): return lax.ppermute(x, axis, [(i, i ^ bits) for i in range(count)])  6.56 us
  transfers between devices with their start and end apart: 16, of which 9 were waited for; matrix products, arithmetic and copies ran while one was open for 1% of the time, Pallas kernels for 17%

profile of v4, /device:TPU:0, one launch (start us, length us, event | category | flops | bytes accessed | tf_op | source)
XLA Modules:
  0.0 36.5 jit_solution(14638537196409432887)
XLA Ops:
  0.6 0.5 %collective-permute-start.1 = (bf16[768,2048]{1,0:T(8,128)(2,1)}, bf16[768,2048]{1,0:T(8,128)(2,1)S(1)}, u32[]{:S(2)}, u32[]{:S(2)}) collective-permute-start(bf16[768,2048]{1,0:T(8,128)(2,1)} %bitcast.18), channel_id=1, source_target_pairs={{0,4},{4,0},{8,12},{12,8},{1,5},{5,1},{9,13},{13,9},{2,6},{6,2},{1... | collective-permute-start | bytes 9437192 | tf_op jit(solution)/shard_map/ppermute | solution.py:93
  1.1 1.4 %shard_map.93 = (bf16[16,2176]{1,0:T(8,128)(2,1)S(1)}, bf16[256,768]{1,0:T(8,128)(2,1)S(1)}, bf16[128,768]{1,0:T(8,128)(2,1)S(1)}, f32[8,128]{1,0:T(8,128)S(1)}) custom-call(bf16[16,2048]{1,0:T(8,128)(2,1)} %grad_hbm.1, s32[8,16]{1,0:T(8,128)} %bitcast.14, bf16[8,16]{1,0:T(8,128)(2,1)} %bitcast.22, bf16[256,768]{1,0:T(8,128)(2,1)} %bitcast.10, ...), custom_call_target="tpu_custom_call" | custom-call | flops 3932160 | bytes 1179648 | tf_op jit(solution)/shard_map/pallas_call | solution.py:108
  2.6 3.7 %collective-permute-start = (bf16[16,2176]{1,0:T(8,128)(2,1)S(1)}, bf16[16,2176]{1,0:T(8,128)(2,1)S(1)}, u32[]{:S(2)}, u32[]{:S(2)}) collective-permute-start(bf16[16,2176]{1,0:T(8,128)(2,1)S(1)} %get-tuple-element.28), channel_id=1, source_target_pairs={{0,2},{1,3},{2,0},{3,1},{4,6},{5,7},{6,4},{7,5},{8,10},{9,11},{10,... | collective-permute-start | bytes 208904 | tf_op jit(solution)/shard_map/ppermute | solution.py:93
  6.2 1.3 %collective-permute-start.3 = (bf16[16,2176]{1,0:T(8,128)(2,1)S(1)}, bf16[16,2176]{1,0:T(8,128)(2,1)S(1)}, u32[]{:S(2)}, u32[]{:S(2)}) collective-permute-start(bf16[16,2176]{1,0:T(8,128)(2,1)S(1)} %get-tuple-element.28), channel_id=1, source_target_pairs={{0,3},{1,2},{2,1},{3,0},{4,7},{5,6},{6,5},{7,4},{8,11},{9,10},{10,... | collective-permute-start | bytes 208904 | tf_op jit(solution)/shard_map/ppermute | solution.py:93
  7.6 0.2 collective-permute-start.4
  7.8 1.5 %collective-permute-start.2 = (bf16[256,768]{1,0:T(8,128)(2,1)S(1)}, bf16[256,768]{1,0:T(8,128)(2,1)S(1)}, u32[]{:S(2)}, u32[]{:S(2)}) collective-permute-start(bf16[256,768]{1,0:T(8,128)(2,1)S(1)} %get-tuple-element.38.hidden_ref), channel_id=1, source_target_pairs={{0,16},{16,0},{1,17},{17,1},{2,18},{18,2},{3,19},{19,3},{4,20},{20... | collective-permute-start | bytes 1179656 | tf_op jit(solution)/shard_map/ppermute | solution.py:93
  9.3 1.4 %collective-permute-done = bf16[16,2176]{1,0:T(8,128)(2,1)S(1)} collective-permute-done((bf16[16,2176]{1,0:T(8,128)(2,1)S(1)}, bf16[16,2176]{1,0:T(8,128)(2,1)S(1)}, u32[]{:S(2)}, u32[]{:S(2)}) %collective-permute-start) | collective-permute-done | bytes 69664 | tf_op jit(solution)/shard_map/ppermute | solution.py:93
  10.8 1.8 %collective-permute-start.5 = (bf16[32,2176]{1,0:T(8,128)(2,1)S(1)}, bf16[32,2176]{1,0:T(8,128)(2,1)S(1)}, u32[]{:S(2)}, u32[]{:S(2)}) collective-permute-start(bf16[32,2176]{1,0:T(8,128)(2,1)S(1)} %constant_dynamic-update-slice_fusion), channel_id=1, source_target_pairs={{0,8},{4,12},{8,0},{12,4},{1,9},{5,13},{9,1},{13,5},{2,10},{6,14},... | collective-permute-start | bytes 417800 | tf_op jit(solution)/shard_map/ppermute | solution.py:93
  12.5 0.5 %collective-permute-done.3 = bf16[16,2176]{1,0:T(8,128)(2,1)S(1)} collective-permute-done((bf16[16,2176]{1,0:T(8,128)(2,1)S(1)}, bf16[16,2176]{1,0:T(8,128)(2,1)S(1)}, u32[]{:S(2)}, u32[]{:S(2)}) %collective-permute-start.3) | collective-permute-done | bytes 69664 | tf_op jit(solution)/shard_map/ppermute | solution.py:93
  13.0 0.4 %collective-permute-done.4 = bf16[16,2176]{1,0:T(8,128)(2,1)S(1)} collective-permute-done((bf16[16,2176]{1,0:T(8,128)(2,1)S(1)}, bf16[16,2176]{1,0:T(8,128)(2,1)S(1)}, u32[]{:S(2)}, u32[]{:S(2)}) %collective-permute-start.4) | collective-permute-done | bytes 69664 | tf_op jit(solution)/shard_map/ppermute | solution.py:93
  13.4 1.6 %collective-permute-start.6 = (bf16[32,2176]{1,0:T(8,128)(2,1)S(1)}, bf16[32,2176]{1,0:T(8,128)(2,1)S(1)}, u32[]{:S(2)}, u32[]{:S(2)}) collective-permute-start(bf16[32,2176]{1,0:T(8,128)(2,1)S(1)} %pad_maximum_fusion.1), channel_id=1, source_target_pairs={{0,8},{4,12},{8,0},{12,4},{1,9},{5,13},{9,1},{13,5},{2,10},{6,14},... | collective-permute-start | bytes 417800 | tf_op jit(solution)/shard_map/ppermute | solution.py:93
  15.1 0.0 collective-permute-start.7
  15.1 0.0 collective-permute-done.1.refs_1_
  15.1 2.6 %shard_map.94 = (bf16[512,768]{1,0:T(8,128)(2,1)S(1)}, bf16[512,768]{1,0:T(8,128)(2,1)S(1)}, bf16[512,768]{1,0:T(8,128)(2,1)S(1)}, bf16[512,768]{1,0:T(8,128)(2,...) custom-call(bf16[768,2048]{1,0:T(8,128)(2,1)} %bitcast.19, ...), custom_call_target="tpu_custom_call" | custom-call | bytes 12582912 | tf_op jit(solution)/shard_map/pallas_call | solution.py:108
  17.7 1.1 %collective-permute-done.2.refs_0_ = bf16[256,768]{1,0:T(8,128)(2,1)S(1)} collective-permute-done((bf16[256,768]{1,0:T(8,128)(2,1)S(1)}, bf16[256,768]{1,0:T(8,128)(2,1)S(1)}, u32[]{:S(2)}, u32[]{:S(2)}) %collective-permute-start.2) | collective-permute-done | bytes 393248 | tf_op jit(solution)/shard_map/ppermute | solution.py:93
  18.8 0.0 collective-permute-done.5
  18.8 0.3 collective-permute-done.6
  19.1 0.0 copy-start
  19.1 0.0 copy-start.1
  19.1 0.0 collective-permute-done.7.other_hidden_ref
  19.1 1.1 %shard_map.95 = (f32[128,768]{1,0:T(8,128)S(1)}, f32[128,768]{1,0:T(8,128)S(1)}, f32[2,128]{1,0:T(2,128)S(1)}) custom-call(bf16[128,2176]{1,0:T(8,128)(2,1)S(1)} %constant_dynamic-update-slice_fusion.2.held_ref, bf16[256,768]{1,0:T(8,128)(2,1)S(1)} %get-tuple-element.38.hidden_ref, bf16[128,768]{1,0:T(8,128)(2,1)S(1)} %collective-permute-done.7.other_hidden_ref, ...), custom_call_target="tpu_custom_call" | custom-call | flops 805306368 | bytes 6291456 | tf_op jit(solution)/shard_map/pallas_call | solution.py:108
  20.3 0.0 copy-start.2
  20.3 0.1 collective-permute-start.8
  20.4 1.5 %collective-permute-start.11 = (f32[1,2,128]{2,1,0:T(2,128)S(1)}, f32[1,2,128]{2,1,0:T(2,128)S(1)}, u32[]{:S(2)}, u32[]{:S(2)}) collective-permute-start(f32[1,2,128]{2,1,0:T(2,128)S(1)} %bitcast.16), channel_id=1, source_target_pairs={{0,8},{4,12},{8,0},{12,4},{1,9},{5,13},{9,1},{13,5},{2,10},{6,14},... | collective-permute-start | bytes 3080 | tf_op jit(solution)/shard_map/ppermute | solution.py:93
  21.9 0.2 collective-permute-start.9
  22.2 1.6 %collective-permute-start.10 = (bf16[128,1152]{1,0:T(8,128)(2,1)S(1)}, bf16[128,1152]{1,0:T(8,128)(2,1)S(1)}, u32[]{:S(2)}, u32[]{:S(2)}) collective-permute-start(bf16[128,1152]{1,0:T(8,128)(2,1)S(1)} %pad_maximum_fusion), channel_id=1, source_target_pairs={{0,16},{16,0},{1,17},{17,1},{2,18},{18,2},{3,19},{19,3},{4,20},{20... | collective-permute-start | bytes 884744 | tf_op jit(solution)/shard_map/ppermute | solution.py:93
  23.8 0.3 collective-permute-done.11
  24.0 2.9 %collective-permute-start.12 = (f32[2,2,128]{2,1,0:T(2,128)S(1)}, f32[2,2,128]{2,1,0:T(2,128)S(1)}, u32[]{:S(2)}, u32[]{:S(2)}) collective-permute-start(f32[2,2,128]{2,1,0:T(2,128)S(1)} %pad_maximum_fusion.2), channel_id=1, source_target_pairs={{0,2},{1,3},{2,0},{3,1},{4,6},{5,7},{6,4},{7,5},{8,10},{9,11},{10,... | collective-permute-start | bytes 6152 | tf_op jit(solution)/shard_map/ppermute | solution.py:93
  26.9 2.4 %collective-permute-start.13 = (f32[2,2,128]{2,1,0:T(2,128)S(1)}, f32[2,2,128]{2,1,0:T(2,128)S(1)}, u32[]{:S(2)}, u32[]{:S(2)}) collective-permute-start(f32[2,2,128]{2,1,0:T(2,128)S(1)} %pad_maximum_fusion.2), channel_id=1, source_target_pairs={{0,3},{1,2},{2,1},{3,0},{4,7},{5,6},{6,5},{7,4},{8,11},{9,10},{10,... | collective-permute-start | bytes 6152 | tf_op jit(solution)/shard_map/ppermute | solution.py:93
  29.3 0.0 collective-permute-done.9.rest_back_ref
  29.3 0.5 %collective-permute-start.14 = (f32[2,2,128]{2,1,0:T(2,128)S(1)}, f32[2,2,128]{2,1,0:T(2,128)S(1)}, u32[]{:S(2)}, u32[]{:S(2)}) collective-permute-start(f32[2,2,128]{2,1,0:T(2,128)S(1)} %pad_maximum_fusion.2), channel_id=1, source_target_pairs={{0,1},{1,0},{2,3},{3,2},{4,5},{5,4},{6,7},{7,6},{8,9},{9,8},{10,11... | collective-permute-start | bytes 6152 | tf_op jit(solution)/shard_map/ppermute | solution.py:93
  29.9 0.0 collective-permute-done.8.rest_ref
  29.9 0.0 copy-done
  29.9 0.0 copy-done.1
  29.9 1.4 %shard_map.96 = (bf16[256,768]{1,0:T(8,128)(2,1)}, bf16[256,768]{1,0:T(8,128)(2,1)}, bf16[256,768]{1,0:T(8,128)(2,1)S(1)}) custom-call(bf16[128,2176]{1,0:T(8,128)(2,1)S(1)} %constant_dynamic-update-slice_fusion.2.held_ref, bf16[128,2176]{1,0:T(8,128)(2,1)S(1)} %collective-permute-done.8.rest_ref, f32[128,768]{1,0:T(8,128)S(1)} %get-tuple-element.44.back_ref, ...), custom_call_target="tpu_custom_call" | custom-call | flops 5898240 | bytes 2359296 | tf_op jit(solution)/shard_map/pallas_call | solution.py:108
  31.2 0.0 collective-permute-done.12
  31.2 1.0 %collective-permute-done.13 = f32[2,2,128]{2,1,0:T(2,128)S(1)} collective-permute-done((f32[2,2,128]{2,1,0:T(2,128)S(1)}, f32[2,2,128]{2,1,0:T(2,128)S(1)}, u32[]{:S(2)}, u32[]{:S(2)}) %collective-permute-start.13) | collective-permute-done | bytes 2080 | tf_op jit(solution)/shard_map/ppermute | solution.py:93
  32.3 0.6 %collective-permute-done.14 = f32[2,2,128]{2,1,0:T(2,128)S(1)} collective-permute-done((f32[2,2,128]{2,1,0:T(2,128)S(1)}, f32[2,2,128]{2,1,0:T(2,128)S(1)}, u32[]{:S(2)}, u32[]{:S(2)}) %collective-permute-start.14) | collective-permute-done | bytes 2080 | tf_op jit(solution)/shard_map/ppermute | solution.py:93
  32.9 0.0 collective-permute-done.10.refs_1_
  32.9 0.0 collective-permute-start.15
  32.9 0.0 copy-done.2
  33.0 0.7 %shard_map.98 = f32[8,16]{1,0:T(8,128)} custom-call(s32[8,16]{1,0:T(8,128)S(1)} %bitcast.15, f32[8,2,128]{2,1,0:T(2,128)S(1)} %constant_dynamic-update-slice_fusion.7.sums_ref), custom_call_target="tpu_custom_call" | custom-call | flops 256 | bytes 256 | tf_op jit(solution)/shard_map/pallas_call | solution.py:108
  33.6 0.9 %collective-permute-done.15.refs_2_ = bf16[128,1152]{1,0:T(8,128)(2,1)S(1)} collective-permute-done((bf16[128,1152]{1,0:T(8,128)(2,1)S(1)}, bf16[128,1152]{1,0:T(8,128)(2,1)S(1)}, u32[]{:S(2)}, u32[]{:S(2)}) %collective-permute-start.15) | collective-permute-done | bytes 294944 | tf_op jit(solution)/shard_map/ppermute | solution.py:93
  34.5 2.0 %shard_map.97 = bf16[768,1024]{1,0:T(8,128)(2,1)} custom-call(bf16[256,768]{1,0:T(8,128)(2,1)S(1)} %get-tuple-element.46.scaled_ref, bf16[128,2176]{1,0:T(8,128)(2,1)S(1)} %constant_dynamic-update-slice_fusion.2.held_ref, bf16[128,2176]{1,0:T(8,128)(2,1)S(1)} %collective-permute-done.8.rest_ref, bf16[256,768]{1,0:T(8,128)(2,1)S(1)} %collective-permute-done.2.refs_0_, ...), custom_call_target="tpu_custom_call" | custom-call | flops 805306368 | bytes 3145728 | tf_op jit(solution)/shard_map/pallas_call | solution.py:108
  (17 shorter events, 0.2 us)
Async XLA Ops:
  0.6 14.5 %collective-permute-start.1 = (bf16[768,2048]{1,0:T(8,128)(2,1)}, bf16[768,2048]{1,0:T(8,128)(2,1)S(1)}, u32[]{:S(2)}, u32[]{:S(2)}) collective-permute-start(bf16[768,2048]{1,0:T(8,128)(2,1)} %bitcast.18), channel_id=1, source_target_pairs={{0,4},{4,0},{8,12},{12,8},{1,5},{5,1},{9,13},{13,9},{2,6},{6,2},{1... | collective-permute-start | bytes 9437192 | tf_op jit(solution)/shard_map/ppermute | solution.py:93
  2.6 8.2 %collective-permute-start = (bf16[16,2176]{1,0:T(8,128)(2,1)S(1)}, bf16[16,2176]{1,0:T(8,128)(2,1)S(1)}, u32[]{:S(2)}, u32[]{:S(2)}) collective-permute-start(bf16[16,2176]{1,0:T(8,128)(2,1)S(1)} %get-tuple-element.28), channel_id=1, source_target_pairs={{0,2},{1,3},{2,0},{3,1},{4,6},{5,7},{6,4},{7,5},{8,10},{9,11},{10,... | collective-permute-start | bytes 208904 | tf_op jit(solution)/shard_map/ppermute | solution.py:93
  6.2 6.8 %collective-permute-start.3 = (bf16[16,2176]{1,0:T(8,128)(2,1)S(1)}, bf16[16,2176]{1,0:T(8,128)(2,1)S(1)}, u32[]{:S(2)}, u32[]{:S(2)}) collective-permute-start(bf16[16,2176]{1,0:T(8,128)(2,1)S(1)} %get-tuple-element.28), channel_id=1, source_target_pairs={{0,3},{1,2},{2,1},{3,0},{4,7},{5,6},{6,5},{7,4},{8,11},{9,10},{10,... | collective-permute-start | bytes 208904 | tf_op jit(solution)/shard_map/ppermute | solution.py:93
  7.6 5.9 %collective-permute-start.4 = (bf16[16,2176]{1,0:T(8,128)(2,1)S(1)}, bf16[16,2176]{1,0:T(8,128)(2,1)S(1)}, u32[]{:S(2)}, u32[]{:S(2)}) collective-permute-start(bf16[16,2176]{1,0:T(8,128)(2,1)S(1)} %get-tuple-element.28), channel_id=1, source_target_pairs={{0,1},{1,0},{2,3},{3,2},{4,5},{5,4},{6,7},{7,6},{8,9},{9,8},{10,11... | collective-permute-start | bytes 208904 | tf_op jit(solution)/shard_map/ppermute | solution.py:93
  7.8 10.9 %collective-permute-start.2 = (bf16[256,768]{1,0:T(8,128)(2,1)S(1)}, bf16[256,768]{1,0:T(8,128)(2,1)S(1)}, u32[]{:S(2)}, u32[]{:S(2)}) collective-permute-start(bf16[256,768]{1,0:T(8,128)(2,1)S(1)} %get-tuple-element.38.hidden_ref), channel_id=1, source_target_pairs={{0,16},{16,0},{1,17},{17,1},{2,18},{18,2},{3,19},{19,3},{4,20},{20... | collective-permute-start | bytes 1179656 | tf_op jit(solution)/shard_map/ppermute | solution.py:93
  10.8 8.0 %collective-permute-start.5 = (bf16[32,2176]{1,0:T(8,128)(2,1)S(1)}, bf16[32,2176]{1,0:T(8,128)(2,1)S(1)}, u32[]{:S(2)}, u32[]{:S(2)}) collective-permute-start(bf16[32,2176]{1,0:T(8,128)(2,1)S(1)} %constant_dynamic-update-slice_fusion), channel_id=1, source_target_pairs={{0,8},{4,12},{8,0},{12,4},{1,9},{5,13},{9,1},{13,5},{2,10},{6,14},... | collective-permute-start | bytes 417800 | tf_op jit(solution)/shard_map/ppermute | solution.py:93
  13.4 5.6 %collective-permute-start.6 = (bf16[32,2176]{1,0:T(8,128)(2,1)S(1)}, bf16[32,2176]{1,0:T(8,128)(2,1)S(1)}, u32[]{:S(2)}, u32[]{:S(2)}) collective-permute-start(bf16[32,2176]{1,0:T(8,128)(2,1)S(1)} %pad_maximum_fusion.1), channel_id=1, source_target_pairs={{0,8},{4,12},{8,0},{12,4},{1,9},{5,13},{9,1},{13,5},{2,10},{6,14},... | collective-permute-start | bytes 417800 | tf_op jit(solution)/shard_map/ppermute | solution.py:93
  15.1 4.1 %collective-permute-start.7 = (bf16[128,768]{1,0:T(8,128)(2,1)S(1)}, bf16[128,768]{1,0:T(8,128)(2,1)S(1)}, u32[]{:S(2)}, u32[]{:S(2)}) collective-permute-start(bf16[128,768]{1,0:T(8,128)(2,1)S(1)} %get-tuple-element.41), channel_id=1, source_target_pairs={{0,4},{4,0},{8,12},{12,8},{1,5},{5,1},{9,13},{13,9},{2,6},{6,2},{1... | collective-permute-start | bytes 589832 | tf_op jit(solution)/shard_map/ppermute | solution.py:93
  19.1 10.7 %copy-start = (bf16[1,1,256,768]{3,2,1,0:T(8,128)(2,1)S(1)}, bf16[1,1,256,768]{3,2,1,0:T(8,128)(2,1)}, u32[]{:S(2)}) copy-start(bf16[1,1,256,768]{3,2,1,0:T(8,128)(2,1)} %param.9) | copy-start | bytes 1179652
  19.1 10.7 %copy-start.1 = (bf16[1,1,256,768]{3,2,1,0:T(8,128)(2,1)S(1)}, bf16[1,1,256,768]{3,2,1,0:T(8,128)(2,1)}, u32[]{:S(2)}) copy-start(bf16[1,1,256,768]{3,2,1,0:T(8,128)(2,1)} %param.10) | copy-start | bytes 1179652
  20.3 12.7 %copy-start.2 = (s32[16,8]{0,1:T(8,128)S(1)}, s32[16,8]{0,1:T(8,128)}, u32[]{:S(2)}) copy-start(s32[16,8]{0,1:T(8,128)} %param.7) | copy-start | bytes 1540
  20.3 9.6 %collective-permute-start.8 = (bf16[128,2176]{1,0:T(8,128)(2,1)S(1)}, bf16[128,2176]{1,0:T(8,128)(2,1)S(1)}, u32[]{:S(2)}, u32[]{:S(2)}) collective-permute-start(bf16[128,2176]{1,0:T(8,128)(2,1)S(1)} %constant_dynamic-update-slice_fusion.2.held_ref), channel_id=1, source_target_pairs={{0,4},{4,0},{8,12},{12,8},{1,5},{5,1},{9,13},{13,9},{2,6},{6,2},{1... | collective-permute-start | bytes 1671176 | tf_op jit(solution)/shard_map/ppermute | solution.py:93
  20.4 3.6 %collective-permute-start.11 = (f32[1,2,128]{2,1,0:T(2,128)S(1)}, f32[1,2,128]{2,1,0:T(2,128)S(1)}, u32[]{:S(2)}, u32[]{:S(2)}) collective-permute-start(f32[1,2,128]{2,1,0:T(2,128)S(1)} %bitcast.16), channel_id=1, source_target_pairs={{0,8},{4,12},{8,0},{12,4},{1,9},{5,13},{9,1},{13,5},{2,10},{6,14},... | collective-permute-start | bytes 3080 | tf_op jit(solution)/shard_map/ppermute | solution.py:93
  21.9 7.4 %collective-permute-start.9 = (f32[128,768]{1,0:T(8,128)S(1)}, f32[128,768]{1,0:T(8,128)S(1)}, u32[]{:S(2)}, u32[]{:S(2)}) collective-permute-start(f32[128,768]{1,0:T(8,128)S(1)} %get-tuple-element.45), channel_id=1, source_target_pairs={{0,4},{4,0},{8,12},{12,8},{1,5},{5,1},{9,13},{13,9},{2,6},{6,2},{1... | collective-permute-start | bytes 1179656 | tf_op jit(solution)/shard_map/ppermute | solution.py:93
  22.2 10.7 %collective-permute-start.10 = (bf16[128,1152]{1,0:T(8,128)(2,1)S(1)}, bf16[128,1152]{1,0:T(8,128)(2,1)S(1)}, u32[]{:S(2)}, u32[]{:S(2)}) collective-permute-start(bf16[128,1152]{1,0:T(8,128)(2,1)S(1)} %pad_maximum_fusion), channel_id=1, source_target_pairs={{0,16},{16,0},{1,17},{17,1},{2,18},{18,2},{3,19},{19,3},{4,20},{20... | collective-permute-start | bytes 884744 | tf_op jit(solution)/shard_map/ppermute | solution.py:93
  24.0 7.2 %collective-permute-start.12 = (f32[2,2,128]{2,1,0:T(2,128)S(1)}, f32[2,2,128]{2,1,0:T(2,128)S(1)}, u32[]{:S(2)}, u32[]{:S(2)}) collective-permute-start(f32[2,2,128]{2,1,0:T(2,128)S(1)} %pad_maximum_fusion.2), channel_id=1, source_target_pairs={{0,2},{1,3},{2,0},{3,1},{4,6},{5,7},{6,4},{7,5},{8,10},{9,11},{10,... | collective-permute-start | bytes 6152 | tf_op jit(solution)/shard_map/ppermute | solution.py:93
  26.9 5.4 %collective-permute-start.13 = (f32[2,2,128]{2,1,0:T(2,128)S(1)}, f32[2,2,128]{2,1,0:T(2,128)S(1)}, u32[]{:S(2)}, u32[]{:S(2)}) collective-permute-start(f32[2,2,128]{2,1,0:T(2,128)S(1)} %pad_maximum_fusion.2), channel_id=1, source_target_pairs={{0,3},{1,2},{2,1},{3,0},{4,7},{5,6},{6,5},{7,4},{8,11},{9,10},{10,... | collective-permute-start | bytes 6152 | tf_op jit(solution)/shard_map/ppermute | solution.py:93
  29.3 3.6 %collective-permute-start.14 = (f32[2,2,128]{2,1,0:T(2,128)S(1)}, f32[2,2,128]{2,1,0:T(2,128)S(1)}, u32[]{:S(2)}, u32[]{:S(2)}) collective-permute-start(f32[2,2,128]{2,1,0:T(2,128)S(1)} %pad_maximum_fusion.2), channel_id=1, source_target_pairs={{0,1},{1,0},{2,3},{3,2},{4,5},{5,4},{6,7},{7,6},{8,9},{9,8},{10,11... | collective-permute-start | bytes 6152 | tf_op jit(solution)/shard_map/ppermute | solution.py:93
  32.9 1.6 %collective-permute-start.15 = (bf16[128,1152]{1,0:T(8,128)(2,1)S(1)}, bf16[128,1152]{1,0:T(8,128)(2,1)S(1)}, u32[]{:S(2)}, u32[]{:S(2)}) collective-permute-start(bf16[128,1152]{1,0:T(8,128)(2,1)S(1)} %collective-permute-done.10.refs_1_), channel_id=1, source_target_pairs={{0,4},{4,0},{8,12},{12,8},{1,5},{5,1},{9,13},{13,9},{2,6},{6,2},{1... | collective-permute-start | bytes 884744 | tf_op jit(solution)/shard_map/ppermute | solution.py:93

commit v5 on v4

--- a/solution.py
+++ b/solution.py
@@ -8,6 +8,7 @@
 from jax.sharding import PartitionSpec as P
 
 LANES = 128
+PIECES = 3
 PARTS = 4
 VMEM_LIMIT = 14 * 1024 * 1024
 
@@ -130,38 +131,17 @@
 
 
 def first_kernel(
-    order,
-    grad_hbm,
-    routes_hbm,
-    gates_hbm,
-    pre_gate_hbm,
-    pre_up_hbm,
-    out_ref,
-    hidden_ref,
-    rest_ref,
-    token_ref,
-    routes_ref,
-    gates_ref,
-    pre_gate_ref,
-    pre_up_ref,
-    sems,
+    grad_hbm, routes_hbm, gates_hbm, out_ref, token_ref, routes_ref, gates_ref, sems
 ):
     rows, features = grad_hbm.shape
+    token_ref[...] = jnp.zeros(token_ref.shape, token_ref.dtype)
     copies = [
-        pltpu.make_async_copy(source, target, sems.at[at])
-        for at, (source, target) in enumerate(
-            (
-                (routes_hbm, routes_ref),
-                (gates_hbm, gates_ref),
-                (grad_hbm, out_ref.at[:, pl.ds(0, features)]),
-                (pre_gate_hbm, pre_gate_ref),
-                (pre_up_hbm, pre_up_ref),
-            )
-        )
+        pltpu.make_async_copy(routes_hbm, routes_ref, sems.at[0]),
+        pltpu.make_async_copy(gates_hbm, gates_ref, sems.at[1]),
+        pltpu.make_async_copy(grad_hbm, out_ref.at[:, pl.ds(0, features)], sems.at[2]),
     ]
     for copy in copies:
         copy.start()
-    token_ref[...] = jnp.zeros(token_ref.shape, token_ref.dtype)
     copies[0].wait()
     copies[1].wait()
     routes = routes_ref[...]
@@ -172,7 +152,19 @@
         table = table + jnp.where(ids == routes[k : k + 1, :], gates[k : k + 1, :], 0.0)
     table = jnp.concatenate([table, jnp.zeros((LANES, LANES - rows), jnp.float32)], axis=1)
     out_ref[:, features:] = table.T[:rows, :].astype(out_ref.dtype)
-    for copy in copies[2:]:
+    copies[2].wait()
+
+
+def hidden_kernel(
+    order, rows, pre_gate_hbm, pre_up_hbm, hidden_ref, rest_ref, pre_gate_ref, pre_up_ref, sems
+):
+    copies = [
+        pltpu.make_async_copy(pre_gate_hbm, pre_gate_ref, sems.at[0]),
+        pltpu.make_async_copy(pre_up_hbm, pre_up_ref, sems.at[1]),
+    ]
+    for copy in copies:
+        copy.start()
+    for copy in copies:
         copy.wait()
     half = len(order) // 2
     for place, xors in enumerate(order):
@@ -209,18 +201,21 @@
                 ].T
 
 
-def back_kernel(features, held_ref, hidden_ref, other_hidden_ref, *refs):
-    back_ref, other_back_ref, sums_ref = refs[-3:]
-    rows = held_ref.shape[0]
+def back_kernel(features, blocks, columns, hidden_ref, other_hidden_ref, *refs):
+    group_refs, refs = refs[:blocks], refs[blocks:]
+    turned_refs, refs = refs[: 2 * PARTS], refs[2 * PARTS :]
+    back_ref, other_back_ref, sums_ref, *cut_refs = refs
+    held = jnp.concatenate([group_ref[...] for group_ref in group_refs], axis=0)
+    rows = held.shape[0]
     for expert, (act_ref, result_ref) in enumerate(
         ((hidden_ref, back_ref), (other_hidden_ref, other_back_ref))
     ):
         back = jnp.zeros(result_ref.shape, jnp.float32)
         for part in range(PARTS):
-            part_ref = refs[expert * PARTS + part]
+            part_ref = turned_refs[expert * PARTS + part]
             depth = part_ref.shape[0]
             back = back + jnp.dot(
-                held_ref[:, part * depth : (part + 1) * depth],
+                held[:, part * depth : (part + 1) * depth],
                 part_ref[...],
                 preferred_element_type=jnp.float32,
             )
@@ -234,6 +229,13 @@
             sums_ref[row : row + 1, :] = jnp.sum(
                 folded[at : at + LANES, :].T, axis=0, keepdims=True
             )
+    step = rows // blocks
+    for bits, cut_ref in enumerate(cut_refs):
+        start = pl.multiple_of((lax.axis_index("dp") ^ bits) * columns, columns)
+        for block, group_ref in enumerate(group_refs):
+            here = slice(block * step, (block + 1) * step)
+            cut_ref[here, :columns] = group_ref[:, pl.ds(start, columns)]
+            cut_ref[here, columns:] = group_ref[:, features:]
 
 
 def own_gates(table):
@@ -246,7 +248,7 @@
 def grads_kernel(
     order,
     rows,
-    features,
+    columns,
     held_ref,
     rest_ref,
     back_ref,
@@ -262,7 +264,7 @@
     for place, xors in enumerate(order):
         tokens_ref, products_ref = ((held_ref, back_ref), (rest_ref, rest_back_ref))[place // half]
         there = slice((place % half) * rows, (place % half + 1) * rows)
-        gate = own_gates(tokens_ref[there, features:])
+        gate = own_gates(tokens_ref[there, columns:])
         here = slice(place * rows, (place + 1) * rows)
         source = pl.ds(pl.multiple_of(peer(xors) * rows, rows), rows)
         value = pre_gate_ref[source, :].astype(jnp.float32)
@@ -278,32 +280,53 @@
         )
 
 
-def down_kernel(pairs, scaled_ref, held_ref, rest_ref, *refs):
+def scale(hidden, table):
+    return (own_gates(table) * hidden.astype(jnp.float32)).astype(jnp.bfloat16)
+
+
+def first_down_kernel(scaled_ref, held_ref, rest_ref, *refs):
+    sum_refs, refs = refs[-PIECES:], refs[:-PIECES]
+    depth, columns = sum_refs[0].shape
+    scaled, tokens = [scaled_ref[...]], [held_ref[:, :columns], rest_ref[:, :columns]]
+    for hidden_ref, one_ref in zip(refs[::2], refs[1::2]):
+        scaled.append(scale(hidden_ref[: one_ref.shape[0], :], one_ref[:, columns:]))
+        tokens.append(one_ref[:, :columns])
+    scaled = jnp.concatenate(scaled, axis=0)
+    tokens = jnp.concatenate(tokens, axis=0)
+    for at, sum_ref in enumerate(sum_refs):
+        sum_ref[...] = lax.dot_general(
+            scaled[:, at * depth : (at + 1) * depth],
+            tokens,
+            (((0,), (0,)), ((), ())),
+            preferred_element_type=jnp.float32,
+        )
+
+
+def last_down_kernel(*refs):
     out_ref, held_out_ref, sems = refs[-3:]
-    columns = out_ref.shape[1]
-    mine = pl.ds(pl.multiple_of(lax.axis_index("dp") * columns, columns), columns)
-    scaled = [scaled_ref[...]]
-    tokens = [held_ref[:, mine], rest_ref[:, mine]]
-    for pair in range(pairs):
-        hidden_ref, one_ref, two_ref = refs[3 * pair : 3 * pair + 3]
-        gate = jnp.concatenate(
-            [own_gates(one_ref[:, columns:]), own_gates(two_ref[:, columns:])], axis=0
-        )
-        scaled.append((gate * hidden_ref[...].astype(jnp.float32)).astype(scaled_ref.dtype))
-        tokens += [one_ref[:, :columns], two_ref[:, :columns]]
+    sum_refs, refs = refs[:PIECES], refs[PIECES:-3]
+    depth, columns = sum_refs[0].shape
+    scaled, tokens = [], []
+    for hidden_ref, two_ref in zip(refs[::2], refs[1::2]):
+        rows = two_ref.shape[0]
+        scaled.append(scale(hidden_ref[rows:, :], two_ref[:, columns:]))
+        tokens.append(two_ref[:, :columns])
     scaled = jnp.concatenate(scaled, axis=0)
     tokens = jnp.concatenate(tokens, axis=0)
     copies = []
-    for at in range(0, out_ref.shape[0], 2 * LANES):
-        here = pl.ds(at, 2 * LANES)
-        held_out_ref[here, :] = lax.dot_general(
-            scaled[:, at : at + 2 * LANES],
-            tokens,
-            (((0,), (0,)), ((), ())),
-            preferred_element_type=jnp.float32,
+    for at, sum_ref in enumerate(sum_refs):
+        here = pl.ds(at * depth, depth)
+        held_out_ref[here, :] = (
+            sum_ref[...]
+            + lax.dot_general(
+                scaled[:, at * depth : (at + 1) * depth],
+                tokens,
+                (((0,), (0,)), ((), ())),
+                preferred_element_type=jnp.float32,
+            )
         ).astype(out_ref.dtype)
         copies.append(
-            pltpu.make_async_copy(held_out_ref.at[here], out_ref.at[here], sems.at[len(copies)])
+            pltpu.make_async_copy(held_out_ref.at[here], out_ref.at[here], sems.at[at])
         )
         copies[-1].start()
     for copy in copies:
@@ -349,26 +372,32 @@
         order += [(w ^ bits, n) for w, n in order]
     order = tuple(order)
 
-    other_weight = swap(weight, "wide", 1)
-    payload, hidden, rest_hidden, token = call(
-        functools.partial(first_kernel, order),
-        (
-            shape((rows, features + LANES), bf16),
-            shape((slot_count, units), bf16),
-            shape((half_count, units), bf16),
-            shape((8, LANES), f32),
-        ),
-        (20 * slot_count * units, 6 * slot_count * units),
-        *in_hbm(out_grad, routes_t, gates_t, pre_gate, pre_up),
-        hbm=5,
+    payload, token = call(
+        first_kernel,
+        (shape((rows, features + LANES), bf16), shape((8, LANES), f32)),
+        (rows * features, 4 * rows * features),
+        *in_hbm(out_grad, routes_t, gates_t),
+        hbm=3,
         scratch=[
             pltpu.VMEM(routes_t.shape, routes_t.dtype),
             pltpu.VMEM(gates_t.shape, gates_t.dtype),
+            pltpu.SemaphoreType.DMA((3,)),
+        ],
+    )
+    hidden, rest_hidden = call(
+        functools.partial(hidden_kernel, order, rows),
+        (shape((slot_count, units), bf16), shape((half_count, units), bf16)),
+        (20 * slot_count * units, 6 * slot_count * units),
+        *in_hbm(pre_gate, pre_up),
+        hbm=2,
+        deps=(token,),
+        scratch=[
             pltpu.VMEM(pre_gate.shape, pre_gate.dtype),
             pltpu.VMEM(pre_up.shape, pre_up.dtype),
-            pltpu.SemaphoreType.DMA((5,)),
+            pltpu.SemaphoreType.DMA((2,)),
         ],
     )
+    other_weight = swap(after(weight, token), "wide", 1)
     along = [swap(payload, "narrow", bits) if bits else payload for bits in reach]
     turned = call(
         turn_kernel,
@@ -390,18 +419,20 @@
         groups.append(jnp.concatenate(along[near:], axis=0))
     for bits in wide_bits:
         groups += [swap(group, "wide", bits) for group in groups]
-    held = jnp.concatenate([after(groups[0], *turned, *over)] + groups[1:], axis=0)
-    back, other_back, sums = call(
-        functools.partial(back_kernel, features),
+    middle = len(groups) // 2
+    groups[middle] = after(groups[middle], *turned, *over)
+    back, other_back, sums, *cuts = call(
+        functools.partial(back_kernel, features, len(groups), columns),
         (
             shape((half_count, units), f32),
             shape((half_count, units), f32),
             shape((slot_count // LANES, LANES), f32),
-        ),
+        )
+        + (shape((half_count, columns + LANES), bf16),) * dp_count,
         (2 * slot_count * units * features, 4 * units * features),
-        held,
         hidden,
         other_hidden,
+        *groups,
         *turned,
     )
     found = sums[None]
@@ -409,16 +440,12 @@
     for bits in wide_bits:
         found = jnp.concatenate([found, swap(found, "wide", bits)], axis=0)
         back_order += [(w ^ bits, n) for w, n in back_order]
-    rest = swap(after(held, sums), "wide", 1)
+    held, *cuts = cuts
+    rest = swap(held, "wide", 1)
     rest_back = swap(other_back, "wide", 1)
-    crossed = []
-    for bits in range(1, dp_count):
-        partner = lax.axis_index("dp") ^ bits
-        cut = lax.dynamic_slice_in_dim(held[:, :features], partner * columns, columns, axis=1)
-        cut = jnp.concatenate([cut, held[:, features:]], axis=1)
-        crossed.append(swap(after(cut, sums), "dp", bits))
+    crossed = [swap(cut, "dp", bits) for bits, cut in enumerate(cuts, 1)]
     grad_a, grad_b, scaled = call(
-        functools.partial(grads_kernel, order, rows, features),
+        functools.partial(grads_kernel, order, rows, columns),
         (shape((slot_count, units), bf16),) * 3,
         (30 * slot_count * units, 12 * slot_count * units),
         held,
@@ -429,26 +456,30 @@
         pre_gate,
         pre_up,
     )
-    mine = found
-    parts = [swap(mine, "narrow", bits) for bits in reach[1:]]
-    found = jnp.concatenate([after(mine, scaled)] + parts, axis=0)
-    back_order = [(w, n ^ bits) for bits in reach for w, n in back_order]
-    others = []
-    for bits in range(1, dp_count):
-        one = after(crossed[bits - 1], found)
-        others += [over[bits - 1], one, swap(one, "wide", 1)]
-    grad_down = call(
-        functools.partial(down_kernel, dp_count - 1),
-        shape((units, columns), bf16),
-        (2 * dp_count * slot_count * units * columns, 4 * units * columns),
+    sums_down = call(
+        first_down_kernel,
+        (shape((units // PIECES, columns), f32),) * PIECES,
+        (2 * slot_count * units * columns, 4 * units * columns),
         scaled,
         held,
         rest,
-        *others,
+        *(x for pair in zip(over, crossed) for x in pair),
+    )
+    bits_of = [1 << b for b in range(narrow_count.bit_length() - 1)]
+    for bits, done in zip(bits_of, [scaled] * (len(bits_of) - 1) + [sums_down[-1]]):
+        found = jnp.concatenate([after(found, done), swap(found, "narrow", bits)], axis=0)
+        back_order += [(w, n ^ bits) for w, n in back_order]
+    across = [swap(after(one, found), "wide", 1) for one in crossed]
+    grad_down = call(
+        last_down_kernel,
+        shape((units, columns), bf16),
+        (2 * dp_count * slot_count * units * columns, 4 * units * columns),
+        *sums_down,
+        *(x for pair in zip(over, across) for x in pair),
         out_space=pltpu.HBM,
         scratch=[
             pltpu.VMEM((units, columns), bf16),
-            pltpu.SemaphoreType.DMA((units // (2 * LANES),)),
+            pltpu.SemaphoreType.DMA((PIECES,)),
         ],
     )
     picked = call(

time: 36.7 us -> 36.3 us (0.989)
  Pallas kernels: 9.14 us -> 10.6 us
  starting transfers between devices: 19.8 us -> 18.5 us
    pallas_call x6 -> x8, Pallas kernels: 9.14 us -> 10.6 us  [call(): pl.pallas_call(body, out_shape=outs, in_specs=[pl.BlockSpec(memory_space=...]
    ppermute x16 -> x15, starting transfers between devices: 19.8 us -> 18.5 us  [swap(): return lax.ppermute(x, axis, [(i, i ^ bits) for i in range(count)])]
    ppermute x16 -> x15, waiting for transfers between devices: 6.56 us -> 6.26 us  [swap(): return lax.ppermute(x, axis, [(i, i ^ bits) for i in range(count)])]
  transfers between devices with their start and end apart: 16 -> 15, of which waited for: 9 -> 9; matrix products, arithmetic and copies ran while one was open for 1% -> 0% of each run, Pallas kernels for 17% -> 19%
where the time goes in v5:
time: 36.3 us; the launch traced here: 36.1 us
  starting transfers between devices  18.5 us (51%)
  Pallas kernels  10.6 us (29%)
  waiting for transfers between devices  6.26 us (17%)
  between operations  0.74 us (2%)
    ppermute x15, starting transfers between devices, swap(): return lax.ppermute(x, axis, [(i, i ^ bits) for i in range(count)])  18.5 us
    pallas_call x8, Pallas kernels, call(): pl.pallas_call(body, out_shape=outs, in_specs=[pl.BlockSpec(memory_space=...  10.6 us
    ppermute x15, waiting for transfers between devices, swap(): return lax.ppermute(x, axis, [(i, i ^ bits) for i in range(count)])  6.26 us
  transfers between devices with their start and end apart: 15, of which 9 were waited for; matrix products, arithmetic and copies ran while one was open for 0% of the time, Pallas kernels for 19%

profile of v5, /device:TPU:0, one launch (start us, length us, event | category | flops | bytes accessed | tf_op | source)
XLA Modules:
  0.0 36.1 jit_solution(2546046453625228358)
XLA Ops:
  0.6 0.9 %shard_map.93 = (bf16[16,2176]{1,0:T(8,128)(2,1)S(1)}, f32[8,128]{1,0:T(8,128)S(1)}) custom-call(bf16[16,2048]{1,0:T(8,128)(2,1)} %grad_hbm.1, s32[8,16]{1,0:T(8,128)} %bitcast.14, bf16[8,16]{1,0:T(8,128)(2,1)} %bitcast.22), custom_call_target="tpu_custom_call" | custom-call | flops 32768 | bytes 131072 | tf_op jit(solution)/shard_map/pallas_call | solution.py:109
  1.5 0.5 %collective-permute-start.5 = (bf16[768,2048]{1,0:T(8,128)(2,1)}, bf16[768,2048]{1,0:T(8,128)(2,1)S(1)}, u32[]{:S(2)}, u32[]{:S(2)}) collective-permute-start(bf16[768,2048]{1,0:T(8,128)(2,1)} %bitcast.18), channel_id=1, source_target_pairs={{0,4},{4,0},{8,12},{12,8},{1,5},{5,1},{9,13},{13,9},{2,6},{6,2},{1... | collective-permute-start | bytes 9437192 | tf_op jit(solution)/shard_map/ppermute | solution.py:94
  2.1 3.7 %collective-permute-start.3 = (bf16[16,2176]{1,0:T(8,128)(2,1)S(1)}, bf16[16,2176]{1,0:T(8,128)(2,1)S(1)}, u32[]{:S(2)}, u32[]{:S(2)}) collective-permute-start(bf16[16,2176]{1,0:T(8,128)(2,1)S(1)} %get-tuple-element.36), channel_id=1, source_target_pairs={{0,2},{1,3},{2,0},{3,1},{4,6},{5,7},{6,4},{7,5},{8,10},{9,11},{10,... | collective-permute-start | bytes 208904 | tf_op jit(solution)/shard_map/ppermute | solution.py:94
  5.7 1.3 %collective-permute-start = (bf16[16,2176]{1,0:T(8,128)(2,1)S(1)}, bf16[16,2176]{1,0:T(8,128)(2,1)S(1)}, u32[]{:S(2)}, u32[]{:S(2)}) collective-permute-start(bf16[16,2176]{1,0:T(8,128)(2,1)S(1)} %get-tuple-element.36), channel_id=1, source_target_pairs={{0,3},{1,2},{2,1},{3,0},{4,7},{5,6},{6,5},{7,4},{8,11},{9,10},{10,... | collective-permute-start | bytes 208904 | tf_op jit(solution)/shard_map/ppermute | solution.py:94
  7.1 0.2 collective-permute-start.1
  7.3 1.3 %shard_map.94 = (bf16[256,768]{1,0:T(8,128)(2,1)S(1)}, bf16[128,768]{1,0:T(8,128)(2,1)S(1)}) custom-call(bf16[256,768]{1,0:T(8,128)(2,1)} %bitcast.10, bf16[256,768]{1,0:T(8,128)(2,1)} %bitcast.12, f32[8,128]{1,0:T(8,128)S(1)} %get-tuple-element.33.refs_2_), custom_call_target="tpu_custom_call" | custom-call | flops 3932160 | bytes 1179648 | tf_op jit(solution)/shard_map/pallas_call | solution.py:109
  8.6 1.6 %collective-permute-start.6 = (bf16[256,768]{1,0:T(8,128)(2,1)S(1)}, bf16[256,768]{1,0:T(8,128)(2,1)S(1)}, u32[]{:S(2)}, u32[]{:S(2)}) collective-permute-start(bf16[256,768]{1,0:T(8,128)(2,1)S(1)} %get-tuple-element.34.hidden_ref), channel_id=1, source_target_pairs={{0,16},{16,0},{1,17},{17,1},{2,18},{18,2},{3,19},{19,3},{4,20},{20... | collective-permute-start | bytes 1179656 | tf_op jit(solution)/shard_map/ppermute | solution.py:94
  10.2 0.1 collective-permute-done.3
  10.3 1.7 %collective-permute-start.4 = (bf16[32,2176]{1,0:T(8,128)(2,1)S(1)}, bf16[32,2176]{1,0:T(8,128)(2,1)S(1)}, u32[]{:S(2)}, u32[]{:S(2)}) collective-permute-start(bf16[32,2176]{1,0:T(8,128)(2,1)S(1)} %constant_dynamic-update-slice_fusion.refs_0_), channel_id=1, source_target_pairs={{0,8},{4,12},{8,0},{12,4},{1,9},{5,13},{9,1},{13,5},{2,10},{6,14},... | collective-permute-start | bytes 417800 | tf_op jit(solution)/shard_map/ppermute | solution.py:94
  12.0 0.6 %collective-permute-done = bf16[16,2176]{1,0:T(8,128)(2,1)S(1)} collective-permute-done((bf16[16,2176]{1,0:T(8,128)(2,1)S(1)}, bf16[16,2176]{1,0:T(8,128)(2,1)S(1)}, u32[]{:S(2)}, u32[]{:S(2)}) %collective-permute-start) | collective-permute-done | bytes 69664 | tf_op jit(solution)/shard_map/ppermute | solution.py:94
  12.5 0.3 collective-permute-done.1
  12.8 0.0 collective-permute-start.2
  12.9 1.7 %collective-permute-start.7 = (bf16[32,2176]{1,0:T(8,128)(2,1)S(1)}, bf16[32,2176]{1,0:T(8,128)(2,1)S(1)}, u32[]{:S(2)}, u32[]{:S(2)}) collective-permute-start(bf16[32,2176]{1,0:T(8,128)(2,1)S(1)} %constant_dynamic-update-slice_fusion.2.refs_1_), channel_id=1, source_target_pairs={{0,8},{4,12},{8,0},{12,4},{1,9},{5,13},{9,1},{13,5},{2,10},{6,14},... | collective-permute-start | bytes 417800 | tf_op jit(solution)/shard_map/ppermute | solution.py:94
  14.5 0.0 collective-permute-done.5.refs_1_
  14.5 2.6 %shard_map.95 = (bf16[512,768]{1,0:T(8,128)(2,1)S(1)}, bf16[512,768]{1,0:T(8,128)(2,1)S(1)}, bf16[512,768]{1,0:T(8,128)(2,1)S(1)}, bf16[512,768]{1,0:T(8,128)(2,...) custom-call(bf16[768,2048]{1,0:T(8,128)(2,1)} %bitcast.19, ...), custom_call_target="tpu_custom_call" | custom-call | bytes 12582912 | tf_op jit(solution)/shard_map/pallas_call | solution.py:109
  17.1 0.0 collective-permute-done.4.refs_2_
  17.1 2.4 %collective-permute-done.6.refs_0_.refs_3_ = bf16[256,768]{1,0:T(8,128)(2,1)S(1)} collective-permute-done((bf16[256,768]{1,0:T(8,128)(2,1)S(1)}, bf16[256,768]{1,0:T(8,128)(2,1)S(1)}, u32[]{:S(2)}, u32[]{:S(2)}) %collective-permute-start.6) | collective-permute-done | bytes 393248 | tf_op jit(solution)/shard_map/ppermute | solution.py:94
  19.6 0.0 copy-start
  19.6 0.0 copy-start.1
  19.6 0.0 collective-permute-done.7.refs_3_
  19.6 0.0 collective-permute-done.2.other_hidden_ref
  19.6 1.1 %shard_map.96 = (f32[128,768]{1,0:T(8,128)S(1)}, f32[128,768]{1,0:T(8,128)S(1)}, f32[2,128]{1,0:T(2,128)S(1)}, bf16[128,1152]{1,0:T(8,128)(2,1)S(1)}, bf16[128,1152]{1,0:T(8,128)(2,1)S(1)}) custom-call(bf16[256,768]{1,0:T(8,128)(2,1)S(1)} %get-tuple-element.34.hidden_ref, bf16[128,768]{1,0:T(8,128)(2,1)S(1)} %collective-permute-done.2.other_hidden_ref, ...), custom_call_target="tpu_custom_call" | custom-call | flops 805306368 | bytes 6291456 | tf_op jit(solution)/shard_map/pallas_call | solution.py:109
  20.7 0.0 copy-start.2
  20.7 0.1 collective-permute-start.9
  20.8 0.5 %collective-permute-start.8 = (bf16[128,1152]{1,0:T(8,128)(2,1)S(1)}, bf16[128,1152]{1,0:T(8,128)(2,1)S(1)}, u32[]{:S(2)}, u32[]{:S(2)}) collective-permute-start(bf16[128,1152]{1,0:T(8,128)(2,1)S(1)} %get-tuple-element.48.held_ref), channel_id=1, source_target_pairs={{0,4},{4,0},{8,12},{12,8},{1,5},{5,1},{9,13},{13,9},{2,6},{6,2},{1... | collective-permute-start | bytes 884744 | tf_op jit(solution)/shard_map/ppermute | solution.py:94
  21.3 1.5 %collective-permute-start.11 = (f32[1,2,128]{2,1,0:T(2,128)S(1)}, f32[1,2,128]{2,1,0:T(2,128)S(1)}, u32[]{:S(2)}, u32[]{:S(2)}) collective-permute-start(f32[1,2,128]{2,1,0:T(2,128)S(1)} %bitcast.16), channel_id=1, source_target_pairs={{0,8},{4,12},{8,0},{12,4},{1,9},{5,13},{9,1},{13,5},{2,10},{6,14},... | collective-permute-start | bytes 3080 | tf_op jit(solution)/shard_map/ppermute | solution.py:94
  22.8 1.5 %collective-permute-start.10 = (bf16[128,1152]{1,0:T(8,128)(2,1)S(1)}, bf16[128,1152]{1,0:T(8,128)(2,1)S(1)}, u32[]{:S(2)}, u32[]{:S(2)}) collective-permute-start(bf16[128,1152]{1,0:T(8,128)(2,1)S(1)} %get-tuple-element.52), channel_id=1, source_target_pairs={{0,16},{16,0},{1,17},{17,1},{2,18},{18,2},{3,19},{19,3},{4,20},{20... | collective-permute-start | bytes 884744 | tf_op jit(solution)/shard_map/ppermute | solution.py:94
  24.3 0.6 %collective-permute-done.11 = f32[1,2,128]{2,1,0:T(2,128)S(1)} collective-permute-done((f32[1,2,128]{2,1,0:T(2,128)S(1)}, f32[1,2,128]{2,1,0:T(2,128)S(1)}, u32[]{:S(2)}, u32[]{:S(2)}) %collective-permute-start.11) | collective-permute-done | bytes 1056 | tf_op jit(solution)/shard_map/ppermute | solution.py:94
  24.9 1.5 %collective-permute-start.12 = (f32[2,2,128]{2,1,0:T(2,128)S(1)}, f32[2,2,128]{2,1,0:T(2,128)S(1)}, u32[]{:S(2)}, u32[]{:S(2)}) collective-permute-start(f32[2,2,128]{2,1,0:T(2,128)S(1)} %pad_maximum_fusion), channel_id=1, source_target_pairs={{0,1},{1,0},{2,3},{3,2},{4,5},{5,4},{6,7},{7,6},{8,9},{9,8},{10,11... | collective-permute-start | bytes 6152 | tf_op jit(solution)/shard_map/ppermute | solution.py:94
  26.4 0.0 collective-permute-done.8.rest_ref
  26.4 0.0 collective-permute-done.9.rest_back_ref
  26.4 0.0 copy-done
  26.4 0.0 copy-done.1
  26.4 1.4 %shard_map.97 = (bf16[256,768]{1,0:T(8,128)(2,1)}, bf16[256,768]{1,0:T(8,128)(2,1)}, bf16[256,768]{1,0:T(8,128)(2,1)S(1)}) custom-call(bf16[128,1152]{1,0:T(8,128)(2,1)S(1)} %get-tuple-element.48.held_ref, bf16[128,1152]{1,0:T(8,128)(2,1)S(1)} %collective-permute-done.8.rest_ref, f32[128,768]{1,0:T(8,128)S(1)} %get-tuple-element.49.back_ref, ...), custom_call_target="tpu_custom_call" | custom-call | flops 5898240 | bytes 2359296 | tf_op jit(solution)/shard_map/pallas_call | solution.py:109
  27.8 0.7 %collective-permute-done.12 = f32[2,2,128]{2,1,0:T(2,128)S(1)} collective-permute-done((f32[2,2,128]{2,1,0:T(2,128)S(1)}, f32[2,2,128]{2,1,0:T(2,128)S(1)}, u32[]{:S(2)}, u32[]{:S(2)}) %collective-permute-start.12) | collective-permute-done | bytes 2080 | tf_op jit(solution)/shard_map/ppermute | solution.py:94
  28.4 2.7 %collective-permute-start.13 = (f32[4,2,128]{2,1,0:T(2,128)S(1)}, f32[4,2,128]{2,1,0:T(2,128)S(1)}, u32[]{:S(2)}, u32[]{:S(2)}) collective-permute-start(f32[4,2,128]{2,1,0:T(2,128)S(1)} %constant_dynamic-update-slice_fusion.4), channel_id=1, source_target_pairs={{0,2},{1,3},{2,0},{3,1},{4,6},{5,7},{6,4},{7,5},{8,10},{9,11},{10,... | collective-permute-start | bytes 12296 | tf_op jit(solution)/shard_map/ppermute | solution.py:94
  31.2 0.3 collective-permute-done.10.refs_1_
  31.5 1.1 %shard_map.98 = (f32[256,1024]{1,0:T(8,128)S(1)}, f32[256,1024]{1,0:T(8,128)S(1)}, f32[256,1024]{1,0:T(8,128)S(1)}) custom-call(bf16[256,768]{1,0:T(8,128)(2,1)S(1)} %get-tuple-element.51.scaled_ref, bf16[128,1152]{1,0:T(8,128)(2,1)S(1)} %get-tuple-element.48.held_ref, bf16[128,1152]{1,0:T(8,128)(2,1)S(1)} %collective-permute-done.8.rest_ref, ...), custom_call_target="tpu_custom_call" | custom-call | flops 402653184 | bytes 3145728 | tf_op jit(solution)/shard_map/pallas_call | solution.py:109
  32.6 0.4 %collective-permute-done.13 = f32[4,2,128]{2,1,0:T(2,128)S(1)} collective-permute-done((f32[4,2,128]{2,1,0:T(2,128)S(1)}, f32[4,2,128]{2,1,0:T(2,128)S(1)}, u32[]{:S(2)}, u32[]{:S(2)}) %collective-permute-start.13) | collective-permute-done | bytes 4128 | tf_op jit(solution)/shard_map/ppermute | solution.py:94
  33.0 0.0 collective-permute-start.14
  33.0 0.0 copy-done.2
  33.0 0.7 %shard_map.100 = f32[8,16]{1,0:T(8,128)} custom-call(s32[8,16]{1,0:T(8,128)S(1)} %bitcast.15, f32[8,2,128]{2,1,0:T(2,128)S(1)} %constant_dynamic-update-slice_fusion.6.sums_ref), custom_call_target="tpu_custom_call" | custom-call | flops 256 | bytes 256 | tf_op jit(solution)/shard_map/pallas_call | solution.py:109
  33.6 0.9 %collective-permute-done.14.refs_4_ = bf16[128,1152]{1,0:T(8,128)(2,1)S(1)} collective-permute-done((bf16[128,1152]{1,0:T(8,128)(2,1)S(1)}, bf16[128,1152]{1,0:T(8,128)(2,1)S(1)}, u32[]{:S(2)}, u32[]{:S(2)}) %collective-permute-start.14) | collective-permute-done | bytes 294944 | tf_op jit(solution)/shard_map/ppermute | solution.py:94
  34.5 1.6 %shard_map.99 = bf16[768,1024]{1,0:T(8,128)(2,1)} custom-call(f32[256,1024]{1,0:T(8,128)S(1)} %get-tuple-element.53.refs_0_, f32[256,1024]{1,0:T(8,128)S(1)} %get-tuple-element.54.refs_1_, f32[256,1024]{1,0:T(8,128)S(1)} %get-tuple-element.55.refs_2_, bf16[256,768]{1,0:T(8,128)(2,1)S(1)} %collective-permute-done.6.refs_0_.refs_3_, ...), custom_call_target="tpu_custom_call" | custom-call | flops 805306368 | bytes 3145728 | tf_op jit(solution)/shard_map/pallas_call | solution.py:109
  (9 shorter events, 0.1 us)
Async XLA Ops:
  1.5 13.0 %collective-permute-start.5 = (bf16[768,2048]{1,0:T(8,128)(2,1)}, bf16[768,2048]{1,0:T(8,128)(2,1)S(1)}, u32[]{:S(2)}, u32[]{:S(2)}) collective-permute-start(bf16[768,2048]{1,0:T(8,128)(2,1)} %bitcast.18), channel_id=1, source_target_pairs={{0,4},{4,0},{8,12},{12,8},{1,5},{5,1},{9,13},{13,9},{2,6},{6,2},{1... | collective-permute-start | bytes 9437192 | tf_op jit(solution)/shard_map/ppermute | solution.py:94
  2.1 8.2 %collective-permute-start.3 = (bf16[16,2176]{1,0:T(8,128)(2,1)S(1)}, bf16[16,2176]{1,0:T(8,128)(2,1)S(1)}, u32[]{:S(2)}, u32[]{:S(2)}) collective-permute-start(bf16[16,2176]{1,0:T(8,128)(2,1)S(1)} %get-tuple-element.36), channel_id=1, source_target_pairs={{0,2},{1,3},{2,0},{3,1},{4,6},{5,7},{6,4},{7,5},{8,10},{9,11},{10,... | collective-permute-start | bytes 208904 | tf_op jit(solution)/shard_map/ppermute | solution.py:94
  5.7 6.8 %collective-permute-start = (bf16[16,2176]{1,0:T(8,128)(2,1)S(1)}, bf16[16,2176]{1,0:T(8,128)(2,1)S(1)}, u32[]{:S(2)}, u32[]{:S(2)}) collective-permute-start(bf16[16,2176]{1,0:T(8,128)(2,1)S(1)} %get-tuple-element.36), channel_id=1, source_target_pairs={{0,3},{1,2},{2,1},{3,0},{4,7},{5,6},{6,5},{7,4},{8,11},{9,10},{10,... | collective-permute-start | bytes 208904 | tf_op jit(solution)/shard_map/ppermute | solution.py:94
  7.1 5.8 %collective-permute-start.1 = (bf16[16,2176]{1,0:T(8,128)(2,1)S(1)}, bf16[16,2176]{1,0:T(8,128)(2,1)S(1)}, u32[]{:S(2)}, u32[]{:S(2)}) collective-permute-start(bf16[16,2176]{1,0:T(8,128)(2,1)S(1)} %get-tuple-element.36), channel_id=1, source_target_pairs={{0,1},{1,0},{2,3},{3,2},{4,5},{5,4},{6,7},{7,6},{8,9},{9,8},{10,11... | collective-permute-start | bytes 208904 | tf_op jit(solution)/shard_map/ppermute | solution.py:94
  8.6 11.0 %collective-permute-start.6 = (bf16[256,768]{1,0:T(8,128)(2,1)S(1)}, bf16[256,768]{1,0:T(8,128)(2,1)S(1)}, u32[]{:S(2)}, u32[]{:S(2)}) collective-permute-start(bf16[256,768]{1,0:T(8,128)(2,1)S(1)} %get-tuple-element.34.hidden_ref), channel_id=1, source_target_pairs={{0,16},{16,0},{1,17},{17,1},{2,18},{18,2},{3,19},{19,3},{4,20},{20... | collective-permute-start | bytes 1179656 | tf_op jit(solution)/shard_map/ppermute | solution.py:94
  10.3 6.9 %collective-permute-start.4 = (bf16[32,2176]{1,0:T(8,128)(2,1)S(1)}, bf16[32,2176]{1,0:T(8,128)(2,1)S(1)}, u32[]{:S(2)}, u32[]{:S(2)}) collective-permute-start(bf16[32,2176]{1,0:T(8,128)(2,1)S(1)} %constant_dynamic-update-slice_fusion.refs_0_), channel_id=1, source_target_pairs={{0,8},{4,12},{8,0},{12,4},{1,9},{5,13},{9,1},{13,5},{2,10},{6,14},... | collective-permute-start | bytes 417800 | tf_op jit(solution)/shard_map/ppermute | solution.py:94
  12.8 6.7 %collective-permute-start.2 = (bf16[128,768]{1,0:T(8,128)(2,1)S(1)}, bf16[128,768]{1,0:T(8,128)(2,1)S(1)}, u32[]{:S(2)}, u32[]{:S(2)}) collective-permute-start(bf16[128,768]{1,0:T(8,128)(2,1)S(1)} %get-tuple-element.37), channel_id=1, source_target_pairs={{0,4},{4,0},{8,12},{12,8},{1,5},{5,1},{9,13},{13,9},{2,6},{6,2},{1... | collective-permute-start | bytes 589832 | tf_op jit(solution)/shard_map/ppermute | solution.py:94
  12.9 6.7 %collective-permute-start.7 = (bf16[32,2176]{1,0:T(8,128)(2,1)S(1)}, bf16[32,2176]{1,0:T(8,128)(2,1)S(1)}, u32[]{:S(2)}, u32[]{:S(2)}) collective-permute-start(bf16[32,2176]{1,0:T(8,128)(2,1)S(1)} %constant_dynamic-update-slice_fusion.2.refs_1_), channel_id=1, source_target_pairs={{0,8},{4,12},{8,0},{12,4},{1,9},{5,13},{9,1},{13,5},{2,10},{6,14},... | collective-permute-start | bytes 417800 | tf_op jit(solution)/shard_map/ppermute | solution.py:94
  19.6 6.8 %copy-start = (bf16[1,1,256,768]{3,2,1,0:T(8,128)(2,1)S(1)}, bf16[1,1,256,768]{3,2,1,0:T(8,128)(2,1)}, u32[]{:S(2)}) copy-start(bf16[1,1,256,768]{3,2,1,0:T(8,128)(2,1)} %param.9) | copy-start | bytes 1179652
  19.6 6.8 %copy-start.1 = (bf16[1,1,256,768]{3,2,1,0:T(8,128)(2,1)S(1)}, bf16[1,1,256,768]{3,2,1,0:T(8,128)(2,1)}, u32[]{:S(2)}) copy-start(bf16[1,1,256,768]{3,2,1,0:T(8,128)(2,1)} %param.10) | copy-start | bytes 1179652
  20.7 12.3 %copy-start.2 = (s32[16,8]{0,1:T(8,128)S(1)}, s32[16,8]{0,1:T(8,128)}, u32[]{:S(2)}) copy-start(s32[16,8]{0,1:T(8,128)} %param.7) | copy-start | bytes 1540
  20.7 5.7 %collective-permute-start.9 = (f32[128,768]{1,0:T(8,128)S(1)}, f32[128,768]{1,0:T(8,128)S(1)}, u32[]{:S(2)}, u32[]{:S(2)}) collective-permute-start(f32[128,768]{1,0:T(8,128)S(1)} %get-tuple-element.50), channel_id=1, source_target_pairs={{0,4},{4,0},{8,12},{12,8},{1,5},{5,1},{9,13},{13,9},{2,6},{6,2},{1... | collective-permute-start | bytes 1179656 | tf_op jit(solution)/shard_map/ppermute | solution.py:94
  20.8 5.6 %collective-permute-start.8 = (bf16[128,1152]{1,0:T(8,128)(2,1)S(1)}, bf16[128,1152]{1,0:T(8,128)(2,1)S(1)}, u32[]{:S(2)}, u32[]{:S(2)}) collective-permute-start(bf16[128,1152]{1,0:T(8,128)(2,1)S(1)} %get-tuple-element.48.held_ref), channel_id=1, source_target_pairs={{0,4},{4,0},{8,12},{12,8},{1,5},{5,1},{9,13},{13,9},{2,6},{6,2},{1... | collective-permute-start | bytes 884744 | tf_op jit(solution)/shard_map/ppermute | solution.py:94
  21.3 3.6 %collective-permute-start.11 = (f32[1,2,128]{2,1,0:T(2,128)S(1)}, f32[1,2,128]{2,1,0:T(2,128)S(1)}, u32[]{:S(2)}, u32[]{:S(2)}) collective-permute-start(f32[1,2,128]{2,1,0:T(2,128)S(1)} %bitcast.16), channel_id=1, source_target_pairs={{0,8},{4,12},{8,0},{12,4},{1,9},{5,13},{9,1},{13,5},{2,10},{6,14},... | collective-permute-start | bytes 3080 | tf_op jit(solution)/shard_map/ppermute | solution.py:94
  22.8 8.7 %collective-permute-start.10 = (bf16[128,1152]{1,0:T(8,128)(2,1)S(1)}, bf16[128,1152]{1,0:T(8,128)(2,1)S(1)}, u32[]{:S(2)}, u32[]{:S(2)}) collective-permute-start(bf16[128,1152]{1,0:T(8,128)(2,1)S(1)} %get-tuple-element.52), channel_id=1, source_target_pairs={{0,16},{16,0},{1,17},{17,1},{2,18},{18,2},{3,19},{19,3},{4,20},{20... | collective-permute-start | bytes 884744 | tf_op jit(solution)/shard_map/ppermute | solution.py:94
  24.9 3.6 %collective-permute-start.12 = (f32[2,2,128]{2,1,0:T(2,128)S(1)}, f32[2,2,128]{2,1,0:T(2,128)S(1)}, u32[]{:S(2)}, u32[]{:S(2)}) collective-permute-start(f32[2,2,128]{2,1,0:T(2,128)S(1)} %pad_maximum_fusion), channel_id=1, source_target_pairs={{0,1},{1,0},{2,3},{3,2},{4,5},{5,4},{6,7},{7,6},{8,9},{9,8},{10,11... | collective-permute-start | bytes 6152 | tf_op jit(solution)/shard_map/ppermute | solution.py:94
  28.4 4.5 %collective-permute-start.13 = (f32[4,2,128]{2,1,0:T(2,128)S(1)}, f32[4,2,128]{2,1,0:T(2,128)S(1)}, u32[]{:S(2)}, u32[]{:S(2)}) collective-permute-start(f32[4,2,128]{2,1,0:T(2,128)S(1)} %constant_dynamic-update-slice_fusion.4), channel_id=1, source_target_pairs={{0,2},{1,3},{2,0},{3,1},{4,6},{5,7},{6,4},{7,5},{8,10},{9,11},{10,... | collective-permute-start | bytes 12296 | tf_op jit(solution)/shard_map/ppermute | solution.py:94
  33.0 1.6 %collective-permute-start.14 = (bf16[128,1152]{1,0:T(8,128)(2,1)S(1)}, bf16[128,1152]{1,0:T(8,128)(2,1)S(1)}, u32[]{:S(2)}, u32[]{:S(2)}) collective-permute-start(bf16[128,1152]{1,0:T(8,128)(2,1)S(1)} %collective-permute-done.10.refs_1_), channel_id=1, source_target_pairs={{0,4},{4,0},{8,12},{12,8},{1,5},{5,1},{9,13},{13,9},{2,6},{6,2},{1... | collective-permute-start | bytes 884744 | tf_op jit(solution)/shard_map/ppermute | solution.py:94

commit v6 on v5

--- a/solution.py
+++ b/solution.py
@@ -8,7 +8,7 @@
 from jax.sharding import PartitionSpec as P
 
 LANES = 128
-PIECES = 3
+CUTS = 2
 PARTS = 4
 VMEM_LIMIT = 14 * 1024 * 1024
 
@@ -98,7 +98,7 @@
     return lax.optimization_barrier((x,) + done)[0]
 
 
-def call(kernel, outs, cost, *args, hbm=0, scratch=(), deps=(), out_space=pltpu.VMEM):
+def call(kernel, outs, cost, *args, hbm=0, scratch=(), deps=(), out_specs=None):
     flops, moved = cost
     body = kernel
     if deps:
@@ -112,7 +112,9 @@
         in_specs=[pl.BlockSpec(memory_space=pltpu.HBM)] * hbm
         + [pl.BlockSpec(memory_space=pltpu.VMEM)] * (len(args) - hbm)
         + [pl.BlockSpec(memory_space=pl.ANY)] * len(deps),
-        out_specs=jax.tree.map(lambda _: pl.BlockSpec(memory_space=out_space), outs),
+        out_specs=jax.tree.map(lambda _: pl.BlockSpec(memory_space=pltpu.VMEM), outs)
+        if out_specs is None
+        else out_specs,
         scratch_shapes=scratch,
         compiler_params=pltpu.CompilerParams(vmem_limit_bytes=VMEM_LIMIT),
         cost_estimate=pl.CostEstimate(flops=flops, bytes_accessed=moved, transcendentals=0),
@@ -204,7 +206,7 @@
 def back_kernel(features, blocks, columns, hidden_ref, other_hidden_ref, *refs):
     group_refs, refs = refs[:blocks], refs[blocks:]
     turned_refs, refs = refs[: 2 * PARTS], refs[2 * PARTS :]
-    back_ref, other_back_ref, sums_ref, *cut_refs = refs
+    back_ref, other_back_ref, sums_ref, own_ref = refs
     held = jnp.concatenate([group_ref[...] for group_ref in group_refs], axis=0)
     rows = held.shape[0]
     for expert, (act_ref, result_ref) in enumerate(
@@ -229,13 +231,21 @@
             sums_ref[row : row + 1, :] = jnp.sum(
                 folded[at : at + LANES, :].T, axis=0, keepdims=True
             )
-    step = rows // blocks
-    for bits, cut_ref in enumerate(cut_refs):
-        start = pl.multiple_of((lax.axis_index("dp") ^ bits) * columns, columns)
-        for block, group_ref in enumerate(group_refs):
-            here = slice(block * step, (block + 1) * step)
-            cut_ref[here, :columns] = group_ref[:, pl.ds(start, columns)]
-            cut_ref[here, columns:] = group_ref[:, features:]
+    copy_columns(features, columns, 0, group_refs, own_ref)
+
+
+def copy_columns(features, columns, bits, group_refs, out_ref):
+    start = pl.multiple_of((lax.axis_index("dp") ^ bits) * columns, columns)
+    step = out_ref.shape[0] // len(group_refs)
+    for block, group_ref in enumerate(group_refs):
+        here = slice(block * step, (block + 1) * step)
+        out_ref[here, :columns] = group_ref[:, pl.ds(start, columns)]
+        out_ref[here, columns:] = group_ref[:, features:]
+
+
+def cut_kernel(features, columns, blocks, *refs):
+    for bits, cut_ref in enumerate(refs[blocks:], 1):
+        copy_columns(features, columns, bits, refs[:blocks], cut_ref)
 
 
 def own_gates(table):
@@ -284,49 +294,31 @@
     return (own_gates(table) * hidden.astype(jnp.float32)).astype(jnp.bfloat16)
 
 
-def first_down_kernel(scaled_ref, held_ref, rest_ref, *refs):
-    sum_refs, refs = refs[-PIECES:], refs[:-PIECES]
-    depth, columns = sum_refs[0].shape
+def down_kernel(scaled_ref, held_ref, rest_ref, *refs):
+    out_ref, held_out_ref, sems = refs[-3:]
+    columns = out_ref.shape[1]
     scaled, tokens = [scaled_ref[...]], [held_ref[:, :columns], rest_ref[:, :columns]]
-    for hidden_ref, one_ref in zip(refs[::2], refs[1::2]):
-        scaled.append(scale(hidden_ref[: one_ref.shape[0], :], one_ref[:, columns:]))
-        tokens.append(one_ref[:, :columns])
+    for at in range(0, len(refs) - 3, CUTS + 2):
+        hidden_ref, *part_refs = refs[at : at + CUTS + 2]
+        start = 0
+        for part_ref in part_refs:
+            stop = start + part_ref.shape[0]
+            scaled.append(scale(hidden_ref[start:stop, :], part_ref[:, columns:]))
+            tokens.append(part_ref[:, :columns])
+            start = stop
     scaled = jnp.concatenate(scaled, axis=0)
     tokens = jnp.concatenate(tokens, axis=0)
-    for at, sum_ref in enumerate(sum_refs):
-        sum_ref[...] = lax.dot_general(
-            scaled[:, at * depth : (at + 1) * depth],
+    copies = []
+    for at in range(0, out_ref.shape[0], 2 * LANES):
+        here = pl.ds(at, 2 * LANES)
+        held_out_ref[here, :] = lax.dot_general(
+            scaled[:, at : at + 2 * LANES],
             tokens,
             (((0,), (0,)), ((), ())),
             preferred_element_type=jnp.float32,
-        )
-
-
-def last_down_kernel(*refs):
-    out_ref, held_out_ref, sems = refs[-3:]
-    sum_refs, refs = refs[:PIECES], refs[PIECES:-3]
-    depth, columns = sum_refs[0].shape
-    scaled, tokens = [], []
-    for hidden_ref, two_ref in zip(refs[::2], refs[1::2]):
-        rows = two_ref.shape[0]
-        scaled.append(scale(hidden_ref[rows:, :], two_ref[:, columns:]))
-        tokens.append(two_ref[:, :columns])
-    scaled = jnp.concatenate(scaled, axis=0)
-    tokens = jnp.concatenate(tokens, axis=0)
-    copies = []
-    for at, sum_ref in enumerate(sum_refs):
-        here = pl.ds(at * depth, depth)
-        held_out_ref[here, :] = (
-            sum_ref[...]
-            + lax.dot_general(
-                scaled[:, at * depth : (at + 1) * depth],
-                tokens,
-                (((0,), (0,)), ((), ())),
-                preferred_element_type=jnp.float32,
-            )
         ).astype(out_ref.dtype)
         copies.append(
-            pltpu.make_async_copy(held_out_ref.at[here], out_ref.at[here], sems.at[at])
+            pltpu.make_async_copy(held_out_ref.at[here], out_ref.at[here], sems.at[len(copies)])
         )
         copies[-1].start()
     for copy in copies:
@@ -421,14 +413,21 @@
         groups += [swap(group, "wide", bits) for group in groups]
     middle = len(groups) // 2
     groups[middle] = after(groups[middle], *turned, *over)
-    back, other_back, sums, *cuts = call(
+    cuts = call(
+        functools.partial(cut_kernel, features, columns, len(groups)),
+        (shape((half_count, columns + LANES), bf16),) * (dp_count - 1),
+        (0, 4 * half_count * columns),
+        *groups,
+    )
+    crossed = [swap(cut, "dp", bits) for bits, cut in enumerate(cuts, 1)]
+    back, other_back, sums, held = call(
         functools.partial(back_kernel, features, len(groups), columns),
         (
             shape((half_count, units), f32),
             shape((half_count, units), f32),
             shape((slot_count // LANES, LANES), f32),
-        )
-        + (shape((half_count, columns + LANES), bf16),) * dp_count,
+            shape((half_count, columns + LANES), bf16),
+        ),
         (2 * slot_count * units * features, 4 * units * features),
         hidden,
         other_hidden,
@@ -440,10 +439,8 @@
     for bits in wide_bits:
         found = jnp.concatenate([found, swap(found, "wide", bits)], axis=0)
         back_order += [(w ^ bits, n) for w, n in back_order]
-    held, *cuts = cuts
     rest = swap(held, "wide", 1)
     rest_back = swap(other_back, "wide", 1)
-    crossed = [swap(cut, "dp", bits) for bits, cut in enumerate(cuts, 1)]
     grad_a, grad_b, scaled = call(
         functools.partial(grads_kernel, order, rows, columns),
         (shape((slot_count, units), bf16),) * 3,
@@ -456,32 +453,32 @@
         pre_gate,
         pre_up,
     )
-    sums_down = call(
-        first_down_kernel,
-        (shape((units // PIECES, columns), f32),) * PIECES,
-        (2 * slot_count * units * columns, 4 * units * columns),
+    steps = [1 << b for b in range(narrow_count.bit_length() - 1)]
+    for bits in steps[:-1]:
+        found = jnp.concatenate([after(found, scaled), swap(found, "narrow", bits)], axis=0)
+        back_order += [(w, n ^ bits) for w, n in back_order]
+    others = []
+    cut = half_count // CUTS
+    for hidden_there, one in zip(over, crossed):
+        others += [hidden_there, one]
+        others += [swap(one[at : at + cut], "wide", 1) for at in range(0, half_count, cut)]
+    grad_down = call(
+        down_kernel,
+        shape((units, columns), bf16),
+        (2 * dp_count * slot_count * units * columns, 4 * units * columns),
         scaled,
         held,
         rest,
-        *(x for pair in zip(over, crossed) for x in pair),
-    )
-    bits_of = [1 << b for b in range(narrow_count.bit_length() - 1)]
-    for bits, done in zip(bits_of, [scaled] * (len(bits_of) - 1) + [sums_down[-1]]):
-        found = jnp.concatenate([after(found, done), swap(found, "narrow", bits)], axis=0)
-        back_order += [(w, n ^ bits) for w, n in back_order]
-    across = [swap(after(one, found), "wide", 1) for one in crossed]
-    grad_down = call(
-        last_down_kernel,
-        shape((units, columns), bf16),
-        (2 * dp_count * slot_count * units * columns, 4 * units * columns),
-        *sums_down,
-        *(x for pair in zip(over, across) for x in pair),
-        out_space=pltpu.HBM,
+        *others,
+        out_specs=pl.BlockSpec(memory_space=pltpu.HBM),
         scratch=[
             pltpu.VMEM((units, columns), bf16),
-            pltpu.SemaphoreType.DMA((PIECES,)),
+            pltpu.SemaphoreType.DMA((units // (2 * LANES),)),
         ],
     )
+    for bits in steps[-1:]:
+        found = jnp.concatenate([after(found, grad_down), swap(found, "narrow", bits)], axis=0)
+        back_order += [(w, n ^ bits) for w, n in back_order]
     picked = call(
         functools.partial(pick_kernel, order, tuple(back_order), rows),
         shape(routes_t.shape, f32),

time: 36.3 us -> 35.7 us (0.983)
  waiting for transfers between devices: 6.26 us -> 5.15 us
  starting transfers between devices: 18.5 us -> 19.5 us
  Pallas kernels: 10.6 us -> 9.88 us
    ppermute x15 -> x16, waiting for transfers between devices: 6.26 us -> 5.15 us  [swap(): return lax.ppermute(x, axis, [(i, i ^ bits) for i in range(count)])]
    ppermute x15 -> x16, starting transfers between devices: 18.5 us -> 19.5 us  [swap(): return lax.ppermute(x, axis, [(i, i ^ bits) for i in range(count)])]
    pallas_call x8, Pallas kernels: 10.6 us -> 9.88 us  [call(): pl.pallas_call(body, out_shape=outs, in_specs=[pl.BlockSpec(memory_space=...]
  transfers between devices with their start and end apart: 15 -> 16, of which waited for: 9 -> 6; matrix products, arithmetic and copies ran while one was open for 0% -> 0% of each run, Pallas kernels for 19% -> 23%
where the time goes in v6:
time: 35.7 us; the launch traced here: 35.4 us
  starting transfers between devices  19.5 us (55%)
  Pallas kernels  9.88 us (28%)
  waiting for transfers between devices  5.15 us (14%)
  between operations  0.77 us (2%)
    ppermute x16, starting transfers between devices, swap(): return lax.ppermute(x, axis, [(i, i ^ bits) for i in range(count)])  19.5 us
    pallas_call x8, Pallas kernels, call(): pl.pallas_call(body, out_shape=outs, in_specs=[pl.BlockSpec(memory_space=...  9.88 us
    ppermute x16, waiting for transfers between devices, swap(): return lax.ppermute(x, axis, [(i, i ^ bits) for i in range(count)])  5.15 us
  transfers between devices with their start and end apart: 16, of which 6 were waited for; matrix products, arithmetic and copies ran while one was open for 0% of the time, Pallas kernels for 23%

profile of v6, /device:TPU:0, one launch (start us, length us, event | category | flops | bytes accessed | tf_op | source)
XLA Modules:
  0.0 35.4 jit_solution(3644633936705005101)
XLA Ops:
  0.6 0.9 %shard_map.93 = (bf16[16,2176]{1,0:T(8,128)(2,1)S(1)}, f32[8,128]{1,0:T(8,128)S(1)}) custom-call(bf16[16,2048]{1,0:T(8,128)(2,1)} %grad_hbm.1, s32[8,16]{1,0:T(8,128)} %bitcast.14, bf16[8,16]{1,0:T(8,128)(2,1)} %bitcast.22), custom_call_target="tpu_custom_call" | custom-call | flops 32768 | bytes 131072 | tf_op jit(solution)/shard_map/pallas_call | solution.py:109
  1.5 0.5 %collective-permute-start.5 = (bf16[768,2048]{1,0:T(8,128)(2,1)}, bf16[768,2048]{1,0:T(8,128)(2,1)S(1)}, u32[]{:S(2)}, u32[]{:S(2)}) collective-permute-start(bf16[768,2048]{1,0:T(8,128)(2,1)} %bitcast.18), channel_id=1, source_target_pairs={{0,4},{4,0},{8,12},{12,8},{1,5},{5,1},{9,13},{13,9},{2,6},{6,2},{1... | collective-permute-start | bytes 9437192 | tf_op jit(solution)/shard_map/ppermute | solution.py:94
  2.1 3.7 %collective-permute-start.3 = (bf16[16,2176]{1,0:T(8,128)(2,1)S(1)}, bf16[16,2176]{1,0:T(8,128)(2,1)S(1)}, u32[]{:S(2)}, u32[]{:S(2)}) collective-permute-start(bf16[16,2176]{1,0:T(8,128)(2,1)S(1)} %get-tuple-element.31), channel_id=1, source_target_pairs={{0,2},{1,3},{2,0},{3,1},{4,6},{5,7},{6,4},{7,5},{8,10},{9,11},{10,... | collective-permute-start | bytes 208904 | tf_op jit(solution)/shard_map/ppermute | solution.py:94
  5.7 1.3 %collective-permute-start = (bf16[16,2176]{1,0:T(8,128)(2,1)S(1)}, bf16[16,2176]{1,0:T(8,128)(2,1)S(1)}, u32[]{:S(2)}, u32[]{:S(2)}) collective-permute-start(bf16[16,2176]{1,0:T(8,128)(2,1)S(1)} %get-tuple-element.31), channel_id=1, source_target_pairs={{0,3},{1,2},{2,1},{3,0},{4,7},{5,6},{6,5},{7,4},{8,11},{9,10},{10,... | collective-permute-start | bytes 208904 | tf_op jit(solution)/shard_map/ppermute | solution.py:94
  7.1 0.2 collective-permute-start.1
  7.3 1.3 %shard_map.94 = (bf16[256,768]{1,0:T(8,128)(2,1)S(1)}, bf16[128,768]{1,0:T(8,128)(2,1)S(1)}) custom-call(bf16[256,768]{1,0:T(8,128)(2,1)} %bitcast.10, bf16[256,768]{1,0:T(8,128)(2,1)} %bitcast.12, f32[8,128]{1,0:T(8,128)S(1)} %get-tuple-element.28.refs_2_), custom_call_target="tpu_custom_call" | custom-call | flops 3932160 | bytes 1179648 | tf_op jit(solution)/shard_map/pallas_call | solution.py:109
  8.6 1.6 %collective-permute-start.6 = (bf16[256,768]{1,0:T(8,128)(2,1)S(1)}, bf16[256,768]{1,0:T(8,128)(2,1)S(1)}, u32[]{:S(2)}, u32[]{:S(2)}) collective-permute-start(bf16[256,768]{1,0:T(8,128)(2,1)S(1)} %get-tuple-element.29.hidden_ref), channel_id=1, source_target_pairs={{0,16},{16,0},{1,17},{17,1},{2,18},{18,2},{3,19},{19,3},{4,20},{20... | collective-permute-start | bytes 1179656 | tf_op jit(solution)/shard_map/ppermute | solution.py:94
  10.2 0.1 collective-permute-done.3
  10.3 1.7 %collective-permute-start.4 = (bf16[32,2176]{1,0:T(8,128)(2,1)S(1)}, bf16[32,2176]{1,0:T(8,128)(2,1)S(1)}, u32[]{:S(2)}, u32[]{:S(2)}) collective-permute-start(bf16[32,2176]{1,0:T(8,128)(2,1)S(1)} %constant_dynamic-update-slice_fusion.refs_0_), channel_id=1, source_target_pairs={{0,8},{4,12},{8,0},{12,4},{1,9},{5,13},{9,1},{13,5},{2,10},{6,14},... | collective-permute-start | bytes 417800 | tf_op jit(solution)/shard_map/ppermute | solution.py:94
  12.0 0.6 %collective-permute-done = bf16[16,2176]{1,0:T(8,128)(2,1)S(1)} collective-permute-done((bf16[16,2176]{1,0:T(8,128)(2,1)S(1)}, bf16[16,2176]{1,0:T(8,128)(2,1)S(1)}, u32[]{:S(2)}, u32[]{:S(2)}) %collective-permute-start) | collective-permute-done | bytes 69664 | tf_op jit(solution)/shard_map/ppermute | solution.py:94
  12.5 0.3 collective-permute-done.1
  12.9 1.6 %collective-permute-start.7 = (bf16[32,2176]{1,0:T(8,128)(2,1)S(1)}, bf16[32,2176]{1,0:T(8,128)(2,1)S(1)}, u32[]{:S(2)}, u32[]{:S(2)}) collective-permute-start(bf16[32,2176]{1,0:T(8,128)(2,1)S(1)} %constant_dynamic-update-slice_fusion.2.refs_1_), channel_id=1, source_target_pairs={{0,8},{4,12},{8,0},{12,4},{1,9},{5,13},{9,1},{13,5},{2,10},{6,14},... | collective-permute-start | bytes 417800 | tf_op jit(solution)/shard_map/ppermute | solution.py:94
  14.5 0.0 collective-permute-start.2
  14.5 0.0 collective-permute-done.5.refs_1_
  14.5 2.6 %shard_map.95 = (bf16[512,768]{1,0:T(8,128)(2,1)S(1)}, bf16[512,768]{1,0:T(8,128)(2,1)S(1)}, bf16[512,768]{1,0:T(8,128)(2,1)S(1)}, bf16[512,768]{1,0:T(8,128)(2,...) custom-call(bf16[768,2048]{1,0:T(8,128)(2,1)} %bitcast.19, ...), custom_call_target="tpu_custom_call" | custom-call | bytes 12582912 | tf_op jit(solution)/shard_map/pallas_call | solution.py:109
  17.1 0.0 collective-permute-done.4.refs_2_
  17.1 2.5 %collective-permute-done.6.refs_0_ = bf16[256,768]{1,0:T(8,128)(2,1)S(1)} collective-permute-done((bf16[256,768]{1,0:T(8,128)(2,1)S(1)}, bf16[256,768]{1,0:T(8,128)(2,1)S(1)}, u32[]{:S(2)}, u32[]{:S(2)}) %collective-permute-start.6) | collective-permute-done | bytes 393248 | tf_op jit(solution)/shard_map/ppermute | solution.py:94
  19.6 0.0 collective-permute-done.7.refs_3_
  19.6 0.0 copy-start
  19.6 0.0 copy-start.1
  19.6 1.6 %collective-permute-start.10 = (bf16[128,1152]{1,0:T(8,128)(2,1)S(1)}, bf16[128,1152]{1,0:T(8,128)(2,1)S(1)}, u32[]{:S(2)}, u32[]{:S(2)}) collective-permute-start(bf16[128,1152]{1,0:T(8,128)(2,1)S(1)} %shard_map.98), channel_id=1, source_target_pairs={{0,16},{16,0},{1,17},{17,1},{2,18},{18,2},{3,19},{19,3},{4,20},{20... | collective-permute-start | bytes 884744 | tf_op jit(solution)/shard_map/ppermute | solution.py:94
  21.2 0.0 collective-permute-done.2.other_hidden_ref
  21.2 1.1 %shard_map.96 = (f32[128,768]{1,0:T(8,128)S(1)}, f32[128,768]{1,0:T(8,128)S(1)}, f32[2,128]{1,0:T(2,128)S(1)}, bf16[128,1152]{1,0:T(8,128)(2,1)S(1)}) custom-call(bf16[256,768]{1,0:T(8,128)(2,1)S(1)} %get-tuple-element.29.hidden_ref, bf16[128,768]{1,0:T(8,128)(2,1)S(1)} %collective-permute-done.2.other_hidden_ref, ...), custom_call_target="tpu_custom_call" | custom-call | flops 805306368 | bytes 6291456 | tf_op jit(solution)/shard_map/pallas_call | solution.py:109
  22.3 1.6 %collective-permute-start.13 = (f32[1,2,128]{2,1,0:T(2,128)S(1)}, f32[1,2,128]{2,1,0:T(2,128)S(1)}, u32[]{:S(2)}, u32[]{:S(2)}) collective-permute-start(f32[1,2,128]{2,1,0:T(2,128)S(1)} %bitcast.16), channel_id=1, source_target_pairs={{0,8},{4,12},{8,0},{12,4},{1,9},{5,13},{9,1},{13,5},{2,10},{6,14},... | collective-permute-start | bytes 3080 | tf_op jit(solution)/shard_map/ppermute | solution.py:94
  23.9 0.0 collective-permute-start.9
  23.9 0.5 %collective-permute-start.8 = (bf16[128,1152]{1,0:T(8,128)(2,1)S(1)}, bf16[128,1152]{1,0:T(8,128)(2,1)S(1)}, u32[]{:S(2)}, u32[]{:S(2)}) collective-permute-start(bf16[128,1152]{1,0:T(8,128)(2,1)S(1)} %get-tuple-element.43.held_ref), channel_id=1, source_target_pairs={{0,4},{4,0},{8,12},{12,8},{1,5},{5,1},{9,13},{13,9},{2,6},{6,2},{1... | collective-permute-start | bytes 884744 | tf_op jit(solution)/shard_map/ppermute | solution.py:94
  24.4 1.5 %collective-permute-done.13 = f32[1,2,128]{2,1,0:T(2,128)S(1)} collective-permute-done((f32[1,2,128]{2,1,0:T(2,128)S(1)}, f32[1,2,128]{2,1,0:T(2,128)S(1)}, u32[]{:S(2)}, u32[]{:S(2)}) %collective-permute-start.13) | collective-permute-done | bytes 1056 | tf_op jit(solution)/shard_map/ppermute | solution.py:94
  25.9 1.5 %collective-permute-start.14 = (f32[2,2,128]{2,1,0:T(2,128)S(1)}, f32[2,2,128]{2,1,0:T(2,128)S(1)}, u32[]{:S(2)}, u32[]{:S(2)}) collective-permute-start(f32[2,2,128]{2,1,0:T(2,128)S(1)} %pad_maximum_fusion.1), channel_id=1, source_target_pairs={{0,1},{1,0},{2,3},{3,2},{4,5},{5,4},{6,7},{7,6},{8,9},{9,8},{10,11... | collective-permute-start | bytes 6152 | tf_op jit(solution)/shard_map/ppermute | solution.py:94
  27.5 0.2 collective-permute-done.10.refs_1_
  27.7 0.0 copy-start.2
  27.7 0.1 collective-permute-start.11
  27.8 0.5 %collective-permute-start.12 = (bf16[64,1152]{1,0:T(8,128)(2,1)S(1)}, bf16[64,1152]{1,0:T(8,128)(2,1)S(1)}, u32[]{:S(2)}, u32[]{:S(2)}) collective-permute-start(bf16[64,1152]{1,0:T(8,128)(2,1)S(1)} %get-tuple-element.52), channel_id=1, source_target_pairs={{0,4},{4,0},{8,12},{12,8},{1,5},{5,1},{9,13},{13,9},{2,6},{6,2},{1... | collective-permute-start | bytes 442376 | tf_op jit(solution)/shard_map/ppermute | solution.py:94
  28.3 0.0 collective-permute-done.8.rest_ref
  28.3 0.0 collective-permute-done.9.rest_back_ref
  28.3 0.0 copy-done
  28.3 0.0 copy-done.1
  28.3 1.4 %shard_map.97 = (bf16[256,768]{1,0:T(8,128)(2,1)}, bf16[256,768]{1,0:T(8,128)(2,1)}, bf16[256,768]{1,0:T(8,128)(2,1)S(1)}) custom-call(bf16[128,1152]{1,0:T(8,128)(2,1)S(1)} %get-tuple-element.43.held_ref, bf16[128,1152]{1,0:T(8,128)(2,1)S(1)} %collective-permute-done.8.rest_ref, f32[128,768]{1,0:T(8,128)S(1)} %get-tuple-element.44.back_ref, ...), custom_call_target="tpu_custom_call" | custom-call | flops 5898240 | bytes 2359296 | tf_op jit(solution)/shard_map/pallas_call | solution.py:109
  29.7 0.0 collective-permute-done.14
  29.7 3.1 %collective-permute-start.15 = (f32[4,2,128]{2,1,0:T(2,128)S(1)}, f32[4,2,128]{2,1,0:T(2,128)S(1)}, u32[]{:S(2)}, u32[]{:S(2)}) collective-permute-start(f32[4,2,128]{2,1,0:T(2,128)S(1)} %constant_dynamic-update-slice_fusion.4), channel_id=1, source_target_pairs={{0,2},{1,3},{2,0},{3,1},{4,6},{5,7},{6,4},{7,5},{8,10},{9,11},{10,... | collective-permute-start | bytes 12296 | tf_op jit(solution)/shard_map/ppermute | solution.py:94
  32.8 0.0 collective-permute-done.11.refs_2_
  32.8 0.0 collective-permute-done.12.refs_3_
  32.8 1.9 %shard_map.99 = bf16[768,1024]{1,0:T(8,128)(2,1)} custom-call(bf16[256,768]{1,0:T(8,128)(2,1)S(1)} %get-tuple-element.46.scaled_ref, bf16[128,1152]{1,0:T(8,128)(2,1)S(1)} %get-tuple-element.43.held_ref, bf16[128,1152]{1,0:T(8,128)(2,1)S(1)} %collective-permute-done.8.rest_ref, bf16[256,768]{1,0:T(8,128)(2,1)S(1)} %collective-permute-done.6.refs_0_, ...), custom_call_target="tpu_custom_call" | custom-call | flops 805306368 | bytes 3145728 | tf_op jit(solution)/shard_map/pallas_call | solution.py:109
  34.7 0.0 collective-permute-done.15
  34.7 0.0 copy-done.2
  34.8 0.7 %shard_map.100 = f32[8,16]{1,0:T(8,128)} custom-call(s32[8,16]{1,0:T(8,128)S(1)} %bitcast.15, f32[8,2,128]{2,1,0:T(2,128)S(1)} %pad_maximum_fusion.sums_ref), custom_call_target="tpu_custom_call" | custom-call | flops 256 | bytes 256 | tf_op jit(solution)/shard_map/pallas_call | solution.py:109
  (10 shorter events, 0.1 us)
Async XLA Ops:
  1.5 13.0 %collective-permute-start.5 = (bf16[768,2048]{1,0:T(8,128)(2,1)}, bf16[768,2048]{1,0:T(8,128)(2,1)S(1)}, u32[]{:S(2)}, u32[]{:S(2)}) collective-permute-start(bf16[768,2048]{1,0:T(8,128)(2,1)} %bitcast.18), channel_id=1, source_target_pairs={{0,4},{4,0},{8,12},{12,8},{1,5},{5,1},{9,13},{13,9},{2,6},{6,2},{1... | collective-permute-start | bytes 9437192 | tf_op jit(solution)/shard_map/ppermute | solution.py:94
  2.1 8.2 %collective-permute-start.3 = (bf16[16,2176]{1,0:T(8,128)(2,1)S(1)}, bf16[16,2176]{1,0:T(8,128)(2,1)S(1)}, u32[]{:S(2)}, u32[]{:S(2)}) collective-permute-start(bf16[16,2176]{1,0:T(8,128)(2,1)S(1)} %get-tuple-element.31), channel_id=1, source_target_pairs={{0,2},{1,3},{2,0},{3,1},{4,6},{5,7},{6,4},{7,5},{8,10},{9,11},{10,... | collective-permute-start | bytes 208904 | tf_op jit(solution)/shard_map/ppermute | solution.py:94
  5.7 6.8 %collective-permute-start = (bf16[16,2176]{1,0:T(8,128)(2,1)S(1)}, bf16[16,2176]{1,0:T(8,128)(2,1)S(1)}, u32[]{:S(2)}, u32[]{:S(2)}) collective-permute-start(bf16[16,2176]{1,0:T(8,128)(2,1)S(1)} %get-tuple-element.31), channel_id=1, source_target_pairs={{0,3},{1,2},{2,1},{3,0},{4,7},{5,6},{6,5},{7,4},{8,11},{9,10},{10,... | collective-permute-start | bytes 208904 | tf_op jit(solution)/shard_map/ppermute | solution.py:94
  7.1 5.8 %collective-permute-start.1 = (bf16[16,2176]{1,0:T(8,128)(2,1)S(1)}, bf16[16,2176]{1,0:T(8,128)(2,1)S(1)}, u32[]{:S(2)}, u32[]{:S(2)}) collective-permute-start(bf16[16,2176]{1,0:T(8,128)(2,1)S(1)} %get-tuple-element.31), channel_id=1, source_target_pairs={{0,1},{1,0},{2,3},{3,2},{4,5},{5,4},{6,7},{7,6},{8,9},{9,8},{10,11... | collective-permute-start | bytes 208904 | tf_op jit(solution)/shard_map/ppermute | solution.py:94
  8.6 11.0 %collective-permute-start.6 = (bf16[256,768]{1,0:T(8,128)(2,1)S(1)}, bf16[256,768]{1,0:T(8,128)(2,1)S(1)}, u32[]{:S(2)}, u32[]{:S(2)}) collective-permute-start(bf16[256,768]{1,0:T(8,128)(2,1)S(1)} %get-tuple-element.29.hidden_ref), channel_id=1, source_target_pairs={{0,16},{16,0},{1,17},{17,1},{2,18},{18,2},{3,19},{19,3},{4,20},{20... | collective-permute-start | bytes 1179656 | tf_op jit(solution)/shard_map/ppermute | solution.py:94
  10.3 6.8 %collective-permute-start.4 = (bf16[32,2176]{1,0:T(8,128)(2,1)S(1)}, bf16[32,2176]{1,0:T(8,128)(2,1)S(1)}, u32[]{:S(2)}, u32[]{:S(2)}) collective-permute-start(bf16[32,2176]{1,0:T(8,128)(2,1)S(1)} %constant_dynamic-update-slice_fusion.refs_0_), channel_id=1, source_target_pairs={{0,8},{4,12},{8,0},{12,4},{1,9},{5,13},{9,1},{13,5},{2,10},{6,14},... | collective-permute-start | bytes 417800 | tf_op jit(solution)/shard_map/ppermute | solution.py:94
  12.9 6.7 %collective-permute-start.7 = (bf16[32,2176]{1,0:T(8,128)(2,1)S(1)}, bf16[32,2176]{1,0:T(8,128)(2,1)S(1)}, u32[]{:S(2)}, u32[]{:S(2)}) collective-permute-start(bf16[32,2176]{1,0:T(8,128)(2,1)S(1)} %constant_dynamic-update-slice_fusion.2.refs_1_), channel_id=1, source_target_pairs={{0,8},{4,12},{8,0},{12,4},{1,9},{5,13},{9,1},{13,5},{2,10},{6,14},... | collective-permute-start | bytes 417800 | tf_op jit(solution)/shard_map/ppermute | solution.py:94
  14.5 6.7 %collective-permute-start.2 = (bf16[128,768]{1,0:T(8,128)(2,1)S(1)}, bf16[128,768]{1,0:T(8,128)(2,1)S(1)}, u32[]{:S(2)}, u32[]{:S(2)}) collective-permute-start(bf16[128,768]{1,0:T(8,128)(2,1)S(1)} %get-tuple-element.32), channel_id=1, source_target_pairs={{0,4},{4,0},{8,12},{12,8},{1,5},{5,1},{9,13},{13,9},{2,6},{6,2},{1... | collective-permute-start | bytes 589832 | tf_op jit(solution)/shard_map/ppermute | solution.py:94
  19.6 8.6 %copy-start = (bf16[1,1,256,768]{3,2,1,0:T(8,128)(2,1)S(1)}, bf16[1,1,256,768]{3,2,1,0:T(8,128)(2,1)}, u32[]{:S(2)}) copy-start(bf16[1,1,256,768]{3,2,1,0:T(8,128)(2,1)} %param.9) | copy-start | bytes 1179652
  19.6 8.6 %copy-start.1 = (bf16[1,1,256,768]{3,2,1,0:T(8,128)(2,1)S(1)}, bf16[1,1,256,768]{3,2,1,0:T(8,128)(2,1)}, u32[]{:S(2)}) copy-start(bf16[1,1,256,768]{3,2,1,0:T(8,128)(2,1)} %param.10) | copy-start | bytes 1179652
  19.6 8.0 %collective-permute-start.10 = (bf16[128,1152]{1,0:T(8,128)(2,1)S(1)}, bf16[128,1152]{1,0:T(8,128)(2,1)S(1)}, u32[]{:S(2)}, u32[]{:S(2)}) collective-permute-start(bf16[128,1152]{1,0:T(8,128)(2,1)S(1)} %shard_map.98), channel_id=1, source_target_pairs={{0,16},{16,0},{1,17},{17,1},{2,18},{18,2},{3,19},{19,3},{4,20},{20... | collective-permute-start | bytes 884744 | tf_op jit(solution)/shard_map/ppermute | solution.py:94
  22.3 3.6 %collective-permute-start.13 = (f32[1,2,128]{2,1,0:T(2,128)S(1)}, f32[1,2,128]{2,1,0:T(2,128)S(1)}, u32[]{:S(2)}, u32[]{:S(2)}) collective-permute-start(f32[1,2,128]{2,1,0:T(2,128)S(1)} %bitcast.16), channel_id=1, source_target_pairs={{0,8},{4,12},{8,0},{12,4},{1,9},{5,13},{9,1},{13,5},{2,10},{6,14},... | collective-permute-start | bytes 3080 | tf_op jit(solution)/shard_map/ppermute | solution.py:94
  23.9 4.4 %collective-permute-start.9 = (f32[128,768]{1,0:T(8,128)S(1)}, f32[128,768]{1,0:T(8,128)S(1)}, u32[]{:S(2)}, u32[]{:S(2)}) collective-permute-start(f32[128,768]{1,0:T(8,128)S(1)} %get-tuple-element.45), channel_id=1, source_target_pairs={{0,4},{4,0},{8,12},{12,8},{1,5},{5,1},{9,13},{13,9},{2,6},{6,2},{1... | collective-permute-start | bytes 1179656 | tf_op jit(solution)/shard_map/ppermute | solution.py:94
  23.9 4.4 %collective-permute-start.8 = (bf16[128,1152]{1,0:T(8,128)(2,1)S(1)}, bf16[128,1152]{1,0:T(8,128)(2,1)S(1)}, u32[]{:S(2)}, u32[]{:S(2)}) collective-permute-start(bf16[128,1152]{1,0:T(8,128)(2,1)S(1)} %get-tuple-element.43.held_ref), channel_id=1, source_target_pairs={{0,4},{4,0},{8,12},{12,8},{1,5},{5,1},{9,13},{13,9},{2,6},{6,2},{1... | collective-permute-start | bytes 884744 | tf_op jit(solution)/shard_map/ppermute | solution.py:94
  25.9 3.7 %collective-permute-start.14 = (f32[2,2,128]{2,1,0:T(2,128)S(1)}, f32[2,2,128]{2,1,0:T(2,128)S(1)}, u32[]{:S(2)}, u32[]{:S(2)}) collective-permute-start(f32[2,2,128]{2,1,0:T(2,128)S(1)} %pad_maximum_fusion.1), channel_id=1, source_target_pairs={{0,1},{1,0},{2,3},{3,2},{4,5},{5,4},{6,7},{7,6},{8,9},{9,8},{10,11... | collective-permute-start | bytes 6152 | tf_op jit(solution)/shard_map/ppermute | solution.py:94
  27.7 7.1 %copy-start.2 = (s32[16,8]{0,1:T(8,128)S(1)}, s32[16,8]{0,1:T(8,128)}, u32[]{:S(2)}) copy-start(s32[16,8]{0,1:T(8,128)} %param.7) | copy-start | bytes 1540
  27.7 5.1 %collective-permute-start.11 = (bf16[64,1152]{1,0:T(8,128)(2,1)S(1)}, bf16[64,1152]{1,0:T(8,128)(2,1)S(1)}, u32[]{:S(2)}, u32[]{:S(2)}) collective-permute-start(bf16[64,1152]{1,0:T(8,128)(2,1)S(1)} %get-tuple-element.53), channel_id=1, source_target_pairs={{0,4},{4,0},{8,12},{12,8},{1,5},{5,1},{9,13},{13,9},{2,6},{6,2},{1... | collective-permute-start | bytes 442376 | tf_op jit(solution)/shard_map/ppermute | solution.py:94
  27.8 5.0 %collective-permute-start.12 = (bf16[64,1152]{1,0:T(8,128)(2,1)S(1)}, bf16[64,1152]{1,0:T(8,128)(2,1)S(1)}, u32[]{:S(2)}, u32[]{:S(2)}) collective-permute-start(bf16[64,1152]{1,0:T(8,128)(2,1)S(1)} %get-tuple-element.52), channel_id=1, source_target_pairs={{0,4},{4,0},{8,12},{12,8},{1,5},{5,1},{9,13},{13,9},{2,6},{6,2},{1... | collective-permute-start | bytes 442376 | tf_op jit(solution)/shard_map/ppermute | solution.py:94
  29.7 5.1 %collective-permute-start.15 = (f32[4,2,128]{2,1,0:T(2,128)S(1)}, f32[4,2,128]{2,1,0:T(2,128)S(1)}, u32[]{:S(2)}, u32[]{:S(2)}) collective-permute-start(f32[4,2,128]{2,1,0:T(2,128)S(1)} %constant_dynamic-update-slice_fusion.4), channel_id=1, source_target_pairs={{0,2},{1,3},{2,0},{3,1},{4,6},{5,7},{6,4},{7,5},{8,10},{9,11},{10,... | collective-permute-start | bytes 12296 | tf_op jit(solution)/shard_map/ppermute | solution.py:94

commit v7 on v6

--- a/solution.py
+++ b/solution.py
@@ -412,7 +412,7 @@
     for bits in wide_bits:
         groups += [swap(group, "wide", bits) for group in groups]
     middle = len(groups) // 2
-    groups[middle] = after(groups[middle], *turned, *over)
+    groups[middle] = after(groups[middle], *turned)
     cuts = call(
         functools.partial(cut_kernel, features, columns, len(groups)),
         (shape((half_count, columns + LANES), bf16),) * (dp_count - 1),
@@ -437,7 +437,7 @@
     found = sums[None]
     back_order = [(0, 0)]
     for bits in wide_bits:
-        found = jnp.concatenate([found, swap(found, "wide", bits)], axis=0)
+        found = jnp.concatenate([after(found, *over), swap(found, "wide", bits)], axis=0)
         back_order += [(w ^ bits, n) for w, n in back_order]
     rest = swap(held, "wide", 1)
     rest_back = swap(other_back, "wide", 1)

time: 35.7 us -> 35.7 us (level)
  no operation moved by 1% of the time
where the time goes in v7:
time: 35.7 us; the launch traced here: 35.4 us
  starting transfers between devices  19.8 us (55%)
  Pallas kernels  9.89 us (28%)
  waiting for transfers between devices  4.9 us (14%)
  between operations  0.78 us (2%)
    ppermute x16, starting transfers between devices, swap(): return lax.ppermute(x, axis, [(i, i ^ bits) for i in range(count)])  19.8 us
    pallas_call x8, Pallas kernels, call(): pl.pallas_call(body, out_shape=outs, in_specs=[pl.BlockSpec(memory_space=...  9.89 us
    ppermute x16, waiting for transfers between devices, swap(): return lax.ppermute(x, axis, [(i, i ^ bits) for i in range(count)])  4.9 us
  transfers between devices with their start and end apart: 16, of which 6 were waited for; matrix products, arithmetic and copies ran while one was open for 0% of the time, Pallas kernels for 23%

profile of v7, /device:TPU:0, one launch (start us, length us, event | category | flops | bytes accessed | tf_op | source)
XLA Modules:
  0.0 35.4 jit_solution(910906973525989423)
XLA Ops:
  0.6 0.9 %shard_map.93 = (bf16[16,2176]{1,0:T(8,128)(2,1)S(1)}, f32[8,128]{1,0:T(8,128)S(1)}) custom-call(bf16[16,2048]{1,0:T(8,128)(2,1)} %grad_hbm.1, s32[8,16]{1,0:T(8,128)} %bitcast.14, bf16[8,16]{1,0:T(8,128)(2,1)} %bitcast.22), custom_call_target="tpu_custom_call" | custom-call | flops 32768 | bytes 131072 | tf_op jit(solution)/shard_map/pallas_call | solution.py:109
  1.5 0.5 %collective-permute-start.5 = (bf16[768,2048]{1,0:T(8,128)(2,1)}, bf16[768,2048]{1,0:T(8,128)(2,1)S(1)}, u32[]{:S(2)}, u32[]{:S(2)}) collective-permute-start(bf16[768,2048]{1,0:T(8,128)(2,1)} %bitcast.18), channel_id=1, source_target_pairs={{0,4},{4,0},{8,12},{12,8},{1,5},{5,1},{9,13},{13,9},{2,6},{6,2},{1... | collective-permute-start | bytes 9437192 | tf_op jit(solution)/shard_map/ppermute | solution.py:94
  2.1 3.7 %collective-permute-start.3 = (bf16[16,2176]{1,0:T(8,128)(2,1)S(1)}, bf16[16,2176]{1,0:T(8,128)(2,1)S(1)}, u32[]{:S(2)}, u32[]{:S(2)}) collective-permute-start(bf16[16,2176]{1,0:T(8,128)(2,1)S(1)} %get-tuple-element.32), channel_id=1, source_target_pairs={{0,2},{1,3},{2,0},{3,1},{4,6},{5,7},{6,4},{7,5},{8,10},{9,11},{10,... | collective-permute-start | bytes 208904 | tf_op jit(solution)/shard_map/ppermute | solution.py:94
  5.7 1.3 %collective-permute-start = (bf16[16,2176]{1,0:T(8,128)(2,1)S(1)}, bf16[16,2176]{1,0:T(8,128)(2,1)S(1)}, u32[]{:S(2)}, u32[]{:S(2)}) collective-permute-start(bf16[16,2176]{1,0:T(8,128)(2,1)S(1)} %get-tuple-element.32), channel_id=1, source_target_pairs={{0,3},{1,2},{2,1},{3,0},{4,7},{5,6},{6,5},{7,4},{8,11},{9,10},{10,... | collective-permute-start | bytes 208904 | tf_op jit(solution)/shard_map/ppermute | solution.py:94
  7.1 0.2 collective-permute-start.1
  7.3 1.3 %shard_map.94 = (bf16[256,768]{1,0:T(8,128)(2,1)S(1)}, bf16[128,768]{1,0:T(8,128)(2,1)S(1)}) custom-call(bf16[256,768]{1,0:T(8,128)(2,1)} %bitcast.10, bf16[256,768]{1,0:T(8,128)(2,1)} %bitcast.12, f32[8,128]{1,0:T(8,128)S(1)} %get-tuple-element.29.refs_2_), custom_call_target="tpu_custom_call" | custom-call | flops 3932160 | bytes 1179648 | tf_op jit(solution)/shard_map/pallas_call | solution.py:109
  8.6 1.6 %collective-permute-start.9 = (bf16[256,768]{1,0:T(8,128)(2,1)S(1)}, bf16[256,768]{1,0:T(8,128)(2,1)S(1)}, u32[]{:S(2)}, u32[]{:S(2)}) collective-permute-start(bf16[256,768]{1,0:T(8,128)(2,1)S(1)} %get-tuple-element.30.hidden_ref), channel_id=1, source_target_pairs={{0,16},{16,0},{1,17},{17,1},{2,18},{18,2},{3,19},{19,3},{4,20},{20... | collective-permute-start | bytes 1179656 | tf_op jit(solution)/shard_map/ppermute | solution.py:94
  10.2 0.1 collective-permute-done.3
  10.3 1.7 %collective-permute-start.4 = (bf16[32,2176]{1,0:T(8,128)(2,1)S(1)}, bf16[32,2176]{1,0:T(8,128)(2,1)S(1)}, u32[]{:S(2)}, u32[]{:S(2)}) collective-permute-start(bf16[32,2176]{1,0:T(8,128)(2,1)S(1)} %constant_dynamic-update-slice_fusion.refs_0_), channel_id=1, source_target_pairs={{0,8},{4,12},{8,0},{12,4},{1,9},{5,13},{9,1},{13,5},{2,10},{6,14},... | collective-permute-start | bytes 417800 | tf_op jit(solution)/shard_map/ppermute | solution.py:94
  12.0 0.6 %collective-permute-done = bf16[16,2176]{1,0:T(8,128)(2,1)S(1)} collective-permute-done((bf16[16,2176]{1,0:T(8,128)(2,1)S(1)}, bf16[16,2176]{1,0:T(8,128)(2,1)S(1)}, u32[]{:S(2)}, u32[]{:S(2)}) %collective-permute-start) | collective-permute-done | bytes 69664 | tf_op jit(solution)/shard_map/ppermute | solution.py:94
  12.5 0.3 collective-permute-done.1
  12.8 0.0 collective-permute-start.2
  12.9 1.7 %collective-permute-start.6 = (bf16[32,2176]{1,0:T(8,128)(2,1)S(1)}, bf16[32,2176]{1,0:T(8,128)(2,1)S(1)}, u32[]{:S(2)}, u32[]{:S(2)}) collective-permute-start(bf16[32,2176]{1,0:T(8,128)(2,1)S(1)} %constant_dynamic-update-slice_fusion.2.refs_1_), channel_id=1, source_target_pairs={{0,8},{4,12},{8,0},{12,4},{1,9},{5,13},{9,1},{13,5},{2,10},{6,14},... | collective-permute-start | bytes 417800 | tf_op jit(solution)/shard_map/ppermute | solution.py:94
  14.5 0.0 collective-permute-done.5.refs_1_
  14.5 2.6 %shard_map.95 = (bf16[512,768]{1,0:T(8,128)(2,1)S(1)}, bf16[512,768]{1,0:T(8,128)(2,1)S(1)}, bf16[512,768]{1,0:T(8,128)(2,1)S(1)}, bf16[512,768]{1,0:T(8,128)(2,...) custom-call(bf16[768,2048]{1,0:T(8,128)(2,1)} %bitcast.19, ...), custom_call_target="tpu_custom_call" | custom-call | bytes 12582912 | tf_op jit(solution)/shard_map/pallas_call | solution.py:109
  17.1 0.0 collective-permute-done.4.refs_2_
  17.1 1.9 %collective-permute-done.6.refs_3_ = bf16[32,2176]{1,0:T(8,128)(2,1)S(1)} collective-permute-done((bf16[32,2176]{1,0:T(8,128)(2,1)S(1)}, bf16[32,2176]{1,0:T(8,128)(2,1)S(1)}, u32[]{:S(2)}, u32[]{:S(2)}) %collective-permute-start.6) | collective-permute-done | bytes 139296 | tf_op jit(solution)/shard_map/ppermute | solution.py:94
  19.0 0.0 copy-start
  19.1 0.0 copy-start.1
  19.1 1.6 %collective-permute-start.10 = (bf16[128,1152]{1,0:T(8,128)(2,1)S(1)}, bf16[128,1152]{1,0:T(8,128)(2,1)S(1)}, u32[]{:S(2)}, u32[]{:S(2)}) collective-permute-start(bf16[128,1152]{1,0:T(8,128)(2,1)S(1)} %shard_map.98), channel_id=1, source_target_pairs={{0,16},{16,0},{1,17},{17,1},{2,18},{18,2},{3,19},{19,3},{4,20},{20... | collective-permute-start | bytes 884744 | tf_op jit(solution)/shard_map/ppermute | solution.py:94
  20.7 0.0 collective-permute-done.2.other_hidden_ref
  20.7 1.1 %shard_map.96 = (f32[128,768]{1,0:T(8,128)S(1)}, f32[128,768]{1,0:T(8,128)S(1)}, f32[2,128]{1,0:T(2,128)S(1)}, bf16[128,1152]{1,0:T(8,128)(2,1)S(1)}) custom-call(bf16[256,768]{1,0:T(8,128)(2,1)S(1)} %get-tuple-element.30.hidden_ref, bf16[128,768]{1,0:T(8,128)(2,1)S(1)} %collective-permute-done.2.other_hidden_ref, ...), custom_call_target="tpu_custom_call" | custom-call | flops 805306368 | bytes 6291456 | tf_op jit(solution)/shard_map/pallas_call | solution.py:109
  21.8 1.6 %collective-permute-start.13 = (f32[1,2,128]{2,1,0:T(2,128)S(1)}, f32[1,2,128]{2,1,0:T(2,128)S(1)}, u32[]{:S(2)}, u32[]{:S(2)}) collective-permute-start(f32[1,2,128]{2,1,0:T(2,128)S(1)} %bitcast.16), channel_id=1, source_target_pairs={{0,8},{4,12},{8,0},{12,4},{1,9},{5,13},{9,1},{13,5},{2,10},{6,14},... | collective-permute-start | bytes 3080 | tf_op jit(solution)/shard_map/ppermute | solution.py:94
  23.4 0.0 collective-permute-done.9.refs_0_
  23.4 0.0 collective-permute-start.8
  23.4 0.5 %collective-permute-start.7 = (bf16[128,1152]{1,0:T(8,128)(2,1)S(1)}, bf16[128,1152]{1,0:T(8,128)(2,1)S(1)}, u32[]{:S(2)}, u32[]{:S(2)}) collective-permute-start(bf16[128,1152]{1,0:T(8,128)(2,1)S(1)} %get-tuple-element.44.held_ref), channel_id=1, source_target_pairs={{0,4},{4,0},{8,12},{12,8},{1,5},{5,1},{9,13},{13,9},{2,6},{6,2},{1... | collective-permute-start | bytes 884744 | tf_op jit(solution)/shard_map/ppermute | solution.py:94
  23.9 1.5 %collective-permute-done.13 = f32[1,2,128]{2,1,0:T(2,128)S(1)} collective-permute-done((f32[1,2,128]{2,1,0:T(2,128)S(1)}, f32[1,2,128]{2,1,0:T(2,128)S(1)}, u32[]{:S(2)}, u32[]{:S(2)}) %collective-permute-start.13) | collective-permute-done | bytes 1056 | tf_op jit(solution)/shard_map/ppermute | solution.py:94
  25.4 1.8 %collective-permute-start.14 = (f32[2,2,128]{2,1,0:T(2,128)S(1)}, f32[2,2,128]{2,1,0:T(2,128)S(1)}, u32[]{:S(2)}, u32[]{:S(2)}) collective-permute-start(f32[2,2,128]{2,1,0:T(2,128)S(1)} %constant_dynamic-update-slice_fusion.4), channel_id=1, source_target_pairs={{0,1},{1,0},{2,3},{3,2},{4,5},{5,4},{6,7},{7,6},{8,9},{9,8},{10,11... | collective-permute-start | bytes 6152 | tf_op jit(solution)/shard_map/ppermute | solution.py:94
  27.3 0.5 %collective-permute-done.10.refs_1_ = bf16[128,1152]{1,0:T(8,128)(2,1)S(1)} collective-permute-done((bf16[128,1152]{1,0:T(8,128)(2,1)S(1)}, bf16[128,1152]{1,0:T(8,128)(2,1)S(1)}, u32[]{:S(2)}, u32[]{:S(2)}) %collective-permute-start.10) | collective-permute-done | bytes 294944 | tf_op jit(solution)/shard_map/ppermute | solution.py:94
  27.8 0.0 copy-start.2
  27.8 0.1 collective-permute-start.11
  27.9 0.5 %collective-permute-start.12 = (bf16[64,1152]{1,0:T(8,128)(2,1)S(1)}, bf16[64,1152]{1,0:T(8,128)(2,1)S(1)}, u32[]{:S(2)}, u32[]{:S(2)}) collective-permute-start(bf16[64,1152]{1,0:T(8,128)(2,1)S(1)} %get-tuple-element.54), channel_id=1, source_target_pairs={{0,4},{4,0},{8,12},{12,8},{1,5},{5,1},{9,13},{13,9},{2,6},{6,2},{1... | collective-permute-start | bytes 442376 | tf_op jit(solution)/shard_map/ppermute | solution.py:94
  28.4 0.0 collective-permute-done.7.rest_ref
  28.4 0.0 collective-permute-done.8.rest_back_ref
  28.4 0.0 copy-done
  28.4 0.0 copy-done.1
  28.4 1.4 %shard_map.97 = (bf16[256,768]{1,0:T(8,128)(2,1)}, bf16[256,768]{1,0:T(8,128)(2,1)}, bf16[256,768]{1,0:T(8,128)(2,1)S(1)}) custom-call(bf16[128,1152]{1,0:T(8,128)(2,1)S(1)} %get-tuple-element.44.held_ref, bf16[128,1152]{1,0:T(8,128)(2,1)S(1)} %collective-permute-done.7.rest_ref, f32[128,768]{1,0:T(8,128)S(1)} %get-tuple-element.45.back_ref, ...), custom_call_target="tpu_custom_call" | custom-call | flops 5898240 | bytes 2359296 | tf_op jit(solution)/shard_map/pallas_call | solution.py:109
  29.8 0.0 collective-permute-done.14
  29.8 3.0 %collective-permute-start.15 = (f32[4,2,128]{2,1,0:T(2,128)S(1)}, f32[4,2,128]{2,1,0:T(2,128)S(1)}, u32[]{:S(2)}, u32[]{:S(2)}) collective-permute-start(f32[4,2,128]{2,1,0:T(2,128)S(1)} %constant_dynamic-update-slice_fusion.6), channel_id=1, source_target_pairs={{0,2},{1,3},{2,0},{3,1},{4,6},{5,7},{6,4},{7,5},{8,10},{9,11},{10,... | collective-permute-start | bytes 12296 | tf_op jit(solution)/shard_map/ppermute | solution.py:94
  32.8 0.0 collective-permute-done.11.refs_2_
  32.8 0.0 collective-permute-done.12.refs_3_
  32.8 1.9 %shard_map.99 = bf16[768,1024]{1,0:T(8,128)(2,1)} custom-call(bf16[256,768]{1,0:T(8,128)(2,1)S(1)} %get-tuple-element.47.scaled_ref, bf16[128,1152]{1,0:T(8,128)(2,1)S(1)} %get-tuple-element.44.held_ref, bf16[128,1152]{1,0:T(8,128)(2,1)S(1)} %collective-permute-done.7.rest_ref, bf16[256,768]{1,0:T(8,128)(2,1)S(1)} %collective-permute-done.9.refs_0_, ...), custom_call_target="tpu_custom_call" | custom-call | flops 805306368 | bytes 3145728 | tf_op jit(solution)/shard_map/pallas_call | solution.py:109
  34.7 0.0 collective-permute-done.15
  34.8 0.0 copy-done.2
  34.8 0.7 %shard_map.100 = f32[8,16]{1,0:T(8,128)} custom-call(s32[8,16]{1,0:T(8,128)S(1)} %bitcast.15, f32[8,2,128]{2,1,0:T(2,128)S(1)} %pad_maximum_fusion.sums_ref), custom_call_target="tpu_custom_call" | custom-call | flops 256 | bytes 256 | tf_op jit(solution)/shard_map/pallas_call | solution.py:109
  (11 shorter events, 0.1 us)
Async XLA Ops:
  1.5 13.0 %collective-permute-start.5 = (bf16[768,2048]{1,0:T(8,128)(2,1)}, bf16[768,2048]{1,0:T(8,128)(2,1)S(1)}, u32[]{:S(2)}, u32[]{:S(2)}) collective-permute-start(bf16[768,2048]{1,0:T(8,128)(2,1)} %bitcast.18), channel_id=1, source_target_pairs={{0,4},{4,0},{8,12},{12,8},{1,5},{5,1},{9,13},{13,9},{2,6},{6,2},{1... | collective-permute-start | bytes 9437192 | tf_op jit(solution)/shard_map/ppermute | solution.py:94
  2.1 8.2 %collective-permute-start.3 = (bf16[16,2176]{1,0:T(8,128)(2,1)S(1)}, bf16[16,2176]{1,0:T(8,128)(2,1)S(1)}, u32[]{:S(2)}, u32[]{:S(2)}) collective-permute-start(bf16[16,2176]{1,0:T(8,128)(2,1)S(1)} %get-tuple-element.32), channel_id=1, source_target_pairs={{0,2},{1,3},{2,0},{3,1},{4,6},{5,7},{6,4},{7,5},{8,10},{9,11},{10,... | collective-permute-start | bytes 208904 | tf_op jit(solution)/shard_map/ppermute | solution.py:94
  5.7 6.8 %collective-permute-start = (bf16[16,2176]{1,0:T(8,128)(2,1)S(1)}, bf16[16,2176]{1,0:T(8,128)(2,1)S(1)}, u32[]{:S(2)}, u32[]{:S(2)}) collective-permute-start(bf16[16,2176]{1,0:T(8,128)(2,1)S(1)} %get-tuple-element.32), channel_id=1, source_target_pairs={{0,3},{1,2},{2,1},{3,0},{4,7},{5,6},{6,5},{7,4},{8,11},{9,10},{10,... | collective-permute-start | bytes 208904 | tf_op jit(solution)/shard_map/ppermute | solution.py:94
  7.1 5.8 %collective-permute-start.1 = (bf16[16,2176]{1,0:T(8,128)(2,1)S(1)}, bf16[16,2176]{1,0:T(8,128)(2,1)S(1)}, u32[]{:S(2)}, u32[]{:S(2)}) collective-permute-start(bf16[16,2176]{1,0:T(8,128)(2,1)S(1)} %get-tuple-element.32), channel_id=1, source_target_pairs={{0,1},{1,0},{2,3},{3,2},{4,5},{5,4},{6,7},{7,6},{8,9},{9,8},{10,11... | collective-permute-start | bytes 208904 | tf_op jit(solution)/shard_map/ppermute | solution.py:94
  8.6 14.8 %collective-permute-start.9 = (bf16[256,768]{1,0:T(8,128)(2,1)S(1)}, bf16[256,768]{1,0:T(8,128)(2,1)S(1)}, u32[]{:S(2)}, u32[]{:S(2)}) collective-permute-start(bf16[256,768]{1,0:T(8,128)(2,1)S(1)} %get-tuple-element.30.hidden_ref), channel_id=1, source_target_pairs={{0,16},{16,0},{1,17},{17,1},{2,18},{18,2},{3,19},{19,3},{4,20},{20... | collective-permute-start | bytes 1179656 | tf_op jit(solution)/shard_map/ppermute | solution.py:94
  10.3 6.9 %collective-permute-start.4 = (bf16[32,2176]{1,0:T(8,128)(2,1)S(1)}, bf16[32,2176]{1,0:T(8,128)(2,1)S(1)}, u32[]{:S(2)}, u32[]{:S(2)}) collective-permute-start(bf16[32,2176]{1,0:T(8,128)(2,1)S(1)} %constant_dynamic-update-slice_fusion.refs_0_), channel_id=1, source_target_pairs={{0,8},{4,12},{8,0},{12,4},{1,9},{5,13},{9,1},{13,5},{2,10},{6,14},... | collective-permute-start | bytes 417800 | tf_op jit(solution)/shard_map/ppermute | solution.py:94
  12.8 7.8 %collective-permute-start.2 = (bf16[128,768]{1,0:T(8,128)(2,1)S(1)}, bf16[128,768]{1,0:T(8,128)(2,1)S(1)}, u32[]{:S(2)}, u32[]{:S(2)}) collective-permute-start(bf16[128,768]{1,0:T(8,128)(2,1)S(1)} %get-tuple-element.33), channel_id=1, source_target_pairs={{0,4},{4,0},{8,12},{12,8},{1,5},{5,1},{9,13},{13,9},{2,6},{6,2},{1... | collective-permute-start | bytes 589832 | tf_op jit(solution)/shard_map/ppermute | solution.py:94
  12.9 6.1 %collective-permute-start.6 = (bf16[32,2176]{1,0:T(8,128)(2,1)S(1)}, bf16[32,2176]{1,0:T(8,128)(2,1)S(1)}, u32[]{:S(2)}, u32[]{:S(2)}) collective-permute-start(bf16[32,2176]{1,0:T(8,128)(2,1)S(1)} %constant_dynamic-update-slice_fusion.2.refs_1_), channel_id=1, source_target_pairs={{0,8},{4,12},{8,0},{12,4},{1,9},{5,13},{9,1},{13,5},{2,10},{6,14},... | collective-permute-start | bytes 417800 | tf_op jit(solution)/shard_map/ppermute | solution.py:94
  19.0 9.3 %copy-start = (bf16[1,1,256,768]{3,2,1,0:T(8,128)(2,1)S(1)}, bf16[1,1,256,768]{3,2,1,0:T(8,128)(2,1)}, u32[]{:S(2)}) copy-start(bf16[1,1,256,768]{3,2,1,0:T(8,128)(2,1)} %param.9) | copy-start | bytes 1179652
  19.1 9.3 %copy-start.1 = (bf16[1,1,256,768]{3,2,1,0:T(8,128)(2,1)S(1)}, bf16[1,1,256,768]{3,2,1,0:T(8,128)(2,1)}, u32[]{:S(2)}) copy-start(bf16[1,1,256,768]{3,2,1,0:T(8,128)(2,1)} %param.10) | copy-start | bytes 1179652
  19.1 8.7 %collective-permute-start.10 = (bf16[128,1152]{1,0:T(8,128)(2,1)S(1)}, bf16[128,1152]{1,0:T(8,128)(2,1)S(1)}, u32[]{:S(2)}, u32[]{:S(2)}) collective-permute-start(bf16[128,1152]{1,0:T(8,128)(2,1)S(1)} %shard_map.98), channel_id=1, source_target_pairs={{0,16},{16,0},{1,17},{17,1},{2,18},{18,2},{3,19},{19,3},{4,20},{20... | collective-permute-start | bytes 884744 | tf_op jit(solution)/shard_map/ppermute | solution.py:94
  21.8 3.6 %collective-permute-start.13 = (f32[1,2,128]{2,1,0:T(2,128)S(1)}, f32[1,2,128]{2,1,0:T(2,128)S(1)}, u32[]{:S(2)}, u32[]{:S(2)}) collective-permute-start(f32[1,2,128]{2,1,0:T(2,128)S(1)} %bitcast.16), channel_id=1, source_target_pairs={{0,8},{4,12},{8,0},{12,4},{1,9},{5,13},{9,1},{13,5},{2,10},{6,14},... | collective-permute-start | bytes 3080 | tf_op jit(solution)/shard_map/ppermute | solution.py:94
  23.4 5.0 %collective-permute-start.8 = (f32[128,768]{1,0:T(8,128)S(1)}, f32[128,768]{1,0:T(8,128)S(1)}, u32[]{:S(2)}, u32[]{:S(2)}) collective-permute-start(f32[128,768]{1,0:T(8,128)S(1)} %get-tuple-element.46), channel_id=1, source_target_pairs={{0,4},{4,0},{8,12},{12,8},{1,5},{5,1},{9,13},{13,9},{2,6},{6,2},{1... | collective-permute-start | bytes 1179656 | tf_op jit(solution)/shard_map/ppermute | solution.py:94
  23.4 5.0 %collective-permute-start.7 = (bf16[128,1152]{1,0:T(8,128)(2,1)S(1)}, bf16[128,1152]{1,0:T(8,128)(2,1)S(1)}, u32[]{:S(2)}, u32[]{:S(2)}) collective-permute-start(bf16[128,1152]{1,0:T(8,128)(2,1)S(1)} %get-tuple-element.44.held_ref), channel_id=1, source_target_pairs={{0,4},{4,0},{8,12},{12,8},{1,5},{5,1},{9,13},{13,9},{2,6},{6,2},{1... | collective-permute-start | bytes 884744 | tf_op jit(solution)/shard_map/ppermute | solution.py:94
  25.4 4.3 %collective-permute-start.14 = (f32[2,2,128]{2,1,0:T(2,128)S(1)}, f32[2,2,128]{2,1,0:T(2,128)S(1)}, u32[]{:S(2)}, u32[]{:S(2)}) collective-permute-start(f32[2,2,128]{2,1,0:T(2,128)S(1)} %constant_dynamic-update-slice_fusion.4), channel_id=1, source_target_pairs={{0,1},{1,0},{2,3},{3,2},{4,5},{5,4},{6,7},{7,6},{8,9},{9,8},{10,11... | collective-permute-start | bytes 6152 | tf_op jit(solution)/shard_map/ppermute | solution.py:94
  27.8 7.0 %copy-start.2 = (s32[16,8]{0,1:T(8,128)S(1)}, s32[16,8]{0,1:T(8,128)}, u32[]{:S(2)}) copy-start(s32[16,8]{0,1:T(8,128)} %param.7) | copy-start | bytes 1540
  27.8 5.0 %collective-permute-start.11 = (bf16[64,1152]{1,0:T(8,128)(2,1)S(1)}, bf16[64,1152]{1,0:T(8,128)(2,1)S(1)}, u32[]{:S(2)}, u32[]{:S(2)}) collective-permute-start(bf16[64,1152]{1,0:T(8,128)(2,1)S(1)} %get-tuple-element.55), channel_id=1, source_target_pairs={{0,4},{4,0},{8,12},{12,8},{1,5},{5,1},{9,13},{13,9},{2,6},{6,2},{1... | collective-permute-start | bytes 442376 | tf_op jit(solution)/shard_map/ppermute | solution.py:94
  27.9 4.9 %collective-permute-start.12 = (bf16[64,1152]{1,0:T(8,128)(2,1)S(1)}, bf16[64,1152]{1,0:T(8,128)(2,1)S(1)}, u32[]{:S(2)}, u32[]{:S(2)}) collective-permute-start(bf16[64,1152]{1,0:T(8,128)(2,1)S(1)} %get-tuple-element.54), channel_id=1, source_target_pairs={{0,4},{4,0},{8,12},{12,8},{1,5},{5,1},{9,13},{13,9},{2,6},{6,2},{1... | collective-permute-start | bytes 442376 | tf_op jit(solution)/shard_map/ppermute | solution.py:94
  29.8 4.9 %collective-permute-start.15 = (f32[4,2,128]{2,1,0:T(2,128)S(1)}, f32[4,2,128]{2,1,0:T(2,128)S(1)}, u32[]{:S(2)}, u32[]{:S(2)}) collective-permute-start(f32[4,2,128]{2,1,0:T(2,128)S(1)} %constant_dynamic-update-slice_fusion.6), channel_id=1, source_target_pairs={{0,2},{1,3},{2,0},{3,1},{4,6},{5,7},{6,4},{7,5},{8,10},{9,11},{10,... | collective-permute-start | bytes 12296 | tf_op jit(solution)/shard_map/ppermute | solution.py:94

commit v8 on v7

--- a/solution.py
+++ b/solution.py
@@ -255,6 +255,17 @@
     )
 
 
+def slopes_kernel(order, rows, pre_gate_ref, pre_up_ref, gate_slope_ref, up_slope_ref):
+    for place, xors in enumerate(order):
+        here = slice(place * rows, (place + 1) * rows)
+        source = pl.ds(pl.multiple_of(peer(xors) * rows, rows), rows)
+        value = pre_gate_ref[source, :].astype(jnp.float32)
+        up = pre_up_ref[source, :].astype(jnp.float32)
+        sig = jax.nn.sigmoid(value)
+        gate_slope_ref[here, :] = up * sig * (1.0 + value * (1.0 - sig))
+        up_slope_ref[here, :] = value * sig
+
+
 def grads_kernel(
     order,
     rows,
@@ -264,8 +275,8 @@
     back_ref,
     rest_back_ref,
     hidden_ref,
-    pre_gate_ref,
-    pre_up_ref,
+    gate_slope_ref,
+    up_slope_ref,
     grad_gate_ref,
     grad_up_ref,
     scaled_ref,
@@ -277,14 +288,9 @@
         gate = own_gates(tokens_ref[there, columns:])
         here = slice(place * rows, (place + 1) * rows)
         source = pl.ds(pl.multiple_of(peer(xors) * rows, rows), rows)
-        value = pre_gate_ref[source, :].astype(jnp.float32)
-        up = pre_up_ref[source, :].astype(jnp.float32)
-        sig = jax.nn.sigmoid(value)
         carried = gate * products_ref[there, :]
-        grad_gate_ref[source, :] = (carried * up * sig * (1.0 + value * (1.0 - sig))).astype(
-            grad_gate_ref.dtype
-        )
-        grad_up_ref[source, :] = (carried * value * sig).astype(grad_up_ref.dtype)
+        grad_gate_ref[source, :] = (carried * gate_slope_ref[here, :]).astype(grad_gate_ref.dtype)
+        grad_up_ref[source, :] = (carried * up_slope_ref[here, :]).astype(grad_up_ref.dtype)
         scaled_ref[here, :] = (gate * hidden_ref[here, :].astype(jnp.float32)).astype(
             scaled_ref.dtype
         )
@@ -434,10 +440,18 @@
         *groups,
         *turned,
     )
+    slopes = call(
+        functools.partial(slopes_kernel, order, rows),
+        (shape((slot_count, units), f32),) * 2,
+        (20 * slot_count * units, 12 * slot_count * units),
+        pre_gate,
+        pre_up,
+        deps=(sums,),
+    )
     found = sums[None]
     back_order = [(0, 0)]
     for bits in wide_bits:
-        found = jnp.concatenate([after(found, *over), swap(found, "wide", bits)], axis=0)
+        found = jnp.concatenate([after(found, *over, *slopes), swap(found, "wide", bits)], axis=0)
         back_order += [(w ^ bits, n) for w, n in back_order]
     rest = swap(held, "wide", 1)
     rest_back = swap(other_back, "wide", 1)
@@ -450,8 +464,7 @@
         back,
         rest_back,
         hidden,
-        pre_gate,
-        pre_up,
+        *slopes,
     )
     steps = [1 << b for b in range(narrow_count.bit_length() - 1)]
     for bits in steps[:-1]:

time: 35.7 us -> 35.4 us (level)
    pallas_call x8 -> x9, Pallas kernels: 9.89 us -> 9.92 us  [call(): pl.pallas_call(body, out_shape=outs, in_specs=[pl.BlockSpec(memory_space=...]
  transfers between devices with their start and end apart: 16 -> 16, of which waited for: 6 -> 6; matrix products, arithmetic and copies ran while one was open for 0% -> 0% of each run, Pallas kernels for 23% -> 24%
where the time goes in v8:
time: 35.4 us; the launch traced here: 35.2 us
  starting transfers between devices  19.8 us (56%)
  Pallas kernels  9.92 us (28%)
  waiting for transfers between devices  4.55 us (13%)
  between operations  0.79 us (2%)
    ppermute x16, starting transfers between devices, swap(): return lax.ppermute(x, axis, [(i, i ^ bits) for i in range(count)])  19.8 us
    pallas_call x9, Pallas kernels, call(): pl.pallas_call(body, out_shape=outs, in_specs=[pl.BlockSpec(memory_space=...  9.92 us
    ppermute x16, waiting for transfers between devices, swap(): return lax.ppermute(x, axis, [(i, i ^ bits) for i in range(count)])  4.55 us
  transfers between devices with their start and end apart: 16, of which 6 were waited for; matrix products, arithmetic and copies ran while one was open for 0% of the time, Pallas kernels for 24%

profile of v8, /device:TPU:0, one launch (start us, length us, event | category | flops | bytes accessed | tf_op | source)
XLA Modules:
  0.0 35.2 jit_solution(8776648479622722246)
XLA Ops:
  0.6 0.9 %shard_map.93 = (bf16[16,2176]{1,0:T(8,128)(2,1)S(1)}, f32[8,128]{1,0:T(8,128)S(1)}) custom-call(bf16[16,2048]{1,0:T(8,128)(2,1)} %grad_hbm.1, s32[8,16]{1,0:T(8,128)} %bitcast.14, bf16[8,16]{1,0:T(8,128)(2,1)} %bitcast.22), custom_call_target="tpu_custom_call" | custom-call | flops 32768 | bytes 131072 | tf_op jit(solution)/shard_map/pallas_call | solution.py:109
  1.5 0.5 %collective-permute-start.5 = (bf16[768,2048]{1,0:T(8,128)(2,1)}, bf16[768,2048]{1,0:T(8,128)(2,1)S(1)}, u32[]{:S(2)}, u32[]{:S(2)}) collective-permute-start(bf16[768,2048]{1,0:T(8,128)(2,1)} %bitcast.18), channel_id=1, source_target_pairs={{0,4},{4,0},{8,12},{12,8},{1,5},{5,1},{9,13},{13,9},{2,6},{6,2},{1... | collective-permute-start | bytes 9437192 | tf_op jit(solution)/shard_map/ppermute | solution.py:94
  2.1 3.7 %collective-permute-start.3 = (bf16[16,2176]{1,0:T(8,128)(2,1)S(1)}, bf16[16,2176]{1,0:T(8,128)(2,1)S(1)}, u32[]{:S(2)}, u32[]{:S(2)}) collective-permute-start(bf16[16,2176]{1,0:T(8,128)(2,1)S(1)} %get-tuple-element.34), channel_id=1, source_target_pairs={{0,2},{1,3},{2,0},{3,1},{4,6},{5,7},{6,4},{7,5},{8,10},{9,11},{10,... | collective-permute-start | bytes 208904 | tf_op jit(solution)/shard_map/ppermute | solution.py:94
  5.7 1.3 %collective-permute-start = (bf16[16,2176]{1,0:T(8,128)(2,1)S(1)}, bf16[16,2176]{1,0:T(8,128)(2,1)S(1)}, u32[]{:S(2)}, u32[]{:S(2)}) collective-permute-start(bf16[16,2176]{1,0:T(8,128)(2,1)S(1)} %get-tuple-element.34), channel_id=1, source_target_pairs={{0,3},{1,2},{2,1},{3,0},{4,7},{5,6},{6,5},{7,4},{8,11},{9,10},{10,... | collective-permute-start | bytes 208904 | tf_op jit(solution)/shard_map/ppermute | solution.py:94
  7.1 0.2 collective-permute-start.1
  7.3 1.3 %shard_map.94 = (bf16[256,768]{1,0:T(8,128)(2,1)S(1)}, bf16[128,768]{1,0:T(8,128)(2,1)S(1)}) custom-call(bf16[256,768]{1,0:T(8,128)(2,1)} %bitcast.10, bf16[256,768]{1,0:T(8,128)(2,1)} %bitcast.12, f32[8,128]{1,0:T(8,128)S(1)} %get-tuple-element.31.refs_2_), custom_call_target="tpu_custom_call" | custom-call | flops 3932160 | bytes 1179648 | tf_op jit(solution)/shard_map/pallas_call | solution.py:109
  8.6 1.6 %collective-permute-start.9 = (bf16[256,768]{1,0:T(8,128)(2,1)S(1)}, bf16[256,768]{1,0:T(8,128)(2,1)S(1)}, u32[]{:S(2)}, u32[]{:S(2)}) collective-permute-start(bf16[256,768]{1,0:T(8,128)(2,1)S(1)} %get-tuple-element.32.hidden_ref), channel_id=1, source_target_pairs={{0,16},{16,0},{1,17},{17,1},{2,18},{18,2},{3,19},{19,3},{4,20},{20... | collective-permute-start | bytes 1179656 | tf_op jit(solution)/shard_map/ppermute | solution.py:94
  10.2 0.1 collective-permute-done.3
  10.3 1.7 %collective-permute-start.4 = (bf16[32,2176]{1,0:T(8,128)(2,1)S(1)}, bf16[32,2176]{1,0:T(8,128)(2,1)S(1)}, u32[]{:S(2)}, u32[]{:S(2)}) collective-permute-start(bf16[32,2176]{1,0:T(8,128)(2,1)S(1)} %constant_dynamic-update-slice_fusion.refs_0_), channel_id=1, source_target_pairs={{0,8},{4,12},{8,0},{12,4},{1,9},{5,13},{9,1},{13,5},{2,10},{6,14},... | collective-permute-start | bytes 417800 | tf_op jit(solution)/shard_map/ppermute | solution.py:94
  12.0 0.6 %collective-permute-done = bf16[16,2176]{1,0:T(8,128)(2,1)S(1)} collective-permute-done((bf16[16,2176]{1,0:T(8,128)(2,1)S(1)}, bf16[16,2176]{1,0:T(8,128)(2,1)S(1)}, u32[]{:S(2)}, u32[]{:S(2)}) %collective-permute-start) | collective-permute-done | bytes 69664 | tf_op jit(solution)/shard_map/ppermute | solution.py:94
  12.5 0.3 collective-permute-done.1
  12.8 0.0 collective-permute-start.2
  12.9 1.7 %collective-permute-start.6 = (bf16[32,2176]{1,0:T(8,128)(2,1)S(1)}, bf16[32,2176]{1,0:T(8,128)(2,1)S(1)}, u32[]{:S(2)}, u32[]{:S(2)}) collective-permute-start(bf16[32,2176]{1,0:T(8,128)(2,1)S(1)} %constant_dynamic-update-slice_fusion.2.refs_1_), channel_id=1, source_target_pairs={{0,8},{4,12},{8,0},{12,4},{1,9},{5,13},{9,1},{13,5},{2,10},{6,14},... | collective-permute-start | bytes 417800 | tf_op jit(solution)/shard_map/ppermute | solution.py:94
  14.5 0.0 collective-permute-done.5.refs_1_
  14.5 2.6 %shard_map.95 = (bf16[512,768]{1,0:T(8,128)(2,1)S(1)}, bf16[512,768]{1,0:T(8,128)(2,1)S(1)}, bf16[512,768]{1,0:T(8,128)(2,1)S(1)}, bf16[512,768]{1,0:T(8,128)(2,...) custom-call(bf16[768,2048]{1,0:T(8,128)(2,1)} %bitcast.19, ...), custom_call_target="tpu_custom_call" | custom-call | bytes 12582912 | tf_op jit(solution)/shard_map/pallas_call | solution.py:109
  17.1 0.0 collective-permute-done.4.refs_2_
  17.1 1.9 %collective-permute-done.6.refs_3_ = bf16[32,2176]{1,0:T(8,128)(2,1)S(1)} collective-permute-done((bf16[32,2176]{1,0:T(8,128)(2,1)S(1)}, bf16[32,2176]{1,0:T(8,128)(2,1)S(1)}, u32[]{:S(2)}, u32[]{:S(2)}) %collective-permute-start.6) | collective-permute-done | bytes 139296 | tf_op jit(solution)/shard_map/ppermute | solution.py:94
  19.0 0.0 copy-start
  19.1 0.0 copy-start.1
  19.1 1.6 %collective-permute-start.10 = (bf16[128,1152]{1,0:T(8,128)(2,1)S(1)}, bf16[128,1152]{1,0:T(8,128)(2,1)S(1)}, u32[]{:S(2)}, u32[]{:S(2)}) collective-permute-start(bf16[128,1152]{1,0:T(8,128)(2,1)S(1)} %shard_map.99), channel_id=1, source_target_pairs={{0,16},{16,0},{1,17},{17,1},{2,18},{18,2},{3,19},{19,3},{4,20},{20... | collective-permute-start | bytes 884744 | tf_op jit(solution)/shard_map/ppermute | solution.py:94
  20.7 0.0 collective-permute-done.2.other_hidden_ref
  20.7 1.1 %shard_map.96 = (f32[128,768]{1,0:T(8,128)S(1)}, f32[128,768]{1,0:T(8,128)S(1)}, f32[2,128]{1,0:T(2,128)S(1)}, bf16[128,1152]{1,0:T(8,128)(2,1)S(1)}) custom-call(bf16[256,768]{1,0:T(8,128)(2,1)S(1)} %get-tuple-element.32.hidden_ref, bf16[128,768]{1,0:T(8,128)(2,1)S(1)} %collective-permute-done.2.other_hidden_ref, ...), custom_call_target="tpu_custom_call" | custom-call | flops 805306368 | bytes 6291456 | tf_op jit(solution)/shard_map/pallas_call | solution.py:109
  21.8 1.6 %collective-permute-start.13 = (f32[1,2,128]{2,1,0:T(2,128)S(1)}, f32[1,2,128]{2,1,0:T(2,128)S(1)}, u32[]{:S(2)}, u32[]{:S(2)}) collective-permute-start(f32[1,2,128]{2,1,0:T(2,128)S(1)} %bitcast.16), channel_id=1, source_target_pairs={{0,8},{4,12},{8,0},{12,4},{1,9},{5,13},{9,1},{13,5},{2,10},{6,14},... | collective-permute-start | bytes 3080 | tf_op jit(solution)/shard_map/ppermute | solution.py:94
  23.4 0.0 copy-done
  23.4 0.0 copy-done.1
  23.4 0.3 shard_map.97
  23.6 0.0 collective-permute-done.9.refs_0_
  23.7 0.1 collective-permute-start.8
  23.7 0.5 %collective-permute-start.7 = (bf16[128,1152]{1,0:T(8,128)(2,1)S(1)}, bf16[128,1152]{1,0:T(8,128)(2,1)S(1)}, u32[]{:S(2)}, u32[]{:S(2)}) collective-permute-start(bf16[128,1152]{1,0:T(8,128)(2,1)S(1)} %get-tuple-element.46.held_ref), channel_id=1, source_target_pairs={{0,4},{4,0},{8,12},{12,8},{1,5},{5,1},{9,13},{13,9},{2,6},{6,2},{1... | collective-permute-start | bytes 884744 | tf_op jit(solution)/shard_map/ppermute | solution.py:94
  24.2 1.2 %collective-permute-done.13 = f32[1,2,128]{2,1,0:T(2,128)S(1)} collective-permute-done((f32[1,2,128]{2,1,0:T(2,128)S(1)}, f32[1,2,128]{2,1,0:T(2,128)S(1)}, u32[]{:S(2)}, u32[]{:S(2)}) %collective-permute-start.13) | collective-permute-done | bytes 1056 | tf_op jit(solution)/shard_map/ppermute | solution.py:94
  25.4 1.8 %collective-permute-start.14 = (f32[2,2,128]{2,1,0:T(2,128)S(1)}, f32[2,2,128]{2,1,0:T(2,128)S(1)}, u32[]{:S(2)}, u32[]{:S(2)}) collective-permute-start(f32[2,2,128]{2,1,0:T(2,128)S(1)} %constant_dynamic-update-slice_fusion.4), channel_id=1, source_target_pairs={{0,1},{1,0},{2,3},{3,2},{4,5},{5,4},{6,7},{7,6},{8,9},{9,8},{10,11... | collective-permute-start | bytes 6152 | tf_op jit(solution)/shard_map/ppermute | solution.py:94
  27.2 0.5 %collective-permute-done.10.refs_1_ = bf16[128,1152]{1,0:T(8,128)(2,1)S(1)} collective-permute-done((bf16[128,1152]{1,0:T(8,128)(2,1)S(1)}, bf16[128,1152]{1,0:T(8,128)(2,1)S(1)}, u32[]{:S(2)}, u32[]{:S(2)}) %collective-permute-start.10) | collective-permute-done | bytes 294944 | tf_op jit(solution)/shard_map/ppermute | solution.py:94
  27.8 0.1 collective-permute-start.11
  27.9 0.5 %collective-permute-start.12 = (bf16[64,1152]{1,0:T(8,128)(2,1)S(1)}, bf16[64,1152]{1,0:T(8,128)(2,1)S(1)}, u32[]{:S(2)}, u32[]{:S(2)}) collective-permute-start(bf16[64,1152]{1,0:T(8,128)(2,1)S(1)} %get-tuple-element.58), channel_id=1, source_target_pairs={{0,4},{4,0},{8,12},{12,8},{1,5},{5,1},{9,13},{13,9},{2,6},{6,2},{1... | collective-permute-start | bytes 442376 | tf_op jit(solution)/shard_map/ppermute | solution.py:94
  28.4 0.0 collective-permute-done.7.rest_ref
  28.4 0.0 collective-permute-done.8.rest_back_ref
  28.4 0.0 copy-start.2
  28.4 1.1 %shard_map.98 = (bf16[256,768]{1,0:T(8,128)(2,1)}, bf16[256,768]{1,0:T(8,128)(2,1)}, bf16[256,768]{1,0:T(8,128)(2,1)S(1)}) custom-call(bf16[128,1152]{1,0:T(8,128)(2,1)S(1)} %get-tuple-element.46.held_ref, bf16[128,1152]{1,0:T(8,128)(2,1)S(1)} %collective-permute-done.7.rest_ref, f32[128,768]{1,0:T(8,128)S(1)} %get-tuple-element.47.back_ref, ...), custom_call_target="tpu_custom_call" | custom-call | flops 5898240 | bytes 2359296 | tf_op jit(solution)/shard_map/pallas_call | solution.py:109
  29.5 0.0 collective-permute-done.14
  29.5 3.0 %collective-permute-start.15 = (f32[4,2,128]{2,1,0:T(2,128)S(1)}, f32[4,2,128]{2,1,0:T(2,128)S(1)}, u32[]{:S(2)}, u32[]{:S(2)}) collective-permute-start(f32[4,2,128]{2,1,0:T(2,128)S(1)} %constant_dynamic-update-slice_fusion.6), channel_id=1, source_target_pairs={{0,2},{1,3},{2,0},{3,1},{4,6},{5,7},{6,4},{7,5},{8,10},{9,11},{10,... | collective-permute-start | bytes 12296 | tf_op jit(solution)/shard_map/ppermute | solution.py:94
  32.5 0.0 collective-permute-done.11.refs_2_
  32.5 0.0 collective-permute-done.12.refs_3_
  32.5 1.9 %shard_map.100 = bf16[768,1024]{1,0:T(8,128)(2,1)} custom-call(bf16[256,768]{1,0:T(8,128)(2,1)S(1)} %get-tuple-element.52.scaled_ref, bf16[128,1152]{1,0:T(8,128)(2,1)S(1)} %get-tuple-element.46.held_ref, bf16[128,1152]{1,0:T(8,128)(2,1)S(1)} %collective-permute-done.7.rest_ref, bf16[256,768]{1,0:T(8,128)(2,1)S(1)} %collective-permute-done.9.refs_0_, ...), custom_call_target="tpu_custom_call" | custom-call | flops 805306368 | bytes 3145728 | tf_op jit(solution)/shard_map/pallas_call | solution.py:109
  34.5 0.0 collective-permute-done.15
  34.5 0.0 copy-done.2
  34.5 0.7 %shard_map.101 = f32[8,16]{1,0:T(8,128)} custom-call(s32[8,16]{1,0:T(8,128)S(1)} %bitcast.15, f32[8,2,128]{2,1,0:T(2,128)S(1)} %pad_maximum_fusion.sums_ref), custom_call_target="tpu_custom_call" | custom-call | flops 256 | bytes 256 | tf_op jit(solution)/shard_map/pallas_call | solution.py:109
  (11 shorter events, 0.1 us)
Async XLA Ops:
  1.5 13.0 %collective-permute-start.5 = (bf16[768,2048]{1,0:T(8,128)(2,1)}, bf16[768,2048]{1,0:T(8,128)(2,1)S(1)}, u32[]{:S(2)}, u32[]{:S(2)}) collective-permute-start(bf16[768,2048]{1,0:T(8,128)(2,1)} %bitcast.18), channel_id=1, source_target_pairs={{0,4},{4,0},{8,12},{12,8},{1,5},{5,1},{9,13},{13,9},{2,6},{6,2},{1... | collective-permute-start | bytes 9437192 | tf_op jit(solution)/shard_map/ppermute | solution.py:94
  2.1 8.2 %collective-permute-start.3 = (bf16[16,2176]{1,0:T(8,128)(2,1)S(1)}, bf16[16,2176]{1,0:T(8,128)(2,1)S(1)}, u32[]{:S(2)}, u32[]{:S(2)}) collective-permute-start(bf16[16,2176]{1,0:T(8,128)(2,1)S(1)} %get-tuple-element.34), channel_id=1, source_target_pairs={{0,2},{1,3},{2,0},{3,1},{4,6},{5,7},{6,4},{7,5},{8,10},{9,11},{10,... | collective-permute-start | bytes 208904 | tf_op jit(solution)/shard_map/ppermute | solution.py:94
  5.7 6.8 %collective-permute-start = (bf16[16,2176]{1,0:T(8,128)(2,1)S(1)}, bf16[16,2176]{1,0:T(8,128)(2,1)S(1)}, u32[]{:S(2)}, u32[]{:S(2)}) collective-permute-start(bf16[16,2176]{1,0:T(8,128)(2,1)S(1)} %get-tuple-element.34), channel_id=1, source_target_pairs={{0,3},{1,2},{2,1},{3,0},{4,7},{5,6},{6,5},{7,4},{8,11},{9,10},{10,... | collective-permute-start | bytes 208904 | tf_op jit(solution)/shard_map/ppermute | solution.py:94
  7.1 5.8 %collective-permute-start.1 = (bf16[16,2176]{1,0:T(8,128)(2,1)S(1)}, bf16[16,2176]{1,0:T(8,128)(2,1)S(1)}, u32[]{:S(2)}, u32[]{:S(2)}) collective-permute-start(bf16[16,2176]{1,0:T(8,128)(2,1)S(1)} %get-tuple-element.34), channel_id=1, source_target_pairs={{0,1},{1,0},{2,3},{3,2},{4,5},{5,4},{6,7},{7,6},{8,9},{9,8},{10,11... | collective-permute-start | bytes 208904 | tf_op jit(solution)/shard_map/ppermute | solution.py:94
  8.6 15.0 %collective-permute-start.9 = (bf16[256,768]{1,0:T(8,128)(2,1)S(1)}, bf16[256,768]{1,0:T(8,128)(2,1)S(1)}, u32[]{:S(2)}, u32[]{:S(2)}) collective-permute-start(bf16[256,768]{1,0:T(8,128)(2,1)S(1)} %get-tuple-element.32.hidden_ref), channel_id=1, source_target_pairs={{0,16},{16,0},{1,17},{17,1},{2,18},{18,2},{3,19},{19,3},{4,20},{20... | collective-permute-start | bytes 1179656 | tf_op jit(solution)/shard_map/ppermute | solution.py:94
  10.3 6.9 %collective-permute-start.4 = (bf16[32,2176]{1,0:T(8,128)(2,1)S(1)}, bf16[32,2176]{1,0:T(8,128)(2,1)S(1)}, u32[]{:S(2)}, u32[]{:S(2)}) collective-permute-start(bf16[32,2176]{1,0:T(8,128)(2,1)S(1)} %constant_dynamic-update-slice_fusion.refs_0_), channel_id=1, source_target_pairs={{0,8},{4,12},{8,0},{12,4},{1,9},{5,13},{9,1},{13,5},{2,10},{6,14},... | collective-permute-start | bytes 417800 | tf_op jit(solution)/shard_map/ppermute | solution.py:94
  12.8 7.8 %collective-permute-start.2 = (bf16[128,768]{1,0:T(8,128)(2,1)S(1)}, bf16[128,768]{1,0:T(8,128)(2,1)S(1)}, u32[]{:S(2)}, u32[]{:S(2)}) collective-permute-start(bf16[128,768]{1,0:T(8,128)(2,1)S(1)} %get-tuple-element.35), channel_id=1, source_target_pairs={{0,4},{4,0},{8,12},{12,8},{1,5},{5,1},{9,13},{13,9},{2,6},{6,2},{1... | collective-permute-start | bytes 589832 | tf_op jit(solution)/shard_map/ppermute | solution.py:94
  12.9 6.1 %collective-permute-start.6 = (bf16[32,2176]{1,0:T(8,128)(2,1)S(1)}, bf16[32,2176]{1,0:T(8,128)(2,1)S(1)}, u32[]{:S(2)}, u32[]{:S(2)}) collective-permute-start(bf16[32,2176]{1,0:T(8,128)(2,1)S(1)} %constant_dynamic-update-slice_fusion.2.refs_1_), channel_id=1, source_target_pairs={{0,8},{4,12},{8,0},{12,4},{1,9},{5,13},{9,1},{13,5},{2,10},{6,14},... | collective-permute-start | bytes 417800 | tf_op jit(solution)/shard_map/ppermute | solution.py:94
  19.0 4.3 %copy-start = (bf16[1,1,256,768]{3,2,1,0:T(8,128)(2,1)S(1)}, bf16[1,1,256,768]{3,2,1,0:T(8,128)(2,1)}, u32[]{:S(2)}) copy-start(bf16[1,1,256,768]{3,2,1,0:T(8,128)(2,1)} %param.9) | copy-start | bytes 1179652
  19.1 4.3 %copy-start.1 = (bf16[1,1,256,768]{3,2,1,0:T(8,128)(2,1)S(1)}, bf16[1,1,256,768]{3,2,1,0:T(8,128)(2,1)}, u32[]{:S(2)}) copy-start(bf16[1,1,256,768]{3,2,1,0:T(8,128)(2,1)} %param.10) | copy-start | bytes 1179652
  19.1 8.7 %collective-permute-start.10 = (bf16[128,1152]{1,0:T(8,128)(2,1)S(1)}, bf16[128,1152]{1,0:T(8,128)(2,1)S(1)}, u32[]{:S(2)}, u32[]{:S(2)}) collective-permute-start(bf16[128,1152]{1,0:T(8,128)(2,1)S(1)} %shard_map.99), channel_id=1, source_target_pairs={{0,16},{16,0},{1,17},{17,1},{2,18},{18,2},{3,19},{19,3},{4,20},{20... | collective-permute-start | bytes 884744 | tf_op jit(solution)/shard_map/ppermute | solution.py:94
  21.8 3.6 %collective-permute-start.13 = (f32[1,2,128]{2,1,0:T(2,128)S(1)}, f32[1,2,128]{2,1,0:T(2,128)S(1)}, u32[]{:S(2)}, u32[]{:S(2)}) collective-permute-start(f32[1,2,128]{2,1,0:T(2,128)S(1)} %bitcast.16), channel_id=1, source_target_pairs={{0,8},{4,12},{8,0},{12,4},{1,9},{5,13},{9,1},{13,5},{2,10},{6,14},... | collective-permute-start | bytes 3080 | tf_op jit(solution)/shard_map/ppermute | solution.py:94
  23.7 4.7 %collective-permute-start.8 = (f32[128,768]{1,0:T(8,128)S(1)}, f32[128,768]{1,0:T(8,128)S(1)}, u32[]{:S(2)}, u32[]{:S(2)}) collective-permute-start(f32[128,768]{1,0:T(8,128)S(1)} %get-tuple-element.48), channel_id=1, source_target_pairs={{0,4},{4,0},{8,12},{12,8},{1,5},{5,1},{9,13},{13,9},{2,6},{6,2},{1... | collective-permute-start | bytes 1179656 | tf_op jit(solution)/shard_map/ppermute | solution.py:94
  23.7 4.6 %collective-permute-start.7 = (bf16[128,1152]{1,0:T(8,128)(2,1)S(1)}, bf16[128,1152]{1,0:T(8,128)(2,1)S(1)}, u32[]{:S(2)}, u32[]{:S(2)}) collective-permute-start(bf16[128,1152]{1,0:T(8,128)(2,1)S(1)} %get-tuple-element.46.held_ref), channel_id=1, source_target_pairs={{0,4},{4,0},{8,12},{12,8},{1,5},{5,1},{9,13},{13,9},{2,6},{6,2},{1... | collective-permute-start | bytes 884744 | tf_op jit(solution)/shard_map/ppermute | solution.py:94
  25.4 4.1 %collective-permute-start.14 = (f32[2,2,128]{2,1,0:T(2,128)S(1)}, f32[2,2,128]{2,1,0:T(2,128)S(1)}, u32[]{:S(2)}, u32[]{:S(2)}) collective-permute-start(f32[2,2,128]{2,1,0:T(2,128)S(1)} %constant_dynamic-update-slice_fusion.4), channel_id=1, source_target_pairs={{0,1},{1,0},{2,3},{3,2},{4,5},{5,4},{6,7},{7,6},{8,9},{9,8},{10,11... | collective-permute-start | bytes 6152 | tf_op jit(solution)/shard_map/ppermute | solution.py:94
  27.8 4.7 %collective-permute-start.11 = (bf16[64,1152]{1,0:T(8,128)(2,1)S(1)}, bf16[64,1152]{1,0:T(8,128)(2,1)S(1)}, u32[]{:S(2)}, u32[]{:S(2)}) collective-permute-start(bf16[64,1152]{1,0:T(8,128)(2,1)S(1)} %get-tuple-element.59), channel_id=1, source_target_pairs={{0,4},{4,0},{8,12},{12,8},{1,5},{5,1},{9,13},{13,9},{2,6},{6,2},{1... | collective-permute-start | bytes 442376 | tf_op jit(solution)/shard_map/ppermute | solution.py:94
  27.9 4.7 %collective-permute-start.12 = (bf16[64,1152]{1,0:T(8,128)(2,1)S(1)}, bf16[64,1152]{1,0:T(8,128)(2,1)S(1)}, u32[]{:S(2)}, u32[]{:S(2)}) collective-permute-start(bf16[64,1152]{1,0:T(8,128)(2,1)S(1)} %get-tuple-element.58), channel_id=1, source_target_pairs={{0,4},{4,0},{8,12},{12,8},{1,5},{5,1},{9,13},{13,9},{2,6},{6,2},{1... | collective-permute-start | bytes 442376 | tf_op jit(solution)/shard_map/ppermute | solution.py:94
  28.4 6.1 %copy-start.2 = (s32[16,8]{0,1:T(8,128)S(1)}, s32[16,8]{0,1:T(8,128)}, u32[]{:S(2)}) copy-start(s32[16,8]{0,1:T(8,128)} %param.7) | copy-start | bytes 1540
  29.5 4.9 %collective-permute-start.15 = (f32[4,2,128]{2,1,0:T(2,128)S(1)}, f32[4,2,128]{2,1,0:T(2,128)S(1)}, u32[]{:S(2)}, u32[]{:S(2)}) collective-permute-start(f32[4,2,128]{2,1,0:T(2,128)S(1)} %constant_dynamic-update-slice_fusion.6), channel_id=1, source_target_pairs={{0,2},{1,3},{2,0},{3,1},{4,6},{5,7},{6,4},{7,5},{8,10},{9,11},{10,... | collective-permute-start | bytes 12296 | tf_op jit(solution)/shard_map/ppermute | solution.py:94

commit v9 on v8

--- a/solution.py
+++ b/solution.py
@@ -450,9 +450,15 @@
     )
     found = sums[None]
     back_order = [(0, 0)]
-    for bits in wide_bits:
-        found = jnp.concatenate([after(found, *over, *slopes), swap(found, "wide", bits)], axis=0)
-        back_order += [(w ^ bits, n) for w, n in back_order]
+    hops = [("narrow", 1 << b) for b in reversed(range(narrow_count.bit_length() - 1))]
+    hops += [("wide", b) for b in wide_bits]
+
+    def hop(found, back_order, axis, bits, *done):
+        wide, narrow = (bits, 0) if axis == "wide" else (0, bits)
+        found = jnp.concatenate([after(found, *done), swap(found, axis, bits)], axis=0)
+        return found, back_order + [(w ^ wide, n ^ narrow) for w, n in back_order]
+
+    found, back_order = hop(found, back_order, *hops[0], *over, *slopes)
     rest = swap(held, "wide", 1)
     rest_back = swap(other_back, "wide", 1)
     grad_a, grad_b, scaled = call(
@@ -466,10 +472,8 @@
         hidden,
         *slopes,
     )
-    steps = [1 << b for b in range(narrow_count.bit_length() - 1)]
-    for bits in steps[:-1]:
-        found = jnp.concatenate([after(found, scaled), swap(found, "narrow", bits)], axis=0)
-        back_order += [(w, n ^ bits) for w, n in back_order]
+    for step in hops[1:-1]:
+        found, back_order = hop(found, back_order, *step, scaled)
     others = []
     cut = half_count // CUTS
     for hidden_there, one in zip(over, crossed):
@@ -489,9 +493,7 @@
             pltpu.SemaphoreType.DMA((units // (2 * LANES),)),
         ],
     )
-    for bits in steps[-1:]:
-        found = jnp.concatenate([after(found, grad_down), swap(found, "narrow", bits)], axis=0)
-        back_order += [(w, n ^ bits) for w, n in back_order]
+    found, back_order = hop(found, back_order, *hops[-1], grad_down)
     picked = call(
         functools.partial(pick_kernel, order, tuple(back_order), rows),
         shape(routes_t.shape, f32),
@@ -507,14 +509,20 @@
     narrow_count = lax.axis_size("narrow")
     experts = wide_count * narrow_count
     rows = out_grad.shape[0]
-    slot_count = pre_gate.shape[2]
+    slot_count, units = pre_gate.shape[2:]
+    features = out_grad.shape[1]
     whole_blocks = (
         slot_count == experts * rows
         and wide_count > 1
         and all(n & (n - 1) == 0 for n in (lax.axis_size("dp"), wide_count, narrow_count))
         and experts <= LANES
         and LANES % rows == 0
+        and narrow_count > 1
+        and rows % 16 == 0
         and (slot_count // 2) % LANES == 0
+        and units % (2 * LANES) == 0
+        and features % (PARTS * LANES) == 0
+        and (features // lax.axis_size("dp")) % LANES == 0
     )
     plan = shards_gather if whole_blocks else shards_exchange
     return plan(out_grad, routes, gates, pre_gate, pre_up, down_weight)

time: 35.4 us -> 35 us (0.989)
  waiting for transfers between devices: 4.55 us -> 3.83 us
  starting transfers between devices: 19.8 us -> 20.2 us
    ppermute x16, waiting for transfers between devices: 4.55 us -> 3.83 us  [swap(): return lax.ppermute(x, axis, [(i, i ^ bits) for i in range(count)])]
where the time goes in v9:
time: 35 us; the launch traced here: 34.8 us
  starting transfers between devices  20.2 us (58%)
  Pallas kernels  9.92 us (28%)
  waiting for transfers between devices  3.83 us (11%)
  between operations  0.77 us (2%)
    ppermute x16, starting transfers between devices, swap(): return lax.ppermute(x, axis, [(i, i ^ bits) for i in range(count)])  20.2 us
    pallas_call x9, Pallas kernels, call(): pl.pallas_call(body, out_shape=outs, in_specs=[pl.BlockSpec(memory_space=...  9.92 us
    ppermute x16, waiting for transfers between devices, swap(): return lax.ppermute(x, axis, [(i, i ^ bits) for i in range(count)])  3.83 us
  transfers between devices with their start and end apart: 16, of which 6 were waited for; matrix products, arithmetic and copies ran while one was open for 0% of the time, Pallas kernels for 24%

profile of v9, /device:TPU:0, one launch (start us, length us, event | category | flops | bytes accessed | tf_op | source)
XLA Modules:
  0.0 34.8 jit_solution(8857349942659618431)
XLA Ops:
  0.6 0.9 %shard_map.93 = (bf16[16,2176]{1,0:T(8,128)(2,1)S(1)}, f32[8,128]{1,0:T(8,128)S(1)}) custom-call(bf16[16,2048]{1,0:T(8,128)(2,1)} %grad_hbm.1, s32[8,16]{1,0:T(8,128)} %bitcast.14, bf16[8,16]{1,0:T(8,128)(2,1)} %bitcast.22), custom_call_target="tpu_custom_call" | custom-call | flops 32768 | bytes 131072 | tf_op jit(solution)/shard_map/pallas_call | solution.py:109
  1.5 0.5 %collective-permute-start.5 = (bf16[768,2048]{1,0:T(8,128)(2,1)}, bf16[768,2048]{1,0:T(8,128)(2,1)S(1)}, u32[]{:S(2)}, u32[]{:S(2)}) collective-permute-start(bf16[768,2048]{1,0:T(8,128)(2,1)} %bitcast.18), channel_id=1, source_target_pairs={{0,4},{4,0},{8,12},{12,8},{1,5},{5,1},{9,13},{13,9},{2,6},{6,2},{1... | collective-permute-start | bytes 9437192 | tf_op jit(solution)/shard_map/ppermute | solution.py:94
  2.1 3.7 %collective-permute-start.3 = (bf16[16,2176]{1,0:T(8,128)(2,1)S(1)}, bf16[16,2176]{1,0:T(8,128)(2,1)S(1)}, u32[]{:S(2)}, u32[]{:S(2)}) collective-permute-start(bf16[16,2176]{1,0:T(8,128)(2,1)S(1)} %get-tuple-element.34), channel_id=1, source_target_pairs={{0,2},{1,3},{2,0},{3,1},{4,6},{5,7},{6,4},{7,5},{8,10},{9,11},{10,... | collective-permute-start | bytes 208904 | tf_op jit(solution)/shard_map/ppermute | solution.py:94
  5.7 1.3 %collective-permute-start = (bf16[16,2176]{1,0:T(8,128)(2,1)S(1)}, bf16[16,2176]{1,0:T(8,128)(2,1)S(1)}, u32[]{:S(2)}, u32[]{:S(2)}) collective-permute-start(bf16[16,2176]{1,0:T(8,128)(2,1)S(1)} %get-tuple-element.34), channel_id=1, source_target_pairs={{0,3},{1,2},{2,1},{3,0},{4,7},{5,6},{6,5},{7,4},{8,11},{9,10},{10,... | collective-permute-start | bytes 208904 | tf_op jit(solution)/shard_map/ppermute | solution.py:94
  7.1 0.2 collective-permute-start.1
  7.3 1.3 %shard_map.94 = (bf16[256,768]{1,0:T(8,128)(2,1)S(1)}, bf16[128,768]{1,0:T(8,128)(2,1)S(1)}) custom-call(bf16[256,768]{1,0:T(8,128)(2,1)} %bitcast.10, bf16[256,768]{1,0:T(8,128)(2,1)} %bitcast.12, f32[8,128]{1,0:T(8,128)S(1)} %get-tuple-element.31.refs_2_), custom_call_target="tpu_custom_call" | custom-call | flops 3932160 | bytes 1179648 | tf_op jit(solution)/shard_map/pallas_call | solution.py:109
  8.6 1.6 %collective-permute-start.9 = (bf16[256,768]{1,0:T(8,128)(2,1)S(1)}, bf16[256,768]{1,0:T(8,128)(2,1)S(1)}, u32[]{:S(2)}, u32[]{:S(2)}) collective-permute-start(bf16[256,768]{1,0:T(8,128)(2,1)S(1)} %get-tuple-element.32.hidden_ref), channel_id=1, source_target_pairs={{0,16},{16,0},{1,17},{17,1},{2,18},{18,2},{3,19},{19,3},{4,20},{20... | collective-permute-start | bytes 1179656 | tf_op jit(solution)/shard_map/ppermute | solution.py:94
  10.2 0.1 collective-permute-done.3
  10.3 1.7 %collective-permute-start.4 = (bf16[32,2176]{1,0:T(8,128)(2,1)S(1)}, bf16[32,2176]{1,0:T(8,128)(2,1)S(1)}, u32[]{:S(2)}, u32[]{:S(2)}) collective-permute-start(bf16[32,2176]{1,0:T(8,128)(2,1)S(1)} %constant_dynamic-update-slice_fusion.refs_0_), channel_id=1, source_target_pairs={{0,8},{4,12},{8,0},{12,4},{1,9},{5,13},{9,1},{13,5},{2,10},{6,14},... | collective-permute-start | bytes 417800 | tf_op jit(solution)/shard_map/ppermute | solution.py:94
  12.0 0.6 %collective-permute-done = bf16[16,2176]{1,0:T(8,128)(2,1)S(1)} collective-permute-done((bf16[16,2176]{1,0:T(8,128)(2,1)S(1)}, bf16[16,2176]{1,0:T(8,128)(2,1)S(1)}, u32[]{:S(2)}, u32[]{:S(2)}) %collective-permute-start) | collective-permute-done | bytes 69664 | tf_op jit(solution)/shard_map/ppermute | solution.py:94
  12.5 0.3 collective-permute-done.1
  12.8 0.0 collective-permute-start.2
  12.9 1.7 %collective-permute-start.6 = (bf16[32,2176]{1,0:T(8,128)(2,1)S(1)}, bf16[32,2176]{1,0:T(8,128)(2,1)S(1)}, u32[]{:S(2)}, u32[]{:S(2)}) collective-permute-start(bf16[32,2176]{1,0:T(8,128)(2,1)S(1)} %constant_dynamic-update-slice_fusion.2.refs_1_), channel_id=1, source_target_pairs={{0,8},{4,12},{8,0},{12,4},{1,9},{5,13},{9,1},{13,5},{2,10},{6,14},... | collective-permute-start | bytes 417800 | tf_op jit(solution)/shard_map/ppermute | solution.py:94
  14.5 0.0 collective-permute-done.5.refs_1_
  14.5 2.6 %shard_map.95 = (bf16[512,768]{1,0:T(8,128)(2,1)S(1)}, bf16[512,768]{1,0:T(8,128)(2,1)S(1)}, bf16[512,768]{1,0:T(8,128)(2,1)S(1)}, bf16[512,768]{1,0:T(8,128)(2,...) custom-call(bf16[768,2048]{1,0:T(8,128)(2,1)} %bitcast.19, ...), custom_call_target="tpu_custom_call" | custom-call | bytes 12582912 | tf_op jit(solution)/shard_map/pallas_call | solution.py:109
  17.1 0.0 collective-permute-done.4.refs_2_
  17.1 1.9 %collective-permute-done.6.refs_3_ = bf16[32,2176]{1,0:T(8,128)(2,1)S(1)} collective-permute-done((bf16[32,2176]{1,0:T(8,128)(2,1)S(1)}, bf16[32,2176]{1,0:T(8,128)(2,1)S(1)}, u32[]{:S(2)}, u32[]{:S(2)}) %collective-permute-start.6) | collective-permute-done | bytes 139296 | tf_op jit(solution)/shard_map/ppermute | solution.py:94
  19.0 0.0 copy-start
  19.1 0.0 copy-start.1
  19.1 1.6 %collective-permute-start.10 = (bf16[128,1152]{1,0:T(8,128)(2,1)S(1)}, bf16[128,1152]{1,0:T(8,128)(2,1)S(1)}, u32[]{:S(2)}, u32[]{:S(2)}) collective-permute-start(bf16[128,1152]{1,0:T(8,128)(2,1)S(1)} %shard_map.99), channel_id=1, source_target_pairs={{0,16},{16,0},{1,17},{17,1},{2,18},{18,2},{3,19},{19,3},{4,20},{20... | collective-permute-start | bytes 884744 | tf_op jit(solution)/shard_map/ppermute | solution.py:94
  20.7 0.0 collective-permute-done.2.other_hidden_ref
  20.7 1.1 %shard_map.96 = (f32[128,768]{1,0:T(8,128)S(1)}, f32[128,768]{1,0:T(8,128)S(1)}, f32[2,128]{1,0:T(2,128)S(1)}, bf16[128,1152]{1,0:T(8,128)(2,1)S(1)}) custom-call(bf16[256,768]{1,0:T(8,128)(2,1)S(1)} %get-tuple-element.32.hidden_ref, bf16[128,768]{1,0:T(8,128)(2,1)S(1)} %collective-permute-done.2.other_hidden_ref, ...), custom_call_target="tpu_custom_call" | custom-call | flops 805306368 | bytes 6291456 | tf_op jit(solution)/shard_map/pallas_call | solution.py:109
  21.8 2.8 %collective-permute-start.13 = (f32[1,2,128]{2,1,0:T(2,128)S(1)}, f32[1,2,128]{2,1,0:T(2,128)S(1)}, u32[]{:S(2)}, u32[]{:S(2)}) collective-permute-start(f32[1,2,128]{2,1,0:T(2,128)S(1)} %bitcast.16), channel_id=1, source_target_pairs={{0,2},{1,3},{2,0},{3,1},{4,6},{5,7},{6,4},{7,5},{8,10},{9,11},{10,... | collective-permute-start | bytes 3080 | tf_op jit(solution)/shard_map/ppermute | solution.py:94
  24.6 0.0 copy-done
  24.6 0.0 copy-done.1
  24.6 0.3 shard_map.97
  24.9 0.0 collective-permute-done.9.refs_0_
  24.9 0.1 collective-permute-start.8
  25.0 0.5 %collective-permute-start.7 = (bf16[128,1152]{1,0:T(8,128)(2,1)S(1)}, bf16[128,1152]{1,0:T(8,128)(2,1)S(1)}, u32[]{:S(2)}, u32[]{:S(2)}) collective-permute-start(bf16[128,1152]{1,0:T(8,128)(2,1)S(1)} %get-tuple-element.46.held_ref), channel_id=1, source_target_pairs={{0,4},{4,0},{8,12},{12,8},{1,5},{5,1},{9,13},{13,9},{2,6},{6,2},{1... | collective-permute-start | bytes 884744 | tf_op jit(solution)/shard_map/ppermute | solution.py:94
  25.5 0.8 %collective-permute-done.13 = f32[1,2,128]{2,1,0:T(2,128)S(1)} collective-permute-done((f32[1,2,128]{2,1,0:T(2,128)S(1)}, f32[1,2,128]{2,1,0:T(2,128)S(1)}, u32[]{:S(2)}, u32[]{:S(2)}) %collective-permute-start.13) | collective-permute-done | bytes 1056 | tf_op jit(solution)/shard_map/ppermute | solution.py:94
  26.3 2.3 %collective-permute-start.14 = (f32[2,2,128]{2,1,0:T(2,128)S(1)}, f32[2,2,128]{2,1,0:T(2,128)S(1)}, u32[]{:S(2)}, u32[]{:S(2)}) collective-permute-start(f32[2,2,128]{2,1,0:T(2,128)S(1)} %constant_dynamic-update-slice_fusion.4), channel_id=1, source_target_pairs={{0,1},{1,0},{2,3},{3,2},{4,5},{5,4},{6,7},{7,6},{8,9},{9,8},{10,11... | collective-permute-start | bytes 6152 | tf_op jit(solution)/shard_map/ppermute | solution.py:94
  28.7 0.0 collective-permute-done.10.refs_1_
  28.7 0.1 collective-permute-start.11
  28.8 0.5 %collective-permute-start.12 = (bf16[64,1152]{1,0:T(8,128)(2,1)S(1)}, bf16[64,1152]{1,0:T(8,128)(2,1)S(1)}, u32[]{:S(2)}, u32[]{:S(2)}) collective-permute-start(bf16[64,1152]{1,0:T(8,128)(2,1)S(1)} %get-tuple-element.58), channel_id=1, source_target_pairs={{0,4},{4,0},{8,12},{12,8},{1,5},{5,1},{9,13},{13,9},{2,6},{6,2},{1... | collective-permute-start | bytes 442376 | tf_op jit(solution)/shard_map/ppermute | solution.py:94
  29.3 0.0 collective-permute-done.7.rest_ref
  29.3 0.0 collective-permute-done.8.rest_back_ref
  29.3 0.0 copy-start.2
  29.3 1.1 %shard_map.98 = (bf16[256,768]{1,0:T(8,128)(2,1)}, bf16[256,768]{1,0:T(8,128)(2,1)}, bf16[256,768]{1,0:T(8,128)(2,1)S(1)}) custom-call(bf16[128,1152]{1,0:T(8,128)(2,1)S(1)} %get-tuple-element.46.held_ref, bf16[128,1152]{1,0:T(8,128)(2,1)S(1)} %collective-permute-done.7.rest_ref, f32[128,768]{1,0:T(8,128)S(1)} %get-tuple-element.47.back_ref, ...), custom_call_target="tpu_custom_call" | custom-call | flops 5898240 | bytes 2359296 | tf_op jit(solution)/shard_map/pallas_call | solution.py:109
  30.4 0.0 collective-permute-done.14
  30.4 1.6 %collective-permute-start.15 = (f32[4,2,128]{2,1,0:T(2,128)S(1)}, f32[4,2,128]{2,1,0:T(2,128)S(1)}, u32[]{:S(2)}, u32[]{:S(2)}) collective-permute-start(f32[4,2,128]{2,1,0:T(2,128)S(1)} %constant_dynamic-update-slice_fusion.6), channel_id=1, source_target_pairs={{0,8},{4,12},{8,0},{12,4},{1,9},{5,13},{9,1},{13,5},{2,10},{6,14},... | collective-permute-start | bytes 12296 | tf_op jit(solution)/shard_map/ppermute | solution.py:94
  32.0 0.0 collective-permute-done.11.refs_2_
  32.0 0.0 collective-permute-done.12.refs_3_
  32.0 1.9 %shard_map.100 = bf16[768,1024]{1,0:T(8,128)(2,1)} custom-call(bf16[256,768]{1,0:T(8,128)(2,1)S(1)} %get-tuple-element.52.scaled_ref, bf16[128,1152]{1,0:T(8,128)(2,1)S(1)} %get-tuple-element.46.held_ref, bf16[128,1152]{1,0:T(8,128)(2,1)S(1)} %collective-permute-done.7.rest_ref, bf16[256,768]{1,0:T(8,128)(2,1)S(1)} %collective-permute-done.9.refs_0_, ...), custom_call_target="tpu_custom_call" | custom-call | flops 805306368 | bytes 3145728 | tf_op jit(solution)/shard_map/pallas_call | solution.py:109
  34.0 0.1 collective-permute-done.15
  34.1 0.0 copy-done.2
  34.1 0.7 %shard_map.101 = f32[8,16]{1,0:T(8,128)} custom-call(s32[8,16]{1,0:T(8,128)S(1)} %bitcast.15, f32[8,2,128]{2,1,0:T(2,128)S(1)} %pad_maximum_fusion.sums_ref), custom_call_target="tpu_custom_call" | custom-call | flops 256 | bytes 256 | tf_op jit(solution)/shard_map/pallas_call | solution.py:109
  (11 shorter events, 0.1 us)
Async XLA Ops:
  1.5 13.0 %collective-permute-start.5 = (bf16[768,2048]{1,0:T(8,128)(2,1)}, bf16[768,2048]{1,0:T(8,128)(2,1)S(1)}, u32[]{:S(2)}, u32[]{:S(2)}) collective-permute-start(bf16[768,2048]{1,0:T(8,128)(2,1)} %bitcast.18), channel_id=1, source_target_pairs={{0,4},{4,0},{8,12},{12,8},{1,5},{5,1},{9,13},{13,9},{2,6},{6,2},{1... | collective-permute-start | bytes 9437192 | tf_op jit(solution)/shard_map/ppermute | solution.py:94
  2.1 8.2 %collective-permute-start.3 = (bf16[16,2176]{1,0:T(8,128)(2,1)S(1)}, bf16[16,2176]{1,0:T(8,128)(2,1)S(1)}, u32[]{:S(2)}, u32[]{:S(2)}) collective-permute-start(bf16[16,2176]{1,0:T(8,128)(2,1)S(1)} %get-tuple-element.34), channel_id=1, source_target_pairs={{0,2},{1,3},{2,0},{3,1},{4,6},{5,7},{6,4},{7,5},{8,10},{9,11},{10,... | collective-permute-start | bytes 208904 | tf_op jit(solution)/shard_map/ppermute | solution.py:94
  5.7 6.8 %collective-permute-start = (bf16[16,2176]{1,0:T(8,128)(2,1)S(1)}, bf16[16,2176]{1,0:T(8,128)(2,1)S(1)}, u32[]{:S(2)}, u32[]{:S(2)}) collective-permute-start(bf16[16,2176]{1,0:T(8,128)(2,1)S(1)} %get-tuple-element.34), channel_id=1, source_target_pairs={{0,3},{1,2},{2,1},{3,0},{4,7},{5,6},{6,5},{7,4},{8,11},{9,10},{10,... | collective-permute-start | bytes 208904 | tf_op jit(solution)/shard_map/ppermute | solution.py:94
  7.1 5.8 %collective-permute-start.1 = (bf16[16,2176]{1,0:T(8,128)(2,1)S(1)}, bf16[16,2176]{1,0:T(8,128)(2,1)S(1)}, u32[]{:S(2)}, u32[]{:S(2)}) collective-permute-start(bf16[16,2176]{1,0:T(8,128)(2,1)S(1)} %get-tuple-element.34), channel_id=1, source_target_pairs={{0,1},{1,0},{2,3},{3,2},{4,5},{5,4},{6,7},{7,6},{8,9},{9,8},{10,11... | collective-permute-start | bytes 208904 | tf_op jit(solution)/shard_map/ppermute | solution.py:94
  8.6 16.3 %collective-permute-start.9 = (bf16[256,768]{1,0:T(8,128)(2,1)S(1)}, bf16[256,768]{1,0:T(8,128)(2,1)S(1)}, u32[]{:S(2)}, u32[]{:S(2)}) collective-permute-start(bf16[256,768]{1,0:T(8,128)(2,1)S(1)} %get-tuple-element.32.hidden_ref), channel_id=1, source_target_pairs={{0,16},{16,0},{1,17},{17,1},{2,18},{18,2},{3,19},{19,3},{4,20},{20... | collective-permute-start | bytes 1179656 | tf_op jit(solution)/shard_map/ppermute | solution.py:94
  10.3 6.9 %collective-permute-start.4 = (bf16[32,2176]{1,0:T(8,128)(2,1)S(1)}, bf16[32,2176]{1,0:T(8,128)(2,1)S(1)}, u32[]{:S(2)}, u32[]{:S(2)}) collective-permute-start(bf16[32,2176]{1,0:T(8,128)(2,1)S(1)} %constant_dynamic-update-slice_fusion.refs_0_), channel_id=1, source_target_pairs={{0,8},{4,12},{8,0},{12,4},{1,9},{5,13},{9,1},{13,5},{2,10},{6,14},... | collective-permute-start | bytes 417800 | tf_op jit(solution)/shard_map/ppermute | solution.py:94
  12.8 7.8 %collective-permute-start.2 = (bf16[128,768]{1,0:T(8,128)(2,1)S(1)}, bf16[128,768]{1,0:T(8,128)(2,1)S(1)}, u32[]{:S(2)}, u32[]{:S(2)}) collective-permute-start(bf16[128,768]{1,0:T(8,128)(2,1)S(1)} %get-tuple-element.35), channel_id=1, source_target_pairs={{0,4},{4,0},{8,12},{12,8},{1,5},{5,1},{9,13},{13,9},{2,6},{6,2},{1... | collective-permute-start | bytes 589832 | tf_op jit(solution)/shard_map/ppermute | solution.py:94
  12.9 6.1 %collective-permute-start.6 = (bf16[32,2176]{1,0:T(8,128)(2,1)S(1)}, bf16[32,2176]{1,0:T(8,128)(2,1)S(1)}, u32[]{:S(2)}, u32[]{:S(2)}) collective-permute-start(bf16[32,2176]{1,0:T(8,128)(2,1)S(1)} %constant_dynamic-update-slice_fusion.2.refs_1_), channel_id=1, source_target_pairs={{0,8},{4,12},{8,0},{12,4},{1,9},{5,13},{9,1},{13,5},{2,10},{6,14},... | collective-permute-start | bytes 417800 | tf_op jit(solution)/shard_map/ppermute | solution.py:94
  19.0 5.6 %copy-start = (bf16[1,1,256,768]{3,2,1,0:T(8,128)(2,1)S(1)}, bf16[1,1,256,768]{3,2,1,0:T(8,128)(2,1)}, u32[]{:S(2)}) copy-start(bf16[1,1,256,768]{3,2,1,0:T(8,128)(2,1)} %param.9) | copy-start | bytes 1179652
  19.1 5.6 %copy-start.1 = (bf16[1,1,256,768]{3,2,1,0:T(8,128)(2,1)S(1)}, bf16[1,1,256,768]{3,2,1,0:T(8,128)(2,1)}, u32[]{:S(2)}) copy-start(bf16[1,1,256,768]{3,2,1,0:T(8,128)(2,1)} %param.10) | copy-start | bytes 1179652
  19.1 9.6 %collective-permute-start.10 = (bf16[128,1152]{1,0:T(8,128)(2,1)S(1)}, bf16[128,1152]{1,0:T(8,128)(2,1)S(1)}, u32[]{:S(2)}, u32[]{:S(2)}) collective-permute-start(bf16[128,1152]{1,0:T(8,128)(2,1)S(1)} %shard_map.99), channel_id=1, source_target_pairs={{0,16},{16,0},{1,17},{17,1},{2,18},{18,2},{3,19},{19,3},{4,20},{20... | collective-permute-start | bytes 884744 | tf_op jit(solution)/shard_map/ppermute | solution.py:94
  21.8 4.5 %collective-permute-start.13 = (f32[1,2,128]{2,1,0:T(2,128)S(1)}, f32[1,2,128]{2,1,0:T(2,128)S(1)}, u32[]{:S(2)}, u32[]{:S(2)}) collective-permute-start(f32[1,2,128]{2,1,0:T(2,128)S(1)} %bitcast.16), channel_id=1, source_target_pairs={{0,2},{1,3},{2,0},{3,1},{4,6},{5,7},{6,4},{7,5},{8,10},{9,11},{10,... | collective-permute-start | bytes 3080 | tf_op jit(solution)/shard_map/ppermute | solution.py:94
  24.9 4.4 %collective-permute-start.8 = (f32[128,768]{1,0:T(8,128)S(1)}, f32[128,768]{1,0:T(8,128)S(1)}, u32[]{:S(2)}, u32[]{:S(2)}) collective-permute-start(f32[128,768]{1,0:T(8,128)S(1)} %get-tuple-element.48), channel_id=1, source_target_pairs={{0,4},{4,0},{8,12},{12,8},{1,5},{5,1},{9,13},{13,9},{2,6},{6,2},{1... | collective-permute-start | bytes 1179656 | tf_op jit(solution)/shard_map/ppermute | solution.py:94
  25.0 4.3 %collective-permute-start.7 = (bf16[128,1152]{1,0:T(8,128)(2,1)S(1)}, bf16[128,1152]{1,0:T(8,128)(2,1)S(1)}, u32[]{:S(2)}, u32[]{:S(2)}) collective-permute-start(bf16[128,1152]{1,0:T(8,128)(2,1)S(1)} %get-tuple-element.46.held_ref), channel_id=1, source_target_pairs={{0,4},{4,0},{8,12},{12,8},{1,5},{5,1},{9,13},{13,9},{2,6},{6,2},{1... | collective-permute-start | bytes 884744 | tf_op jit(solution)/shard_map/ppermute | solution.py:94
  26.3 4.1 %collective-permute-start.14 = (f32[2,2,128]{2,1,0:T(2,128)S(1)}, f32[2,2,128]{2,1,0:T(2,128)S(1)}, u32[]{:S(2)}, u32[]{:S(2)}) collective-permute-start(f32[2,2,128]{2,1,0:T(2,128)S(1)} %constant_dynamic-update-slice_fusion.4), channel_id=1, source_target_pairs={{0,1},{1,0},{2,3},{3,2},{4,5},{5,4},{6,7},{7,6},{8,9},{9,8},{10,11... | collective-permute-start | bytes 6152 | tf_op jit(solution)/shard_map/ppermute | solution.py:94
  28.7 3.3 %collective-permute-start.11 = (bf16[64,1152]{1,0:T(8,128)(2,1)S(1)}, bf16[64,1152]{1,0:T(8,128)(2,1)S(1)}, u32[]{:S(2)}, u32[]{:S(2)}) collective-permute-start(bf16[64,1152]{1,0:T(8,128)(2,1)S(1)} %get-tuple-element.59), channel_id=1, source_target_pairs={{0,4},{4,0},{8,12},{12,8},{1,5},{5,1},{9,13},{13,9},{2,6},{6,2},{1... | collective-permute-start | bytes 442376 | tf_op jit(solution)/shard_map/ppermute | solution.py:94
  28.8 3.3 %collective-permute-start.12 = (bf16[64,1152]{1,0:T(8,128)(2,1)S(1)}, bf16[64,1152]{1,0:T(8,128)(2,1)S(1)}, u32[]{:S(2)}, u32[]{:S(2)}) collective-permute-start(bf16[64,1152]{1,0:T(8,128)(2,1)S(1)} %get-tuple-element.58), channel_id=1, source_target_pairs={{0,4},{4,0},{8,12},{12,8},{1,5},{5,1},{9,13},{13,9},{2,6},{6,2},{1... | collective-permute-start | bytes 442376 | tf_op jit(solution)/shard_map/ppermute | solution.py:94
  29.3 4.8 %copy-start.2 = (s32[16,8]{0,1:T(8,128)S(1)}, s32[16,8]{0,1:T(8,128)}, u32[]{:S(2)}) copy-start(s32[16,8]{0,1:T(8,128)} %param.7) | copy-start | bytes 1540
  30.4 3.7 %collective-permute-start.15 = (f32[4,2,128]{2,1,0:T(2,128)S(1)}, f32[4,2,128]{2,1,0:T(2,128)S(1)}, u32[]{:S(2)}, u32[]{:S(2)}) collective-permute-start(f32[4,2,128]{2,1,0:T(2,128)S(1)} %constant_dynamic-update-slice_fusion.6), channel_id=1, source_target_pairs={{0,8},{4,12},{8,0},{12,4},{1,9},{5,13},{9,1},{13,5},{2,10},{6,14},... | collective-permute-start | bytes 12296 | tf_op jit(solution)/shard_map/ppermute | solution.py:94

commit v10 on v9

--- a/solution.py
+++ b/solution.py
@@ -206,7 +206,7 @@
 def back_kernel(features, blocks, columns, hidden_ref, other_hidden_ref, *refs):
     group_refs, refs = refs[:blocks], refs[blocks:]
     turned_refs, refs = refs[: 2 * PARTS], refs[2 * PARTS :]
-    back_ref, other_back_ref, sums_ref, own_ref = refs
+    back_ref, other_back_ref, sums_ref = refs
     held = jnp.concatenate([group_ref[...] for group_ref in group_refs], axis=0)
     rows = held.shape[0]
     for expert, (act_ref, result_ref) in enumerate(
@@ -231,7 +231,6 @@
             sums_ref[row : row + 1, :] = jnp.sum(
                 folded[at : at + LANES, :].T, axis=0, keepdims=True
             )
-    copy_columns(features, columns, 0, group_refs, own_ref)
 
 
 def copy_columns(features, columns, bits, group_refs, out_ref):
@@ -244,7 +243,7 @@
 
 
 def cut_kernel(features, columns, blocks, *refs):
-    for bits, cut_ref in enumerate(refs[blocks:], 1):
+    for bits, cut_ref in enumerate(refs[blocks:]):
         copy_columns(features, columns, bits, refs[:blocks], cut_ref)
 
 
@@ -315,10 +314,10 @@
     scaled = jnp.concatenate(scaled, axis=0)
     tokens = jnp.concatenate(tokens, axis=0)
     copies = []
-    for at in range(0, out_ref.shape[0], 2 * LANES):
-        here = pl.ds(at, 2 * LANES)
+    for at in range(0, out_ref.shape[0], LANES):
+        here = pl.ds(at, LANES)
         held_out_ref[here, :] = lax.dot_general(
-            scaled[:, at : at + 2 * LANES],
+            scaled[:, at : at + LANES],
             tokens,
             (((0,), (0,)), ((), ())),
             preferred_element_type=jnp.float32,
@@ -419,20 +418,19 @@
         groups += [swap(group, "wide", bits) for group in groups]
     middle = len(groups) // 2
     groups[middle] = after(groups[middle], *turned)
-    cuts = call(
+    held, *cuts = call(
         functools.partial(cut_kernel, features, columns, len(groups)),
-        (shape((half_count, columns + LANES), bf16),) * (dp_count - 1),
+        (shape((half_count, columns + LANES), bf16),) * dp_count,
         (0, 4 * half_count * columns),
         *groups,
     )
     crossed = [swap(cut, "dp", bits) for bits, cut in enumerate(cuts, 1)]
-    back, other_back, sums, held = call(
+    back, other_back, sums = call(
         functools.partial(back_kernel, features, len(groups), columns),
         (
             shape((half_count, units), f32),
             shape((half_count, units), f32),
             shape((slot_count // LANES, LANES), f32),
-            shape((half_count, columns + LANES), bf16),
         ),
         (2 * slot_count * units * features, 4 * units * features),
         hidden,
@@ -459,7 +457,7 @@
         return found, back_order + [(w ^ wide, n ^ narrow) for w, n in back_order]
 
     found, back_order = hop(found, back_order, *hops[0], *over, *slopes)
-    rest = swap(held, "wide", 1)
+    rest = swap(after(held, sums), "wide", 1)
     rest_back = swap(other_back, "wide", 1)
     grad_a, grad_b, scaled = call(
         functools.partial(grads_kernel, order, rows, columns),
@@ -490,7 +488,7 @@
         out_specs=pl.BlockSpec(memory_space=pltpu.HBM),
         scratch=[
             pltpu.VMEM((units, columns), bf16),
-            pltpu.SemaphoreType.DMA((units // (2 * LANES),)),
+            pltpu.SemaphoreType.DMA((units // LANES,)),
         ],
     )
     found, back_order = hop(found, back_order, *hops[-1], grad_down)

time: 35 us -> 35.1 us (level)
  no operation moved by 1% of the time
where the time goes in v10:
time: 35.1 us; the launch traced here: 34.8 us
  starting transfers between devices  20.2 us (58%)
  Pallas kernels  9.91 us (28%)
  waiting for transfers between devices  3.88 us (11%)
  between operations  0.77 us (2%)
    ppermute x16, starting transfers between devices, swap(): return lax.ppermute(x, axis, [(i, i ^ bits) for i in range(count)])  20.2 us
    pallas_call x9, Pallas kernels, call(): pl.pallas_call(body, out_shape=outs, in_specs=[pl.BlockSpec(memory_space=...  9.91 us
    ppermute x16, waiting for transfers between devices, swap(): return lax.ppermute(x, axis, [(i, i ^ bits) for i in range(count)])  3.88 us
  transfers between devices with their start and end apart: 16, of which 6 were waited for; matrix products, arithmetic and copies ran while one was open for 0% of the time, Pallas kernels for 24%

profile of v10, /device:TPU:0, one launch (start us, length us, event | category | flops | bytes accessed | tf_op | source)
XLA Modules:
  0.0 34.8 jit_solution(16569484634863166480)
XLA Ops:
  0.6 0.9 %shard_map.93 = (bf16[16,2176]{1,0:T(8,128)(2,1)S(1)}, f32[8,128]{1,0:T(8,128)S(1)}) custom-call(bf16[16,2048]{1,0:T(8,128)(2,1)} %grad_hbm.1, s32[8,16]{1,0:T(8,128)} %bitcast.14, bf16[8,16]{1,0:T(8,128)(2,1)} %bitcast.22), custom_call_target="tpu_custom_call" | custom-call | flops 32768 | bytes 131072 | tf_op jit(solution)/shard_map/pallas_call | solution.py:109
  1.5 0.5 %collective-permute-start.4 = (bf16[768,2048]{1,0:T(8,128)(2,1)}, bf16[768,2048]{1,0:T(8,128)(2,1)S(1)}, u32[]{:S(2)}, u32[]{:S(2)}) collective-permute-start(bf16[768,2048]{1,0:T(8,128)(2,1)} %bitcast.18), channel_id=1, source_target_pairs={{0,4},{4,0},{8,12},{12,8},{1,5},{5,1},{9,13},{13,9},{2,6},{6,2},{1... | collective-permute-start | bytes 9437192 | tf_op jit(solution)/shard_map/ppermute | solution.py:94
  2.1 3.7 %collective-permute-start = (bf16[16,2176]{1,0:T(8,128)(2,1)S(1)}, bf16[16,2176]{1,0:T(8,128)(2,1)S(1)}, u32[]{:S(2)}, u32[]{:S(2)}) collective-permute-start(bf16[16,2176]{1,0:T(8,128)(2,1)S(1)} %get-tuple-element.33), channel_id=1, source_target_pairs={{0,2},{1,3},{2,0},{3,1},{4,6},{5,7},{6,4},{7,5},{8,10},{9,11},{10,... | collective-permute-start | bytes 208904 | tf_op jit(solution)/shard_map/ppermute | solution.py:94
  5.7 1.3 %collective-permute-start.1 = (bf16[16,2176]{1,0:T(8,128)(2,1)S(1)}, bf16[16,2176]{1,0:T(8,128)(2,1)S(1)}, u32[]{:S(2)}, u32[]{:S(2)}) collective-permute-start(bf16[16,2176]{1,0:T(8,128)(2,1)S(1)} %get-tuple-element.33), channel_id=1, source_target_pairs={{0,3},{1,2},{2,1},{3,0},{4,7},{5,6},{6,5},{7,4},{8,11},{9,10},{10,... | collective-permute-start | bytes 208904 | tf_op jit(solution)/shard_map/ppermute | solution.py:94
  7.1 0.2 collective-permute-start.2
  7.3 1.3 %shard_map.96 = (bf16[256,768]{1,0:T(8,128)(2,1)S(1)}, bf16[128,768]{1,0:T(8,128)(2,1)S(1)}) custom-call(bf16[256,768]{1,0:T(8,128)(2,1)} %bitcast.10, bf16[256,768]{1,0:T(8,128)(2,1)} %bitcast.12, f32[8,128]{1,0:T(8,128)S(1)} %get-tuple-element.34.refs_2_), custom_call_target="tpu_custom_call" | custom-call | flops 3932160 | bytes 1179648 | tf_op jit(solution)/shard_map/pallas_call | solution.py:109
  8.6 1.6 %collective-permute-start.9 = (bf16[256,768]{1,0:T(8,128)(2,1)S(1)}, bf16[256,768]{1,0:T(8,128)(2,1)S(1)}, u32[]{:S(2)}, u32[]{:S(2)}) collective-permute-start(bf16[256,768]{1,0:T(8,128)(2,1)S(1)} %get-tuple-element.46.hidden_ref), channel_id=1, source_target_pairs={{0,16},{16,0},{1,17},{17,1},{2,18},{18,2},{3,19},{19,3},{4,20},{20... | collective-permute-start | bytes 1179656 | tf_op jit(solution)/shard_map/ppermute | solution.py:94
  10.2 0.1 collective-permute-done
  10.3 1.7 %collective-permute-start.3 = (bf16[32,2176]{1,0:T(8,128)(2,1)S(1)}, bf16[32,2176]{1,0:T(8,128)(2,1)S(1)}, u32[]{:S(2)}, u32[]{:S(2)}) collective-permute-start(bf16[32,2176]{1,0:T(8,128)(2,1)S(1)} %constant_dynamic-update-slice_fusion.refs_0_), channel_id=1, source_target_pairs={{0,8},{4,12},{8,0},{12,4},{1,9},{5,13},{9,1},{13,5},{2,10},{6,14},... | collective-permute-start | bytes 417800 | tf_op jit(solution)/shard_map/ppermute | solution.py:94
  12.0 0.6 %collective-permute-done.1 = bf16[16,2176]{1,0:T(8,128)(2,1)S(1)} collective-permute-done((bf16[16,2176]{1,0:T(8,128)(2,1)S(1)}, bf16[16,2176]{1,0:T(8,128)(2,1)S(1)}, u32[]{:S(2)}, u32[]{:S(2)}) %collective-permute-start.1) | collective-permute-done | bytes 69664 | tf_op jit(solution)/shard_map/ppermute | solution.py:94
  12.5 0.3 collective-permute-done.2
  12.8 0.0 collective-permute-start.6
  12.9 1.7 %collective-permute-start.5 = (bf16[32,2176]{1,0:T(8,128)(2,1)S(1)}, bf16[32,2176]{1,0:T(8,128)(2,1)S(1)}, u32[]{:S(2)}, u32[]{:S(2)}) collective-permute-start(bf16[32,2176]{1,0:T(8,128)(2,1)S(1)} %constant_dynamic-update-slice_fusion.2.refs_1_), channel_id=1, source_target_pairs={{0,8},{4,12},{8,0},{12,4},{1,9},{5,13},{9,1},{13,5},{2,10},{6,14},... | collective-permute-start | bytes 417800 | tf_op jit(solution)/shard_map/ppermute | solution.py:94
  14.5 0.0 collective-permute-done.4.refs_1_
  14.5 2.6 %shard_map.94 = (bf16[512,768]{1,0:T(8,128)(2,1)S(1)}, bf16[512,768]{1,0:T(8,128)(2,1)S(1)}, bf16[512,768]{1,0:T(8,128)(2,1)S(1)}, bf16[512,768]{1,0:T(8,128)(2,...) custom-call(bf16[768,2048]{1,0:T(8,128)(2,1)} %bitcast.19, ...), custom_call_target="tpu_custom_call" | custom-call | bytes 12582912 | tf_op jit(solution)/shard_map/pallas_call | solution.py:109
  17.1 0.0 collective-permute-done.3.refs_2_
  17.1 1.9 %collective-permute-done.5.refs_3_ = bf16[32,2176]{1,0:T(8,128)(2,1)S(1)} collective-permute-done((bf16[32,2176]{1,0:T(8,128)(2,1)S(1)}, bf16[32,2176]{1,0:T(8,128)(2,1)S(1)}, u32[]{:S(2)}, u32[]{:S(2)}) %collective-permute-start.5) | collective-permute-done | bytes 139296 | tf_op jit(solution)/shard_map/ppermute | solution.py:94
  19.1 0.0 copy-start
  19.1 0.0 copy-start.1
  19.1 1.6 %collective-permute-start.10 = (bf16[128,1152]{1,0:T(8,128)(2,1)S(1)}, bf16[128,1152]{1,0:T(8,128)(2,1)S(1)}, u32[]{:S(2)}, u32[]{:S(2)}) collective-permute-start(bf16[128,1152]{1,0:T(8,128)(2,1)S(1)} %get-tuple-element.56), channel_id=1, source_target_pairs={{0,16},{16,0},{1,17},{17,1},{2,18},{18,2},{3,19},{19,3},{4,20},{20... | collective-permute-start | bytes 884744 | tf_op jit(solution)/shard_map/ppermute | solution.py:94
  20.7 0.0 collective-permute-done.6.other_hidden_ref
  20.7 1.1 %shard_map.97 = (f32[128,768]{1,0:T(8,128)S(1)}, f32[128,768]{1,0:T(8,128)S(1)}, f32[2,128]{1,0:T(2,128)S(1)}) custom-call(bf16[256,768]{1,0:T(8,128)(2,1)S(1)} %get-tuple-element.46.hidden_ref, bf16[128,768]{1,0:T(8,128)(2,1)S(1)} %collective-permute-done.6.other_hidden_ref, bf16[32,2176]{1,0:T(8,128)(2,1)S(1)} %constant_dynamic-update-slice_fusion.refs_0_, ...), custom_call_target="tpu_custom_call" | custom-call | flops 805306368 | bytes 6291456 | tf_op jit(solution)/shard_map/pallas_call | solution.py:109
  21.8 2.8 %collective-permute-start.13 = (f32[1,2,128]{2,1,0:T(2,128)S(1)}, f32[1,2,128]{2,1,0:T(2,128)S(1)}, u32[]{:S(2)}, u32[]{:S(2)}) collective-permute-start(f32[1,2,128]{2,1,0:T(2,128)S(1)} %bitcast.16), channel_id=1, source_target_pairs={{0,2},{1,3},{2,0},{3,1},{4,6},{5,7},{6,4},{7,5},{8,10},{9,11},{10,... | collective-permute-start | bytes 3080 | tf_op jit(solution)/shard_map/ppermute | solution.py:94
  24.6 0.0 copy-done
  24.6 0.0 copy-done.1
  24.6 0.3 shard_map.98
  24.9 0.0 collective-permute-done.9.refs_0_
  24.9 0.1 collective-permute-start.8
  25.0 0.5 %collective-permute-start.7 = (bf16[128,1152]{1,0:T(8,128)(2,1)S(1)}, bf16[128,1152]{1,0:T(8,128)(2,1)S(1)}, u32[]{:S(2)}, u32[]{:S(2)}) collective-permute-start(bf16[128,1152]{1,0:T(8,128)(2,1)S(1)} %get-tuple-element.50.held_ref), channel_id=1, source_target_pairs={{0,4},{4,0},{8,12},{12,8},{1,5},{5,1},{9,13},{13,9},{2,6},{6,2},{1... | collective-permute-start | bytes 884744 | tf_op jit(solution)/shard_map/ppermute | solution.py:94
  25.5 0.8 %collective-permute-done.13 = f32[1,2,128]{2,1,0:T(2,128)S(1)} collective-permute-done((f32[1,2,128]{2,1,0:T(2,128)S(1)}, f32[1,2,128]{2,1,0:T(2,128)S(1)}, u32[]{:S(2)}, u32[]{:S(2)}) %collective-permute-start.13) | collective-permute-done | bytes 1056 | tf_op jit(solution)/shard_map/ppermute | solution.py:94
  26.3 2.3 %collective-permute-start.14 = (f32[2,2,128]{2,1,0:T(2,128)S(1)}, f32[2,2,128]{2,1,0:T(2,128)S(1)}, u32[]{:S(2)}, u32[]{:S(2)}) collective-permute-start(f32[2,2,128]{2,1,0:T(2,128)S(1)} %constant_dynamic-update-slice_fusion.4), channel_id=1, source_target_pairs={{0,1},{1,0},{2,3},{3,2},{4,5},{5,4},{6,7},{7,6},{8,9},{9,8},{10,11... | collective-permute-start | bytes 6152 | tf_op jit(solution)/shard_map/ppermute | solution.py:94
  28.7 0.0 collective-permute-done.10.refs_1_
  28.7 0.1 collective-permute-start.11
  28.8 0.5 %collective-permute-start.12 = (bf16[64,1152]{1,0:T(8,128)(2,1)S(1)}, bf16[64,1152]{1,0:T(8,128)(2,1)S(1)}, u32[]{:S(2)}, u32[]{:S(2)}) collective-permute-start(bf16[64,1152]{1,0:T(8,128)(2,1)S(1)} %get-tuple-element.62), channel_id=1, source_target_pairs={{0,4},{4,0},{8,12},{12,8},{1,5},{5,1},{9,13},{13,9},{2,6},{6,2},{1... | collective-permute-start | bytes 442376 | tf_op jit(solution)/shard_map/ppermute | solution.py:94
  29.3 0.0 collective-permute-done.7.rest_ref
  29.3 0.0 collective-permute-done.8.rest_back_ref
  29.3 0.0 copy-start.2
  29.3 1.2 %shard_map.99 = (bf16[256,768]{1,0:T(8,128)(2,1)}, bf16[256,768]{1,0:T(8,128)(2,1)}, bf16[256,768]{1,0:T(8,128)(2,1)S(1)}) custom-call(bf16[128,1152]{1,0:T(8,128)(2,1)S(1)} %get-tuple-element.50.held_ref, bf16[128,1152]{1,0:T(8,128)(2,1)S(1)} %collective-permute-done.7.rest_ref, f32[128,768]{1,0:T(8,128)S(1)} %get-tuple-element.51.back_ref, ...), custom_call_target="tpu_custom_call" | custom-call | flops 5898240 | bytes 2359296 | tf_op jit(solution)/shard_map/pallas_call | solution.py:109
  30.5 0.0 collective-permute-done.14
  30.5 1.6 %collective-permute-start.15 = (f32[4,2,128]{2,1,0:T(2,128)S(1)}, f32[4,2,128]{2,1,0:T(2,128)S(1)}, u32[]{:S(2)}, u32[]{:S(2)}) collective-permute-start(f32[4,2,128]{2,1,0:T(2,128)S(1)} %constant_dynamic-update-slice_fusion.6), channel_id=1, source_target_pairs={{0,8},{4,12},{8,0},{12,4},{1,9},{5,13},{9,1},{13,5},{2,10},{6,14},... | collective-permute-start | bytes 12296 | tf_op jit(solution)/shard_map/ppermute | solution.py:94
  32.1 0.0 collective-permute-done.11.refs_2_
  32.1 0.0 collective-permute-done.12.refs_3_
  32.1 1.9 %shard_map.100 = bf16[768,1024]{1,0:T(8,128)(2,1)} custom-call(bf16[256,768]{1,0:T(8,128)(2,1)S(1)} %get-tuple-element.55.scaled_ref, bf16[128,1152]{1,0:T(8,128)(2,1)S(1)} %get-tuple-element.50.held_ref, bf16[128,1152]{1,0:T(8,128)(2,1)S(1)} %collective-permute-done.7.rest_ref, bf16[256,768]{1,0:T(8,128)(2,1)S(1)} %collective-permute-done.9.refs_0_, ...), custom_call_target="tpu_custom_call" | custom-call | flops 805306368 | bytes 3145728 | tf_op jit(solution)/shard_map/pallas_call | solution.py:109
  34.0 0.2 collective-permute-done.15
  34.2 0.0 copy-done.2
  34.2 0.7 %shard_map.101 = f32[8,16]{1,0:T(8,128)} custom-call(s32[8,16]{1,0:T(8,128)S(1)} %bitcast.15, f32[8,2,128]{2,1,0:T(2,128)S(1)} %pad_maximum_fusion.sums_ref), custom_call_target="tpu_custom_call" | custom-call | flops 256 | bytes 256 | tf_op jit(solution)/shard_map/pallas_call | solution.py:109
  (11 shorter events, 0.1 us)
Async XLA Ops:
  1.5 13.0 %collective-permute-start.4 = (bf16[768,2048]{1,0:T(8,128)(2,1)}, bf16[768,2048]{1,0:T(8,128)(2,1)S(1)}, u32[]{:S(2)}, u32[]{:S(2)}) collective-permute-start(bf16[768,2048]{1,0:T(8,128)(2,1)} %bitcast.18), channel_id=1, source_target_pairs={{0,4},{4,0},{8,12},{12,8},{1,5},{5,1},{9,13},{13,9},{2,6},{6,2},{1... | collective-permute-start | bytes 9437192 | tf_op jit(solution)/shard_map/ppermute | solution.py:94
  2.1 8.2 %collective-permute-start = (bf16[16,2176]{1,0:T(8,128)(2,1)S(1)}, bf16[16,2176]{1,0:T(8,128)(2,1)S(1)}, u32[]{:S(2)}, u32[]{:S(2)}) collective-permute-start(bf16[16,2176]{1,0:T(8,128)(2,1)S(1)} %get-tuple-element.33), channel_id=1, source_target_pairs={{0,2},{1,3},{2,0},{3,1},{4,6},{5,7},{6,4},{7,5},{8,10},{9,11},{10,... | collective-permute-start | bytes 208904 | tf_op jit(solution)/shard_map/ppermute | solution.py:94
  5.7 6.8 %collective-permute-start.1 = (bf16[16,2176]{1,0:T(8,128)(2,1)S(1)}, bf16[16,2176]{1,0:T(8,128)(2,1)S(1)}, u32[]{:S(2)}, u32[]{:S(2)}) collective-permute-start(bf16[16,2176]{1,0:T(8,128)(2,1)S(1)} %get-tuple-element.33), channel_id=1, source_target_pairs={{0,3},{1,2},{2,1},{3,0},{4,7},{5,6},{6,5},{7,4},{8,11},{9,10},{10,... | collective-permute-start | bytes 208904 | tf_op jit(solution)/shard_map/ppermute | solution.py:94
  7.1 5.8 %collective-permute-start.2 = (bf16[16,2176]{1,0:T(8,128)(2,1)S(1)}, bf16[16,2176]{1,0:T(8,128)(2,1)S(1)}, u32[]{:S(2)}, u32[]{:S(2)}) collective-permute-start(bf16[16,2176]{1,0:T(8,128)(2,1)S(1)} %get-tuple-element.33), channel_id=1, source_target_pairs={{0,1},{1,0},{2,3},{3,2},{4,5},{5,4},{6,7},{7,6},{8,9},{9,8},{10,11... | collective-permute-start | bytes 208904 | tf_op jit(solution)/shard_map/ppermute | solution.py:94
  8.6 16.3 %collective-permute-start.9 = (bf16[256,768]{1,0:T(8,128)(2,1)S(1)}, bf16[256,768]{1,0:T(8,128)(2,1)S(1)}, u32[]{:S(2)}, u32[]{:S(2)}) collective-permute-start(bf16[256,768]{1,0:T(8,128)(2,1)S(1)} %get-tuple-element.46.hidden_ref), channel_id=1, source_target_pairs={{0,16},{16,0},{1,17},{17,1},{2,18},{18,2},{3,19},{19,3},{4,20},{20... | collective-permute-start | bytes 1179656 | tf_op jit(solution)/shard_map/ppermute | solution.py:94
  10.3 6.9 %collective-permute-start.3 = (bf16[32,2176]{1,0:T(8,128)(2,1)S(1)}, bf16[32,2176]{1,0:T(8,128)(2,1)S(1)}, u32[]{:S(2)}, u32[]{:S(2)}) collective-permute-start(bf16[32,2176]{1,0:T(8,128)(2,1)S(1)} %constant_dynamic-update-slice_fusion.refs_0_), channel_id=1, source_target_pairs={{0,8},{4,12},{8,0},{12,4},{1,9},{5,13},{9,1},{13,5},{2,10},{6,14},... | collective-permute-start | bytes 417800 | tf_op jit(solution)/shard_map/ppermute | solution.py:94
  12.8 7.9 %collective-permute-start.6 = (bf16[128,768]{1,0:T(8,128)(2,1)S(1)}, bf16[128,768]{1,0:T(8,128)(2,1)S(1)}, u32[]{:S(2)}, u32[]{:S(2)}) collective-permute-start(bf16[128,768]{1,0:T(8,128)(2,1)S(1)} %get-tuple-element.48), channel_id=1, source_target_pairs={{0,4},{4,0},{8,12},{12,8},{1,5},{5,1},{9,13},{13,9},{2,6},{6,2},{1... | collective-permute-start | bytes 589832 | tf_op jit(solution)/shard_map/ppermute | solution.py:94
  12.9 6.1 %collective-permute-start.5 = (bf16[32,2176]{1,0:T(8,128)(2,1)S(1)}, bf16[32,2176]{1,0:T(8,128)(2,1)S(1)}, u32[]{:S(2)}, u32[]{:S(2)}) collective-permute-start(bf16[32,2176]{1,0:T(8,128)(2,1)S(1)} %constant_dynamic-update-slice_fusion.2.refs_1_), channel_id=1, source_target_pairs={{0,8},{4,12},{8,0},{12,4},{1,9},{5,13},{9,1},{13,5},{2,10},{6,14},... | collective-permute-start | bytes 417800 | tf_op jit(solution)/shard_map/ppermute | solution.py:94
  19.1 5.6 %copy-start = (bf16[1,1,256,768]{3,2,1,0:T(8,128)(2,1)S(1)}, bf16[1,1,256,768]{3,2,1,0:T(8,128)(2,1)}, u32[]{:S(2)}) copy-start(bf16[1,1,256,768]{3,2,1,0:T(8,128)(2,1)} %param.9) | copy-start | bytes 1179652
  19.1 5.6 %copy-start.1 = (bf16[1,1,256,768]{3,2,1,0:T(8,128)(2,1)S(1)}, bf16[1,1,256,768]{3,2,1,0:T(8,128)(2,1)}, u32[]{:S(2)}) copy-start(bf16[1,1,256,768]{3,2,1,0:T(8,128)(2,1)} %param.10) | copy-start | bytes 1179652
  19.1 9.6 %collective-permute-start.10 = (bf16[128,1152]{1,0:T(8,128)(2,1)S(1)}, bf16[128,1152]{1,0:T(8,128)(2,1)S(1)}, u32[]{:S(2)}, u32[]{:S(2)}) collective-permute-start(bf16[128,1152]{1,0:T(8,128)(2,1)S(1)} %get-tuple-element.56), channel_id=1, source_target_pairs={{0,16},{16,0},{1,17},{17,1},{2,18},{18,2},{3,19},{19,3},{4,20},{20... | collective-permute-start | bytes 884744 | tf_op jit(solution)/shard_map/ppermute | solution.py:94
  21.8 4.5 %collective-permute-start.13 = (f32[1,2,128]{2,1,0:T(2,128)S(1)}, f32[1,2,128]{2,1,0:T(2,128)S(1)}, u32[]{:S(2)}, u32[]{:S(2)}) collective-permute-start(f32[1,2,128]{2,1,0:T(2,128)S(1)} %bitcast.16), channel_id=1, source_target_pairs={{0,2},{1,3},{2,0},{3,1},{4,6},{5,7},{6,4},{7,5},{8,10},{9,11},{10,... | collective-permute-start | bytes 3080 | tf_op jit(solution)/shard_map/ppermute | solution.py:94
  24.9 4.4 %collective-permute-start.8 = (f32[128,768]{1,0:T(8,128)S(1)}, f32[128,768]{1,0:T(8,128)S(1)}, u32[]{:S(2)}, u32[]{:S(2)}) collective-permute-start(f32[128,768]{1,0:T(8,128)S(1)} %get-tuple-element.52), channel_id=1, source_target_pairs={{0,4},{4,0},{8,12},{12,8},{1,5},{5,1},{9,13},{13,9},{2,6},{6,2},{1... | collective-permute-start | bytes 1179656 | tf_op jit(solution)/shard_map/ppermute | solution.py:94
  25.0 4.3 %collective-permute-start.7 = (bf16[128,1152]{1,0:T(8,128)(2,1)S(1)}, bf16[128,1152]{1,0:T(8,128)(2,1)S(1)}, u32[]{:S(2)}, u32[]{:S(2)}) collective-permute-start(bf16[128,1152]{1,0:T(8,128)(2,1)S(1)} %get-tuple-element.50.held_ref), channel_id=1, source_target_pairs={{0,4},{4,0},{8,12},{12,8},{1,5},{5,1},{9,13},{13,9},{2,6},{6,2},{1... | collective-permute-start | bytes 884744 | tf_op jit(solution)/shard_map/ppermute | solution.py:94
  26.3 4.1 %collective-permute-start.14 = (f32[2,2,128]{2,1,0:T(2,128)S(1)}, f32[2,2,128]{2,1,0:T(2,128)S(1)}, u32[]{:S(2)}, u32[]{:S(2)}) collective-permute-start(f32[2,2,128]{2,1,0:T(2,128)S(1)} %constant_dynamic-update-slice_fusion.4), channel_id=1, source_target_pairs={{0,1},{1,0},{2,3},{3,2},{4,5},{5,4},{6,7},{7,6},{8,9},{9,8},{10,11... | collective-permute-start | bytes 6152 | tf_op jit(solution)/shard_map/ppermute | solution.py:94
  28.7 3.4 %collective-permute-start.11 = (bf16[64,1152]{1,0:T(8,128)(2,1)S(1)}, bf16[64,1152]{1,0:T(8,128)(2,1)S(1)}, u32[]{:S(2)}, u32[]{:S(2)}) collective-permute-start(bf16[64,1152]{1,0:T(8,128)(2,1)S(1)} %get-tuple-element.63), channel_id=1, source_target_pairs={{0,4},{4,0},{8,12},{12,8},{1,5},{5,1},{9,13},{13,9},{2,6},{6,2},{1... | collective-permute-start | bytes 442376 | tf_op jit(solution)/shard_map/ppermute | solution.py:94
  28.8 3.3 %collective-permute-start.12 = (bf16[64,1152]{1,0:T(8,128)(2,1)S(1)}, bf16[64,1152]{1,0:T(8,128)(2,1)S(1)}, u32[]{:S(2)}, u32[]{:S(2)}) collective-permute-start(bf16[64,1152]{1,0:T(8,128)(2,1)S(1)} %get-tuple-element.62), channel_id=1, source_target_pairs={{0,4},{4,0},{8,12},{12,8},{1,5},{5,1},{9,13},{13,9},{2,6},{6,2},{1... | collective-permute-start | bytes 442376 | tf_op jit(solution)/shard_map/ppermute | solution.py:94
  29.3 4.9 %copy-start.2 = (s32[16,8]{0,1:T(8,128)S(1)}, s32[16,8]{0,1:T(8,128)}, u32[]{:S(2)}) copy-start(s32[16,8]{0,1:T(8,128)} %param.7) | copy-start | bytes 1540
  30.5 3.7 %collective-permute-start.15 = (f32[4,2,128]{2,1,0:T(2,128)S(1)}, f32[4,2,128]{2,1,0:T(2,128)S(1)}, u32[]{:S(2)}, u32[]{:S(2)}) collective-permute-start(f32[4,2,128]{2,1,0:T(2,128)S(1)} %constant_dynamic-update-slice_fusion.6), channel_id=1, source_target_pairs={{0,8},{4,12},{8,0},{12,4},{1,9},{5,13},{9,1},{13,5},{2,10},{6,14},... | collective-permute-start | bytes 12296 | tf_op jit(solution)/shard_map/ppermute | solution.py:94

commit v11 on v10

--- a/solution.py
+++ b/solution.py
@@ -448,7 +448,7 @@
     )
     found = sums[None]
     back_order = [(0, 0)]
-    hops = [("narrow", 1 << b) for b in reversed(range(narrow_count.bit_length() - 1))]
+    hops = [("narrow", 1 << b) for b in range(narrow_count.bit_length() - 1)]
     hops += [("wide", b) for b in wide_bits]
 
     def hop(found, back_order, axis, bits, *done):

time: 35.1 us -> 35.1 us (level)
  no operation moved by 1% of the time
where the time goes in v11:
time: 35.1 us; the launch traced here: 34.8 us
  starting transfers between devices  20.1 us (57%)
  Pallas kernels  9.91 us (28%)
  waiting for transfers between devices  3.93 us (11%)
  between operations  0.77 us (2%)
    ppermute x16, starting transfers between devices, swap(): return lax.ppermute(x, axis, [(i, i ^ bits) for i in range(count)])  20.1 us
    pallas_call x9, Pallas kernels, call(): pl.pallas_call(body, out_shape=outs, in_specs=[pl.BlockSpec(memory_space=...  9.91 us
    ppermute x16, waiting for transfers between devices, swap(): return lax.ppermute(x, axis, [(i, i ^ bits) for i in range(count)])  3.93 us
  transfers between devices with their start and end apart: 16, of which 6 were waited for; matrix products, arithmetic and copies ran while one was open for 0% of the time, Pallas kernels for 24%

profile of v11, /device:TPU:0, one launch (start us, length us, event | category | flops | bytes accessed | tf_op | source)
XLA Modules:
  0.0 34.8 jit_solution(2637798568582852590)
XLA Ops:
  0.6 0.9 %shard_map.93 = (bf16[16,2176]{1,0:T(8,128)(2,1)S(1)}, f32[8,128]{1,0:T(8,128)S(1)}) custom-call(bf16[16,2048]{1,0:T(8,128)(2,1)} %grad_hbm.1, s32[8,16]{1,0:T(8,128)} %bitcast.14, bf16[8,16]{1,0:T(8,128)(2,1)} %bitcast.22), custom_call_target="tpu_custom_call" | custom-call | flops 32768 | bytes 131072 | tf_op jit(solution)/shard_map/pallas_call | solution.py:109
  1.5 0.5 %collective-permute-start.4 = (bf16[768,2048]{1,0:T(8,128)(2,1)}, bf16[768,2048]{1,0:T(8,128)(2,1)S(1)}, u32[]{:S(2)}, u32[]{:S(2)}) collective-permute-start(bf16[768,2048]{1,0:T(8,128)(2,1)} %bitcast.18), channel_id=1, source_target_pairs={{0,4},{4,0},{8,12},{12,8},{1,5},{5,1},{9,13},{13,9},{2,6},{6,2},{1... | collective-permute-start | bytes 9437192 | tf_op jit(solution)/shard_map/ppermute | solution.py:94
  2.1 3.7 %collective-permute-start = (bf16[16,2176]{1,0:T(8,128)(2,1)S(1)}, bf16[16,2176]{1,0:T(8,128)(2,1)S(1)}, u32[]{:S(2)}, u32[]{:S(2)}) collective-permute-start(bf16[16,2176]{1,0:T(8,128)(2,1)S(1)} %get-tuple-element.33), channel_id=1, source_target_pairs={{0,2},{1,3},{2,0},{3,1},{4,6},{5,7},{6,4},{7,5},{8,10},{9,11},{10,... | collective-permute-start | bytes 208904 | tf_op jit(solution)/shard_map/ppermute | solution.py:94
  5.7 1.3 %collective-permute-start.1 = (bf16[16,2176]{1,0:T(8,128)(2,1)S(1)}, bf16[16,2176]{1,0:T(8,128)(2,1)S(1)}, u32[]{:S(2)}, u32[]{:S(2)}) collective-permute-start(bf16[16,2176]{1,0:T(8,128)(2,1)S(1)} %get-tuple-element.33), channel_id=1, source_target_pairs={{0,3},{1,2},{2,1},{3,0},{4,7},{5,6},{6,5},{7,4},{8,11},{9,10},{10,... | collective-permute-start | bytes 208904 | tf_op jit(solution)/shard_map/ppermute | solution.py:94
  7.1 0.2 collective-permute-start.2
  7.3 1.3 %shard_map.96 = (bf16[256,768]{1,0:T(8,128)(2,1)S(1)}, bf16[128,768]{1,0:T(8,128)(2,1)S(1)}) custom-call(bf16[256,768]{1,0:T(8,128)(2,1)} %bitcast.10, bf16[256,768]{1,0:T(8,128)(2,1)} %bitcast.12, f32[8,128]{1,0:T(8,128)S(1)} %get-tuple-element.34.refs_2_), custom_call_target="tpu_custom_call" | custom-call | flops 3932160 | bytes 1179648 | tf_op jit(solution)/shard_map/pallas_call | solution.py:109
  8.6 1.6 %collective-permute-start.9 = (bf16[256,768]{1,0:T(8,128)(2,1)S(1)}, bf16[256,768]{1,0:T(8,128)(2,1)S(1)}, u32[]{:S(2)}, u32[]{:S(2)}) collective-permute-start(bf16[256,768]{1,0:T(8,128)(2,1)S(1)} %get-tuple-element.46.hidden_ref), channel_id=1, source_target_pairs={{0,16},{16,0},{1,17},{17,1},{2,18},{18,2},{3,19},{19,3},{4,20},{20... | collective-permute-start | bytes 1179656 | tf_op jit(solution)/shard_map/ppermute | solution.py:94
  10.2 0.1 collective-permute-done
  10.3 1.7 %collective-permute-start.3 = (bf16[32,2176]{1,0:T(8,128)(2,1)S(1)}, bf16[32,2176]{1,0:T(8,128)(2,1)S(1)}, u32[]{:S(2)}, u32[]{:S(2)}) collective-permute-start(bf16[32,2176]{1,0:T(8,128)(2,1)S(1)} %constant_dynamic-update-slice_fusion.refs_0_), channel_id=1, source_target_pairs={{0,8},{4,12},{8,0},{12,4},{1,9},{5,13},{9,1},{13,5},{2,10},{6,14},... | collective-permute-start | bytes 417800 | tf_op jit(solution)/shard_map/ppermute | solution.py:94
  12.0 0.6 %collective-permute-done.1 = bf16[16,2176]{1,0:T(8,128)(2,1)S(1)} collective-permute-done((bf16[16,2176]{1,0:T(8,128)(2,1)S(1)}, bf16[16,2176]{1,0:T(8,128)(2,1)S(1)}, u32[]{:S(2)}, u32[]{:S(2)}) %collective-permute-start.1) | collective-permute-done | bytes 69664 | tf_op jit(solution)/shard_map/ppermute | solution.py:94
  12.5 0.3 collective-permute-done.2
  12.8 0.0 collective-permute-start.6
  12.9 1.7 %collective-permute-start.5 = (bf16[32,2176]{1,0:T(8,128)(2,1)S(1)}, bf16[32,2176]{1,0:T(8,128)(2,1)S(1)}, u32[]{:S(2)}, u32[]{:S(2)}) collective-permute-start(bf16[32,2176]{1,0:T(8,128)(2,1)S(1)} %constant_dynamic-update-slice_fusion.2.refs_1_), channel_id=1, source_target_pairs={{0,8},{4,12},{8,0},{12,4},{1,9},{5,13},{9,1},{13,5},{2,10},{6,14},... | collective-permute-start | bytes 417800 | tf_op jit(solution)/shard_map/ppermute | solution.py:94
  14.5 0.0 collective-permute-done.4.refs_1_
  14.5 2.6 %shard_map.94 = (bf16[512,768]{1,0:T(8,128)(2,1)S(1)}, bf16[512,768]{1,0:T(8,128)(2,1)S(1)}, bf16[512,768]{1,0:T(8,128)(2,1)S(1)}, bf16[512,768]{1,0:T(8,128)(2,...) custom-call(bf16[768,2048]{1,0:T(8,128)(2,1)} %bitcast.19, ...), custom_call_target="tpu_custom_call" | custom-call | bytes 12582912 | tf_op jit(solution)/shard_map/pallas_call | solution.py:109
  17.1 0.0 collective-permute-done.3.refs_2_
  17.1 1.9 %collective-permute-done.5.refs_3_ = bf16[32,2176]{1,0:T(8,128)(2,1)S(1)} collective-permute-done((bf16[32,2176]{1,0:T(8,128)(2,1)S(1)}, bf16[32,2176]{1,0:T(8,128)(2,1)S(1)}, u32[]{:S(2)}, u32[]{:S(2)}) %collective-permute-start.5) | collective-permute-done | bytes 139296 | tf_op jit(solution)/shard_map/ppermute | solution.py:94
  19.1 0.0 copy-start
  19.1 0.0 copy-start.1
  19.1 1.6 %collective-permute-start.10 = (bf16[128,1152]{1,0:T(8,128)(2,1)S(1)}, bf16[128,1152]{1,0:T(8,128)(2,1)S(1)}, u32[]{:S(2)}, u32[]{:S(2)}) collective-permute-start(bf16[128,1152]{1,0:T(8,128)(2,1)S(1)} %get-tuple-element.56), channel_id=1, source_target_pairs={{0,16},{16,0},{1,17},{17,1},{2,18},{18,2},{3,19},{19,3},{4,20},{20... | collective-permute-start | bytes 884744 | tf_op jit(solution)/shard_map/ppermute | solution.py:94
  20.7 0.0 collective-permute-done.6.other_hidden_ref
  20.7 1.1 %shard_map.97 = (f32[128,768]{1,0:T(8,128)S(1)}, f32[128,768]{1,0:T(8,128)S(1)}, f32[2,128]{1,0:T(2,128)S(1)}) custom-call(bf16[256,768]{1,0:T(8,128)(2,1)S(1)} %get-tuple-element.46.hidden_ref, bf16[128,768]{1,0:T(8,128)(2,1)S(1)} %collective-permute-done.6.other_hidden_ref, bf16[32,2176]{1,0:T(8,128)(2,1)S(1)} %constant_dynamic-update-slice_fusion.refs_0_, ...), custom_call_target="tpu_custom_call" | custom-call | flops 805306368 | bytes 6291456 | tf_op jit(solution)/shard_map/pallas_call | solution.py:109
  21.8 1.9 %collective-permute-start.13 = (f32[1,2,128]{2,1,0:T(2,128)S(1)}, f32[1,2,128]{2,1,0:T(2,128)S(1)}, u32[]{:S(2)}, u32[]{:S(2)}) collective-permute-start(f32[1,2,128]{2,1,0:T(2,128)S(1)} %bitcast.16), channel_id=1, source_target_pairs={{0,1},{1,0},{2,3},{3,2},{4,5},{5,4},{6,7},{7,6},{8,9},{9,8},{10,11... | collective-permute-start | bytes 3080 | tf_op jit(solution)/shard_map/ppermute | solution.py:94
  23.7 0.0 copy-done
  23.7 0.0 copy-done.1
  23.7 0.3 shard_map.98
  24.0 0.0 collective-permute-done.9.refs_0_
  24.0 0.1 collective-permute-start.8
  24.1 0.5 %collective-permute-start.7 = (bf16[128,1152]{1,0:T(8,128)(2,1)S(1)}, bf16[128,1152]{1,0:T(8,128)(2,1)S(1)}, u32[]{:S(2)}, u32[]{:S(2)}) collective-permute-start(bf16[128,1152]{1,0:T(8,128)(2,1)S(1)} %get-tuple-element.50.held_ref), channel_id=1, source_target_pairs={{0,4},{4,0},{8,12},{12,8},{1,5},{5,1},{9,13},{13,9},{2,6},{6,2},{1... | collective-permute-start | bytes 884744 | tf_op jit(solution)/shard_map/ppermute | solution.py:94
  24.6 0.9 %collective-permute-done.13 = f32[1,2,128]{2,1,0:T(2,128)S(1)} collective-permute-done((f32[1,2,128]{2,1,0:T(2,128)S(1)}, f32[1,2,128]{2,1,0:T(2,128)S(1)}, u32[]{:S(2)}, u32[]{:S(2)}) %collective-permute-start.13) | collective-permute-done | bytes 1056 | tf_op jit(solution)/shard_map/ppermute | solution.py:94
  25.4 3.2 %collective-permute-start.14 = (f32[2,2,128]{2,1,0:T(2,128)S(1)}, f32[2,2,128]{2,1,0:T(2,128)S(1)}, u32[]{:S(2)}, u32[]{:S(2)}) collective-permute-start(f32[2,2,128]{2,1,0:T(2,128)S(1)} %constant_dynamic-update-slice_fusion.4), channel_id=1, source_target_pairs={{0,2},{1,3},{2,0},{3,1},{4,6},{5,7},{6,4},{7,5},{8,10},{9,11},{10,... | collective-permute-start | bytes 6152 | tf_op jit(solution)/shard_map/ppermute | solution.py:94
  28.7 0.0 collective-permute-done.10.refs_1_
  28.7 0.1 collective-permute-start.11
  28.8 0.5 %collective-permute-start.12 = (bf16[64,1152]{1,0:T(8,128)(2,1)S(1)}, bf16[64,1152]{1,0:T(8,128)(2,1)S(1)}, u32[]{:S(2)}, u32[]{:S(2)}) collective-permute-start(bf16[64,1152]{1,0:T(8,128)(2,1)S(1)} %get-tuple-element.62), channel_id=1, source_target_pairs={{0,4},{4,0},{8,12},{12,8},{1,5},{5,1},{9,13},{13,9},{2,6},{6,2},{1... | collective-permute-start | bytes 442376 | tf_op jit(solution)/shard_map/ppermute | solution.py:94
  29.3 0.0 collective-permute-done.7.rest_ref
  29.3 0.0 collective-permute-done.8.rest_back_ref
  29.3 0.0 copy-start.2
  29.3 1.2 %shard_map.99 = (bf16[256,768]{1,0:T(8,128)(2,1)}, bf16[256,768]{1,0:T(8,128)(2,1)}, bf16[256,768]{1,0:T(8,128)(2,1)S(1)}) custom-call(bf16[128,1152]{1,0:T(8,128)(2,1)S(1)} %get-tuple-element.50.held_ref, bf16[128,1152]{1,0:T(8,128)(2,1)S(1)} %collective-permute-done.7.rest_ref, f32[128,768]{1,0:T(8,128)S(1)} %get-tuple-element.51.back_ref, ...), custom_call_target="tpu_custom_call" | custom-call | flops 5898240 | bytes 2359296 | tf_op jit(solution)/shard_map/pallas_call | solution.py:109
  30.5 0.0 collective-permute-done.14
  30.5 1.6 %collective-permute-start.15 = (f32[4,2,128]{2,1,0:T(2,128)S(1)}, f32[4,2,128]{2,1,0:T(2,128)S(1)}, u32[]{:S(2)}, u32[]{:S(2)}) collective-permute-start(f32[4,2,128]{2,1,0:T(2,128)S(1)} %constant_dynamic-update-slice_fusion.6), channel_id=1, source_target_pairs={{0,8},{4,12},{8,0},{12,4},{1,9},{5,13},{9,1},{13,5},{2,10},{6,14},... | collective-permute-start | bytes 12296 | tf_op jit(solution)/shard_map/ppermute | solution.py:94
  32.1 0.0 collective-permute-done.11.refs_2_
  32.1 0.0 collective-permute-done.12.refs_3_
  32.1 1.9 %shard_map.100 = bf16[768,1024]{1,0:T(8,128)(2,1)} custom-call(bf16[256,768]{1,0:T(8,128)(2,1)S(1)} %get-tuple-element.55.scaled_ref, bf16[128,1152]{1,0:T(8,128)(2,1)S(1)} %get-tuple-element.50.held_ref, bf16[128,1152]{1,0:T(8,128)(2,1)S(1)} %collective-permute-done.7.rest_ref, bf16[256,768]{1,0:T(8,128)(2,1)S(1)} %collective-permute-done.9.refs_0_, ...), custom_call_target="tpu_custom_call" | custom-call | flops 805306368 | bytes 3145728 | tf_op jit(solution)/shard_map/pallas_call | solution.py:109
  34.0 0.2 collective-permute-done.15
  34.2 0.0 copy-done.2
  34.2 0.7 %shard_map.101 = f32[8,16]{1,0:T(8,128)} custom-call(s32[8,16]{1,0:T(8,128)S(1)} %bitcast.15, f32[8,2,128]{2,1,0:T(2,128)S(1)} %pad_maximum_fusion.sums_ref), custom_call_target="tpu_custom_call" | custom-call | flops 256 | bytes 256 | tf_op jit(solution)/shard_map/pallas_call | solution.py:109
  (11 shorter events, 0.1 us)
Async XLA Ops:
  1.5 13.0 %collective-permute-start.4 = (bf16[768,2048]{1,0:T(8,128)(2,1)}, bf16[768,2048]{1,0:T(8,128)(2,1)S(1)}, u32[]{:S(2)}, u32[]{:S(2)}) collective-permute-start(bf16[768,2048]{1,0:T(8,128)(2,1)} %bitcast.18), channel_id=1, source_target_pairs={{0,4},{4,0},{8,12},{12,8},{1,5},{5,1},{9,13},{13,9},{2,6},{6,2},{1... | collective-permute-start | bytes 9437192 | tf_op jit(solution)/shard_map/ppermute | solution.py:94
  2.1 8.2 %collective-permute-start = (bf16[16,2176]{1,0:T(8,128)(2,1)S(1)}, bf16[16,2176]{1,0:T(8,128)(2,1)S(1)}, u32[]{:S(2)}, u32[]{:S(2)}) collective-permute-start(bf16[16,2176]{1,0:T(8,128)(2,1)S(1)} %get-tuple-element.33), channel_id=1, source_target_pairs={{0,2},{1,3},{2,0},{3,1},{4,6},{5,7},{6,4},{7,5},{8,10},{9,11},{10,... | collective-permute-start | bytes 208904 | tf_op jit(solution)/shard_map/ppermute | solution.py:94
  5.7 6.8 %collective-permute-start.1 = (bf16[16,2176]{1,0:T(8,128)(2,1)S(1)}, bf16[16,2176]{1,0:T(8,128)(2,1)S(1)}, u32[]{:S(2)}, u32[]{:S(2)}) collective-permute-start(bf16[16,2176]{1,0:T(8,128)(2,1)S(1)} %get-tuple-element.33), channel_id=1, source_target_pairs={{0,3},{1,2},{2,1},{3,0},{4,7},{5,6},{6,5},{7,4},{8,11},{9,10},{10,... | collective-permute-start | bytes 208904 | tf_op jit(solution)/shard_map/ppermute | solution.py:94
  7.1 5.8 %collective-permute-start.2 = (bf16[16,2176]{1,0:T(8,128)(2,1)S(1)}, bf16[16,2176]{1,0:T(8,128)(2,1)S(1)}, u32[]{:S(2)}, u32[]{:S(2)}) collective-permute-start(bf16[16,2176]{1,0:T(8,128)(2,1)S(1)} %get-tuple-element.33), channel_id=1, source_target_pairs={{0,1},{1,0},{2,3},{3,2},{4,5},{5,4},{6,7},{7,6},{8,9},{9,8},{10,11... | collective-permute-start | bytes 208904 | tf_op jit(solution)/shard_map/ppermute | solution.py:94
  8.6 15.4 %collective-permute-start.9 = (bf16[256,768]{1,0:T(8,128)(2,1)S(1)}, bf16[256,768]{1,0:T(8,128)(2,1)S(1)}, u32[]{:S(2)}, u32[]{:S(2)}) collective-permute-start(bf16[256,768]{1,0:T(8,128)(2,1)S(1)} %get-tuple-element.46.hidden_ref), channel_id=1, source_target_pairs={{0,16},{16,0},{1,17},{17,1},{2,18},{18,2},{3,19},{19,3},{4,20},{20... | collective-permute-start | bytes 1179656 | tf_op jit(solution)/shard_map/ppermute | solution.py:94
  10.3 6.9 %collective-permute-start.3 = (bf16[32,2176]{1,0:T(8,128)(2,1)S(1)}, bf16[32,2176]{1,0:T(8,128)(2,1)S(1)}, u32[]{:S(2)}, u32[]{:S(2)}) collective-permute-start(bf16[32,2176]{1,0:T(8,128)(2,1)S(1)} %constant_dynamic-update-slice_fusion.refs_0_), channel_id=1, source_target_pairs={{0,8},{4,12},{8,0},{12,4},{1,9},{5,13},{9,1},{13,5},{2,10},{6,14},... | collective-permute-start | bytes 417800 | tf_op jit(solution)/shard_map/ppermute | solution.py:94
  12.8 7.9 %collective-permute-start.6 = (bf16[128,768]{1,0:T(8,128)(2,1)S(1)}, bf16[128,768]{1,0:T(8,128)(2,1)S(1)}, u32[]{:S(2)}, u32[]{:S(2)}) collective-permute-start(bf16[128,768]{1,0:T(8,128)(2,1)S(1)} %get-tuple-element.48), channel_id=1, source_target_pairs={{0,4},{4,0},{8,12},{12,8},{1,5},{5,1},{9,13},{13,9},{2,6},{6,2},{1... | collective-permute-start | bytes 589832 | tf_op jit(solution)/shard_map/ppermute | solution.py:94
  12.9 6.1 %collective-permute-start.5 = (bf16[32,2176]{1,0:T(8,128)(2,1)S(1)}, bf16[32,2176]{1,0:T(8,128)(2,1)S(1)}, u32[]{:S(2)}, u32[]{:S(2)}) collective-permute-start(bf16[32,2176]{1,0:T(8,128)(2,1)S(1)} %constant_dynamic-update-slice_fusion.2.refs_1_), channel_id=1, source_target_pairs={{0,8},{4,12},{8,0},{12,4},{1,9},{5,13},{9,1},{13,5},{2,10},{6,14},... | collective-permute-start | bytes 417800 | tf_op jit(solution)/shard_map/ppermute | solution.py:94
  19.1 4.6 %copy-start = (bf16[1,1,256,768]{3,2,1,0:T(8,128)(2,1)S(1)}, bf16[1,1,256,768]{3,2,1,0:T(8,128)(2,1)}, u32[]{:S(2)}) copy-start(bf16[1,1,256,768]{3,2,1,0:T(8,128)(2,1)} %param.9) | copy-start | bytes 1179652
  19.1 4.6 %copy-start.1 = (bf16[1,1,256,768]{3,2,1,0:T(8,128)(2,1)S(1)}, bf16[1,1,256,768]{3,2,1,0:T(8,128)(2,1)}, u32[]{:S(2)}) copy-start(bf16[1,1,256,768]{3,2,1,0:T(8,128)(2,1)} %param.10) | copy-start | bytes 1179652
  19.1 9.6 %collective-permute-start.10 = (bf16[128,1152]{1,0:T(8,128)(2,1)S(1)}, bf16[128,1152]{1,0:T(8,128)(2,1)S(1)}, u32[]{:S(2)}, u32[]{:S(2)}) collective-permute-start(bf16[128,1152]{1,0:T(8,128)(2,1)S(1)} %get-tuple-element.56), channel_id=1, source_target_pairs={{0,16},{16,0},{1,17},{17,1},{2,18},{18,2},{3,19},{19,3},{4,20},{20... | collective-permute-start | bytes 884744 | tf_op jit(solution)/shard_map/ppermute | solution.py:94
  21.8 3.6 %collective-permute-start.13 = (f32[1,2,128]{2,1,0:T(2,128)S(1)}, f32[1,2,128]{2,1,0:T(2,128)S(1)}, u32[]{:S(2)}, u32[]{:S(2)}) collective-permute-start(f32[1,2,128]{2,1,0:T(2,128)S(1)} %bitcast.16), channel_id=1, source_target_pairs={{0,1},{1,0},{2,3},{3,2},{4,5},{5,4},{6,7},{7,6},{8,9},{9,8},{10,11... | collective-permute-start | bytes 3080 | tf_op jit(solution)/shard_map/ppermute | solution.py:94
  24.0 5.3 %collective-permute-start.8 = (f32[128,768]{1,0:T(8,128)S(1)}, f32[128,768]{1,0:T(8,128)S(1)}, u32[]{:S(2)}, u32[]{:S(2)}) collective-permute-start(f32[128,768]{1,0:T(8,128)S(1)} %get-tuple-element.52), channel_id=1, source_target_pairs={{0,4},{4,0},{8,12},{12,8},{1,5},{5,1},{9,13},{13,9},{2,6},{6,2},{1... | collective-permute-start | bytes 1179656 | tf_op jit(solution)/shard_map/ppermute | solution.py:94
  24.1 5.2 %collective-permute-start.7 = (bf16[128,1152]{1,0:T(8,128)(2,1)S(1)}, bf16[128,1152]{1,0:T(8,128)(2,1)S(1)}, u32[]{:S(2)}, u32[]{:S(2)}) collective-permute-start(bf16[128,1152]{1,0:T(8,128)(2,1)S(1)} %get-tuple-element.50.held_ref), channel_id=1, source_target_pairs={{0,4},{4,0},{8,12},{12,8},{1,5},{5,1},{9,13},{13,9},{2,6},{6,2},{1... | collective-permute-start | bytes 884744 | tf_op jit(solution)/shard_map/ppermute | solution.py:94
  25.4 5.0 %collective-permute-start.14 = (f32[2,2,128]{2,1,0:T(2,128)S(1)}, f32[2,2,128]{2,1,0:T(2,128)S(1)}, u32[]{:S(2)}, u32[]{:S(2)}) collective-permute-start(f32[2,2,128]{2,1,0:T(2,128)S(1)} %constant_dynamic-update-slice_fusion.4), channel_id=1, source_target_pairs={{0,2},{1,3},{2,0},{3,1},{4,6},{5,7},{6,4},{7,5},{8,10},{9,11},{10,... | collective-permute-start | bytes 6152 | tf_op jit(solution)/shard_map/ppermute | solution.py:94
  28.7 3.4 %collective-permute-start.11 = (bf16[64,1152]{1,0:T(8,128)(2,1)S(1)}, bf16[64,1152]{1,0:T(8,128)(2,1)S(1)}, u32[]{:S(2)}, u32[]{:S(2)}) collective-permute-start(bf16[64,1152]{1,0:T(8,128)(2,1)S(1)} %get-tuple-element.63), channel_id=1, source_target_pairs={{0,4},{4,0},{8,12},{12,8},{1,5},{5,1},{9,13},{13,9},{2,6},{6,2},{1... | collective-permute-start | bytes 442376 | tf_op jit(solution)/shard_map/ppermute | solution.py:94
  28.8 3.3 %collective-permute-start.12 = (bf16[64,1152]{1,0:T(8,128)(2,1)S(1)}, bf16[64,1152]{1,0:T(8,128)(2,1)S(1)}, u32[]{:S(2)}, u32[]{:S(2)}) collective-permute-start(bf16[64,1152]{1,0:T(8,128)(2,1)S(1)} %get-tuple-element.62), channel_id=1, source_target_pairs={{0,4},{4,0},{8,12},{12,8},{1,5},{5,1},{9,13},{13,9},{2,6},{6,2},{1... | collective-permute-start | bytes 442376 | tf_op jit(solution)/shard_map/ppermute | solution.py:94
  29.3 4.9 %copy-start.2 = (s32[16,8]{0,1:T(8,128)S(1)}, s32[16,8]{0,1:T(8,128)}, u32[]{:S(2)}) copy-start(s32[16,8]{0,1:T(8,128)} %param.7) | copy-start | bytes 1540
  30.5 3.7 %collective-permute-start.15 = (f32[4,2,128]{2,1,0:T(2,128)S(1)}, f32[4,2,128]{2,1,0:T(2,128)S(1)}, u32[]{:S(2)}, u32[]{:S(2)}) collective-permute-start(f32[4,2,128]{2,1,0:T(2,128)S(1)} %constant_dynamic-update-slice_fusion.6), channel_id=1, source_target_pairs={{0,8},{4,12},{8,0},{12,4},{1,9},{5,13},{9,1},{13,5},{2,10},{6,14},... | collective-permute-start | bytes 12296 | tf_op jit(solution)/shard_map/ppermute | solution.py:94

commit v12 on v10

--- a/solution.py
+++ b/solution.py
@@ -446,7 +446,7 @@
         pre_up,
         deps=(sums,),
     )
-    found = sums[None]
+    found = after(sums, *over)[None]
     back_order = [(0, 0)]
     hops = [("narrow", 1 << b) for b in reversed(range(narrow_count.bit_length() - 1))]
     hops += [("wide", b) for b in wide_bits]
@@ -456,7 +456,7 @@
         found = jnp.concatenate([after(found, *done), swap(found, axis, bits)], axis=0)
         return found, back_order + [(w ^ wide, n ^ narrow) for w, n in back_order]
 
-    found, back_order = hop(found, back_order, *hops[0], *over, *slopes)
+    found, back_order = hop(found, back_order, *hops[0], *slopes)
     rest = swap(after(held, sums), "wide", 1)
     rest_back = swap(other_back, "wide", 1)
     grad_a, grad_b, scaled = call(

time: 35.1 us -> 35.1 us (level)
  no operation moved by 1% of the time
where the time goes in v12:
time: 35.1 us; the launch traced here: 34.9 us
  starting transfers between devices  20.2 us (58%)
  Pallas kernels  9.91 us (28%)
  waiting for transfers between devices  3.89 us (11%)
  between operations  0.77 us (2%)
    ppermute x16, starting transfers between devices, swap(): return lax.ppermute(x, axis, [(i, i ^ bits) for i in range(count)])  20.2 us
    pallas_call x9, Pallas kernels, call(): pl.pallas_call(body, out_shape=outs, in_specs=[pl.BlockSpec(memory_space=...  9.91 us
    ppermute x16, waiting for transfers between devices, swap(): return lax.ppermute(x, axis, [(i, i ^ bits) for i in range(count)])  3.89 us
  transfers between devices with their start and end apart: 16, of which 6 were waited for; matrix products, arithmetic and copies ran while one was open for 0% of the time, Pallas kernels for 24%

profile of v12, /device:TPU:0, one launch (start us, length us, event | category | flops | bytes accessed | tf_op | source)
XLA Modules:
  0.0 34.9 jit_solution(17849745579396291616)
XLA Ops:
  0.6 0.9 %shard_map.93 = (bf16[16,2176]{1,0:T(8,128)(2,1)S(1)}, f32[8,128]{1,0:T(8,128)S(1)}) custom-call(bf16[16,2048]{1,0:T(8,128)(2,1)} %grad_hbm.1, s32[8,16]{1,0:T(8,128)} %bitcast.14, bf16[8,16]{1,0:T(8,128)(2,1)} %bitcast.22), custom_call_target="tpu_custom_call" | custom-call | flops 32768 | bytes 131072 | tf_op jit(solution)/shard_map/pallas_call | solution.py:109
  1.5 0.5 %collective-permute-start.4 = (bf16[768,2048]{1,0:T(8,128)(2,1)}, bf16[768,2048]{1,0:T(8,128)(2,1)S(1)}, u32[]{:S(2)}, u32[]{:S(2)}) collective-permute-start(bf16[768,2048]{1,0:T(8,128)(2,1)} %bitcast.18), channel_id=1, source_target_pairs={{0,4},{4,0},{8,12},{12,8},{1,5},{5,1},{9,13},{13,9},{2,6},{6,2},{1... | collective-permute-start | bytes 9437192 | tf_op jit(solution)/shard_map/ppermute | solution.py:94
  2.1 3.7 %collective-permute-start = (bf16[16,2176]{1,0:T(8,128)(2,1)S(1)}, bf16[16,2176]{1,0:T(8,128)(2,1)S(1)}, u32[]{:S(2)}, u32[]{:S(2)}) collective-permute-start(bf16[16,2176]{1,0:T(8,128)(2,1)S(1)} %get-tuple-element.34), channel_id=1, source_target_pairs={{0,2},{1,3},{2,0},{3,1},{4,6},{5,7},{6,4},{7,5},{8,10},{9,11},{10,... | collective-permute-start | bytes 208904 | tf_op jit(solution)/shard_map/ppermute | solution.py:94
  5.7 1.3 %collective-permute-start.1 = (bf16[16,2176]{1,0:T(8,128)(2,1)S(1)}, bf16[16,2176]{1,0:T(8,128)(2,1)S(1)}, u32[]{:S(2)}, u32[]{:S(2)}) collective-permute-start(bf16[16,2176]{1,0:T(8,128)(2,1)S(1)} %get-tuple-element.34), channel_id=1, source_target_pairs={{0,3},{1,2},{2,1},{3,0},{4,7},{5,6},{6,5},{7,4},{8,11},{9,10},{10,... | collective-permute-start | bytes 208904 | tf_op jit(solution)/shard_map/ppermute | solution.py:94
  7.1 0.2 collective-permute-start.2
  7.3 1.3 %shard_map.96 = (bf16[256,768]{1,0:T(8,128)(2,1)S(1)}, bf16[128,768]{1,0:T(8,128)(2,1)S(1)}) custom-call(bf16[256,768]{1,0:T(8,128)(2,1)} %bitcast.10, bf16[256,768]{1,0:T(8,128)(2,1)} %bitcast.12, f32[8,128]{1,0:T(8,128)S(1)} %get-tuple-element.35.refs_2_), custom_call_target="tpu_custom_call" | custom-call | flops 3932160 | bytes 1179648 | tf_op jit(solution)/shard_map/pallas_call | solution.py:109
  8.6 1.6 %collective-permute-start.9 = (bf16[256,768]{1,0:T(8,128)(2,1)S(1)}, bf16[256,768]{1,0:T(8,128)(2,1)S(1)}, u32[]{:S(2)}, u32[]{:S(2)}) collective-permute-start(bf16[256,768]{1,0:T(8,128)(2,1)S(1)} %get-tuple-element.47.hidden_ref), channel_id=1, source_target_pairs={{0,16},{16,0},{1,17},{17,1},{2,18},{18,2},{3,19},{19,3},{4,20},{20... | collective-permute-start | bytes 1179656 | tf_op jit(solution)/shard_map/ppermute | solution.py:94
  10.2 0.1 collective-permute-done
  10.3 1.7 %collective-permute-start.3 = (bf16[32,2176]{1,0:T(8,128)(2,1)S(1)}, bf16[32,2176]{1,0:T(8,128)(2,1)S(1)}, u32[]{:S(2)}, u32[]{:S(2)}) collective-permute-start(bf16[32,2176]{1,0:T(8,128)(2,1)S(1)} %constant_dynamic-update-slice_fusion.refs_0_), channel_id=1, source_target_pairs={{0,8},{4,12},{8,0},{12,4},{1,9},{5,13},{9,1},{13,5},{2,10},{6,14},... | collective-permute-start | bytes 417800 | tf_op jit(solution)/shard_map/ppermute | solution.py:94
  12.0 0.6 %collective-permute-done.1 = bf16[16,2176]{1,0:T(8,128)(2,1)S(1)} collective-permute-done((bf16[16,2176]{1,0:T(8,128)(2,1)S(1)}, bf16[16,2176]{1,0:T(8,128)(2,1)S(1)}, u32[]{:S(2)}, u32[]{:S(2)}) %collective-permute-start.1) | collective-permute-done | bytes 69664 | tf_op jit(solution)/shard_map/ppermute | solution.py:94
  12.5 0.3 collective-permute-done.2
  12.8 0.0 collective-permute-start.6
  12.9 1.7 %collective-permute-start.5 = (bf16[32,2176]{1,0:T(8,128)(2,1)S(1)}, bf16[32,2176]{1,0:T(8,128)(2,1)S(1)}, u32[]{:S(2)}, u32[]{:S(2)}) collective-permute-start(bf16[32,2176]{1,0:T(8,128)(2,1)S(1)} %constant_dynamic-update-slice_fusion.2.refs_1_), channel_id=1, source_target_pairs={{0,8},{4,12},{8,0},{12,4},{1,9},{5,13},{9,1},{13,5},{2,10},{6,14},... | collective-permute-start | bytes 417800 | tf_op jit(solution)/shard_map/ppermute | solution.py:94
  14.5 0.0 collective-permute-done.4.refs_1_
  14.5 2.6 %shard_map.94 = (bf16[512,768]{1,0:T(8,128)(2,1)S(1)}, bf16[512,768]{1,0:T(8,128)(2,1)S(1)}, bf16[512,768]{1,0:T(8,128)(2,1)S(1)}, bf16[512,768]{1,0:T(8,128)(2,...) custom-call(bf16[768,2048]{1,0:T(8,128)(2,1)} %bitcast.19, ...), custom_call_target="tpu_custom_call" | custom-call | bytes 12582912 | tf_op jit(solution)/shard_map/pallas_call | solution.py:109
  17.1 0.0 collective-permute-done.3.refs_2_
  17.1 1.9 %collective-permute-done.5.refs_3_ = bf16[32,2176]{1,0:T(8,128)(2,1)S(1)} collective-permute-done((bf16[32,2176]{1,0:T(8,128)(2,1)S(1)}, bf16[32,2176]{1,0:T(8,128)(2,1)S(1)}, u32[]{:S(2)}, u32[]{:S(2)}) %collective-permute-start.5) | collective-permute-done | bytes 139296 | tf_op jit(solution)/shard_map/ppermute | solution.py:94
  19.1 0.0 copy-start
  19.1 0.0 copy-start.1
  19.1 1.6 %collective-permute-start.10 = (bf16[128,1152]{1,0:T(8,128)(2,1)S(1)}, bf16[128,1152]{1,0:T(8,128)(2,1)S(1)}, u32[]{:S(2)}, u32[]{:S(2)}) collective-permute-start(bf16[128,1152]{1,0:T(8,128)(2,1)S(1)} %get-tuple-element.57), channel_id=1, source_target_pairs={{0,16},{16,0},{1,17},{17,1},{2,18},{18,2},{3,19},{19,3},{4,20},{20... | collective-permute-start | bytes 884744 | tf_op jit(solution)/shard_map/ppermute | solution.py:94
  20.7 0.0 collective-permute-done.6.other_hidden_ref
  20.7 1.1 %shard_map.97 = (f32[128,768]{1,0:T(8,128)S(1)}, f32[128,768]{1,0:T(8,128)S(1)}, f32[2,128]{1,0:T(2,128)S(1)}) custom-call(bf16[256,768]{1,0:T(8,128)(2,1)S(1)} %get-tuple-element.47.hidden_ref, bf16[128,768]{1,0:T(8,128)(2,1)S(1)} %collective-permute-done.6.other_hidden_ref, bf16[32,2176]{1,0:T(8,128)(2,1)S(1)} %constant_dynamic-update-slice_fusion.refs_0_, ...), custom_call_target="tpu_custom_call" | custom-call | flops 805306368 | bytes 6291456 | tf_op jit(solution)/shard_map/pallas_call | solution.py:109
  21.8 0.0 collective-permute-done.9.refs_0_
  21.8 2.8 %collective-permute-start.13 = (f32[1,2,128]{2,1,0:T(2,128)S(1)}, f32[1,2,128]{2,1,0:T(2,128)S(1)}, u32[]{:S(2)}, u32[]{:S(2)}) collective-permute-start(f32[1,2,128]{2,1,0:T(2,128)S(1)} %bitcast.16), channel_id=1, source_target_pairs={{0,2},{1,3},{2,0},{3,1},{4,6},{5,7},{6,4},{7,5},{8,10},{9,11},{10,... | collective-permute-start | bytes 3080 | tf_op jit(solution)/shard_map/ppermute | solution.py:94
  24.6 0.0 copy-done
  24.6 0.0 copy-done.1
  24.6 0.3 shard_map.98
  24.9 0.1 collective-permute-start.8
  25.0 0.5 %collective-permute-start.7 = (bf16[128,1152]{1,0:T(8,128)(2,1)S(1)}, bf16[128,1152]{1,0:T(8,128)(2,1)S(1)}, u32[]{:S(2)}, u32[]{:S(2)}) collective-permute-start(bf16[128,1152]{1,0:T(8,128)(2,1)S(1)} %get-tuple-element.51.held_ref), channel_id=1, source_target_pairs={{0,4},{4,0},{8,12},{12,8},{1,5},{5,1},{9,13},{13,9},{2,6},{6,2},{1... | collective-permute-start | bytes 884744 | tf_op jit(solution)/shard_map/ppermute | solution.py:94
  25.5 0.8 %collective-permute-done.13 = f32[1,2,128]{2,1,0:T(2,128)S(1)} collective-permute-done((f32[1,2,128]{2,1,0:T(2,128)S(1)}, f32[1,2,128]{2,1,0:T(2,128)S(1)}, u32[]{:S(2)}, u32[]{:S(2)}) %collective-permute-start.13) | collective-permute-done | bytes 1056 | tf_op jit(solution)/shard_map/ppermute | solution.py:94
  26.4 2.3 %collective-permute-start.14 = (f32[2,2,128]{2,1,0:T(2,128)S(1)}, f32[2,2,128]{2,1,0:T(2,128)S(1)}, u32[]{:S(2)}, u32[]{:S(2)}) collective-permute-start(f32[2,2,128]{2,1,0:T(2,128)S(1)} %constant_dynamic-update-slice_fusion.4), channel_id=1, source_target_pairs={{0,1},{1,0},{2,3},{3,2},{4,5},{5,4},{6,7},{7,6},{8,9},{9,8},{10,11... | collective-permute-start | bytes 6152 | tf_op jit(solution)/shard_map/ppermute | solution.py:94
  28.7 0.0 collective-permute-done.10.refs_1_
  28.7 0.1 collective-permute-start.11
  28.8 0.5 %collective-permute-start.12 = (bf16[64,1152]{1,0:T(8,128)(2,1)S(1)}, bf16[64,1152]{1,0:T(8,128)(2,1)S(1)}, u32[]{:S(2)}, u32[]{:S(2)}) collective-permute-start(bf16[64,1152]{1,0:T(8,128)(2,1)S(1)} %get-tuple-element.64), channel_id=1, source_target_pairs={{0,4},{4,0},{8,12},{12,8},{1,5},{5,1},{9,13},{13,9},{2,6},{6,2},{1... | collective-permute-start | bytes 442376 | tf_op jit(solution)/shard_map/ppermute | solution.py:94
  29.3 0.0 collective-permute-done.7.rest_ref
  29.3 0.0 collective-permute-done.8.rest_back_ref
  29.3 0.0 copy-start.2
  29.3 1.2 %shard_map.99 = (bf16[256,768]{1,0:T(8,128)(2,1)}, bf16[256,768]{1,0:T(8,128)(2,1)}, bf16[256,768]{1,0:T(8,128)(2,1)S(1)}) custom-call(bf16[128,1152]{1,0:T(8,128)(2,1)S(1)} %get-tuple-element.51.held_ref, bf16[128,1152]{1,0:T(8,128)(2,1)S(1)} %collective-permute-done.7.rest_ref, f32[128,768]{1,0:T(8,128)S(1)} %get-tuple-element.52.back_ref, ...), custom_call_target="tpu_custom_call" | custom-call | flops 5898240 | bytes 2359296 | tf_op jit(solution)/shard_map/pallas_call | solution.py:109
  30.5 0.0 collective-permute-done.14
  30.5 1.6 %collective-permute-start.15 = (f32[4,2,128]{2,1,0:T(2,128)S(1)}, f32[4,2,128]{2,1,0:T(2,128)S(1)}, u32[]{:S(2)}, u32[]{:S(2)}) collective-permute-start(f32[4,2,128]{2,1,0:T(2,128)S(1)} %constant_dynamic-update-slice_fusion.6), channel_id=1, source_target_pairs={{0,8},{4,12},{8,0},{12,4},{1,9},{5,13},{9,1},{13,5},{2,10},{6,14},... | collective-permute-start | bytes 12296 | tf_op jit(solution)/shard_map/ppermute | solution.py:94
  32.1 0.0 collective-permute-done.11.refs_2_
  32.1 0.0 collective-permute-done.12.refs_3_
  32.1 1.9 %shard_map.100 = bf16[768,1024]{1,0:T(8,128)(2,1)} custom-call(bf16[256,768]{1,0:T(8,128)(2,1)S(1)} %get-tuple-element.56.scaled_ref, bf16[128,1152]{1,0:T(8,128)(2,1)S(1)} %get-tuple-element.51.held_ref, bf16[128,1152]{1,0:T(8,128)(2,1)S(1)} %collective-permute-done.7.rest_ref, bf16[256,768]{1,0:T(8,128)(2,1)S(1)} %collective-permute-done.9.refs_0_, ...), custom_call_target="tpu_custom_call" | custom-call | flops 805306368 | bytes 3145728 | tf_op jit(solution)/shard_map/pallas_call | solution.py:109
  34.0 0.2 collective-permute-done.15
  34.2 0.0 copy-done.2
  34.2 0.7 %shard_map.101 = f32[8,16]{1,0:T(8,128)} custom-call(s32[8,16]{1,0:T(8,128)S(1)} %bitcast.15, f32[8,2,128]{2,1,0:T(2,128)S(1)} %pad_maximum_fusion.sums_ref), custom_call_target="tpu_custom_call" | custom-call | flops 256 | bytes 256 | tf_op jit(solution)/shard_map/pallas_call | solution.py:109
  (11 shorter events, 0.1 us)
Async XLA Ops:
  1.5 13.0 %collective-permute-start.4 = (bf16[768,2048]{1,0:T(8,128)(2,1)}, bf16[768,2048]{1,0:T(8,128)(2,1)S(1)}, u32[]{:S(2)}, u32[]{:S(2)}) collective-permute-start(bf16[768,2048]{1,0:T(8,128)(2,1)} %bitcast.18), channel_id=1, source_target_pairs={{0,4},{4,0},{8,12},{12,8},{1,5},{5,1},{9,13},{13,9},{2,6},{6,2},{1... | collective-permute-start | bytes 9437192 | tf_op jit(solution)/shard_map/ppermute | solution.py:94
  2.1 8.2 %collective-permute-start = (bf16[16,2176]{1,0:T(8,128)(2,1)S(1)}, bf16[16,2176]{1,0:T(8,128)(2,1)S(1)}, u32[]{:S(2)}, u32[]{:S(2)}) collective-permute-start(bf16[16,2176]{1,0:T(8,128)(2,1)S(1)} %get-tuple-element.34), channel_id=1, source_target_pairs={{0,2},{1,3},{2,0},{3,1},{4,6},{5,7},{6,4},{7,5},{8,10},{9,11},{10,... | collective-permute-start | bytes 208904 | tf_op jit(solution)/shard_map/ppermute | solution.py:94
  5.7 6.8 %collective-permute-start.1 = (bf16[16,2176]{1,0:T(8,128)(2,1)S(1)}, bf16[16,2176]{1,0:T(8,128)(2,1)S(1)}, u32[]{:S(2)}, u32[]{:S(2)}) collective-permute-start(bf16[16,2176]{1,0:T(8,128)(2,1)S(1)} %get-tuple-element.34), channel_id=1, source_target_pairs={{0,3},{1,2},{2,1},{3,0},{4,7},{5,6},{6,5},{7,4},{8,11},{9,10},{10,... | collective-permute-start | bytes 208904 | tf_op jit(solution)/shard_map/ppermute | solution.py:94
  7.1 5.8 %collective-permute-start.2 = (bf16[16,2176]{1,0:T(8,128)(2,1)S(1)}, bf16[16,2176]{1,0:T(8,128)(2,1)S(1)}, u32[]{:S(2)}, u32[]{:S(2)}) collective-permute-start(bf16[16,2176]{1,0:T(8,128)(2,1)S(1)} %get-tuple-element.34), channel_id=1, source_target_pairs={{0,1},{1,0},{2,3},{3,2},{4,5},{5,4},{6,7},{7,6},{8,9},{9,8},{10,11... | collective-permute-start | bytes 208904 | tf_op jit(solution)/shard_map/ppermute | solution.py:94
  8.6 13.2 %collective-permute-start.9 = (bf16[256,768]{1,0:T(8,128)(2,1)S(1)}, bf16[256,768]{1,0:T(8,128)(2,1)S(1)}, u32[]{:S(2)}, u32[]{:S(2)}) collective-permute-start(bf16[256,768]{1,0:T(8,128)(2,1)S(1)} %get-tuple-element.47.hidden_ref), channel_id=1, source_target_pairs={{0,16},{16,0},{1,17},{17,1},{2,18},{18,2},{3,19},{19,3},{4,20},{20... | collective-permute-start | bytes 1179656 | tf_op jit(solution)/shard_map/ppermute | solution.py:94
  10.3 6.9 %collective-permute-start.3 = (bf16[32,2176]{1,0:T(8,128)(2,1)S(1)}, bf16[32,2176]{1,0:T(8,128)(2,1)S(1)}, u32[]{:S(2)}, u32[]{:S(2)}) collective-permute-start(bf16[32,2176]{1,0:T(8,128)(2,1)S(1)} %constant_dynamic-update-slice_fusion.refs_0_), channel_id=1, source_target_pairs={{0,8},{4,12},{8,0},{12,4},{1,9},{5,13},{9,1},{13,5},{2,10},{6,14},... | collective-permute-start | bytes 417800 | tf_op jit(solution)/shard_map/ppermute | solution.py:94
  12.8 7.9 %collective-permute-start.6 = (bf16[128,768]{1,0:T(8,128)(2,1)S(1)}, bf16[128,768]{1,0:T(8,128)(2,1)S(1)}, u32[]{:S(2)}, u32[]{:S(2)}) collective-permute-start(bf16[128,768]{1,0:T(8,128)(2,1)S(1)} %get-tuple-element.49), channel_id=1, source_target_pairs={{0,4},{4,0},{8,12},{12,8},{1,5},{5,1},{9,13},{13,9},{2,6},{6,2},{1... | collective-permute-start | bytes 589832 | tf_op jit(solution)/shard_map/ppermute | solution.py:94
  12.9 6.1 %collective-permute-start.5 = (bf16[32,2176]{1,0:T(8,128)(2,1)S(1)}, bf16[32,2176]{1,0:T(8,128)(2,1)S(1)}, u32[]{:S(2)}, u32[]{:S(2)}) collective-permute-start(bf16[32,2176]{1,0:T(8,128)(2,1)S(1)} %constant_dynamic-update-slice_fusion.2.refs_1_), channel_id=1, source_target_pairs={{0,8},{4,12},{8,0},{12,4},{1,9},{5,13},{9,1},{13,5},{2,10},{6,14},... | collective-permute-start | bytes 417800 | tf_op jit(solution)/shard_map/ppermute | solution.py:94
  19.1 5.6 %copy-start = (bf16[1,1,256,768]{3,2,1,0:T(8,128)(2,1)S(1)}, bf16[1,1,256,768]{3,2,1,0:T(8,128)(2,1)}, u32[]{:S(2)}) copy-start(bf16[1,1,256,768]{3,2,1,0:T(8,128)(2,1)} %param.9) | copy-start | bytes 1179652
  19.1 5.6 %copy-start.1 = (bf16[1,1,256,768]{3,2,1,0:T(8,128)(2,1)S(1)}, bf16[1,1,256,768]{3,2,1,0:T(8,128)(2,1)}, u32[]{:S(2)}) copy-start(bf16[1,1,256,768]{3,2,1,0:T(8,128)(2,1)} %param.10) | copy-start | bytes 1179652
  19.1 9.6 %collective-permute-start.10 = (bf16[128,1152]{1,0:T(8,128)(2,1)S(1)}, bf16[128,1152]{1,0:T(8,128)(2,1)S(1)}, u32[]{:S(2)}, u32[]{:S(2)}) collective-permute-start(bf16[128,1152]{1,0:T(8,128)(2,1)S(1)} %get-tuple-element.57), channel_id=1, source_target_pairs={{0,16},{16,0},{1,17},{17,1},{2,18},{18,2},{3,19},{19,3},{4,20},{20... | collective-permute-start | bytes 884744 | tf_op jit(solution)/shard_map/ppermute | solution.py:94
  21.8 4.5 %collective-permute-start.13 = (f32[1,2,128]{2,1,0:T(2,128)S(1)}, f32[1,2,128]{2,1,0:T(2,128)S(1)}, u32[]{:S(2)}, u32[]{:S(2)}) collective-permute-start(f32[1,2,128]{2,1,0:T(2,128)S(1)} %bitcast.16), channel_id=1, source_target_pairs={{0,2},{1,3},{2,0},{3,1},{4,6},{5,7},{6,4},{7,5},{8,10},{9,11},{10,... | collective-permute-start | bytes 3080 | tf_op jit(solution)/shard_map/ppermute | solution.py:94
  24.9 4.4 %collective-permute-start.8 = (f32[128,768]{1,0:T(8,128)S(1)}, f32[128,768]{1,0:T(8,128)S(1)}, u32[]{:S(2)}, u32[]{:S(2)}) collective-permute-start(f32[128,768]{1,0:T(8,128)S(1)} %get-tuple-element.53), channel_id=1, source_target_pairs={{0,4},{4,0},{8,12},{12,8},{1,5},{5,1},{9,13},{13,9},{2,6},{6,2},{1... | collective-permute-start | bytes 1179656 | tf_op jit(solution)/shard_map/ppermute | solution.py:94
  25.0 4.3 %collective-permute-start.7 = (bf16[128,1152]{1,0:T(8,128)(2,1)S(1)}, bf16[128,1152]{1,0:T(8,128)(2,1)S(1)}, u32[]{:S(2)}, u32[]{:S(2)}) collective-permute-start(bf16[128,1152]{1,0:T(8,128)(2,1)S(1)} %get-tuple-element.51.held_ref), channel_id=1, source_target_pairs={{0,4},{4,0},{8,12},{12,8},{1,5},{5,1},{9,13},{13,9},{2,6},{6,2},{1... | collective-permute-start | bytes 884744 | tf_op jit(solution)/shard_map/ppermute | solution.py:94
  26.4 4.1 %collective-permute-start.14 = (f32[2,2,128]{2,1,0:T(2,128)S(1)}, f32[2,2,128]{2,1,0:T(2,128)S(1)}, u32[]{:S(2)}, u32[]{:S(2)}) collective-permute-start(f32[2,2,128]{2,1,0:T(2,128)S(1)} %constant_dynamic-update-slice_fusion.4), channel_id=1, source_target_pairs={{0,1},{1,0},{2,3},{3,2},{4,5},{5,4},{6,7},{7,6},{8,9},{9,8},{10,11... | collective-permute-start | bytes 6152 | tf_op jit(solution)/shard_map/ppermute | solution.py:94
  28.7 3.4 %collective-permute-start.11 = (bf16[64,1152]{1,0:T(8,128)(2,1)S(1)}, bf16[64,1152]{1,0:T(8,128)(2,1)S(1)}, u32[]{:S(2)}, u32[]{:S(2)}) collective-permute-start(bf16[64,1152]{1,0:T(8,128)(2,1)S(1)} %get-tuple-element.65), channel_id=1, source_target_pairs={{0,4},{4,0},{8,12},{12,8},{1,5},{5,1},{9,13},{13,9},{2,6},{6,2},{1... | collective-permute-start | bytes 442376 | tf_op jit(solution)/shard_map/ppermute | solution.py:94
  28.8 3.3 %collective-permute-start.12 = (bf16[64,1152]{1,0:T(8,128)(2,1)S(1)}, bf16[64,1152]{1,0:T(8,128)(2,1)S(1)}, u32[]{:S(2)}, u32[]{:S(2)}) collective-permute-start(bf16[64,1152]{1,0:T(8,128)(2,1)S(1)} %get-tuple-element.64), channel_id=1, source_target_pairs={{0,4},{4,0},{8,12},{12,8},{1,5},{5,1},{9,13},{13,9},{2,6},{6,2},{1... | collective-permute-start | bytes 442376 | tf_op jit(solution)/shard_map/ppermute | solution.py:94
  29.3 4.9 %copy-start.2 = (s32[16,8]{0,1:T(8,128)S(1)}, s32[16,8]{0,1:T(8,128)}, u32[]{:S(2)}) copy-start(s32[16,8]{0,1:T(8,128)} %param.7) | copy-start | bytes 1540
  30.5 3.7 %collective-permute-start.15 = (f32[4,2,128]{2,1,0:T(2,128)S(1)}, f32[4,2,128]{2,1,0:T(2,128)S(1)}, u32[]{:S(2)}, u32[]{:S(2)}) collective-permute-start(f32[4,2,128]{2,1,0:T(2,128)S(1)} %constant_dynamic-update-slice_fusion.6), channel_id=1, source_target_pairs={{0,8},{4,12},{8,0},{12,4},{1,9},{5,13},{9,1},{13,5},{2,10},{6,14},... | collective-permute-start | bytes 12296 | tf_op jit(solution)/shard_map/ppermute | solution.py:94
